TPU v7x, 256 devices: a whole 4x4x8 slice. The times are simulated.
256 devices in a mesh: gx: 4 (over x), gy: 8 (over z), gz: 8 (over y, core).
Axes of the slice: x: 4, y: 4, z: 8, core: 2. Of those that a mesh axis runs over, the one named last changes fastest.
Arguments:
- rhs: float32 [7, 7, 7, 4, 32, 1024], P(None, None, None, 'gx', 'gy', 'gz'), may hold values from -6 to 6
- orders: int32 [4, 32, 1024], P('gx', 'gy', 'gz'), may hold values from 3 to 6
Outputs:
- smoothed: float32 [7, 7, 7, 4, 32, 1024], P(None, None, None, 'gx', 'gy', 'gz')
- coarse_residual: float32 [4, 32, 1024], P('gx', 'gy')
All inputs are finite; a program needn't handle non-finite values.
Results may differ from a plain program's by a relative error of at most 0.00016.
Values sent between devices are 32-bit elements; how exact they have to be, the bound alone decides.
No kernel may reach another device: no remote copies, remote signals or barrier semaphores. Data moves between devices by JAX's collectives and lax.ppermute only.
A program may use at most 64 MiB of HBM per device.

v0:
```python
import jax
import jax.numpy as jnp
import numpy as np
from jax import lax
from jax.experimental import pallas as pl
from jax.experimental.pallas import tpu as pltpu
from jax.sharding import PartitionSpec as P

PENALTY = 49.0
EIGEN_HIGH = 2.4
EIGEN_LOW = 0.24
THETA = 0.5 * (EIGEN_HIGH + EIGEN_LOW)
DELTA = 0.5 * (EIGEN_HIGH - EIGEN_LOW)
RHO_FIRST = DELTA / THETA
RHO_SECOND = 1.0 / (2.0 * THETA / DELTA - RHO_FIRST)
MODES = 7
PAIRS = 4
FACE_ROWS = 14


def basis_tables():
    degree = np.arange(MODES)
    normed = np.sqrt((2.0 * degree + 1.0) / 2.0)
    smaller = np.minimum(degree[:, None], degree[None, :])
    parity = (degree[:, None] + degree[None, :]) % 2 == 0
    stiffness = np.where(parity, normed[:, None] * normed[None, :] * smaller * (smaller + 1), 0.0)
    signs = (-1.0) ** degree
    slope = normed * degree * (degree + 1) / 2.0
    high, high_slope = normed, slope
    low, low_slope = normed * signs, -slope * signs
    own = (
        stiffness
        + PENALTY * (np.outer(high, high) + np.outer(low, low))
        - 0.5 * (np.outer(high, high_slope) + np.outer(high_slope, high))
        + 0.5 * (np.outer(low, low_slope) + np.outer(low_slope, low))
    )
    own = np.where(parity, own, 0.0)
    to_next = np.outer(low, 0.5 * high_slope - PENALTY * high) - 0.5 * np.outer(low_slope, high)
    to_last = np.outer(high, -PENALTY * low - 0.5 * low_slope) + 0.5 * np.outer(high_slope, low)
    one_axis = normed * normed * degree * (degree + 1) + 2.0 * (
        PENALTY * normed * normed - normed * slope
    )
    third = np.sqrt(1.5) / 3.0
    vertex = np.zeros((MODES, 2))
    vertex[0] = np.sqrt(0.5)
    vertex[1] = -third, third
    spread = np.stack(
        [
            vertex[:, 0] @ to_last,
            vertex[:, 1] @ to_last + vertex[:, 0] @ own,
            vertex[:, 1] @ own + vertex[:, 0] @ to_next,
            vertex[:, 1] @ to_next,
        ]
    )
    return normed, slope, own, one_axis, spread, third


NORMED, SLOPE, OWN, ONE_AXIS, SPREAD, THIRD = basis_tables()
ROOT_HALF = float(np.sqrt(0.5))


def diag(a, b, e):
    return float((ONE_AXIS[a] + ONE_AXIS[b] + ONE_AXIS[e]) / PENALTY)


def half_mask():
    return lax.broadcasted_iota(jnp.int32, (8, 128), 0) < 4


def row_in_half():
    return lax.broadcasted_iota(jnp.int32, (8, 128), 0) % 4


def lanes():
    return lax.broadcasted_iota(jnp.int32, (8, 128), 1)


def swap(value):
    return pltpu.roll(value, 4, 0)


class Pairs:
    def __init__(self):
        self.top = half_mask()
        self.known = {}

    def __call__(self, upper, lower):
        key = (float(upper), float(lower))
        if key[0] == key[1]:
            return jnp.float32(key[0])
        if key not in self.known:
            self.known[key] = jnp.where(self.top, jnp.float32(key[0]), jnp.float32(key[1]))
        return self.known[key]

    def once(self, upper, lower):
        if float(upper) == float(lower):
            return jnp.float32(upper)
        return jnp.where(self.top, jnp.float32(upper), jnp.float32(lower))


def total(terms):
    terms = list(terms)
    while len(terms) > 1:
        terms = [
            terms[k] + terms[k + 1] if k + 1 < len(terms) else terms[k]
            for k in range(0, len(terms), 2)
        ]
    return terms[0]


def keep_masks(orders, top):
    both = jnp.concatenate([orders, orders], axis=0)
    known = {}

    def get(upper, lower):
        if (upper, lower) not in known:
            if upper == lower:
                bound = jnp.int32(upper)
            else:
                bound = jnp.where(top, jnp.int32(upper), jnp.int32(lower))
            known[upper, lower] = (both >= bound).astype(jnp.float32)
        return known[upper, lower]

    return get


def odd_of(pair):
    return min(2 * pair + 1, MODES - 1)


def line_traces(line):
    even = total(float(NORMED[n]) * line[n] for n in range(0, MODES, 2))
    odd = total(float(NORMED[n]) * line[n] for n in range(1, MODES, 2))
    even_slope = total(float(SLOPE[n]) * line[n] for n in range(2, MODES, 2))
    odd_slope = total(float(SLOPE[n]) * line[n] for n in range(1, MODES, 2))
    return even + odd, even_slope + odd_slope, even - odd, odd_slope - even_slope


def trace_kernel(
    rhs, orders, first, x_up, x_down, y_up, y_down, z_up, z_down, y_low, y_high, z_low, z_high
):
    pairs = Pairs()
    top = pairs.top
    keep = keep_masks(orders[0], top)
    row, lane = row_in_half(), lanes()
    for b in range(MODES):
        for e in range(MODES):
            column = []
            for i in range(PAIRS):
                upper = rhs[2 * i, b, e, 0]
                lower = rhs[2 * i + 1, b, e, 0] if 2 * i + 1 < MODES else jnp.zeros_like(upper)
                cell = jnp.concatenate([upper, lower], axis=0)
                mask = keep(max(2 * i, b, e), max(odd_of(i), b, e))
                scale = pairs.once(
                    1.0 / (THETA * diag(2 * i, b, e)), 1.0 / (THETA * diag(odd_of(i), b, e))
                )
                cell = cell * mask * scale
                first[i, b, e] = cell
                column.append(cell)
            odd = [odd_of(i) if 2 * i + 1 < MODES else None for i in range(PAIRS)]
            value = total(
                pairs(NORMED[2 * i], NORMED[odd[i]] if odd[i] else 0.0) * column[i]
                for i in range(PAIRS)
            )
            slope = total(
                pairs(SLOPE[2 * i], SLOPE[odd[i]] if odd[i] else 0.0) * column[i]
                for i in range(PAIRS)
            )
            sign = pairs(1.0, -1.0)
            both_value = sign * value + swap(value)
            both_value = jnp.where(top, value + swap(value), swap(value) - value)
            both_slope = jnp.where(top, slope + swap(slope), slope - swap(slope))
            x_up[b * MODES + e] = jnp.where(top, both_value, swap(both_slope))
            x_down[b * MODES + e] = jnp.where(top, swap(both_value), both_slope)
    packed_up = packed_down = None
    for kind in range(2):
        for i in range(PAIRS):
            for e in range(MODES):
                m = i * MODES + e
                q = m % 4
                line = [first[i, b, e] for b in range(MODES)]
                traces = line_traces(line)
                high, low = traces[kind], traces[2 + kind]
                y_high[kind, m] = high
                y_low[kind, m] = low
                up, down = pltpu.roll(high, 5 + q, 0), pltpu.roll(low, q, 0) if q else low
                packed_up = up if q == 0 else jnp.where(row == q, up, packed_up)
                packed_down = down if q == 0 else jnp.where(row == q, down, packed_down)
                if q == 3:
                    y_up[kind * 7 + m // 4] = packed_up
                    y_down[kind * 7 + m // 4] = packed_down
    packed_up = packed_down = jnp.zeros((8, 128), jnp.float32)
    for i in range(PAIRS):
        for b in range(MODES):
            m = i * MODES + b
            line = [first[i, b, e] for e in range(MODES)]
            traces = line_traces(line)
            for kind in range(2):
                high, low = traces[kind], traces[2 + kind]
                z_high[kind, m] = high
                z_low[kind, m] = low
                place = 2 * m + kind
                packed_up = jnp.where(lane == place, pltpu.roll(high, 1 + place, 1), packed_up)
                down = pltpu.roll(low, place, 1) if place else low
                packed_down = jnp.where(lane == place, down, packed_down)
    z_up[...] = packed_up
    z_down[...] = packed_down


def own_kernel(first, out):
    pairs = Pairs()
    for b in range(MODES):
        for e in range(MODES):
            column = [first[i, b, e] for i in range(PAIRS)]
            for i in range(PAIRS):
                terms = []
                for j in range(PAIRS):
                    lower = OWN[2 * i + 1, 2 * j + 1] if max(i, j) < 3 else 0.0
                    terms.append(pairs(OWN[2 * i, 2 * j], lower) * column[j])
                out[i, b, e] = total(terms)
    for i in range(PAIRS):
        for b in range(MODES):
            line = [first[i, b, e] for e in range(MODES)]
            for n in range(MODES):
                out[i, b, n] += total(
                    float(OWN[n, k]) * line[k] for k in range(n % 2, MODES, 2)
                )
        for e in range(MODES):
            line = [first[i, b, e] for b in range(MODES)]
            for n in range(MODES):
                out[i, n, e] += total(
                    float(OWN[n, k]) * line[k] for k in range(n % 2, MODES, 2)
                )


def neighbour_line(low_value, low_slope, high_value, high_slope):
    plus, minus = high_value + low_value, high_value - low_value
    even = 0.5 * (low_slope - high_slope) - PENALTY * plus
    odd = -0.5 * (low_slope + high_slope) - PENALTY * minus
    return (even, 0.5 * plus), (odd, 0.5 * minus)


def vertex_pair(first_mode, second_mode):
    base, tilt = ROOT_HALF * first_mode, THIRD * second_mode
    return base - tilt, base + tilt


def sum_to_vertices(grid, pairs, row, lane):
    top = pairs.top
    rows = {}
    for (dy, dz), value in grid.items():
        rows.setdefault(dy, []).append((dz, value))
    result = [[[], []], [[], []]]
    for dy, entries in rows.items():
        inner, outer = [], []
        for dz, value in entries:
            if dz == 0:
                inner.append(value)
                continue
            moved = pltpu.roll(value, dz % 128, 1)
            inside = lane >= dz if dz > 0 else lane < 128 + dz
            inner.append(jnp.where(inside, moved, 0.0))
            outer.append(jnp.where(inside, 0.0, moved))
        for beyond, terms in ((0, inner), (1, outer)):
            if not terms:
                continue
            value = total(terms)
            if dy == 0:
                result[0][beyond].append(value)
                continue
            moved = pltpu.roll(value, dy % 8, 0)
            inside = row >= dy if dy > 0 else row < 4 + dy
            result[0][beyond].append(jnp.where(inside, moved, 0.0))
            result[1][beyond].append(jnp.where(inside, 0.0, swap(moved)))
    return [[total(result[r][z]) for z in range(2)] for r in range(2)]


def finish_kernel(
    first, local, orders, x_low, x_high, y_low, y_high, z_low, z_high,
    y_below, y_above, z_below, z_above, smoothed, here, ahead, behind, far, field,
):
    pairs = Pairs()
    top = pairs.top
    row, lane = row_in_half(), lanes()
    keep = keep_masks(orders[0], top)

    def inside(axis, distance):
        place = lax.axis_index(axis) + distance
        return jnp.where((place >= 0) & (place < lax.axis_size(axis)), 1.0, 0.0).astype(
            jnp.float32
        )

    x_has_low, x_has_high = inside("gx", -1), inside("gx", 1)
    y_has_low, y_has_high = inside("gy", -1), inside("gy", 1)
    z_has_low, z_has_high = inside("gz", -1), inside("gz", 1)
    for b in range(MODES):
        for e in range(MODES):
            below = x_has_low * x_low[b * MODES + e]
            above = x_has_high * x_high[b * MODES + e]
            plus, minus = above + below, swap(above - below)
            slope = 0.5 * jnp.where(top, plus, minus)
            value = (-2.0 * PENALTY) * slope - 0.5 * jnp.where(top, minus, plus)
            for i in range(PAIRS):
                last = 2 * i + 1 >= MODES
                k = odd_of(i)
                local[i, b, e] += (
                    pairs(NORMED[2 * i], 0.0 if last else NORMED[k]) * value
                    + pairs(SLOPE[2 * i], 0.0 if last else SLOPE[k]) * slope
                )
    for i in range(PAIRS):
        for e in range(MODES):
            m = i * MODES + e
            q = m % 4
            seen = []
            for kind in range(2):
                halo = y_has_low * y_low[kind * 7 + m // 4]
                halo = pltpu.roll(halo, 8 - q, 0) if q else halo
                moved = pltpu.roll(y_below[kind, m], 1, 0)
                seen.append(jnp.where(row == 0, halo, moved))
            for kind in range(2):
                halo = y_has_high * y_high[kind * 7 + m // 4]
                halo = pltpu.roll(halo, 3 - q, 0) if q < 3 else halo
                moved = pltpu.roll(y_above[kind, m], 7, 0)
                seen.append(jnp.where(row == 3, halo, moved))
            parts = neighbour_line(*seen)
            for n in range(MODES):
                value, slope = parts[n % 2]
                add = float(NORMED[n]) * value
                local[i, n, e] += add + float(SLOPE[n]) * slope if n else add
    z_low_halo, z_high_halo = z_has_low * z_low[...], z_has_high * z_high[...]
    for i in range(PAIRS):
        for b in range(MODES):
            m = i * MODES + b
            seen = []
            for kind in range(2):
                place = 2 * m + kind
                halo = pltpu.roll(z_low_halo, 128 - place, 1) if place else z_low_halo
                moved = pltpu.roll(z_below[kind, m], 1, 1)
                seen.append(jnp.where(lane == 0, halo, moved))
            for kind in range(2):
                place = 2 * m + kind
                halo = pltpu.roll(z_high_halo, 127 - place, 1)
                moved = pltpu.roll(z_above[kind, m], 127, 1)
                seen.append(jnp.where(lane == 127, halo, moved))
            parts = neighbour_line(*seen)
            for e in range(MODES):
                value, slope = parts[e % 2]
                add = float(NORMED[e]) * value
                if e:
                    add = add + float(SLOPE[e]) * slope
                applied = local[i, b, e] + add
                one = 2.0 * RHO_SECOND / (DELTA * PENALTY)
                scale = pairs.once(one / diag(2 * i, b, e), one / diag(odd_of(i), b, e))
                mask = keep(max(2 * i, b, e), max(odd_of(i), b, e))
                kappa = 1.0 + RHO_SECOND * RHO_FIRST + 2.0 * RHO_SECOND * THETA / DELTA
                after = kappa * first[i, b, e] - (mask * scale) * applied
                field[i, b, e] = after
                smoothed[2 * i, b, e, 0] = after[:4]
                if 2 * i + 1 < MODES:
                    smoothed[2 * i + 1, b, e, 0] = after[4:]

    grid = {}

    def add(key, value):
        grid[key] = grid[key] + value if key in grid else value

    spread = -SPREAD / PENALTY
    for e in range(MODES):
        low, high = vertex_pair(field[0, 0, e], field[0, 1, e])
        for dz in range(-1, 3):
            add((0, dz), float(spread[dz + 1, e]) * low)
            add((1, dz), float(spread[dz + 1, e]) * high)
    for b in range(MODES):
        low, high = vertex_pair(field[0, b, 0], field[0, b, 1])
        for dy in range(-1, 3):
            add((dy, 0), float(spread[dy + 1, b]) * low)
            add((dy, 1), float(spread[dy + 1, b]) * high)
    force = [
        [
            pairs.once(THETA * diag(0, b, e), THETA * diag(1, b, e)) * first[0, b, e]
            for e in range(2)
        ]
        for b in range(2)
    ]
    force = [vertex_pair(force[0][e], force[1][e]) for e in range(2)]
    for dy in range(2):
        low, high = vertex_pair(force[0][dy], force[1][dy])
        add((dy, 0), low)
        add((dy, 1), high)
    kept, turned = pairs(ROOT_HALF, THIRD), pairs(-THIRD, ROOT_HALF)
    near = {key: kept * value + turned * swap(value) for key, value in grid.items()}
    outer = {}
    corners = []
    for i in range(PAIRS):
        line = [vertex_pair(field[i, 0, e], field[i, 1, e]) for e in range(2)]
        corners.append([vertex_pair(line[0][dy], line[1][dy]) for dy in range(2)])
    for dy in range(2):
        for dz in range(2):
            sums = []
            for dx in range(-1, 3):
                part = total(
                    pairs(
                        spread[dx + 1, 2 * i],
                        spread[dx + 1, 2 * i + 1] if 2 * i + 1 < MODES else 0.0,
                    )
                    * corners[i][dy][dz]
                    for i in range(PAIRS)
                )
                sums.append(part + swap(part))
            near[dy, dz] += jnp.where(top, sums[1], sums[2])
            outer[dy, dz] = jnp.where(top, sums[0], sums[3])
    near = sum_to_vertices(near, pairs, row, lane)
    outer = sum_to_vertices(outer, pairs, row, lane)
    for z in range(2):
        here[z] = jnp.where(top, near[0][z], swap(near[1][z]))
        ahead[z] = jnp.where(top, swap(near[0][z]), near[1][z])
        behind[z] = jnp.where(top, outer[0][z], swap(outer[1][z]))
        far[z] = jnp.where(top, swap(outer[0][z]), outer[1][z])


def shape(*dims):
    return jax.ShapeDtypeStruct(dims, jnp.float32)


def in_vmem(count):
    return [pl.BlockSpec(memory_space=pltpu.VMEM)] * count


def call(kernel, name, inputs, outputs, flops, scratch=(), alias=None):
    size = sum(4 * int(np.prod(o.shape)) for o in outputs) + sum(
        4 * int(np.prod(v.shape)) for v in inputs
    )
    return pl.pallas_call(
        kernel,
        out_shape=outputs,
        in_specs=in_vmem(len(inputs)),
        out_specs=in_vmem(len(outputs)),
        scratch_shapes=list(scratch),
        input_output_aliases=alias or {},
        name=name,
        cost_estimate=pl.CostEstimate(flops=flops, bytes_accessed=size, transcendentals=0),
        compiler_params=pltpu.CompilerParams(vmem_limit_bytes=24 * 1024 * 1024),
    )(*inputs)


def shift(value, axis, distance):
    count = lax.axis_size(axis)
    return lax.ppermute(value, axis, [(i, (i + distance) % count) for i in range(count)])


def inside(axis, distance):
    place = lax.axis_index(axis) + distance
    return ((place >= 0) & (place < lax.axis_size(axis))).astype(jnp.float32)


def per_device(rhs, orders):
    cells = (PAIRS, MODES, MODES, 8, 128)
    first, x_up, x_down, y_up, y_down, z_up, z_down, y_low, y_high, z_low, z_high = call(
        trace_kernel,
        "face_traces",
        (rhs, orders),
        (
            shape(*cells), shape(49, 8, 128), shape(49, 8, 128),
            shape(FACE_ROWS, 8, 128), shape(FACE_ROWS, 8, 128), shape(8, 128), shape(8, 128),
            shape(2, 28, 8, 128), shape(2, 28, 8, 128), shape(2, 28, 8, 128), shape(2, 28, 8, 128),
        ),
        4_000_000,
    )
    x_from_low, x_from_high = shift(x_up, "gx", 1), shift(x_down, "gx", -1)
    y_from_low, y_from_high = shift(y_up, "gy", 1), shift(y_down, "gy", -1)
    z_from_low, z_from_high = shift(z_up, "gz", 1), shift(z_down, "gz", -1)
    (local,) = call(own_kernel, "own_cells", (first,), (shape(*cells),), 4_000_000)
    smoothed, here, ahead, behind, far = call(
        finish_in_place,
        "smooth_and_restrict",
        (
            first, local, orders, x_from_low, x_from_high, y_from_low, y_from_high,
            z_from_low, z_from_high, y_high, y_low, z_high, z_low,
        ),
        (shape(*rhs.shape),) + (shape(2, 8, 128),) * 4,
        5_000_000,
        scratch=(pltpu.VMEM(cells, jnp.float32), pltpu.VMEM(cells, jnp.float32)),
    )
    sums = (
        here
        + inside("gx", -1) * shift(ahead, "gx", 1)
        + inside("gx", 1) * shift(behind, "gx", -1)
        + inside("gx", -2) * shift(far, "gx", 2)
    )
    from_low, from_high = shift(sums, "gy", 1), shift(sums, "gy", -1)
    row = lax.broadcasted_iota(jnp.int32, (1, 4, 1), 1)
    owned = (
        sums[:, :4]
        + jnp.where(row < 2, from_low[:, 4:], 0.0) * inside("gy", -1)
        + jnp.where(row == 3, from_high[:, 4:], 0.0) * inside("gy", 1)
    )
    return smoothed, gather_columns(owned)


def finish_in_place(
    first, local, orders, x_low, x_high, y_low, y_high, z_low, z_high,
    y_below, y_above, z_below, z_above, smoothed, here, ahead, behind, far, field, work,
):
    work[...] = local[...]
    finish_kernel(
        first, work, orders, x_low, x_high, y_low, y_high, z_low, z_high,
        y_below, y_above, z_below, z_above, smoothed, here, ahead, behind, far, field,
    )


def gather_columns(owned):
    count = lax.axis_size("gz")
    packed = owned.reshape(8, 128)
    me = lax.axis_index("gz")
    other = lax.ppermute(packed, "gz", [(i, i ^ 1) for i in range(count)])
    even = me % 2 == 0
    chip = jnp.stack([jnp.where(even, packed, other), jnp.where(even, other, packed)])
    chips = [chip] + [shift(chip, "gz", -2 * k) for k in range(1, count // 2)]
    blocks = jnp.concatenate(chips)
    blocks = jnp.roll(blocks, me - me % 2, axis=0)
    lane = lax.broadcasted_iota(jnp.int32, (1, 1, 128), 2)
    inner, outer = blocks[:, :4], blocks[:, 4:]
    zero = jnp.zeros_like(outer[:1])
    before = jnp.concatenate([zero, outer[:-1]])
    after = jnp.concatenate([outer[1:], zero])
    column = inner + jnp.where(lane < 2, before, 0.0) + jnp.where(lane == 127, after, 0.0)
    column = column.transpose(1, 0, 2).reshape(1, 4, 128 * count)
    place_y = lax.axis_index("gy") * 4 + jnp.arange(4)
    place_z = jnp.arange(128 * count)
    interior = (
        (lax.axis_index("gx") > 0) & (place_y > 0)[:, None] & (place_z > 0)[None, :]
    )
    return jnp.where(interior[None], column, 0.0)


def solution(mesh):
    return jax.shard_map(
        per_device,
        mesh=mesh,
        in_specs=(P(None, None, None, "gx", "gy", "gz"), P("gx", "gy", "gz")),
        out_specs=(P(None, None, None, "gx", "gy", "gz"), P("gx", "gy", None)),
        check_vma=False,
    )
```

profile of v0, /device:TPU:1, one launch (start us, length us, event | category | flops | bytes accessed | tf_op | source)
XLA Modules:
  0.0 43.2 jit_solution(17286394284757986774)
XLA Ops:
  0.6 0.0 copy-start
  0.6 1.1 %copy-done = f32[7,7,7,1,4,128]{5,4,3,2,1,0:T(4,128)S(1)} copy-done((f32[7,7,7,1,4,128]{5,4,3,2,1,0:T(4,128)S(1)}, f32[7,7,7,1,4,128]{5,4,3,2,1,0:T(4,128)}, u32[]{:S(2)}) %copy-start) | copy-done | bytes 702488
  1.7 0.0 copy-start.1
  1.7 0.7 %copy-done.1 = s32[1,4,128]{2,1,0:T(4,128)S(1)} copy-done((s32[1,4,128]{2,1,0:T(4,128)S(1)}, s32[1,4,128]{2,1,0:T(4,128)}, u32[]{:S(2)}) %copy-start.1) | copy-done | bytes 2072
  2.4 0.6 %face_traces.1 = (f32[4,7,7,8,128]{4,3,2,1,0:T(8,128)S(1)}, f32[49,8,128]{2,1,0:T(8,128)S(1)}, f32[49,8,128]{2,1,0:T(8,128)S(1)}, f32[14,8,128]{2,1,0:T(8,128)S(...) custom-call(f32[7,7,7,1,4,128]{5,4,3,2,1,0:T(4,128)S(1)} %copy-done,, ...), custom_call_target="tpu_custom_call" | custom-call | flops 4000000 | bytes 2949120 | tf_op jit(solution)/shard_map/face_traces/pallas_call | solution.py:433
  3.0 2.1 %collective-permute-start = (f32[49,8,128]{2,1,0:T(8,128)S(1)}, f32[49,8,128]{2,1,0:T(8,128)S(1)}, u32[]{:S(2)}, u32[]{:S(2)}) collective-permute-start(f32[49,8,128]{2,1,0:T(8,128)S(1)} %get-tuple-element.19), channel_id=1, source_target_pairs={{0,64},{64,128},{128,192},{192,0},{1,65},{65,129},{129,193},{193,1... | collective-permute-start | bytes 602120 | tf_op jit(solution)/shard_map/ppermute | solution.py:448
  5.1 1.4 %collective-permute-start.1 = (f32[49,8,128]{2,1,0:T(8,128)S(1)}, f32[49,8,128]{2,1,0:T(8,128)S(1)}, u32[]{:S(2)}, u32[]{:S(2)}) collective-permute-start(f32[49,8,128]{2,1,0:T(8,128)S(1)} %get-tuple-element.20), channel_id=1, source_target_pairs={{0,192},{64,0},{128,64},{192,128},{1,193},{65,1},{129,65},{193,129... | collective-permute-start | bytes 602120 | tf_op jit(solution)/shard_map/ppermute | solution.py:448
  6.5 1.7 %collective-permute-start.2 = (f32[14,8,128]{2,1,0:T(8,128)S(1)}, f32[14,8,128]{2,1,0:T(8,128)S(1)}, u32[]{:S(2)}, u32[]{:S(2)}) collective-permute-start(f32[14,8,128]{2,1,0:T(8,128)S(1)} %get-tuple-element.21), channel_id=1, source_target_pairs={{0,8},{8,16},{16,24},{24,32},{32,40},{40,48},{48,56},{56,0},{1,9},... | collective-permute-start | bytes 172040 | tf_op jit(solution)/shard_map/ppermute | solution.py:448
  8.2 3.9 %collective-permute-start.3 = (f32[14,8,128]{2,1,0:T(8,128)S(1)}, f32[14,8,128]{2,1,0:T(8,128)S(1)}, u32[]{:S(2)}, u32[]{:S(2)}) collective-permute-start(f32[14,8,128]{2,1,0:T(8,128)S(1)} %get-tuple-element.22), channel_id=1, source_target_pairs={{0,56},{8,0},{16,8},{24,16},{32,24},{40,32},{48,40},{56,48},{1,57}... | collective-permute-start | bytes 172040 | tf_op jit(solution)/shard_map/ppermute | solution.py:448
  12.2 2.7 %collective-permute-start.4 = (f32[8,128]{1,0:T(8,128)S(1)}, f32[8,128]{1,0:T(8,128)S(1)}, u32[]{:S(2)}, u32[]{:S(2)}) collective-permute-start(f32[8,128]{1,0:T(8,128)S(1)} %get-tuple-element.23), channel_id=1, source_target_pairs={{0,1},{1,2},{2,3},{3,4},{4,5},{5,6},{6,7},{7,0},{8,9},{9,10},{10,1... | collective-permute-start | bytes 12296 | tf_op jit(solution)/shard_map/ppermute | solution.py:448
  14.9 0.8 %collective-permute-done.4.z_low = f32[8,128]{1,0:T(8,128)S(1)} collective-permute-done((f32[8,128]{1,0:T(8,128)S(1)}, f32[8,128]{1,0:T(8,128)S(1)}, u32[]{:S(2)}, u32[]{:S(2)}) %collective-permute-start.4) | collective-permute-done | bytes 4128 | tf_op jit(solution)/shard_map/ppermute | solution.py:448
  15.6 2.3 %collective-permute-start.5 = (f32[8,128]{1,0:T(8,128)S(1)}, f32[8,128]{1,0:T(8,128)S(1)}, u32[]{:S(2)}, u32[]{:S(2)}) collective-permute-start(f32[8,128]{1,0:T(8,128)S(1)} %get-tuple-element.24), channel_id=1, source_target_pairs={{0,7},{1,0},{2,1},{3,2},{4,3},{5,4},{6,5},{7,6},{8,15},{9,8},{10,9... | collective-permute-start | bytes 12296 | tf_op jit(solution)/shard_map/ppermute | solution.py:448
  17.9 0.6 %own_cells.1.local = f32[4,7,7,8,128]{4,3,2,1,0:T(8,128)S(1)} custom-call(f32[4,7,7,8,128]{4,3,2,1,0:T(8,128)S(1)} %get-tuple-element.18.first), custom_call_target="tpu_custom_call" | custom-call | flops 4000000 | bytes 1605632 | tf_op jit(solution)/shard_map/own_cells/pallas_call | solution.py:433
  18.5 0.7 %collective-permute-done.5.z_high = f32[8,128]{1,0:T(8,128)S(1)} collective-permute-done((f32[8,128]{1,0:T(8,128)S(1)}, f32[8,128]{1,0:T(8,128)S(1)}, u32[]{:S(2)}, u32[]{:S(2)}) %collective-permute-start.5) | collective-permute-done | bytes 4128 | tf_op jit(solution)/shard_map/ppermute | solution.py:448
  19.2 0.0 collective-permute-done.2.y_low
  19.2 0.0 collective-permute-done.3.y_high
  19.2 0.0 collective-permute-done.x_low
  19.2 0.0 collective-permute-done.1.x_high
  19.2 1.7 %smooth_and_restrict.1 = (f32[7,7,7,1,4,128]{5,4,3,2,1,0:T(4,128)}, f32[2,8,128]{2,1,0:T(8,128)S(1)}, f32[2,8,128]{2,1,0:T(8,128)S(1)}, f32[2,8,128]{2,1,0:T(8,128)S(1)}, f32[2,8,128]{2,1,0:T(8,128)S(1)}) custom-call(f32[4,7,7,8,128]{4,3,2,1,0:T(8,128)S(1)} %get-tuple-element.18.first, f32[4,7,7,8,128]{4,3,2,1,0:T(8,128)S(1)} %own_cells.1.local, ...), custom_call_target="tpu_custom_call" | custom-call | flops 5000000 | bytes 3784704 | tf_op jit(solution)/shard_map/smooth_and_restrict/pallas_call | solution.py:433
  20.9 1.5 %collective-permute-start.8 = (f32[2,8,128]{2,1,0:T(8,128)S(1)}, f32[2,8,128]{2,1,0:T(8,128)S(1)}, u32[]{:S(2)}, u32[]{:S(2)}) collective-permute-start(f32[2,8,128]{2,1,0:T(8,128)S(1)} %get-tuple-element.33), channel_id=1, source_target_pairs={{0,128},{64,192},{128,0},{192,64},{1,129},{65,193},{129,1},{193,65... | collective-permute-start | bytes 24584 | tf_op jit(solution)/shard_map/ppermute | solution.py:448
  22.5 0.9 %collective-permute-start.7 = (f32[2,8,128]{2,1,0:T(8,128)S(1)}, f32[2,8,128]{2,1,0:T(8,128)S(1)}, u32[]{:S(2)}, u32[]{:S(2)}) collective-permute-start(f32[2,8,128]{2,1,0:T(8,128)S(1)} %get-tuple-element.32), channel_id=1, source_target_pairs={{0,192},{64,0},{128,64},{192,128},{1,193},{65,1},{129,65},{193,129... | collective-permute-start | bytes 24584 | tf_op jit(solution)/shard_map/ppermute | solution.py:448
  23.3 0.6 %collective-permute-start.6 = (f32[2,8,128]{2,1,0:T(8,128)S(1)}, f32[2,8,128]{2,1,0:T(8,128)S(1)}, u32[]{:S(2)}, u32[]{:S(2)}) collective-permute-start(f32[2,8,128]{2,1,0:T(8,128)S(1)} %get-tuple-element.31), channel_id=1, source_target_pairs={{0,64},{64,128},{128,192},{192,0},{1,65},{65,129},{129,193},{193,1... | collective-permute-start | bytes 24584 | tf_op jit(solution)/shard_map/ppermute | solution.py:448
  23.9 1.0 %collective-permute-done.8 = f32[2,8,128]{2,1,0:T(8,128)S(1)} collective-permute-done((f32[2,8,128]{2,1,0:T(8,128)S(1)}, f32[2,8,128]{2,1,0:T(8,128)S(1)}, u32[]{:S(2)}, u32[]{:S(2)}) %collective-permute-start.8) | collective-permute-done | bytes 8224 | tf_op jit(solution)/shard_map/ppermute | solution.py:448
  24.9 0.3 collective-permute-done.7
  25.3 1.8 %collective-permute-done.6 = f32[2,8,128]{2,1,0:T(8,128)S(1)} collective-permute-done((f32[2,8,128]{2,1,0:T(8,128)S(1)}, f32[2,8,128]{2,1,0:T(8,128)S(1)}, u32[]{:S(2)}, u32[]{:S(2)}) %collective-permute-start.6) | collective-permute-done | bytes 8224 | tf_op jit(solution)/shard_map/ppermute | solution.py:448
  27.1 1.7 %collective-permute-start.10 = (f32[2,8,128]{2,1,0:T(8,128)S(1)}, f32[2,8,128]{2,1,0:T(8,128)S(1)}, u32[]{:S(2)}, u32[]{:S(2)}) collective-permute-start(f32[2,8,128]{2,1,0:T(8,128)S(1)} %multiply_add_fusion), channel_id=1, source_target_pairs={{0,56},{8,0},{16,8},{24,16},{32,24},{40,32},{48,40},{56,48},{1,57}... | collective-permute-start | bytes 24584 | tf_op jit(solution)/shard_map/ppermute | solution.py:448
  28.8 0.0 collective-permute-start.9
  28.8 0.8 %collective-permute-done.10 = f32[2,8,128]{2,1,0:T(8,128)S(1)} collective-permute-done((f32[2,8,128]{2,1,0:T(8,128)S(1)}, f32[2,8,128]{2,1,0:T(8,128)S(1)}, u32[]{:S(2)}, u32[]{:S(2)}) %collective-permute-start.10) | collective-permute-done | bytes 8224 | tf_op jit(solution)/shard_map/ppermute | solution.py:448
  29.6 2.9 %collective-permute-done.9 = f32[2,8,128]{2,1,0:T(8,128)S(1)} collective-permute-done((f32[2,8,128]{2,1,0:T(8,128)S(1)}, f32[2,8,128]{2,1,0:T(8,128)S(1)}, u32[]{:S(2)}, u32[]{:S(2)}) %collective-permute-start.9) | collective-permute-done | bytes 8224 | tf_op jit(solution)/shard_map/ppermute | solution.py:448
  32.5 0.1 fusion.4
  32.6 3.2 %collective-permute-start.11 = (f32[8,128]{1,0:T(8,128)S(1)}, f32[8,128]{1,0:T(8,128)S(1)}, u32[]{:S(2)}, u32[]{:S(2)}) collective-permute-start(f32[8,128]{1,0:T(8,128)S(1)} %bitcast.13), channel_id=1, source_target_pairs={{0,1},{1,0},{2,3},{3,2},{4,5},{5,4},{6,7},{7,6},{8,9},{9,8},{10,11... | collective-permute-start | bytes 12296 | tf_op jit(solution)/shard_map/ppermute | solution.py:515
  35.8 0.8 %collective-permute-done.11 = f32[8,128]{1,0:T(8,128)S(1)} collective-permute-done((f32[8,128]{1,0:T(8,128)S(1)}, f32[8,128]{1,0:T(8,128)S(1)}, u32[]{:S(2)}, u32[]{:S(2)}) %collective-permute-start.11) | collective-permute-done | bytes 4128 | tf_op jit(solution)/shard_map/ppermute | solution.py:515
  36.7 1.7 %collective-permute-start.12 = (f32[2,8,128]{2,1,0:T(8,128)S(1)}, f32[2,8,128]{2,1,0:T(8,128)S(1)}, u32[]{:S(2)}, u32[]{:S(2)}) collective-permute-start(f32[2,8,128]{2,1,0:T(8,128)S(1)} %pad_maximum_fusion), channel_id=1, source_target_pairs={{0,6},{1,7},{2,0},{3,1},{4,2},{5,3},{6,4},{7,5},{8,14},{9,15},{10,... | collective-permute-start | bytes 24584 | tf_op jit(solution)/shard_map/ppermute | solution.py:448
  38.3 0.3 collective-permute-start.13
  38.6 0.7 %collective-permute-start.14 = (f32[2,8,128]{2,1,0:T(8,128)S(1)}, f32[2,8,128]{2,1,0:T(8,128)S(1)}, u32[]{:S(2)}, u32[]{:S(2)}) collective-permute-start(f32[2,8,128]{2,1,0:T(8,128)S(1)} %pad_maximum_fusion), channel_id=1, source_target_pairs={{0,2},{1,3},{2,4},{3,5},{4,6},{5,7},{6,0},{7,1},{8,10},{9,11},{10,... | collective-permute-start | bytes 24584 | tf_op jit(solution)/shard_map/ppermute | solution.py:448
  39.3 0.0 collective-permute-done.12
  39.3 3.1 %collective-permute-done.13 = f32[2,8,128]{2,1,0:T(8,128)S(1)} collective-permute-done((f32[2,8,128]{2,1,0:T(8,128)S(1)}, f32[2,8,128]{2,1,0:T(8,128)S(1)}, u32[]{:S(2)}, u32[]{:S(2)}) %collective-permute-start.13) | collective-permute-done | bytes 8224 | tf_op jit(solution)/shard_map/ppermute | solution.py:448
  42.4 0.0 collective-permute-done.14
  42.5 0.7 %fusion.2 = f32[1,4,1024]{2,1,0:T(4,128)} fusion(f32[16,8,128]{2,1,0:T(8,128)S(1)} %constant_dynamic-update-slice_fusion, s32[]{:T(128)S(6)} %select_n.66, f32[7,4,128]{2,1,0:T(4,128)S(1)} %get-tuple-element.39, f32[7,4,128]{2,1,0:T(4,128)S(1)} %get-tuple-element.38, pred[128]{0:T(512)(128)(4,1)S(1)} %get-tuple-element.42, ...), kind=kLoop, calls=%fused_computation.13 | loop fusion | flops 24576 | bytes 62728 | tf_op jit(solution)/shard_map/jit(_where)/select_n | solution.py:533
  (17 shorter events, 0.1 us)
Async XLA Ops:
  0.6 1.1 %copy-start = (f32[7,7,7,1,4,128]{5,4,3,2,1,0:T(4,128)S(1)}, f32[7,7,7,1,4,128]{5,4,3,2,1,0:T(4,128)}, u32[]{:S(2)}) copy-start(f32[7,7,7,1,4,128]{5,4,3,2,1,0:T(4,128)} %rhs.1) | copy-start | bytes 2107396
  1.7 0.7 %copy-start.1 = (s32[1,4,128]{2,1,0:T(4,128)S(1)}, s32[1,4,128]{2,1,0:T(4,128)}, u32[]{:S(2)}) copy-start(s32[1,4,128]{2,1,0:T(4,128)} %orders.3) | copy-start | bytes 6148
  3.0 16.2 %collective-permute-start = (f32[49,8,128]{2,1,0:T(8,128)S(1)}, f32[49,8,128]{2,1,0:T(8,128)S(1)}, u32[]{:S(2)}, u32[]{:S(2)}) collective-permute-start(f32[49,8,128]{2,1,0:T(8,128)S(1)} %get-tuple-element.19), channel_id=1, source_target_pairs={{0,64},{64,128},{128,192},{192,0},{1,65},{65,129},{129,193},{193,1... | collective-permute-start | bytes 602120 | tf_op jit(solution)/shard_map/ppermute | solution.py:448
  5.1 14.1 %collective-permute-start.1 = (f32[49,8,128]{2,1,0:T(8,128)S(1)}, f32[49,8,128]{2,1,0:T(8,128)S(1)}, u32[]{:S(2)}, u32[]{:S(2)}) collective-permute-start(f32[49,8,128]{2,1,0:T(8,128)S(1)} %get-tuple-element.20), channel_id=1, source_target_pairs={{0,192},{64,0},{128,64},{192,128},{1,193},{65,1},{129,65},{193,129... | collective-permute-start | bytes 602120 | tf_op jit(solution)/shard_map/ppermute | solution.py:448
  6.5 12.7 %collective-permute-start.2 = (f32[14,8,128]{2,1,0:T(8,128)S(1)}, f32[14,8,128]{2,1,0:T(8,128)S(1)}, u32[]{:S(2)}, u32[]{:S(2)}) collective-permute-start(f32[14,8,128]{2,1,0:T(8,128)S(1)} %get-tuple-element.21), channel_id=1, source_target_pairs={{0,8},{8,16},{16,24},{24,32},{32,40},{40,48},{48,56},{56,0},{1,9},... | collective-permute-start | bytes 172040 | tf_op jit(solution)/shard_map/ppermute | solution.py:448
  8.2 11.0 %collective-permute-start.3 = (f32[14,8,128]{2,1,0:T(8,128)S(1)}, f32[14,8,128]{2,1,0:T(8,128)S(1)}, u32[]{:S(2)}, u32[]{:S(2)}) collective-permute-start(f32[14,8,128]{2,1,0:T(8,128)S(1)} %get-tuple-element.22), channel_id=1, source_target_pairs={{0,56},{8,0},{16,8},{24,16},{32,24},{40,32},{48,40},{56,48},{1,57}... | collective-permute-start | bytes 172040 | tf_op jit(solution)/shard_map/ppermute | solution.py:448
  12.2 3.5 %collective-permute-start.4 = (f32[8,128]{1,0:T(8,128)S(1)}, f32[8,128]{1,0:T(8,128)S(1)}, u32[]{:S(2)}, u32[]{:S(2)}) collective-permute-start(f32[8,128]{1,0:T(8,128)S(1)} %get-tuple-element.23), channel_id=1, source_target_pairs={{0,1},{1,2},{2,3},{3,4},{4,5},{5,6},{6,7},{7,0},{8,9},{9,10},{10,1... | collective-permute-start | bytes 12296 | tf_op jit(solution)/shard_map/ppermute | solution.py:448
  15.6 3.6 %collective-permute-start.5 = (f32[8,128]{1,0:T(8,128)S(1)}, f32[8,128]{1,0:T(8,128)S(1)}, u32[]{:S(2)}, u32[]{:S(2)}) collective-permute-start(f32[8,128]{1,0:T(8,128)S(1)} %get-tuple-element.24), channel_id=1, source_target_pairs={{0,7},{1,0},{2,1},{3,2},{4,3},{5,4},{6,5},{7,6},{8,15},{9,8},{10,9... | collective-permute-start | bytes 12296 | tf_op jit(solution)/shard_map/ppermute | solution.py:448
  20.9 4.0 %collective-permute-start.8 = (f32[2,8,128]{2,1,0:T(8,128)S(1)}, f32[2,8,128]{2,1,0:T(8,128)S(1)}, u32[]{:S(2)}, u32[]{:S(2)}) collective-permute-start(f32[2,8,128]{2,1,0:T(8,128)S(1)} %get-tuple-element.33), channel_id=1, source_target_pairs={{0,128},{64,192},{128,0},{192,64},{1,129},{65,193},{129,1},{193,65... | collective-permute-start | bytes 24584 | tf_op jit(solution)/shard_map/ppermute | solution.py:448
  22.5 2.8 %collective-permute-start.7 = (f32[2,8,128]{2,1,0:T(8,128)S(1)}, f32[2,8,128]{2,1,0:T(8,128)S(1)}, u32[]{:S(2)}, u32[]{:S(2)}) collective-permute-start(f32[2,8,128]{2,1,0:T(8,128)S(1)} %get-tuple-element.32), channel_id=1, source_target_pairs={{0,192},{64,0},{128,64},{192,128},{1,193},{65,1},{129,65},{193,129... | collective-permute-start | bytes 24584 | tf_op jit(solution)/shard_map/ppermute | solution.py:448
  23.3 3.7 %collective-permute-start.6 = (f32[2,8,128]{2,1,0:T(8,128)S(1)}, f32[2,8,128]{2,1,0:T(8,128)S(1)}, u32[]{:S(2)}, u32[]{:S(2)}) collective-permute-start(f32[2,8,128]{2,1,0:T(8,128)S(1)} %get-tuple-element.31), channel_id=1, source_target_pairs={{0,64},{64,128},{128,192},{192,0},{1,65},{65,129},{129,193},{193,1... | collective-permute-start | bytes 24584 | tf_op jit(solution)/shard_map/ppermute | solution.py:448
  27.1 2.5 %collective-permute-start.10 = (f32[2,8,128]{2,1,0:T(8,128)S(1)}, f32[2,8,128]{2,1,0:T(8,128)S(1)}, u32[]{:S(2)}, u32[]{:S(2)}) collective-permute-start(f32[2,8,128]{2,1,0:T(8,128)S(1)} %multiply_add_fusion), channel_id=1, source_target_pairs={{0,56},{8,0},{16,8},{24,16},{32,24},{40,32},{48,40},{56,48},{1,57}... | collective-permute-start | bytes 24584 | tf_op jit(solution)/shard_map/ppermute | solution.py:448
  28.8 3.7 %collective-permute-start.9 = (f32[2,8,128]{2,1,0:T(8,128)S(1)}, f32[2,8,128]{2,1,0:T(8,128)S(1)}, u32[]{:S(2)}, u32[]{:S(2)}) collective-permute-start(f32[2,8,128]{2,1,0:T(8,128)S(1)} %multiply_add_fusion), channel_id=1, source_target_pairs={{0,8},{8,16},{16,24},{24,32},{32,40},{40,48},{48,56},{56,0},{1,9},... | collective-permute-start | bytes 24584 | tf_op jit(solution)/shard_map/ppermute | solution.py:448
  32.6 4.1 %collective-permute-start.11 = (f32[8,128]{1,0:T(8,128)S(1)}, f32[8,128]{1,0:T(8,128)S(1)}, u32[]{:S(2)}, u32[]{:S(2)}) collective-permute-start(f32[8,128]{1,0:T(8,128)S(1)} %bitcast.13), channel_id=1, source_target_pairs={{0,1},{1,0},{2,3},{3,2},{4,5},{5,4},{6,7},{7,6},{8,9},{9,8},{10,11... | collective-permute-start | bytes 12296 | tf_op jit(solution)/shard_map/ppermute | solution.py:515
  36.7 2.7 %collective-permute-start.12 = (f32[2,8,128]{2,1,0:T(8,128)S(1)}, f32[2,8,128]{2,1,0:T(8,128)S(1)}, u32[]{:S(2)}, u32[]{:S(2)}) collective-permute-start(f32[2,8,128]{2,1,0:T(8,128)S(1)} %pad_maximum_fusion), channel_id=1, source_target_pairs={{0,6},{1,7},{2,0},{3,1},{4,2},{5,3},{6,4},{7,5},{8,14},{9,15},{10,... | collective-permute-start | bytes 24584 | tf_op jit(solution)/shard_map/ppermute | solution.py:448
  38.3 4.1 %collective-permute-start.13 = (f32[2,8,128]{2,1,0:T(8,128)S(1)}, f32[2,8,128]{2,1,0:T(8,128)S(1)}, u32[]{:S(2)}, u32[]{:S(2)}) collective-permute-start(f32[2,8,128]{2,1,0:T(8,128)S(1)} %pad_maximum_fusion), channel_id=1, source_target_pairs={{0,4},{1,5},{2,6},{3,7},{4,0},{5,1},{6,2},{7,3},{8,12},{9,13},{10,... | collective-permute-start | bytes 24584 | tf_op jit(solution)/shard_map/ppermute | solution.py:448
  38.6 3.8 %collective-permute-start.14 = (f32[2,8,128]{2,1,0:T(8,128)S(1)}, f32[2,8,128]{2,1,0:T(8,128)S(1)}, u32[]{:S(2)}, u32[]{:S(2)}) collective-permute-start(f32[2,8,128]{2,1,0:T(8,128)S(1)} %pad_maximum_fusion), channel_id=1, source_target_pairs={{0,2},{1,3},{2,4},{3,5},{4,6},{5,7},{6,0},{7,1},{8,10},{9,11},{10,... | collective-permute-start | bytes 24584 | tf_op jit(solution)/shard_map/ppermute | solution.py:448
where the time goes:
time: 43.3 us; the launch traced here: 43.2 us
  starting transfers between devices  24.8 us (57%)
  waiting for transfers between devices  12.2 us (28%)
  Pallas kernels  2.9 us (7%)
  local copies, waits for them, and re-layouts  1.81 us (4%)
  other arithmetic  0.8 us (2%)
  between operations  0.72 us (2%)
    ppermute x14, starting transfers between devices, shift(): lax.ppermute(value, axis, [(i, (i + distance) % count) for i in range(cou...  21.5 us
    ppermute x14, waiting for transfers between devices, shift(): lax.ppermute(value, axis, [(i, (i + distance) % count) for i in range(cou...  11.4 us
    ppermute x1, starting transfers between devices, gather_columns(): other = lax.ppermute(packed, 'gz', [(i, i ^ 1) for i in range(count)])  3.23 us
    pallas_call x3, Pallas kernels, call(): pl.pallas_call(kernel, out_shape=outputs, in_specs=in_vmem(len(inputs)),...  2.9 us
    unnamed x11, local copies, waits for them, and re-layouts  1.79 us
  transfers between devices with their start and end apart: 15, of which 9 were waited for; matrix products, arithmetic and copies ran while one was open for 0% of the time, Pallas kernels for 1%

commit v1 on v0

--- a/solution.py
+++ b/solution.py
@@ -137,13 +137,21 @@
 
 
 def trace_kernel(
-    rhs, orders, first, x_up, x_down, y_up, y_down, z_up, z_down, y_low, y_high, z_low, z_high
+    rhs_hbm, orders_hbm, first, x_up, x_down, y_up, y_down, z_up, z_down, y_low, y_high, z_low,
+    z_high, orders, rhs, arrived,
 ):
+    copies = [pltpu.make_async_copy(orders_hbm, orders, arrived.at[MODES])]
+    for b in range(MODES):
+        copies.append(pltpu.make_async_copy(rhs_hbm.at[:, b], rhs.at[:, b], arrived.at[b]))
+    for copy in copies:
+        copy.start()
     pairs = Pairs()
     top = pairs.top
+    row, lane = row_in_half(), lanes()
+    copies[0].wait()
     keep = keep_masks(orders[0], top)
-    row, lane = row_in_half(), lanes()
     for b in range(MODES):
+        copies[1 + b].wait()
         for e in range(MODES):
             column = []
             for i in range(PAIRS):
@@ -166,8 +174,6 @@
                 pairs(SLOPE[2 * i], SLOPE[odd[i]] if odd[i] else 0.0) * column[i]
                 for i in range(PAIRS)
             )
-            sign = pairs(1.0, -1.0)
-            both_value = sign * value + swap(value)
             both_value = jnp.where(top, value + swap(value), swap(value) - value)
             both_slope = jnp.where(top, slope + swap(slope), slope - swap(slope))
             x_up[b * MODES + e] = jnp.where(top, both_value, swap(both_slope))
@@ -277,7 +283,7 @@
 
 def finish_kernel(
     first, local, orders, x_low, x_high, y_low, y_high, z_low, z_high,
-    y_below, y_above, z_below, z_above, smoothed, here, ahead, behind, far, field,
+    y_below, y_above, z_below, z_above, field, here, ahead, behind, far,
 ):
     pairs = Pairs()
     top = pairs.top
@@ -355,9 +361,6 @@
                 kappa = 1.0 + RHO_SECOND * RHO_FIRST + 2.0 * RHO_SECOND * THETA / DELTA
                 after = kappa * first[i, b, e] - (mask * scale) * applied
                 field[i, b, e] = after
-                smoothed[2 * i, b, e, 0] = after[:4]
-                if 2 * i + 1 < MODES:
-                    smoothed[2 * i + 1, b, e, 0] = after[4:]
 
     grid = {}
 
@@ -418,6 +421,41 @@
         far[z] = jnp.where(top, swap(outer[0][z]), outer[1][z])
 
 
+def unpack_kernel(field, smoothed):
+    for b in range(MODES):
+        for e in range(MODES):
+            for i in range(PAIRS):
+                value = field[i, b, e]
+                smoothed[2 * i, b, e, 0] = value[:4]
+                if 2 * i + 1 < MODES:
+                    smoothed[2 * i + 1, b, e, 0] = value[4:]
+
+
+def column_kernel(own, other, next_chip, over_chip, last_chip, column, blocks):
+    count = lax.axis_size("gz")
+    me = lax.axis_index("gz")
+    mate = me + 1 - 2 * lax.rem(me, 2)
+    zero = jnp.zeros((8, 128), jnp.float32)
+    blocks[0] = zero
+    blocks[count + 1] = zero
+    blocks[me + 1] = own[...]
+    blocks[mate + 1] = other[...]
+    for k, chip in ((1, next_chip), (2, over_chip), (3, last_chip)):
+        blocks[lax.rem(me + 2 * k, count) + 1] = chip[0]
+        blocks[lax.rem(mate + 2 * k, count) + 1] = chip[1]
+    lane = lax.broadcasted_iota(jnp.int32, (4, 128), 1)
+    row = lax.broadcasted_iota(jnp.int32, (4, 128), 0)
+    interior = (lax.axis_index("gx") > 0) & (lax.axis_index("gy") * 4 + row > 0)
+    for k in range(count):
+        value = (
+            blocks[k + 1, :4]
+            + jnp.where(lane < 2, blocks[k, 4:], 0.0)
+            + jnp.where(lane == 127, blocks[k + 2, 4:], 0.0)
+        )
+        here = interior & (lane > 0) if k == 0 else interior
+        column[0, :, k * 128 : (k + 1) * 128] = jnp.where(here, value, 0.0)
+
+
 def shape(*dims):
     return jax.ShapeDtypeStruct(dims, jnp.float32)
 
@@ -426,17 +464,15 @@
     return [pl.BlockSpec(memory_space=pltpu.VMEM)] * count
 
 
-def call(kernel, name, inputs, outputs, flops, scratch=(), alias=None):
-    size = sum(4 * int(np.prod(o.shape)) for o in outputs) + sum(
-        4 * int(np.prod(v.shape)) for v in inputs
-    )
+def call(kernel, name, inputs, outputs, flops, scratch=(), in_hbm=False):
+    size = sum(4 * int(np.prod(v.shape)) for v in (*inputs, *outputs))
+    space = pltpu.HBM if in_hbm else pltpu.VMEM
     return pl.pallas_call(
         kernel,
         out_shape=outputs,
-        in_specs=in_vmem(len(inputs)),
-        out_specs=in_vmem(len(outputs)),
+        in_specs=[pl.BlockSpec(memory_space=space)] * len(inputs),
+        out_specs=[pl.BlockSpec(memory_space=pltpu.VMEM)] * len(outputs),
         scratch_shapes=list(scratch),
-        input_output_aliases=alias or {},
         name=name,
         cost_estimate=pl.CostEstimate(flops=flops, bytes_accessed=size, transcendentals=0),
         compiler_params=pltpu.CompilerParams(vmem_limit_bytes=24 * 1024 * 1024),
@@ -455,32 +491,39 @@
 
 def per_device(rhs, orders):
     cells = (PAIRS, MODES, MODES, 8, 128)
-    first, x_up, x_down, y_up, y_down, z_up, z_down, y_low, y_high, z_low, z_high = call(
+    first, x_up, x_down, y_up, y_down, z_up, z_down, y_low, y_high, z_low, z_high, held = call(
         trace_kernel,
         "face_traces",
-        (rhs, orders),
+        tuple(pltpu.with_memory_space_constraint(v, pltpu.HBM) for v in (rhs, orders)),
         (
             shape(*cells), shape(49, 8, 128), shape(49, 8, 128),
             shape(FACE_ROWS, 8, 128), shape(FACE_ROWS, 8, 128), shape(8, 128), shape(8, 128),
             shape(2, 28, 8, 128), shape(2, 28, 8, 128), shape(2, 28, 8, 128), shape(2, 28, 8, 128),
+            jax.ShapeDtypeStruct(orders.shape, jnp.int32),
         ),
         4_000_000,
+        scratch=(
+            pltpu.VMEM(rhs.shape, jnp.float32),
+            pltpu.SemaphoreType.DMA((MODES + 1,)),
+        ),
+        in_hbm=True,
     )
     x_from_low, x_from_high = shift(x_up, "gx", 1), shift(x_down, "gx", -1)
     y_from_low, y_from_high = shift(y_up, "gy", 1), shift(y_down, "gy", -1)
     z_from_low, z_from_high = shift(z_up, "gz", 1), shift(z_down, "gz", -1)
-    (local,) = call(own_kernel, "own_cells", (first,), (shape(*cells),), 4_000_000)
-    smoothed, here, ahead, behind, far = call(
+    (local,) = call(own_kernel, "own_cells", (first,), (shape(*cells),), 4_000_000_000)
+    field, here, ahead, behind, far = call(
         finish_in_place,
         "smooth_and_restrict",
         (
-            first, local, orders, x_from_low, x_from_high, y_from_low, y_from_high,
+            first, local, held, x_from_low, x_from_high, y_from_low, y_from_high,
             z_from_low, z_from_high, y_high, y_low, z_high, z_low,
         ),
-        (shape(*rhs.shape),) + (shape(2, 8, 128),) * 4,
+        (shape(*cells),) + (shape(2, 8, 128),) * 4,
         5_000_000,
-        scratch=(pltpu.VMEM(cells, jnp.float32), pltpu.VMEM(cells, jnp.float32)),
-    )
+        scratch=(pltpu.VMEM(cells, jnp.float32),),
+    )
+    (smoothed,) = call(unpack_kernel, "unpack_modes", (field,), (shape(*rhs.shape),), 200_000)
     sums = (
         here
         + inside("gx", -1) * shift(ahead, "gx", 1)
@@ -493,44 +536,31 @@
         sums[:, :4]
         + jnp.where(row < 2, from_low[:, 4:], 0.0) * inside("gy", -1)
         + jnp.where(row == 3, from_high[:, 4:], 0.0) * inside("gy", 1)
-    )
-    return smoothed, gather_columns(owned)
+    ).reshape(8, 128)
+    count = lax.axis_size("gz")
+    other = lax.ppermute(owned, "gz", [(i, i ^ 1) for i in range(count)])
+    chip = jnp.stack([owned, other])
+    chips = [shift(chip, "gz", -2 * k) for k in range(1, count // 2)]
+    (column,) = call(
+        column_kernel,
+        "column",
+        (owned, other, *chips),
+        (shape(1, 4, 128 * count),),
+        20_000,
+        scratch=(pltpu.VMEM((count + 2, 8, 128), jnp.float32),),
+    )
+    return smoothed, column
 
 
 def finish_in_place(
     first, local, orders, x_low, x_high, y_low, y_high, z_low, z_high,
-    y_below, y_above, z_below, z_above, smoothed, here, ahead, behind, far, field, work,
+    y_below, y_above, z_below, z_above, field, here, ahead, behind, far, work,
 ):
     work[...] = local[...]
     finish_kernel(
         first, work, orders, x_low, x_high, y_low, y_high, z_low, z_high,
-        y_below, y_above, z_below, z_above, smoothed, here, ahead, behind, far, field,
-    )
-
-
-def gather_columns(owned):
-    count = lax.axis_size("gz")
-    packed = owned.reshape(8, 128)
-    me = lax.axis_index("gz")
-    other = lax.ppermute(packed, "gz", [(i, i ^ 1) for i in range(count)])
-    even = me % 2 == 0
-    chip = jnp.stack([jnp.where(even, packed, other), jnp.where(even, other, packed)])
-    chips = [chip] + [shift(chip, "gz", -2 * k) for k in range(1, count // 2)]
-    blocks = jnp.concatenate(chips)
-    blocks = jnp.roll(blocks, me - me % 2, axis=0)
-    lane = lax.broadcasted_iota(jnp.int32, (1, 1, 128), 2)
-    inner, outer = blocks[:, :4], blocks[:, 4:]
-    zero = jnp.zeros_like(outer[:1])
-    before = jnp.concatenate([zero, outer[:-1]])
-    after = jnp.concatenate([outer[1:], zero])
-    column = inner + jnp.where(lane < 2, before, 0.0) + jnp.where(lane == 127, after, 0.0)
-    column = column.transpose(1, 0, 2).reshape(1, 4, 128 * count)
-    place_y = lax.axis_index("gy") * 4 + jnp.arange(4)
-    place_z = jnp.arange(128 * count)
-    interior = (
-        (lax.axis_index("gx") > 0) & (place_y > 0)[:, None] & (place_z > 0)[None, :]
-    )
-    return jnp.where(interior[None], column, 0.0)
+        y_below, y_above, z_below, z_above, field, here, ahead, behind, far,
+    )
 
 
 def solution(mesh):

time: 43.3 us -> 41.6 us (0.961)
  local copies, waits for them, and re-layouts: 1.81 us -> 0 us
  Pallas kernels: 2.9 us -> 4.6 us
  starting transfers between devices: 24.8 us -> 23.4 us
  other arithmetic: 0.8 us -> 0.09 us
    unnamed x11 -> x0, local copies, waits for them, and re-layouts: 1.79 us -> none
    pallas_call x3 -> x5, Pallas kernels: 2.9 us -> 4.6 us  [call(): pl.pallas_call(kernel, out_shape=outputs, in_specs=[pl.BlockSpec(memory_s...]
    ppermute x14, starting transfers between devices: 21.5 us -> 19.9 us  [shift(): lax.ppermute(value, axis, [(i, (i + distance) % count) for i in range(cou...]
    select_n x1 -> x0, other arithmetic: 0.69 us -> none  [gather_columns(): return jnp.where(interior[None], column, 0.0)]
    ppermute x14, waiting for transfers between devices: 11.4 us -> 11.8 us  [shift(): lax.ppermute(value, axis, [(i, (i + distance) % count) for i in range(cou...]
  transfers between devices with their start and end apart: 15 -> 15, of which waited for: 9 -> 8; matrix products, arithmetic and copies ran while one was open for 0% -> 0% of each run, Pallas kernels for 1% -> 4%
where the time goes in v1:
time: 41.6 us; the launch traced here: 41.4 us
  starting transfers between devices  23.4 us (56%)
  waiting for transfers between devices  12.6 us (30%)
  Pallas kernels  4.6 us (11%)
  between operations  0.68 us (2%)
    ppermute x14, starting transfers between devices, shift(): lax.ppermute(value, axis, [(i, (i + distance) % count) for i in range(cou...  19.9 us
    ppermute x14, waiting for transfers between devices, shift(): lax.ppermute(value, axis, [(i, (i + distance) % count) for i in range(cou...  11.8 us
    pallas_call x5, Pallas kernels, call(): pl.pallas_call(kernel, out_shape=outputs, in_specs=[pl.BlockSpec(memory_s...  4.6 us
    ppermute x1, starting transfers between devices, per_device(): other = lax.ppermute(owned, 'gz', [(i, i ^ 1) for i in range(count)])  3.55 us
  transfers between devices with their start and end apart: 15, of which 8 were waited for; matrix products, arithmetic and copies ran while one was open for 0% of the time, Pallas kernels for 4%

profile of v1, /device:TPU:1, one launch (start us, length us, event | category | flops | bytes accessed | tf_op | source)
XLA Modules:
  0.0 41.4 jit_solution(13174702364921058270)
XLA Ops:
  0.6 1.6 %face_traces.1 = (f32[4,7,7,8,128]{4,3,2,1,0:T(8,128)S(1)}, f32[49,8,128]{2,1,0:T(8,128)S(1)}, f32[49,8,128]{2,1,0:T(8,128)S(1)}, f32[14,8,128]{2,1,0:T(8,128)S(...) custom-call(f32[7,7,7,1,4,128]{5,4,3,2,1,0:T(4,128)} %rhs_hbm.1, ...), custom_call_target="tpu_custom_call" | custom-call | flops 4000000 | bytes 2951168 | tf_op jit(solution)/shard_map/face_traces/pallas_call | solution.py:470
  2.3 2.7 %collective-permute-start.4 = (f32[8,128]{1,0:T(8,128)S(1)}, f32[8,128]{1,0:T(8,128)S(1)}, u32[]{:S(2)}, u32[]{:S(2)}) collective-permute-start(f32[8,128]{1,0:T(8,128)S(1)} %get-tuple-element.25), channel_id=1, source_target_pairs={{0,1},{1,2},{2,3},{3,4},{4,5},{5,6},{6,7},{7,0},{8,9},{9,10},{10,1... | collective-permute-start | bytes 12296 | tf_op jit(solution)/shard_map/ppermute | solution.py:484
  5.0 1.2 %collective-permute-start = (f32[49,8,128]{2,1,0:T(8,128)S(1)}, f32[49,8,128]{2,1,0:T(8,128)S(1)}, u32[]{:S(2)}, u32[]{:S(2)}) collective-permute-start(f32[49,8,128]{2,1,0:T(8,128)S(1)} %get-tuple-element.21), channel_id=1, source_target_pairs={{0,64},{64,128},{128,192},{192,0},{1,65},{65,129},{129,193},{193,1... | collective-permute-start | bytes 602120 | tf_op jit(solution)/shard_map/ppermute | solution.py:484
  6.2 1.5 %collective-permute-start.1 = (f32[49,8,128]{2,1,0:T(8,128)S(1)}, f32[49,8,128]{2,1,0:T(8,128)S(1)}, u32[]{:S(2)}, u32[]{:S(2)}) collective-permute-start(f32[49,8,128]{2,1,0:T(8,128)S(1)} %get-tuple-element.22), channel_id=1, source_target_pairs={{0,192},{64,0},{128,64},{192,128},{1,193},{65,1},{129,65},{193,129... | collective-permute-start | bytes 602120 | tf_op jit(solution)/shard_map/ppermute | solution.py:484
  7.6 1.6 %collective-permute-start.2 = (f32[14,8,128]{2,1,0:T(8,128)S(1)}, f32[14,8,128]{2,1,0:T(8,128)S(1)}, u32[]{:S(2)}, u32[]{:S(2)}) collective-permute-start(f32[14,8,128]{2,1,0:T(8,128)S(1)} %get-tuple-element.23), channel_id=1, source_target_pairs={{0,8},{8,16},{16,24},{24,32},{32,40},{40,48},{48,56},{56,0},{1,9},... | collective-permute-start | bytes 172040 | tf_op jit(solution)/shard_map/ppermute | solution.py:484
  9.3 3.9 %collective-permute-start.3 = (f32[14,8,128]{2,1,0:T(8,128)S(1)}, f32[14,8,128]{2,1,0:T(8,128)S(1)}, u32[]{:S(2)}, u32[]{:S(2)}) collective-permute-start(f32[14,8,128]{2,1,0:T(8,128)S(1)} %get-tuple-element.24), channel_id=1, source_target_pairs={{0,56},{8,0},{16,8},{24,16},{32,24},{40,32},{48,40},{56,48},{1,57}... | collective-permute-start | bytes 172040 | tf_op jit(solution)/shard_map/ppermute | solution.py:484
  13.2 0.0 collective-permute-done.4.z_low
  13.2 0.0 collective-permute-start.5
  13.2 0.6 %own_cells.1.local = f32[4,7,7,8,128]{4,3,2,1,0:T(8,128)S(1)} custom-call(f32[4,7,7,8,128]{4,3,2,1,0:T(8,128)S(1)} %get-tuple-element.19.first), custom_call_target="tpu_custom_call" | custom-call | flops 4000000000 | bytes 1605632 | tf_op jit(solution)/shard_map/own_cells/pallas_call | solution.py:470
  13.8 2.5 %collective-permute-done.5.z_high = f32[8,128]{1,0:T(8,128)S(1)} collective-permute-done((f32[8,128]{1,0:T(8,128)S(1)}, f32[8,128]{1,0:T(8,128)S(1)}, u32[]{:S(2)}, u32[]{:S(2)}) %collective-permute-start.5) | collective-permute-done | bytes 4128 | tf_op jit(solution)/shard_map/ppermute | solution.py:484
  16.3 0.0 collective-permute-done.2.y_low
  16.3 0.0 collective-permute-done.3.y_high
  16.3 0.0 collective-permute-done.x_low
  16.3 0.0 collective-permute-done.1.x_high
  16.3 0.8 %smooth_and_restrict.1 = (f32[4,7,7,8,128]{4,3,2,1,0:T(8,128)S(1)}, f32[2,8,128]{2,1,0:T(8,128)S(1)}, f32[2,8,128]{2,1,0:T(8,128)S(1)}, f32[2,8,128]{2,1,0:T(8,128)S(1)}, f32[2,8,128]{2,1,0:T(8,128)S(1)}) custom-call(f32[4,7,7,8,128]{4,3,2,1,0:T(8,128)S(1)} %get-tuple-element.19.first, f32[4,7,7,8,128]{4,3,2,1,0:T(8,128)S(1)} %own_cells.1.local, ...), custom_call_target="tpu_custom_call" | custom-call | flops 5000000 | bytes 3885056 | tf_op jit(solution)/shard_map/smooth_and_restrict/pallas_call | solution.py:470
  17.1 0.1 collective-permute-start.6
  17.2 2.7 %collective-permute-start.7 = (f32[2,8,128]{2,1,0:T(8,128)S(1)}, f32[2,8,128]{2,1,0:T(8,128)S(1)}, u32[]{:S(2)}, u32[]{:S(2)}) collective-permute-start(f32[2,8,128]{2,1,0:T(8,128)S(1)} %get-tuple-element.34), channel_id=1, source_target_pairs={{0,192},{64,0},{128,64},{192,128},{1,193},{65,1},{129,65},{193,129... | collective-permute-start | bytes 24584 | tf_op jit(solution)/shard_map/ppermute | solution.py:484
  19.9 0.3 collective-permute-start.8
  20.2 0.7 %collective-permute-done.6 = f32[2,8,128]{2,1,0:T(8,128)S(1)} collective-permute-done((f32[2,8,128]{2,1,0:T(8,128)S(1)}, f32[2,8,128]{2,1,0:T(8,128)S(1)}, u32[]{:S(2)}, u32[]{:S(2)}) %collective-permute-start.6) | collective-permute-done | bytes 8224 | tf_op jit(solution)/shard_map/ppermute | solution.py:484
  20.9 0.0 collective-permute-done.7
  20.9 3.0 %collective-permute-done.8 = f32[2,8,128]{2,1,0:T(8,128)S(1)} collective-permute-done((f32[2,8,128]{2,1,0:T(8,128)S(1)}, f32[2,8,128]{2,1,0:T(8,128)S(1)}, u32[]{:S(2)}, u32[]{:S(2)}) %collective-permute-start.8) | collective-permute-done | bytes 8224 | tf_op jit(solution)/shard_map/ppermute | solution.py:484
  23.9 1.9 %collective-permute-start.10 = (f32[2,8,128]{2,1,0:T(8,128)S(1)}, f32[2,8,128]{2,1,0:T(8,128)S(1)}, u32[]{:S(2)}, u32[]{:S(2)}) collective-permute-start(f32[2,8,128]{2,1,0:T(8,128)S(1)} %multiply_add_fusion), channel_id=1, source_target_pairs={{0,56},{8,0},{16,8},{24,16},{32,24},{40,32},{48,40},{56,48},{1,57}... | collective-permute-start | bytes 24584 | tf_op jit(solution)/shard_map/ppermute | solution.py:484
  25.8 0.0 collective-permute-start.9
  25.9 0.8 %collective-permute-done.10 = f32[2,8,128]{2,1,0:T(8,128)S(1)} collective-permute-done((f32[2,8,128]{2,1,0:T(8,128)S(1)}, f32[2,8,128]{2,1,0:T(8,128)S(1)}, u32[]{:S(2)}, u32[]{:S(2)}) %collective-permute-start.10) | collective-permute-done | bytes 8224 | tf_op jit(solution)/shard_map/ppermute | solution.py:484
  26.6 2.9 %collective-permute-done.9 = f32[2,8,128]{2,1,0:T(8,128)S(1)} collective-permute-done((f32[2,8,128]{2,1,0:T(8,128)S(1)}, f32[2,8,128]{2,1,0:T(8,128)S(1)}, u32[]{:S(2)}, u32[]{:S(2)}) %collective-permute-start.9) | collective-permute-done | bytes 8224 | tf_op jit(solution)/shard_map/ppermute | solution.py:484
  29.6 0.1 fusion.1
  29.6 3.6 %collective-permute-start.11 = (f32[8,128]{1,0:T(8,128)S(1)}, f32[8,128]{1,0:T(8,128)S(1)}, u32[]{:S(2)}, u32[]{:S(2)}) collective-permute-start(f32[8,128]{1,0:T(8,128)S(1)} %bitcast.3), channel_id=1, source_target_pairs={{0,1},{1,0},{2,3},{3,2},{4,5},{5,4},{6,7},{7,6},{8,9},{9,8},{10,11... | collective-permute-start | bytes 12296 | tf_op jit(solution)/shard_map/ppermute | solution.py:541
  33.2 0.8 %collective-permute-done.11.other = f32[8,128]{1,0:T(8,128)S(1)} collective-permute-done((f32[8,128]{1,0:T(8,128)S(1)}, f32[8,128]{1,0:T(8,128)S(1)}, u32[]{:S(2)}, u32[]{:S(2)}) %collective-permute-start.11) | collective-permute-done | bytes 4128 | tf_op jit(solution)/shard_map/ppermute | solution.py:541
  34.0 2.2 %collective-permute-start.12 = (f32[2,8,128]{2,1,0:T(8,128)S(1)}, f32[2,8,128]{2,1,0:T(8,128)S(1)}, u32[]{:S(2)}, u32[]{:S(2)}) collective-permute-start(f32[2,8,128]{2,1,0:T(8,128)S(1)} %pad_maximum_fusion), channel_id=1, source_target_pairs={{0,6},{1,7},{2,0},{3,1},{4,2},{5,3},{6,4},{7,5},{8,14},{9,15},{10,... | collective-permute-start | bytes 24584 | tf_op jit(solution)/shard_map/ppermute | solution.py:484
  36.2 0.9 %collective-permute-start.13 = (f32[2,8,128]{2,1,0:T(8,128)S(1)}, f32[2,8,128]{2,1,0:T(8,128)S(1)}, u32[]{:S(2)}, u32[]{:S(2)}) collective-permute-start(f32[2,8,128]{2,1,0:T(8,128)S(1)} %pad_maximum_fusion), channel_id=1, source_target_pairs={{0,4},{1,5},{2,6},{3,7},{4,0},{5,1},{6,2},{7,3},{8,12},{9,13},{10,... | collective-permute-start | bytes 24584 | tf_op jit(solution)/shard_map/ppermute | solution.py:484
  37.1 0.8 %collective-permute-start.14 = (f32[2,8,128]{2,1,0:T(8,128)S(1)}, f32[2,8,128]{2,1,0:T(8,128)S(1)}, u32[]{:S(2)}, u32[]{:S(2)}) collective-permute-start(f32[2,8,128]{2,1,0:T(8,128)S(1)} %pad_maximum_fusion), channel_id=1, source_target_pairs={{0,2},{1,3},{2,4},{3,5},{4,6},{5,7},{6,0},{7,1},{8,10},{9,11},{10,... | collective-permute-start | bytes 24584 | tf_op jit(solution)/shard_map/ppermute | solution.py:484
  37.9 0.9 %unpack_modes.1 = f32[7,7,7,1,4,128]{5,4,3,2,1,0:T(4,128)} custom-call(f32[4,7,7,8,128]{4,3,2,1,0:T(8,128)S(1)} %get-tuple-element.31.field), custom_call_target="tpu_custom_call" | custom-call | flops 200000 | bytes 1505280 | tf_op jit(solution)/shard_map/unpack_modes/pallas_call | solution.py:470
  38.9 0.0 collective-permute-done.12.next_chip
  38.9 1.4 %collective-permute-done.13.over_chip = f32[2,8,128]{2,1,0:T(8,128)S(1)} collective-permute-done((f32[2,8,128]{2,1,0:T(8,128)S(1)}, f32[2,8,128]{2,1,0:T(8,128)S(1)}, u32[]{:S(2)}, u32[]{:S(2)}) %collective-permute-start.13) | collective-permute-done | bytes 8224 | tf_op jit(solution)/shard_map/ppermute | solution.py:484
  40.2 0.6 %collective-permute-done.14.last_chip = f32[2,8,128]{2,1,0:T(8,128)S(1)} collective-permute-done((f32[2,8,128]{2,1,0:T(8,128)S(1)}, f32[2,8,128]{2,1,0:T(8,128)S(1)}, u32[]{:S(2)}, u32[]{:S(2)}) %collective-permute-start.14) | collective-permute-done | bytes 8224 | tf_op jit(solution)/shard_map/ppermute | solution.py:484
  40.8 0.6 %column.1 = f32[1,4,1024]{2,1,0:T(4,128)} custom-call(f32[8,128]{1,0:T(8,128)S(1)} %bitcast.5, f32[8,128]{1,0:T(8,128)S(1)} %collective-permute-done.11.other, f32[2,8,128]{2,1,0:T(8,128)S(1)} %collective-permute-done.12.next_chip, f32[2,8,128]{2,1,0:T(8,128)S(1)} %collective-permute-done.13.over_chip, f32[2,8,128]{2,1,0:T(8,128)S(1)} %collective-permute-done.14.last_chip), custom_call_target="tpu_custom_call" | custom-call | flops 20000 | bytes 49152 | tf_op jit(solution)/shard_map/column/pallas_call | solution.py:470
  (3 shorter events, 0.0 us)
Async XLA Ops:
  2.3 11.0 %collective-permute-start.4 = (f32[8,128]{1,0:T(8,128)S(1)}, f32[8,128]{1,0:T(8,128)S(1)}, u32[]{:S(2)}, u32[]{:S(2)}) collective-permute-start(f32[8,128]{1,0:T(8,128)S(1)} %get-tuple-element.25), channel_id=1, source_target_pairs={{0,1},{1,2},{2,3},{3,4},{4,5},{5,6},{6,7},{7,0},{8,9},{9,10},{10,1... | collective-permute-start | bytes 12296 | tf_op jit(solution)/shard_map/ppermute | solution.py:484
  5.0 11.3 %collective-permute-start = (f32[49,8,128]{2,1,0:T(8,128)S(1)}, f32[49,8,128]{2,1,0:T(8,128)S(1)}, u32[]{:S(2)}, u32[]{:S(2)}) collective-permute-start(f32[49,8,128]{2,1,0:T(8,128)S(1)} %get-tuple-element.21), channel_id=1, source_target_pairs={{0,64},{64,128},{128,192},{192,0},{1,65},{65,129},{129,193},{193,1... | collective-permute-start | bytes 602120 | tf_op jit(solution)/shard_map/ppermute | solution.py:484
  6.2 10.1 %collective-permute-start.1 = (f32[49,8,128]{2,1,0:T(8,128)S(1)}, f32[49,8,128]{2,1,0:T(8,128)S(1)}, u32[]{:S(2)}, u32[]{:S(2)}) collective-permute-start(f32[49,8,128]{2,1,0:T(8,128)S(1)} %get-tuple-element.22), channel_id=1, source_target_pairs={{0,192},{64,0},{128,64},{192,128},{1,193},{65,1},{129,65},{193,129... | collective-permute-start | bytes 602120 | tf_op jit(solution)/shard_map/ppermute | solution.py:484
  7.6 8.6 %collective-permute-start.2 = (f32[14,8,128]{2,1,0:T(8,128)S(1)}, f32[14,8,128]{2,1,0:T(8,128)S(1)}, u32[]{:S(2)}, u32[]{:S(2)}) collective-permute-start(f32[14,8,128]{2,1,0:T(8,128)S(1)} %get-tuple-element.23), channel_id=1, source_target_pairs={{0,8},{8,16},{16,24},{24,32},{32,40},{40,48},{48,56},{56,0},{1,9},... | collective-permute-start | bytes 172040 | tf_op jit(solution)/shard_map/ppermute | solution.py:484
  9.3 7.0 %collective-permute-start.3 = (f32[14,8,128]{2,1,0:T(8,128)S(1)}, f32[14,8,128]{2,1,0:T(8,128)S(1)}, u32[]{:S(2)}, u32[]{:S(2)}) collective-permute-start(f32[14,8,128]{2,1,0:T(8,128)S(1)} %get-tuple-element.24), channel_id=1, source_target_pairs={{0,56},{8,0},{16,8},{24,16},{32,24},{40,32},{48,40},{56,48},{1,57}... | collective-permute-start | bytes 172040 | tf_op jit(solution)/shard_map/ppermute | solution.py:484
  13.2 3.0 %collective-permute-start.5 = (f32[8,128]{1,0:T(8,128)S(1)}, f32[8,128]{1,0:T(8,128)S(1)}, u32[]{:S(2)}, u32[]{:S(2)}) collective-permute-start(f32[8,128]{1,0:T(8,128)S(1)} %get-tuple-element.26), channel_id=1, source_target_pairs={{0,7},{1,0},{2,1},{3,2},{4,3},{5,4},{6,5},{7,6},{8,15},{9,8},{10,9... | collective-permute-start | bytes 12296 | tf_op jit(solution)/shard_map/ppermute | solution.py:484
  17.1 3.8 %collective-permute-start.6 = (f32[2,8,128]{2,1,0:T(8,128)S(1)}, f32[2,8,128]{2,1,0:T(8,128)S(1)}, u32[]{:S(2)}, u32[]{:S(2)}) collective-permute-start(f32[2,8,128]{2,1,0:T(8,128)S(1)} %get-tuple-element.33), channel_id=1, source_target_pairs={{0,64},{64,128},{128,192},{192,0},{1,65},{65,129},{129,193},{193,1... | collective-permute-start | bytes 24584 | tf_op jit(solution)/shard_map/ppermute | solution.py:484
  17.2 3.7 %collective-permute-start.7 = (f32[2,8,128]{2,1,0:T(8,128)S(1)}, f32[2,8,128]{2,1,0:T(8,128)S(1)}, u32[]{:S(2)}, u32[]{:S(2)}) collective-permute-start(f32[2,8,128]{2,1,0:T(8,128)S(1)} %get-tuple-element.34), channel_id=1, source_target_pairs={{0,192},{64,0},{128,64},{192,128},{1,193},{65,1},{129,65},{193,129... | collective-permute-start | bytes 24584 | tf_op jit(solution)/shard_map/ppermute | solution.py:484
  19.9 4.0 %collective-permute-start.8 = (f32[2,8,128]{2,1,0:T(8,128)S(1)}, f32[2,8,128]{2,1,0:T(8,128)S(1)}, u32[]{:S(2)}, u32[]{:S(2)}) collective-permute-start(f32[2,8,128]{2,1,0:T(8,128)S(1)} %get-tuple-element.35), channel_id=1, source_target_pairs={{0,128},{64,192},{128,0},{192,64},{1,129},{65,193},{129,1},{193,65... | collective-permute-start | bytes 24584 | tf_op jit(solution)/shard_map/ppermute | solution.py:484
  23.9 2.7 %collective-permute-start.10 = (f32[2,8,128]{2,1,0:T(8,128)S(1)}, f32[2,8,128]{2,1,0:T(8,128)S(1)}, u32[]{:S(2)}, u32[]{:S(2)}) collective-permute-start(f32[2,8,128]{2,1,0:T(8,128)S(1)} %multiply_add_fusion), channel_id=1, source_target_pairs={{0,56},{8,0},{16,8},{24,16},{32,24},{40,32},{48,40},{56,48},{1,57}... | collective-permute-start | bytes 24584 | tf_op jit(solution)/shard_map/ppermute | solution.py:484
  25.8 3.7 %collective-permute-start.9 = (f32[2,8,128]{2,1,0:T(8,128)S(1)}, f32[2,8,128]{2,1,0:T(8,128)S(1)}, u32[]{:S(2)}, u32[]{:S(2)}) collective-permute-start(f32[2,8,128]{2,1,0:T(8,128)S(1)} %multiply_add_fusion), channel_id=1, source_target_pairs={{0,8},{8,16},{16,24},{24,32},{32,40},{40,48},{48,56},{56,0},{1,9},... | collective-permute-start | bytes 24584 | tf_op jit(solution)/shard_map/ppermute | solution.py:484
  29.6 4.4 %collective-permute-start.11 = (f32[8,128]{1,0:T(8,128)S(1)}, f32[8,128]{1,0:T(8,128)S(1)}, u32[]{:S(2)}, u32[]{:S(2)}) collective-permute-start(f32[8,128]{1,0:T(8,128)S(1)} %bitcast.3), channel_id=1, source_target_pairs={{0,1},{1,0},{2,3},{3,2},{4,5},{5,4},{6,7},{7,6},{8,9},{9,8},{10,11... | collective-permute-start | bytes 12296 | tf_op jit(solution)/shard_map/ppermute | solution.py:541
  34.0 4.8 %collective-permute-start.12 = (f32[2,8,128]{2,1,0:T(8,128)S(1)}, f32[2,8,128]{2,1,0:T(8,128)S(1)}, u32[]{:S(2)}, u32[]{:S(2)}) collective-permute-start(f32[2,8,128]{2,1,0:T(8,128)S(1)} %pad_maximum_fusion), channel_id=1, source_target_pairs={{0,6},{1,7},{2,0},{3,1},{4,2},{5,3},{6,4},{7,5},{8,14},{9,15},{10,... | collective-permute-start | bytes 24584 | tf_op jit(solution)/shard_map/ppermute | solution.py:484
  36.2 4.0 %collective-permute-start.13 = (f32[2,8,128]{2,1,0:T(8,128)S(1)}, f32[2,8,128]{2,1,0:T(8,128)S(1)}, u32[]{:S(2)}, u32[]{:S(2)}) collective-permute-start(f32[2,8,128]{2,1,0:T(8,128)S(1)} %pad_maximum_fusion), channel_id=1, source_target_pairs={{0,4},{1,5},{2,6},{3,7},{4,0},{5,1},{6,2},{7,3},{8,12},{9,13},{10,... | collective-permute-start | bytes 24584 | tf_op jit(solution)/shard_map/ppermute | solution.py:484
  37.1 3.7 %collective-permute-start.14 = (f32[2,8,128]{2,1,0:T(8,128)S(1)}, f32[2,8,128]{2,1,0:T(8,128)S(1)}, u32[]{:S(2)}, u32[]{:S(2)}) collective-permute-start(f32[2,8,128]{2,1,0:T(8,128)S(1)} %pad_maximum_fusion), channel_id=1, source_target_pairs={{0,2},{1,3},{2,4},{3,5},{4,6},{5,7},{6,0},{7,1},{8,10},{9,11},{10,... | collective-permute-start | bytes 24584 | tf_op jit(solution)/shard_map/ppermute | solution.py:484

commit v2 on v1

--- a/solution.py
+++ b/solution.py
@@ -137,8 +137,8 @@
 
 
 def trace_kernel(
-    rhs_hbm, orders_hbm, first, x_up, x_down, y_up, y_down, z_up, z_down, y_low, y_high, z_low,
-    z_high, orders, rhs, arrived,
+    rhs_hbm, orders_hbm, first, x_a, x_b, y_a, y_b, z_a, z_b, y_low, y_high, z_low, z_high,
+    orders, rhs, arrived,
 ):
     copies = [pltpu.make_async_copy(orders_hbm, orders, arrived.at[MODES])]
     for b in range(MODES):
@@ -148,6 +148,12 @@
     pairs = Pairs()
     top = pairs.top
     row, lane = row_in_half(), lanes()
+
+    def put(ref, other_ref, index, axis, up, down):
+        even = jnp.full((8, 128), lax.rem(lax.axis_index(axis), 2), jnp.int32) == 0
+        ref[index] = jnp.where(even, up, down)
+        other_ref[index] = jnp.where(even, down, up)
+
     copies[0].wait()
     keep = keep_masks(orders[0], top)
     for b in range(MODES):
@@ -176,8 +182,9 @@
             )
             both_value = jnp.where(top, value + swap(value), swap(value) - value)
             both_slope = jnp.where(top, slope + swap(slope), slope - swap(slope))
-            x_up[b * MODES + e] = jnp.where(top, both_value, swap(both_slope))
-            x_down[b * MODES + e] = jnp.where(top, swap(both_value), both_slope)
+            up = jnp.where(top, both_value, swap(both_slope))
+            down = jnp.where(top, swap(both_value), both_slope)
+            put(x_a, x_b, b * MODES + e, "gx", up, down)
     packed_up = packed_down = None
     for kind in range(2):
         for i in range(PAIRS):
@@ -193,8 +200,7 @@
                 packed_up = up if q == 0 else jnp.where(row == q, up, packed_up)
                 packed_down = down if q == 0 else jnp.where(row == q, down, packed_down)
                 if q == 3:
-                    y_up[kind * 7 + m // 4] = packed_up
-                    y_down[kind * 7 + m // 4] = packed_down
+                    put(y_a, y_b, kind * 7 + m // 4, "gy", packed_up, packed_down)
     packed_up = packed_down = jnp.zeros((8, 128), jnp.float32)
     for i in range(PAIRS):
         for b in range(MODES):
@@ -209,8 +215,7 @@
                 packed_up = jnp.where(lane == place, pltpu.roll(high, 1 + place, 1), packed_up)
                 down = pltpu.roll(low, place, 1) if place else low
                 packed_down = jnp.where(lane == place, down, packed_down)
-    z_up[...] = packed_up
-    z_down[...] = packed_down
+    put(z_a, z_b, ..., "gz", packed_up, packed_down)
 
 
 def own_kernel(first, out):
@@ -282,8 +287,8 @@
 
 
 def finish_kernel(
-    first, local, orders, x_low, x_high, y_low, y_high, z_low, z_high,
-    y_below, y_above, z_below, z_above, field, here, ahead, behind, far,
+    first, local, orders, x_a, x_b, y_a, y_b, z_a, z_b,
+    y_below, y_above, z_below, z_above, field, here, sum_a, sum_b, far,
 ):
     pairs = Pairs()
     top = pairs.top
@@ -296,14 +301,18 @@
             jnp.float32
         )
 
-    x_has_low, x_has_high = inside("gx", -1), inside("gx", 1)
+    def is_even(axis):
+        return jnp.full((8, 128), lax.rem(lax.axis_index(axis), 2), jnp.int32) == 0
+
+    x_has_b = inside("gx", -1) * inside("gx", 1)
+    x_even, y_even, z_even = is_even("gx"), is_even("gy"), is_even("gz")
+    x_sign = jnp.where(x_even, 1.0, -1.0)
     y_has_low, y_has_high = inside("gy", -1), inside("gy", 1)
     z_has_low, z_has_high = inside("gz", -1), inside("gz", 1)
     for b in range(MODES):
         for e in range(MODES):
-            below = x_has_low * x_low[b * MODES + e]
-            above = x_has_high * x_high[b * MODES + e]
-            plus, minus = above + below, swap(above - below)
+            one, two = x_a[b * MODES + e], x_has_b * x_b[b * MODES + e]
+            plus, minus = one + two, swap(x_sign * (one - two))
             slope = 0.5 * jnp.where(top, plus, minus)
             value = (-2.0 * PENALTY) * slope - 0.5 * jnp.where(top, minus, plus)
             for i in range(PAIRS):
@@ -313,18 +322,23 @@
                     pairs(NORMED[2 * i], 0.0 if last else NORMED[k]) * value
                     + pairs(SLOPE[2 * i], 0.0 if last else SLOPE[k]) * slope
                 )
+    y_low, y_high = [], []
+    for k in range(FACE_ROWS):
+        one, two = y_a[k], y_b[k]
+        y_low.append(y_has_low * jnp.where(y_even, two, one))
+        y_high.append(y_has_high * jnp.where(y_even, one, two))
     for i in range(PAIRS):
         for e in range(MODES):
             m = i * MODES + e
             q = m % 4
             seen = []
             for kind in range(2):
-                halo = y_has_low * y_low[kind * 7 + m // 4]
+                halo = y_low[kind * 7 + m // 4]
                 halo = pltpu.roll(halo, 8 - q, 0) if q else halo
                 moved = pltpu.roll(y_below[kind, m], 1, 0)
                 seen.append(jnp.where(row == 0, halo, moved))
             for kind in range(2):
-                halo = y_has_high * y_high[kind * 7 + m // 4]
+                halo = y_high[kind * 7 + m // 4]
                 halo = pltpu.roll(halo, 3 - q, 0) if q < 3 else halo
                 moved = pltpu.roll(y_above[kind, m], 7, 0)
                 seen.append(jnp.where(row == 3, halo, moved))
@@ -333,7 +347,8 @@
                 value, slope = parts[n % 2]
                 add = float(NORMED[n]) * value
                 local[i, n, e] += add + float(SLOPE[n]) * slope if n else add
-    z_low_halo, z_high_halo = z_has_low * z_low[...], z_has_high * z_high[...]
+    z_low_halo = z_has_low * jnp.where(z_even, z_b[...], z_a[...])
+    z_high_halo = z_has_high * jnp.where(z_even, z_a[...], z_b[...])
     for i in range(PAIRS):
         for b in range(MODES):
             m = i * MODES + b
@@ -416,8 +431,10 @@
     outer = sum_to_vertices(outer, pairs, row, lane)
     for z in range(2):
         here[z] = jnp.where(top, near[0][z], swap(near[1][z]))
-        ahead[z] = jnp.where(top, swap(near[0][z]), near[1][z])
-        behind[z] = jnp.where(top, outer[0][z], swap(outer[1][z]))
+        ahead = jnp.where(top, swap(near[0][z]), near[1][z])
+        behind = jnp.where(top, outer[0][z], swap(outer[1][z]))
+        sum_a[z] = jnp.where(x_even, ahead, behind)
+        sum_b[z] = jnp.where(x_even, behind, ahead)
         far[z] = jnp.where(top, swap(outer[0][z]), outer[1][z])
 
 
@@ -440,9 +457,13 @@
     blocks[count + 1] = zero
     blocks[me + 1] = own[...]
     blocks[mate + 1] = other[...]
-    for k, chip in ((1, next_chip), (2, over_chip), (3, last_chip)):
-        blocks[lax.rem(me + 2 * k, count) + 1] = chip[0]
-        blocks[lax.rem(mate + 2 * k, count) + 1] = chip[1]
+    core = lax.rem(me, 2)
+    place = lax.div(me, 2)
+    beside = place + 1 - 2 * lax.rem(place, 2)
+    across = lax.rem(place + 2, 4)
+    for source, chip in ((beside, next_chip), (across, over_chip), (3 - place, last_chip)):
+        blocks[2 * source + core + 1] = chip[0]
+        blocks[2 * source + 2 - core] = chip[1]
     lane = lax.broadcasted_iota(jnp.int32, (4, 128), 1)
     row = lax.broadcasted_iota(jnp.int32, (4, 128), 0)
     interior = (lax.axis_index("gx") > 0) & (lax.axis_index("gy") * 4 + row > 0)
@@ -484,6 +505,32 @@
     return lax.ppermute(value, axis, [(i, (i + distance) % count) for i in range(count)])
 
 
+def flip(value, axis, bits):
+    return lax.ppermute(value, axis, [(i, i ^ bits) for i in range(lax.axis_size(axis))])
+
+
+def second_pairs(value, axis):
+    axes = ("gx", "gy", "gz")
+    sizes = [lax.axis_size(name) for name in axes]
+    route = []
+    for source, place in enumerate(np.ndindex(*sizes)):
+        target = list(place)
+        k = axes.index(axis)
+        if place[k] in (0, sizes[k] - 1):
+            target[2] ^= 1
+        else:
+            target[k] += 1 if place[k] % 2 else -1
+        route.append((source, int(np.ravel_multi_index(target, sizes))))
+    return lax.ppermute(value, axes, route)
+
+
+def second_ring(value, axis):
+    count = lax.axis_size(axis)
+    return lax.ppermute(
+        value, axis, [(i, (i + (1 if i % 2 else -1)) % count) for i in range(count)]
+    )
+
+
 def inside(axis, distance):
     place = lax.axis_index(axis) + distance
     return ((place >= 0) & (place < lax.axis_size(axis))).astype(jnp.float32)
@@ -491,7 +538,7 @@
 
 def per_device(rhs, orders):
     cells = (PAIRS, MODES, MODES, 8, 128)
-    first, x_up, x_down, y_up, y_down, z_up, z_down, y_low, y_high, z_low, z_high, held = call(
+    first, x_a, x_b, y_a, y_b, z_a, z_b, y_low, y_high, z_low, z_high, held = call(
         trace_kernel,
         "face_traces",
         tuple(pltpu.with_memory_space_constraint(v, pltpu.HBM) for v in (rhs, orders)),
@@ -508,16 +555,15 @@
         ),
         in_hbm=True,
     )
-    x_from_low, x_from_high = shift(x_up, "gx", 1), shift(x_down, "gx", -1)
-    y_from_low, y_from_high = shift(y_up, "gy", 1), shift(y_down, "gy", -1)
-    z_from_low, z_from_high = shift(z_up, "gz", 1), shift(z_down, "gz", -1)
+    x_a, x_b = flip(x_a, "gx", 1), second_pairs(x_b, "gx")
+    y_a, y_b = flip(y_a, "gy", 1), second_pairs(y_b, "gy")
+    z_a, z_b = flip(z_a, "gz", 1), second_ring(z_b, "gz")
     (local,) = call(own_kernel, "own_cells", (first,), (shape(*cells),), 4_000_000_000)
-    field, here, ahead, behind, far = call(
+    field, here, sum_a, sum_b, far = call(
         finish_in_place,
         "smooth_and_restrict",
         (
-            first, local, held, x_from_low, x_from_high, y_from_low, y_from_high,
-            z_from_low, z_from_high, y_high, y_low, z_high, z_low,
+            first, local, held, x_a, x_b, y_a, y_b, z_a, z_b, y_high, y_low, z_high, z_low,
         ),
         (shape(*cells),) + (shape(2, 8, 128),) * 4,
         5_000_000,
@@ -526,9 +572,9 @@
     (smoothed,) = call(unpack_kernel, "unpack_modes", (field,), (shape(*rhs.shape),), 200_000)
     sums = (
         here
-        + inside("gx", -1) * shift(ahead, "gx", 1)
-        + inside("gx", 1) * shift(behind, "gx", -1)
-        + inside("gx", -2) * shift(far, "gx", 2)
+        + flip(sum_a, "gx", 1)
+        + inside("gx", -1) * inside("gx", 1) * second_pairs(sum_b, "gx")
+        + inside("gx", -2) * flip(far, "gx", 2)
     )
     from_low, from_high = shift(sums, "gy", 1), shift(sums, "gy", -1)
     row = lax.broadcasted_iota(jnp.int32, (1, 4, 1), 1)
@@ -538,9 +584,9 @@
         + jnp.where(row == 3, from_high[:, 4:], 0.0) * inside("gy", 1)
     ).reshape(8, 128)
     count = lax.axis_size("gz")
-    other = lax.ppermute(owned, "gz", [(i, i ^ 1) for i in range(count)])
+    other = flip(owned, "gz", 1)
     chip = jnp.stack([owned, other])
-    chips = [shift(chip, "gz", -2 * k) for k in range(1, count // 2)]
+    chips = [flip(chip, "gz", 2 * k) for k in range(1, count // 2)]
     (column,) = call(
         column_kernel,
         "column",
@@ -553,13 +599,13 @@
 
 
 def finish_in_place(
-    first, local, orders, x_low, x_high, y_low, y_high, z_low, z_high,
-    y_below, y_above, z_below, z_above, field, here, ahead, behind, far, work,
+    first, local, orders, x_a, x_b, y_a, y_b, z_a, z_b,
+    y_below, y_above, z_below, z_above, field, here, sum_a, sum_b, far, work,
 ):
     work[...] = local[...]
     finish_kernel(
-        first, work, orders, x_low, x_high, y_low, y_high, z_low, z_high,
-        y_below, y_above, z_below, z_above, field, here, ahead, behind, far,
+        first, work, orders, x_a, x_b, y_a, y_b, z_a, z_b,
+        y_below, y_above, z_below, z_above, field, here, sum_a, sum_b, far,
     )
 
 

time: 41.6 us -> 40.6 us (0.976)
  the two profiles are of different devices: /device:TPU:1 before, /device:TPU:2 now
where the time goes in v2:
time: 40.6 us; the launch traced here: 40.5 us
  starting transfers between devices  20.4 us (50%)
  waiting for transfers between devices  14.7 us (36%)
  Pallas kernels  4.6 us (11%)
  between operations  0.68 us (2%)
    ppermute x9, starting transfers between devices, flip(): lax.ppermute(value, axis, [(i, i ^ bits) for i in range(lax.axis_size(axi...  10.6 us
    ppermute x9, waiting for transfers between devices, flip(): lax.ppermute(value, axis, [(i, i ^ bits) for i in range(lax.axis_size(axi...  8.61 us
    ppermute x2, starting transfers between devices, shift(): lax.ppermute(value, axis, [(i, (i + distance) % count) for i in range(cou...  5.78 us
    ppermute x2, waiting for transfers between devices, shift(): lax.ppermute(value, axis, [(i, (i + distance) % count) for i in range(cou...  4.85 us
    pallas_call x5, Pallas kernels, call(): pl.pallas_call(kernel, out_shape=outputs, in_specs=[pl.BlockSpec(memory_s...  4.6 us
    ppermute x1, starting transfers between devices, second_ring(): lax.ppermute(value, axis, [(i, (i + (1 if i % 2 else -1)) % count) for i...  3.13 us
    ppermute x3, starting transfers between devices, second_pairs(): return lax.ppermute(value, axes, route)  0.91 us
  transfers between devices with their start and end apart: 15, of which 10 were waited for; matrix products, arithmetic and copies ran while one was open for 0% of the time, Pallas kernels for 4%

profile of v2, /device:TPU:2, one launch (start us, length us, event | category | flops | bytes accessed | tf_op | source)
XLA Modules:
  0.0 40.5 jit_solution(5094479880544011739)
XLA Ops:
  0.6 1.6 %face_traces.1 = (f32[4,7,7,8,128]{4,3,2,1,0:T(8,128)S(1)}, f32[49,8,128]{2,1,0:T(8,128)S(1)}, f32[49,8,128]{2,1,0:T(8,128)S(1)}, f32[14,8,128]{2,1,0:T(8,128)S(...) custom-call(f32[7,7,7,1,4,128]{5,4,3,2,1,0:T(4,128)} %rhs_hbm.1, ...), custom_call_target="tpu_custom_call" | custom-call | flops 4000000 | bytes 2951168 | tf_op jit(solution)/shard_map/face_traces/pallas_call | solution.py:491
  2.3 0.1 collective-permute-start.4
  2.4 2.4 %collective-permute-start = (f32[49,8,128]{2,1,0:T(8,128)S(1)}, f32[49,8,128]{2,1,0:T(8,128)S(1)}, u32[]{:S(2)}, u32[]{:S(2)}) collective-permute-start(f32[49,8,128]{2,1,0:T(8,128)S(1)} %get-tuple-element.21), channel_id=1, source_target_pairs={{0,64},{64,0},{128,192},{192,128},{1,65},{65,1},{129,193},{193,129... | collective-permute-start | bytes 602120 | tf_op jit(solution)/shard_map/ppermute | solution.py:509
  4.7 0.4 %collective-permute-start.1 = (f32[49,8,128]{2,1,0:T(8,128)S(1)}, f32[49,8,128]{2,1,0:T(8,128)S(1)}, u32[]{:S(2)}, u32[]{:S(2)}) collective-permute-start(f32[49,8,128]{2,1,0:T(8,128)S(1)} %get-tuple-element.22), channel_id=1, source_target_pairs={{0,1},{1,0},{2,3},{3,2},{4,5},{5,4},{6,7},{7,6},{8,9},{9,8},{10,11... | collective-permute-start | bytes 602120 | tf_op jit(solution)/shard_map/ppermute | solution.py:524
  5.1 1.9 %collective-permute-start.2 = (f32[14,8,128]{2,1,0:T(8,128)S(1)}, f32[14,8,128]{2,1,0:T(8,128)S(1)}, u32[]{:S(2)}, u32[]{:S(2)}) collective-permute-start(f32[14,8,128]{2,1,0:T(8,128)S(1)} %get-tuple-element.23), channel_id=1, source_target_pairs={{0,8},{8,0},{16,24},{24,16},{32,40},{40,32},{48,56},{56,48},{1,9},... | collective-permute-start | bytes 172040 | tf_op jit(solution)/shard_map/ppermute | solution.py:509
  7.1 0.0 collective-permute-start.3
  7.1 0.0 collective-permute-done.4.z_a
  7.1 3.1 %collective-permute-start.5 = (f32[8,128]{1,0:T(8,128)S(1)}, f32[8,128]{1,0:T(8,128)S(1)}, u32[]{:S(2)}, u32[]{:S(2)}) collective-permute-start(f32[8,128]{1,0:T(8,128)S(1)} %get-tuple-element.26), channel_id=1, source_target_pairs={{0,7},{1,2},{2,1},{3,4},{4,3},{5,6},{6,5},{7,0},{8,15},{9,10},{10,... | collective-permute-start | bytes 12296 | tf_op jit(solution)/shard_map/ppermute | solution.py:529
  10.2 0.6 %own_cells.1.local = f32[4,7,7,8,128]{4,3,2,1,0:T(8,128)S(1)} custom-call(f32[4,7,7,8,128]{4,3,2,1,0:T(8,128)S(1)} %get-tuple-element.19.first), custom_call_target="tpu_custom_call" | custom-call | flops 4000000000 | bytes 1605632 | tf_op jit(solution)/shard_map/own_cells/pallas_call | solution.py:491
  10.8 0.8 %collective-permute-done.5.z_b = f32[8,128]{1,0:T(8,128)S(1)} collective-permute-done((f32[8,128]{1,0:T(8,128)S(1)}, f32[8,128]{1,0:T(8,128)S(1)}, u32[]{:S(2)}, u32[]{:S(2)}) %collective-permute-start.5) | collective-permute-done | bytes 4128 | tf_op jit(solution)/shard_map/ppermute | solution.py:529
  11.5 0.0 collective-permute-done.2.y_a
  11.5 0.0 collective-permute-done.3.y_b
  11.5 0.0 collective-permute-done.x_a
  11.5 0.2 collective-permute-done.1.x_b
  11.8 0.8 %smooth_and_restrict.1 = (f32[4,7,7,8,128]{4,3,2,1,0:T(8,128)S(1)}, f32[2,8,128]{2,1,0:T(8,128)S(1)}, f32[2,8,128]{2,1,0:T(8,128)S(1)}, f32[2,8,128]{2,1,0:T(8,128)S(1)}, f32[2,8,128]{2,1,0:T(8,128)S(1)}) custom-call(f32[4,7,7,8,128]{4,3,2,1,0:T(8,128)S(1)} %get-tuple-element.19.first, f32[4,7,7,8,128]{4,3,2,1,0:T(8,128)S(1)} %own_cells.1.local, ...), custom_call_target="tpu_custom_call" | custom-call | flops 5000000 | bytes 3885056 | tf_op jit(solution)/shard_map/smooth_and_restrict/pallas_call | solution.py:491
  12.6 0.4 collective-permute-start.6
  13.0 0.5 %collective-permute-start.7 = (f32[2,8,128]{2,1,0:T(8,128)S(1)}, f32[2,8,128]{2,1,0:T(8,128)S(1)}, u32[]{:S(2)}, u32[]{:S(2)}) collective-permute-start(f32[2,8,128]{2,1,0:T(8,128)S(1)} %get-tuple-element.34), channel_id=1, source_target_pairs={{0,1},{1,0},{2,3},{3,2},{4,5},{5,4},{6,7},{7,6},{8,9},{9,8},{10,11... | collective-permute-start | bytes 24584 | tf_op jit(solution)/shard_map/ppermute | solution.py:524
  13.5 1.1 %collective-permute-start.8 = (f32[2,8,128]{2,1,0:T(8,128)S(1)}, f32[2,8,128]{2,1,0:T(8,128)S(1)}, u32[]{:S(2)}, u32[]{:S(2)}) collective-permute-start(f32[2,8,128]{2,1,0:T(8,128)S(1)} %get-tuple-element.35), channel_id=1, source_target_pairs={{0,128},{64,192},{128,0},{192,64},{1,129},{65,193},{129,1},{193,65... | collective-permute-start | bytes 24584 | tf_op jit(solution)/shard_map/ppermute | solution.py:509
  14.6 1.8 %collective-permute-done.6 = f32[2,8,128]{2,1,0:T(8,128)S(1)} collective-permute-done((f32[2,8,128]{2,1,0:T(8,128)S(1)}, f32[2,8,128]{2,1,0:T(8,128)S(1)}, u32[]{:S(2)}, u32[]{:S(2)}) %collective-permute-start.6) | collective-permute-done | bytes 8224 | tf_op jit(solution)/shard_map/ppermute | solution.py:509
  16.4 0.3 collective-permute-done.7
  16.6 2.0 %collective-permute-done.8 = f32[2,8,128]{2,1,0:T(8,128)S(1)} collective-permute-done((f32[2,8,128]{2,1,0:T(8,128)S(1)}, f32[2,8,128]{2,1,0:T(8,128)S(1)}, u32[]{:S(2)}, u32[]{:S(2)}) %collective-permute-start.8) | collective-permute-done | bytes 8224 | tf_op jit(solution)/shard_map/ppermute | solution.py:509
  18.6 5.8 %collective-permute-start.10 = (f32[2,8,128]{2,1,0:T(8,128)S(1)}, f32[2,8,128]{2,1,0:T(8,128)S(1)}, u32[]{:S(2)}, u32[]{:S(2)}) collective-permute-start(f32[2,8,128]{2,1,0:T(8,128)S(1)} %multiply_add_fusion), channel_id=1, source_target_pairs={{0,56},{8,0},{16,8},{24,16},{32,24},{40,32},{48,40},{56,48},{1,57}... | collective-permute-start | bytes 24584 | tf_op jit(solution)/shard_map/ppermute | solution.py:505
  24.4 0.0 collective-permute-start.9
  24.4 1.4 %collective-permute-done.10 = f32[2,8,128]{2,1,0:T(8,128)S(1)} collective-permute-done((f32[2,8,128]{2,1,0:T(8,128)S(1)}, f32[2,8,128]{2,1,0:T(8,128)S(1)}, u32[]{:S(2)}, u32[]{:S(2)}) %collective-permute-start.10) | collective-permute-done | bytes 8224 | tf_op jit(solution)/shard_map/ppermute | solution.py:505
  25.8 3.5 %collective-permute-done.9 = f32[2,8,128]{2,1,0:T(8,128)S(1)} collective-permute-done((f32[2,8,128]{2,1,0:T(8,128)S(1)}, f32[2,8,128]{2,1,0:T(8,128)S(1)}, u32[]{:S(2)}, u32[]{:S(2)}) %collective-permute-start.9) | collective-permute-done | bytes 8224 | tf_op jit(solution)/shard_map/ppermute | solution.py:505
  29.3 0.1 fusion.1
  29.4 0.0 collective-permute-start.11
  29.4 1.2 %collective-permute-done.11.other = f32[8,128]{1,0:T(8,128)S(1)} collective-permute-done((f32[8,128]{1,0:T(8,128)S(1)}, f32[8,128]{1,0:T(8,128)S(1)}, u32[]{:S(2)}, u32[]{:S(2)}) %collective-permute-start.11) | collective-permute-done | bytes 4128 | tf_op jit(solution)/shard_map/ppermute | solution.py:509
  30.6 1.6 %collective-permute-start.12 = (f32[2,8,128]{2,1,0:T(8,128)S(1)}, f32[2,8,128]{2,1,0:T(8,128)S(1)}, u32[]{:S(2)}, u32[]{:S(2)}) collective-permute-start(f32[2,8,128]{2,1,0:T(8,128)S(1)} %pad_maximum_fusion), channel_id=1, source_target_pairs={{0,2},{1,3},{2,0},{3,1},{4,6},{5,7},{6,4},{7,5},{8,10},{9,11},{10,... | collective-permute-start | bytes 24584 | tf_op jit(solution)/shard_map/ppermute | solution.py:509
  32.1 2.9 %collective-permute-start.13 = (f32[2,8,128]{2,1,0:T(8,128)S(1)}, f32[2,8,128]{2,1,0:T(8,128)S(1)}, u32[]{:S(2)}, u32[]{:S(2)}) collective-permute-start(f32[2,8,128]{2,1,0:T(8,128)S(1)} %pad_maximum_fusion), channel_id=1, source_target_pairs={{0,4},{1,5},{2,6},{3,7},{4,0},{5,1},{6,2},{7,3},{8,12},{9,13},{10,... | collective-permute-start | bytes 24584 | tf_op jit(solution)/shard_map/ppermute | solution.py:509
  35.0 0.2 collective-permute-start.14
  35.3 0.9 %unpack_modes.1 = f32[7,7,7,1,4,128]{5,4,3,2,1,0:T(4,128)} custom-call(f32[4,7,7,8,128]{4,3,2,1,0:T(8,128)S(1)} %get-tuple-element.31.field), custom_call_target="tpu_custom_call" | custom-call | flops 200000 | bytes 1505280 | tf_op jit(solution)/shard_map/unpack_modes/pallas_call | solution.py:491
  36.2 0.0 collective-permute-done.12.next_chip
  36.2 1.1 %collective-permute-done.13.over_chip = f32[2,8,128]{2,1,0:T(8,128)S(1)} collective-permute-done((f32[2,8,128]{2,1,0:T(8,128)S(1)}, f32[2,8,128]{2,1,0:T(8,128)S(1)}, u32[]{:S(2)}, u32[]{:S(2)}) %collective-permute-start.13) | collective-permute-done | bytes 8224 | tf_op jit(solution)/shard_map/ppermute | solution.py:509
  37.3 2.6 %collective-permute-done.14.last_chip = f32[2,8,128]{2,1,0:T(8,128)S(1)} collective-permute-done((f32[2,8,128]{2,1,0:T(8,128)S(1)}, f32[2,8,128]{2,1,0:T(8,128)S(1)}, u32[]{:S(2)}, u32[]{:S(2)}) %collective-permute-start.14) | collective-permute-done | bytes 8224 | tf_op jit(solution)/shard_map/ppermute | solution.py:509
  39.9 0.6 %column.1 = f32[1,4,1024]{2,1,0:T(4,128)} custom-call(f32[8,128]{1,0:T(8,128)S(1)} %bitcast.5, f32[8,128]{1,0:T(8,128)S(1)} %collective-permute-done.11.other, f32[2,8,128]{2,1,0:T(8,128)S(1)} %collective-permute-done.12.next_chip, f32[2,8,128]{2,1,0:T(8,128)S(1)} %collective-permute-done.13.over_chip, f32[2,8,128]{2,1,0:T(8,128)S(1)} %collective-permute-done.14.last_chip), custom_call_target="tpu_custom_call" | custom-call | flops 20000 | bytes 49152 | tf_op jit(solution)/shard_map/column/pallas_call | solution.py:491
  (3 shorter events, 0.0 us)
Async XLA Ops:
  2.3 4.8 %collective-permute-start.4 = (f32[8,128]{1,0:T(8,128)S(1)}, f32[8,128]{1,0:T(8,128)S(1)}, u32[]{:S(2)}, u32[]{:S(2)}) collective-permute-start(f32[8,128]{1,0:T(8,128)S(1)} %get-tuple-element.25), channel_id=1, source_target_pairs={{0,1},{1,0},{2,3},{3,2},{4,5},{5,4},{6,7},{7,6},{8,9},{9,8},{10,11... | collective-permute-start | bytes 12296 | tf_op jit(solution)/shard_map/ppermute | solution.py:509
  2.4 9.2 %collective-permute-start = (f32[49,8,128]{2,1,0:T(8,128)S(1)}, f32[49,8,128]{2,1,0:T(8,128)S(1)}, u32[]{:S(2)}, u32[]{:S(2)}) collective-permute-start(f32[49,8,128]{2,1,0:T(8,128)S(1)} %get-tuple-element.21), channel_id=1, source_target_pairs={{0,64},{64,0},{128,192},{192,128},{1,65},{65,1},{129,193},{193,129... | collective-permute-start | bytes 602120 | tf_op jit(solution)/shard_map/ppermute | solution.py:509
  4.7 7.0 %collective-permute-start.1 = (f32[49,8,128]{2,1,0:T(8,128)S(1)}, f32[49,8,128]{2,1,0:T(8,128)S(1)}, u32[]{:S(2)}, u32[]{:S(2)}) collective-permute-start(f32[49,8,128]{2,1,0:T(8,128)S(1)} %get-tuple-element.22), channel_id=1, source_target_pairs={{0,1},{1,0},{2,3},{3,2},{4,5},{5,4},{6,7},{7,6},{8,9},{9,8},{10,11... | collective-permute-start | bytes 602120 | tf_op jit(solution)/shard_map/ppermute | solution.py:524
  5.1 6.4 %collective-permute-start.2 = (f32[14,8,128]{2,1,0:T(8,128)S(1)}, f32[14,8,128]{2,1,0:T(8,128)S(1)}, u32[]{:S(2)}, u32[]{:S(2)}) collective-permute-start(f32[14,8,128]{2,1,0:T(8,128)S(1)} %get-tuple-element.23), channel_id=1, source_target_pairs={{0,8},{8,0},{16,24},{24,16},{32,40},{40,32},{48,56},{56,48},{1,9},... | collective-permute-start | bytes 172040 | tf_op jit(solution)/shard_map/ppermute | solution.py:509
  7.1 4.5 %collective-permute-start.3 = (f32[14,8,128]{2,1,0:T(8,128)S(1)}, f32[14,8,128]{2,1,0:T(8,128)S(1)}, u32[]{:S(2)}, u32[]{:S(2)}) collective-permute-start(f32[14,8,128]{2,1,0:T(8,128)S(1)} %get-tuple-element.24), channel_id=1, source_target_pairs={{0,1},{1,0},{2,3},{3,2},{4,5},{5,4},{6,7},{7,6},{8,16},{9,17},{10,... | collective-permute-start | bytes 172040 | tf_op jit(solution)/shard_map/ppermute | solution.py:524
  7.1 4.5 %collective-permute-start.5 = (f32[8,128]{1,0:T(8,128)S(1)}, f32[8,128]{1,0:T(8,128)S(1)}, u32[]{:S(2)}, u32[]{:S(2)}) collective-permute-start(f32[8,128]{1,0:T(8,128)S(1)} %get-tuple-element.26), channel_id=1, source_target_pairs={{0,7},{1,2},{2,1},{3,4},{4,3},{5,6},{6,5},{7,0},{8,15},{9,10},{10,... | collective-permute-start | bytes 12296 | tf_op jit(solution)/shard_map/ppermute | solution.py:529
  12.6 3.7 %collective-permute-start.6 = (f32[2,8,128]{2,1,0:T(8,128)S(1)}, f32[2,8,128]{2,1,0:T(8,128)S(1)}, u32[]{:S(2)}, u32[]{:S(2)}) collective-permute-start(f32[2,8,128]{2,1,0:T(8,128)S(1)} %get-tuple-element.33), channel_id=1, source_target_pairs={{0,64},{64,0},{128,192},{192,128},{1,65},{65,1},{129,193},{193,129... | collective-permute-start | bytes 24584 | tf_op jit(solution)/shard_map/ppermute | solution.py:509
  13.0 3.7 %collective-permute-start.7 = (f32[2,8,128]{2,1,0:T(8,128)S(1)}, f32[2,8,128]{2,1,0:T(8,128)S(1)}, u32[]{:S(2)}, u32[]{:S(2)}) collective-permute-start(f32[2,8,128]{2,1,0:T(8,128)S(1)} %get-tuple-element.34), channel_id=1, source_target_pairs={{0,1},{1,0},{2,3},{3,2},{4,5},{5,4},{6,7},{7,6},{8,9},{9,8},{10,11... | collective-permute-start | bytes 24584 | tf_op jit(solution)/shard_map/ppermute | solution.py:524
  13.5 5.2 %collective-permute-start.8 = (f32[2,8,128]{2,1,0:T(8,128)S(1)}, f32[2,8,128]{2,1,0:T(8,128)S(1)}, u32[]{:S(2)}, u32[]{:S(2)}) collective-permute-start(f32[2,8,128]{2,1,0:T(8,128)S(1)} %get-tuple-element.35), channel_id=1, source_target_pairs={{0,128},{64,192},{128,0},{192,64},{1,129},{65,193},{129,1},{193,65... | collective-permute-start | bytes 24584 | tf_op jit(solution)/shard_map/ppermute | solution.py:509
  18.6 7.1 %collective-permute-start.10 = (f32[2,8,128]{2,1,0:T(8,128)S(1)}, f32[2,8,128]{2,1,0:T(8,128)S(1)}, u32[]{:S(2)}, u32[]{:S(2)}) collective-permute-start(f32[2,8,128]{2,1,0:T(8,128)S(1)} %multiply_add_fusion), channel_id=1, source_target_pairs={{0,56},{8,0},{16,8},{24,16},{32,24},{40,32},{48,40},{56,48},{1,57}... | collective-permute-start | bytes 24584 | tf_op jit(solution)/shard_map/ppermute | solution.py:505
  24.4 4.9 %collective-permute-start.9 = (f32[2,8,128]{2,1,0:T(8,128)S(1)}, f32[2,8,128]{2,1,0:T(8,128)S(1)}, u32[]{:S(2)}, u32[]{:S(2)}) collective-permute-start(f32[2,8,128]{2,1,0:T(8,128)S(1)} %multiply_add_fusion), channel_id=1, source_target_pairs={{0,8},{8,16},{16,24},{24,32},{32,40},{40,48},{48,56},{56,0},{1,9},... | collective-permute-start | bytes 24584 | tf_op jit(solution)/shard_map/ppermute | solution.py:505
  29.4 1.2 %collective-permute-start.11 = (f32[8,128]{1,0:T(8,128)S(1)}, f32[8,128]{1,0:T(8,128)S(1)}, u32[]{:S(2)}, u32[]{:S(2)}) collective-permute-start(f32[8,128]{1,0:T(8,128)S(1)} %bitcast.3), channel_id=1, source_target_pairs={{0,1},{1,0},{2,3},{3,2},{4,5},{5,4},{6,7},{7,6},{8,9},{9,8},{10,11... | collective-permute-start | bytes 12296 | tf_op jit(solution)/shard_map/ppermute | solution.py:509
  30.6 5.6 %collective-permute-start.12 = (f32[2,8,128]{2,1,0:T(8,128)S(1)}, f32[2,8,128]{2,1,0:T(8,128)S(1)}, u32[]{:S(2)}, u32[]{:S(2)}) collective-permute-start(f32[2,8,128]{2,1,0:T(8,128)S(1)} %pad_maximum_fusion), channel_id=1, source_target_pairs={{0,2},{1,3},{2,0},{3,1},{4,6},{5,7},{6,4},{7,5},{8,10},{9,11},{10,... | collective-permute-start | bytes 24584 | tf_op jit(solution)/shard_map/ppermute | solution.py:509
  32.1 5.2 %collective-permute-start.13 = (f32[2,8,128]{2,1,0:T(8,128)S(1)}, f32[2,8,128]{2,1,0:T(8,128)S(1)}, u32[]{:S(2)}, u32[]{:S(2)}) collective-permute-start(f32[2,8,128]{2,1,0:T(8,128)S(1)} %pad_maximum_fusion), channel_id=1, source_target_pairs={{0,4},{1,5},{2,6},{3,7},{4,0},{5,1},{6,2},{7,3},{8,12},{9,13},{10,... | collective-permute-start | bytes 24584 | tf_op jit(solution)/shard_map/ppermute | solution.py:509
  35.0 4.9 %collective-permute-start.14 = (f32[2,8,128]{2,1,0:T(8,128)S(1)}, f32[2,8,128]{2,1,0:T(8,128)S(1)}, u32[]{:S(2)}, u32[]{:S(2)}) collective-permute-start(f32[2,8,128]{2,1,0:T(8,128)S(1)} %pad_maximum_fusion), channel_id=1, source_target_pairs={{0,6},{1,7},{2,4},{3,5},{4,2},{5,3},{6,0},{7,1},{8,14},{9,15},{10,... | collective-permute-start | bytes 24584 | tf_op jit(solution)/shard_map/ppermute | solution.py:509

commit v3 on v2

--- a/solution.py
+++ b/solution.py
@@ -448,7 +448,7 @@
                     smoothed[2 * i + 1, b, e, 0] = value[4:]
 
 
-def column_kernel(own, other, next_chip, over_chip, last_chip, column, blocks):
+def column_kernel(own, other, over_chip, next_chip, last_chip, column, blocks):
     count = lax.axis_size("gz")
     me = lax.axis_index("gz")
     mate = me + 1 - 2 * lax.rem(me, 2)
@@ -500,11 +500,6 @@
     )(*inputs)
 
 
-def shift(value, axis, distance):
-    count = lax.axis_size(axis)
-    return lax.ppermute(value, axis, [(i, (i + distance) % count) for i in range(count)])
-
-
 def flip(value, axis, bits):
     return lax.ppermute(value, axis, [(i, i ^ bits) for i in range(lax.axis_size(axis))])
 
@@ -517,18 +512,11 @@
         target = list(place)
         k = axes.index(axis)
         if place[k] in (0, sizes[k] - 1):
-            target[2] ^= 1
+            target[0 if axis == "gz" else 2] ^= 1
         else:
             target[k] += 1 if place[k] % 2 else -1
         route.append((source, int(np.ravel_multi_index(target, sizes))))
     return lax.ppermute(value, axes, route)
-
-
-def second_ring(value, axis):
-    count = lax.axis_size(axis)
-    return lax.ppermute(
-        value, axis, [(i, (i + (1 if i % 2 else -1)) % count) for i in range(count)]
-    )
 
 
 def inside(axis, distance):
@@ -557,7 +545,7 @@
     )
     x_a, x_b = flip(x_a, "gx", 1), second_pairs(x_b, "gx")
     y_a, y_b = flip(y_a, "gy", 1), second_pairs(y_b, "gy")
-    z_a, z_b = flip(z_a, "gz", 1), second_ring(z_b, "gz")
+    z_a, z_b = flip(z_a, "gz", 1), second_pairs(z_b, "gz")
     (local,) = call(own_kernel, "own_cells", (first,), (shape(*cells),), 4_000_000_000)
     field, here, sum_a, sum_b, far = call(
         finish_in_place,
@@ -570,13 +558,18 @@
         scratch=(pltpu.VMEM(cells, jnp.float32),),
     )
     (smoothed,) = call(unpack_kernel, "unpack_modes", (field,), (shape(*rhs.shape),), 200_000)
+    from_far = flip(far, "gx", 2)
+    from_a = flip(sum_a, "gx", 1)
+    from_b = second_pairs(sum_b, "gx")
     sums = (
         here
-        + flip(sum_a, "gx", 1)
-        + inside("gx", -1) * inside("gx", 1) * second_pairs(sum_b, "gx")
-        + inside("gx", -2) * flip(far, "gx", 2)
-    )
-    from_low, from_high = shift(sums, "gy", 1), shift(sums, "gy", -1)
+        + inside("gx", -2) * from_far
+        + from_a
+        + inside("gx", -1) * inside("gx", 1) * from_b
+    )
+    even = lax.axis_index("gy") % 2 == 0
+    from_a, from_b = flip(sums, "gy", 1), second_pairs(sums, "gy")
+    from_low, from_high = jnp.where(even, from_b, from_a), jnp.where(even, from_a, from_b)
     row = lax.broadcasted_iota(jnp.int32, (1, 4, 1), 1)
     owned = (
         sums[:, :4]
@@ -586,11 +579,11 @@
     count = lax.axis_size("gz")
     other = flip(owned, "gz", 1)
     chip = jnp.stack([owned, other])
-    chips = [flip(chip, "gz", 2 * k) for k in range(1, count // 2)]
+    across, beside, opposite = (flip(chip, "gz", bits) for bits in (4, 2, 6))
     (column,) = call(
         column_kernel,
         "column",
-        (owned, other, *chips),
+        (owned, other, across, beside, opposite),
         (shape(1, 4, 128 * count),),
         20_000,
         scratch=(pltpu.VMEM((count + 2, 8, 128), jnp.float32),),

time: 40.6 us -> 35.9 us (0.88)
  the two profiles are of different devices: /device:TPU:2 before, /device:TPU:68 now
where the time goes in v3:
time: 35.9 us; the launch traced here: 35.7 us
  starting transfers between devices  16.2 us (45%)
  waiting for transfers between devices  14.2 us (40%)
  Pallas kernels  4.6 us (13%)
  between operations  0.68 us (2%)
    ppermute x10, starting transfers between devices, flip(): lax.ppermute(value, axis, [(i, i ^ bits) for i in range(lax.axis_size(axi...  14.3 us
    ppermute x5, waiting for transfers between devices, second_pairs(): return lax.ppermute(value, axes, route)  7.21 us
    ppermute x10, waiting for transfers between devices, flip(): lax.ppermute(value, axis, [(i, i ^ bits) for i in range(lax.axis_size(axi...  6.96 us
    pallas_call x5, Pallas kernels, call(): pl.pallas_call(kernel, out_shape=outputs, in_specs=[pl.BlockSpec(memory_s...  4.6 us
    ppermute x5, starting transfers between devices, second_pairs(): return lax.ppermute(value, axes, route)  1.94 us
  transfers between devices with their start and end apart: 15, of which 10 were waited for; matrix products, arithmetic and copies ran while one was open for 0% of the time, Pallas kernels for 4%

profile of v3, /device:TPU:68, one launch (start us, length us, event | category | flops | bytes accessed | tf_op | source)
XLA Modules:
  0.0 35.7 jit_solution(13945127132113859922)
XLA Ops:
  0.6 1.6 %face_traces.1 = (f32[4,7,7,8,128]{4,3,2,1,0:T(8,128)S(1)}, f32[49,8,128]{2,1,0:T(8,128)S(1)}, f32[49,8,128]{2,1,0:T(8,128)S(1)}, f32[14,8,128]{2,1,0:T(8,128)S(...) custom-call(f32[7,7,7,1,4,128]{5,4,3,2,1,0:T(4,128)} %rhs_hbm.1, ...), custom_call_target="tpu_custom_call" | custom-call | flops 4000000 | bytes 2951168 | tf_op jit(solution)/shard_map/face_traces/pallas_call | solution.py:491
  2.3 0.1 collective-permute-start.4
  2.4 1.3 %collective-permute-start = (f32[49,8,128]{2,1,0:T(8,128)S(1)}, f32[49,8,128]{2,1,0:T(8,128)S(1)}, u32[]{:S(2)}, u32[]{:S(2)}) collective-permute-start(f32[49,8,128]{2,1,0:T(8,128)S(1)} %get-tuple-element.21), channel_id=1, source_target_pairs={{0,64},{64,0},{128,192},{192,128},{1,65},{65,1},{129,193},{193,129... | collective-permute-start | bytes 602120 | tf_op jit(solution)/shard_map/ppermute | solution.py:504
  3.7 0.0 collective-permute-start.1
  3.7 1.9 %collective-permute-start.2 = (f32[14,8,128]{2,1,0:T(8,128)S(1)}, f32[14,8,128]{2,1,0:T(8,128)S(1)}, u32[]{:S(2)}, u32[]{:S(2)}) collective-permute-start(f32[14,8,128]{2,1,0:T(8,128)S(1)} %get-tuple-element.23), channel_id=1, source_target_pairs={{0,8},{8,0},{16,24},{24,16},{32,40},{40,32},{48,56},{56,48},{1,9},... | collective-permute-start | bytes 172040 | tf_op jit(solution)/shard_map/ppermute | solution.py:504
  5.6 0.0 collective-permute-start.3
  5.6 0.0 collective-permute-done.4.z_a
  5.6 1.0 %collective-permute-start.5 = (f32[8,128]{1,0:T(8,128)S(1)}, f32[8,128]{1,0:T(8,128)S(1)}, u32[]{:S(2)}, u32[]{:S(2)}) collective-permute-start(f32[8,128]{1,0:T(8,128)S(1)} %get-tuple-element.26), channel_id=1, source_target_pairs={{0,64},{1,2},{2,1},{3,4},{4,3},{5,6},{6,5},{7,71},{8,72},{9,10},{1... | collective-permute-start | bytes 12296 | tf_op jit(solution)/shard_map/ppermute | solution.py:519
  6.6 0.6 %own_cells.1.local = f32[4,7,7,8,128]{4,3,2,1,0:T(8,128)S(1)} custom-call(f32[4,7,7,8,128]{4,3,2,1,0:T(8,128)S(1)} %get-tuple-element.19.first), custom_call_target="tpu_custom_call" | custom-call | flops 4000000000 | bytes 1605632 | tf_op jit(solution)/shard_map/own_cells/pallas_call | solution.py:491
  7.1 2.7 %collective-permute-done.5.z_b = f32[8,128]{1,0:T(8,128)S(1)} collective-permute-done((f32[8,128]{1,0:T(8,128)S(1)}, f32[8,128]{1,0:T(8,128)S(1)}, u32[]{:S(2)}, u32[]{:S(2)}) %collective-permute-start.5) | collective-permute-done | bytes 4128 | tf_op jit(solution)/shard_map/ppermute | solution.py:519
  9.8 0.0 collective-permute-done.2.y_a
  9.8 0.0 collective-permute-done.3.y_b
  9.8 0.0 collective-permute-done.x_a
  9.8 0.9 %collective-permute-done.1.x_b = f32[49,8,128]{2,1,0:T(8,128)S(1)} collective-permute-done((f32[49,8,128]{2,1,0:T(8,128)S(1)}, f32[49,8,128]{2,1,0:T(8,128)S(1)}, u32[]{:S(2)}, u32[]{:S(2)}) %collective-permute-start.1) | collective-permute-done | bytes 200736 | tf_op jit(solution)/shard_map/ppermute | solution.py:519
  10.7 0.8 %smooth_and_restrict.1 = (f32[4,7,7,8,128]{4,3,2,1,0:T(8,128)S(1)}, f32[2,8,128]{2,1,0:T(8,128)S(1)}, f32[2,8,128]{2,1,0:T(8,128)S(1)}, f32[2,8,128]{2,1,0:T(8,128)S(1)}, f32[2,8,128]{2,1,0:T(8,128)S(1)}) custom-call(f32[4,7,7,8,128]{4,3,2,1,0:T(8,128)S(1)} %get-tuple-element.19.first, f32[4,7,7,8,128]{4,3,2,1,0:T(8,128)S(1)} %own_cells.1.local, ...), custom_call_target="tpu_custom_call" | custom-call | flops 5000000 | bytes 3885056 | tf_op jit(solution)/shard_map/smooth_and_restrict/pallas_call | solution.py:491
  11.5 0.1 collective-permute-start.6
  11.7 3.1 %collective-permute-start.7 = (f32[2,8,128]{2,1,0:T(8,128)S(1)}, f32[2,8,128]{2,1,0:T(8,128)S(1)}, u32[]{:S(2)}, u32[]{:S(2)}) collective-permute-start(f32[2,8,128]{2,1,0:T(8,128)S(1)} %get-tuple-element.34), channel_id=1, source_target_pairs={{0,64},{64,0},{128,192},{192,128},{1,65},{65,1},{129,193},{193,129... | collective-permute-start | bytes 24584 | tf_op jit(solution)/shard_map/ppermute | solution.py:504
  14.8 0.9 %collective-permute-start.8 = (f32[2,8,128]{2,1,0:T(8,128)S(1)}, f32[2,8,128]{2,1,0:T(8,128)S(1)}, u32[]{:S(2)}, u32[]{:S(2)}) collective-permute-start(f32[2,8,128]{2,1,0:T(8,128)S(1)} %get-tuple-element.35), channel_id=1, source_target_pairs={{0,1},{1,0},{2,3},{3,2},{4,5},{5,4},{6,7},{7,6},{8,9},{9,8},{10,11... | collective-permute-start | bytes 24584 | tf_op jit(solution)/shard_map/ppermute | solution.py:519
  15.7 1.1 %collective-permute-done.6 = f32[2,8,128]{2,1,0:T(8,128)S(1)} collective-permute-done((f32[2,8,128]{2,1,0:T(8,128)S(1)}, f32[2,8,128]{2,1,0:T(8,128)S(1)}, u32[]{:S(2)}, u32[]{:S(2)}) %collective-permute-start.6) | collective-permute-done | bytes 8224 | tf_op jit(solution)/shard_map/ppermute | solution.py:504
  16.8 0.0 collective-permute-done.7
  16.8 1.6 %collective-permute-done.8 = f32[2,8,128]{2,1,0:T(8,128)S(1)} collective-permute-done((f32[2,8,128]{2,1,0:T(8,128)S(1)}, f32[2,8,128]{2,1,0:T(8,128)S(1)}, u32[]{:S(2)}, u32[]{:S(2)}) %collective-permute-start.8) | collective-permute-done | bytes 8224 | tf_op jit(solution)/shard_map/ppermute | solution.py:519
  18.4 3.6 %collective-permute-start.10 = (f32[2,8,128]{2,1,0:T(8,128)S(1)}, f32[2,8,128]{2,1,0:T(8,128)S(1)}, u32[]{:S(2)}, u32[]{:S(2)}) collective-permute-start(f32[2,8,128]{2,1,0:T(8,128)S(1)} %multiply_add_fusion), channel_id=1, source_target_pairs={{0,8},{8,0},{16,24},{24,16},{32,40},{40,32},{48,56},{56,48},{1,9},... | collective-permute-start | bytes 24584 | tf_op jit(solution)/shard_map/ppermute | solution.py:504
  22.0 0.0 collective-permute-start.9
  22.1 1.6 %collective-permute-done.10 = f32[2,8,128]{2,1,0:T(8,128)S(1)} collective-permute-done((f32[2,8,128]{2,1,0:T(8,128)S(1)}, f32[2,8,128]{2,1,0:T(8,128)S(1)}, u32[]{:S(2)}, u32[]{:S(2)}) %collective-permute-start.10) | collective-permute-done | bytes 8224 | tf_op jit(solution)/shard_map/ppermute | solution.py:504
  23.7 2.0 %collective-permute-done.9 = f32[2,8,128]{2,1,0:T(8,128)S(1)} collective-permute-done((f32[2,8,128]{2,1,0:T(8,128)S(1)}, f32[2,8,128]{2,1,0:T(8,128)S(1)}, u32[]{:S(2)}, u32[]{:S(2)}) %collective-permute-start.9) | collective-permute-done | bytes 8224 | tf_op jit(solution)/shard_map/ppermute | solution.py:519
  25.7 0.1 fusion
  25.8 0.0 collective-permute-start.11
  25.8 1.2 %collective-permute-done.11.other = f32[8,128]{1,0:T(8,128)S(1)} collective-permute-done((f32[8,128]{1,0:T(8,128)S(1)}, f32[8,128]{1,0:T(8,128)S(1)}, u32[]{:S(2)}, u32[]{:S(2)}) %collective-permute-start.11) | collective-permute-done | bytes 4128 | tf_op jit(solution)/shard_map/ppermute | solution.py:504
  27.0 2.6 %collective-permute-start.12 = (f32[2,8,128]{2,1,0:T(8,128)S(1)}, f32[2,8,128]{2,1,0:T(8,128)S(1)}, u32[]{:S(2)}, u32[]{:S(2)}) collective-permute-start(f32[2,8,128]{2,1,0:T(8,128)S(1)} %pad_maximum_fusion), channel_id=1, source_target_pairs={{0,4},{1,5},{2,6},{3,7},{4,0},{5,1},{6,2},{7,3},{8,12},{9,13},{10,... | collective-permute-start | bytes 24584 | tf_op jit(solution)/shard_map/ppermute | solution.py:504
  29.6 0.7 %collective-permute-start.13 = (f32[2,8,128]{2,1,0:T(8,128)S(1)}, f32[2,8,128]{2,1,0:T(8,128)S(1)}, u32[]{:S(2)}, u32[]{:S(2)}) collective-permute-start(f32[2,8,128]{2,1,0:T(8,128)S(1)} %pad_maximum_fusion), channel_id=1, source_target_pairs={{0,2},{1,3},{2,0},{3,1},{4,6},{5,7},{6,4},{7,5},{8,10},{9,11},{10,... | collective-permute-start | bytes 24584 | tf_op jit(solution)/shard_map/ppermute | solution.py:504
  30.3 0.8 %collective-permute-start.14 = (f32[2,8,128]{2,1,0:T(8,128)S(1)}, f32[2,8,128]{2,1,0:T(8,128)S(1)}, u32[]{:S(2)}, u32[]{:S(2)}) collective-permute-start(f32[2,8,128]{2,1,0:T(8,128)S(1)} %pad_maximum_fusion), channel_id=1, source_target_pairs={{0,6},{1,7},{2,4},{3,5},{4,2},{5,3},{6,0},{7,1},{8,14},{9,15},{10,... | collective-permute-start | bytes 24584 | tf_op jit(solution)/shard_map/ppermute | solution.py:504
  31.1 0.9 %unpack_modes.1 = f32[7,7,7,1,4,128]{5,4,3,2,1,0:T(4,128)} custom-call(f32[4,7,7,8,128]{4,3,2,1,0:T(8,128)S(1)} %get-tuple-element.31.field), custom_call_target="tpu_custom_call" | custom-call | flops 200000 | bytes 1505280 | tf_op jit(solution)/shard_map/unpack_modes/pallas_call | solution.py:491
  32.0 0.1 collective-permute-done.12.over_chip
  32.1 1.1 %collective-permute-done.13.next_chip = f32[2,8,128]{2,1,0:T(8,128)S(1)} collective-permute-done((f32[2,8,128]{2,1,0:T(8,128)S(1)}, f32[2,8,128]{2,1,0:T(8,128)S(1)}, u32[]{:S(2)}, u32[]{:S(2)}) %collective-permute-start.13) | collective-permute-done | bytes 8224 | tf_op jit(solution)/shard_map/ppermute | solution.py:504
  33.2 1.9 %collective-permute-done.14.last_chip = f32[2,8,128]{2,1,0:T(8,128)S(1)} collective-permute-done((f32[2,8,128]{2,1,0:T(8,128)S(1)}, f32[2,8,128]{2,1,0:T(8,128)S(1)}, u32[]{:S(2)}, u32[]{:S(2)}) %collective-permute-start.14) | collective-permute-done | bytes 8224 | tf_op jit(solution)/shard_map/ppermute | solution.py:504
  35.1 0.6 %column.1 = f32[1,4,1024]{2,1,0:T(4,128)} custom-call(f32[8,128]{1,0:T(8,128)S(1)} %bitcast.5, f32[8,128]{1,0:T(8,128)S(1)} %collective-permute-done.11.other, f32[2,8,128]{2,1,0:T(8,128)S(1)} %collective-permute-done.12.over_chip, f32[2,8,128]{2,1,0:T(8,128)S(1)} %collective-permute-done.13.next_chip, f32[2,8,128]{2,1,0:T(8,128)S(1)} %collective-permute-done.14.last_chip), custom_call_target="tpu_custom_call" | custom-call | flops 20000 | bytes 49152 | tf_op jit(solution)/shard_map/column/pallas_call | solution.py:491
  (3 shorter events, 0.0 us)
Async XLA Ops:
  2.3 3.3 %collective-permute-start.4 = (f32[8,128]{1,0:T(8,128)S(1)}, f32[8,128]{1,0:T(8,128)S(1)}, u32[]{:S(2)}, u32[]{:S(2)}) collective-permute-start(f32[8,128]{1,0:T(8,128)S(1)} %get-tuple-element.25), channel_id=1, source_target_pairs={{0,1},{1,0},{2,3},{3,2},{4,5},{5,4},{6,7},{7,6},{8,9},{9,8},{10,11... | collective-permute-start | bytes 12296 | tf_op jit(solution)/shard_map/ppermute | solution.py:504
  2.4 7.5 %collective-permute-start = (f32[49,8,128]{2,1,0:T(8,128)S(1)}, f32[49,8,128]{2,1,0:T(8,128)S(1)}, u32[]{:S(2)}, u32[]{:S(2)}) collective-permute-start(f32[49,8,128]{2,1,0:T(8,128)S(1)} %get-tuple-element.21), channel_id=1, source_target_pairs={{0,64},{64,0},{128,192},{192,128},{1,65},{65,1},{129,193},{193,129... | collective-permute-start | bytes 602120 | tf_op jit(solution)/shard_map/ppermute | solution.py:504
  3.7 7.0 %collective-permute-start.1 = (f32[49,8,128]{2,1,0:T(8,128)S(1)}, f32[49,8,128]{2,1,0:T(8,128)S(1)}, u32[]{:S(2)}, u32[]{:S(2)}) collective-permute-start(f32[49,8,128]{2,1,0:T(8,128)S(1)} %get-tuple-element.22), channel_id=1, source_target_pairs={{0,1},{1,0},{2,3},{3,2},{4,5},{5,4},{6,7},{7,6},{8,9},{9,8},{10,11... | collective-permute-start | bytes 602120 | tf_op jit(solution)/shard_map/ppermute | solution.py:519
  3.7 6.2 %collective-permute-start.2 = (f32[14,8,128]{2,1,0:T(8,128)S(1)}, f32[14,8,128]{2,1,0:T(8,128)S(1)}, u32[]{:S(2)}, u32[]{:S(2)}) collective-permute-start(f32[14,8,128]{2,1,0:T(8,128)S(1)} %get-tuple-element.23), channel_id=1, source_target_pairs={{0,8},{8,0},{16,24},{24,16},{32,40},{40,32},{48,56},{56,48},{1,9},... | collective-permute-start | bytes 172040 | tf_op jit(solution)/shard_map/ppermute | solution.py:504
  5.6 4.3 %collective-permute-start.3 = (f32[14,8,128]{2,1,0:T(8,128)S(1)}, f32[14,8,128]{2,1,0:T(8,128)S(1)}, u32[]{:S(2)}, u32[]{:S(2)}) collective-permute-start(f32[14,8,128]{2,1,0:T(8,128)S(1)} %get-tuple-element.24), channel_id=1, source_target_pairs={{0,1},{1,0},{2,3},{3,2},{4,5},{5,4},{6,7},{7,6},{8,16},{9,17},{10,... | collective-permute-start | bytes 172040 | tf_op jit(solution)/shard_map/ppermute | solution.py:519
  5.6 4.2 %collective-permute-start.5 = (f32[8,128]{1,0:T(8,128)S(1)}, f32[8,128]{1,0:T(8,128)S(1)}, u32[]{:S(2)}, u32[]{:S(2)}) collective-permute-start(f32[8,128]{1,0:T(8,128)S(1)} %get-tuple-element.26), channel_id=1, source_target_pairs={{0,64},{1,2},{2,1},{3,4},{4,3},{5,6},{6,5},{7,71},{8,72},{9,10},{1... | collective-permute-start | bytes 12296 | tf_op jit(solution)/shard_map/ppermute | solution.py:519
  11.5 5.2 %collective-permute-start.6 = (f32[2,8,128]{2,1,0:T(8,128)S(1)}, f32[2,8,128]{2,1,0:T(8,128)S(1)}, u32[]{:S(2)}, u32[]{:S(2)}) collective-permute-start(f32[2,8,128]{2,1,0:T(8,128)S(1)} %get-tuple-element.33), channel_id=1, source_target_pairs={{0,128},{64,192},{128,0},{192,64},{1,129},{65,193},{129,1},{193,65... | collective-permute-start | bytes 24584 | tf_op jit(solution)/shard_map/ppermute | solution.py:504
  11.7 5.1 %collective-permute-start.7 = (f32[2,8,128]{2,1,0:T(8,128)S(1)}, f32[2,8,128]{2,1,0:T(8,128)S(1)}, u32[]{:S(2)}, u32[]{:S(2)}) collective-permute-start(f32[2,8,128]{2,1,0:T(8,128)S(1)} %get-tuple-element.34), channel_id=1, source_target_pairs={{0,64},{64,0},{128,192},{192,128},{1,65},{65,1},{129,193},{193,129... | collective-permute-start | bytes 24584 | tf_op jit(solution)/shard_map/ppermute | solution.py:504
  14.8 3.7 %collective-permute-start.8 = (f32[2,8,128]{2,1,0:T(8,128)S(1)}, f32[2,8,128]{2,1,0:T(8,128)S(1)}, u32[]{:S(2)}, u32[]{:S(2)}) collective-permute-start(f32[2,8,128]{2,1,0:T(8,128)S(1)} %get-tuple-element.35), channel_id=1, source_target_pairs={{0,1},{1,0},{2,3},{3,2},{4,5},{5,4},{6,7},{7,6},{8,9},{9,8},{10,11... | collective-permute-start | bytes 24584 | tf_op jit(solution)/shard_map/ppermute | solution.py:519
  18.4 5.2 %collective-permute-start.10 = (f32[2,8,128]{2,1,0:T(8,128)S(1)}, f32[2,8,128]{2,1,0:T(8,128)S(1)}, u32[]{:S(2)}, u32[]{:S(2)}) collective-permute-start(f32[2,8,128]{2,1,0:T(8,128)S(1)} %multiply_add_fusion), channel_id=1, source_target_pairs={{0,8},{8,0},{16,24},{24,16},{32,40},{40,32},{48,56},{56,48},{1,9},... | collective-permute-start | bytes 24584 | tf_op jit(solution)/shard_map/ppermute | solution.py:504
  22.0 3.7 %collective-permute-start.9 = (f32[2,8,128]{2,1,0:T(8,128)S(1)}, f32[2,8,128]{2,1,0:T(8,128)S(1)}, u32[]{:S(2)}, u32[]{:S(2)}) collective-permute-start(f32[2,8,128]{2,1,0:T(8,128)S(1)} %multiply_add_fusion), channel_id=1, source_target_pairs={{0,1},{1,0},{2,3},{3,2},{4,5},{5,4},{6,7},{7,6},{8,16},{9,17},{10,... | collective-permute-start | bytes 24584 | tf_op jit(solution)/shard_map/ppermute | solution.py:519
  25.8 1.2 %collective-permute-start.11 = (f32[8,128]{1,0:T(8,128)S(1)}, f32[8,128]{1,0:T(8,128)S(1)}, u32[]{:S(2)}, u32[]{:S(2)}) collective-permute-start(f32[8,128]{1,0:T(8,128)S(1)} %bitcast.3), channel_id=1, source_target_pairs={{0,1},{1,0},{2,3},{3,2},{4,5},{5,4},{6,7},{7,6},{8,9},{9,8},{10,11... | collective-permute-start | bytes 12296 | tf_op jit(solution)/shard_map/ppermute | solution.py:504
  27.0 5.2 %collective-permute-start.12 = (f32[2,8,128]{2,1,0:T(8,128)S(1)}, f32[2,8,128]{2,1,0:T(8,128)S(1)}, u32[]{:S(2)}, u32[]{:S(2)}) collective-permute-start(f32[2,8,128]{2,1,0:T(8,128)S(1)} %pad_maximum_fusion), channel_id=1, source_target_pairs={{0,4},{1,5},{2,6},{3,7},{4,0},{5,1},{6,2},{7,3},{8,12},{9,13},{10,... | collective-permute-start | bytes 24584 | tf_op jit(solution)/shard_map/ppermute | solution.py:504
  29.6 3.7 %collective-permute-start.13 = (f32[2,8,128]{2,1,0:T(8,128)S(1)}, f32[2,8,128]{2,1,0:T(8,128)S(1)}, u32[]{:S(2)}, u32[]{:S(2)}) collective-permute-start(f32[2,8,128]{2,1,0:T(8,128)S(1)} %pad_maximum_fusion), channel_id=1, source_target_pairs={{0,2},{1,3},{2,0},{3,1},{4,6},{5,7},{6,4},{7,5},{8,10},{9,11},{10,... | collective-permute-start | bytes 24584 | tf_op jit(solution)/shard_map/ppermute | solution.py:504
  30.3 4.9 %collective-permute-start.14 = (f32[2,8,128]{2,1,0:T(8,128)S(1)}, f32[2,8,128]{2,1,0:T(8,128)S(1)}, u32[]{:S(2)}, u32[]{:S(2)}) collective-permute-start(f32[2,8,128]{2,1,0:T(8,128)S(1)} %pad_maximum_fusion), channel_id=1, source_target_pairs={{0,6},{1,7},{2,4},{3,5},{4,2},{5,3},{6,0},{7,1},{8,14},{9,15},{10,... | collective-permute-start | bytes 24584 | tf_op jit(solution)/shard_map/ppermute | solution.py:504

commit v4 on v3

--- a/solution.py
+++ b/solution.py
@@ -448,22 +448,24 @@
                     smoothed[2 * i + 1, b, e, 0] = value[4:]
 
 
-def column_kernel(own, other, over_chip, next_chip, last_chip, column, blocks):
+def column_kernel(chip, fetched, mated, third, column, blocks):
     count = lax.axis_size("gz")
     me = lax.axis_index("gz")
-    mate = me + 1 - 2 * lax.rem(me, 2)
+    core, place = lax.rem(me, 2), lax.div(me, 2)
+    beside = place + 1 - 2 * lax.rem(place, 2)
+    across = lax.rem(place + 2, 4)
+    asked = beside + core * (across - beside)
     zero = jnp.zeros((8, 128), jnp.float32)
     blocks[0] = zero
     blocks[count + 1] = zero
-    blocks[me + 1] = own[...]
-    blocks[mate + 1] = other[...]
-    core = lax.rem(me, 2)
-    place = lax.div(me, 2)
-    beside = place + 1 - 2 * lax.rem(place, 2)
-    across = lax.rem(place + 2, 4)
-    for source, chip in ((beside, next_chip), (across, over_chip), (3 - place, last_chip)):
-        blocks[2 * source + core + 1] = chip[0]
-        blocks[2 * source + 2 - core] = chip[1]
+    for source, sender, pair in (
+        (place, core, chip),
+        (asked, core, fetched),
+        (beside + across - asked, 1 - core, mated),
+        (3 - place, core, third),
+    ):
+        blocks[2 * source + sender + 1] = pair[0]
+        blocks[2 * source + 2 - sender] = pair[1]
     lane = lax.broadcasted_iota(jnp.int32, (4, 128), 1)
     row = lax.broadcasted_iota(jnp.int32, (4, 128), 0)
     interior = (lax.axis_index("gx") > 0) & (lax.axis_index("gy") * 4 + row > 0)
@@ -504,19 +506,47 @@
     return lax.ppermute(value, axis, [(i, i ^ bits) for i in range(lax.axis_size(axis))])
 
 
-def second_pairs(value, axis):
+def exchange(value, partner):
     axes = ("gx", "gy", "gz")
     sizes = [lax.axis_size(name) for name in axes]
-    route = []
-    for source, place in enumerate(np.ndindex(*sizes)):
-        target = list(place)
-        k = axes.index(axis)
-        if place[k] in (0, sizes[k] - 1):
-            target[0 if axis == "gz" else 2] ^= 1
-        else:
-            target[k] += 1 if place[k] % 2 else -1
-        route.append((source, int(np.ravel_multi_index(target, sizes))))
+    route = [
+        (source, int(np.ravel_multi_index(partner(list(place)), sizes)))
+        for source, place in enumerate(np.ndindex(*sizes))
+    ]
     return lax.ppermute(value, axes, route)
+
+
+def second_of_pair(place, k, count, spare, bit):
+    if place[k] in (0, count - 1):
+        place[spare] ^= bit
+    else:
+        place[k] += 1 if place[k] % 2 else -1
+    return place
+
+
+def second_pairs(value, axis):
+    k, count = ("gx", "gy", "gz").index(axis), lax.axis_size(axis)
+    return exchange(value, lambda place: second_of_pair(place, k, count, 0 if k == 2 else 2, 1))
+
+
+def both_y_sides(value):
+    count = lax.axis_size("gy")
+
+    def partner(place):
+        if place[2] % 2:
+            place[1] ^= 1
+            return place
+        return second_of_pair(place, 1, count, 0, 1)
+
+    return exchange(value, partner)
+
+
+def two_chips(value):
+    def partner(place):
+        place[2] ^= 4 if place[2] % 2 else 2
+        return place
+
+    return exchange(value, partner)
 
 
 def inside(axis, distance):
@@ -567,23 +597,23 @@
         + from_a
         + inside("gx", -1) * inside("gx", 1) * from_b
     )
-    even = lax.axis_index("gy") % 2 == 0
-    from_a, from_b = flip(sums, "gy", 1), second_pairs(sums, "gy")
-    from_low, from_high = jnp.where(even, from_b, from_a), jnp.where(even, from_a, from_b)
-    row = lax.broadcasted_iota(jnp.int32, (1, 4, 1), 1)
-    owned = (
-        sums[:, :4]
-        + jnp.where(row < 2, from_low[:, 4:], 0.0) * inside("gy", -1)
-        + jnp.where(row == 3, from_high[:, 4:], 0.0) * inside("gy", 1)
-    ).reshape(8, 128)
     count = lax.axis_size("gz")
-    other = flip(owned, "gz", 1)
-    chip = jnp.stack([owned, other])
-    across, beside, opposite = (flip(chip, "gz", bits) for bits in (4, 2, 6))
+    chip = jnp.stack([sums, flip(sums, "gz", 1)])
+    from_beside = both_y_sides(chip)
+    from_low = (lax.axis_index("gy") + lax.axis_index("gz")) % 2 == 0
+    row = lax.broadcasted_iota(jnp.int32, (1, 1, 4, 1), 2)
+    wanted = jnp.where(from_low, row < 2, row == 3)
+    valid = jnp.where(from_low, inside("gy", -1), inside("gy", 1))
+    edges = jnp.where(wanted, from_beside[:, :, 4:], 0.0) * valid
+    edges = edges.reshape(2, 8, 128)
+    mated = flip(edges, "gz", 1)
+    owned = chip[:, :, :4].reshape(2, 8, 128) + edges + mated[::-1]
+    fetched = two_chips(owned)
+    third = flip(owned, "gz", 6)
     (column,) = call(
         column_kernel,
         "column",
-        (owned, other, across, beside, opposite),
+        (owned, fetched, flip(fetched, "gz", 1), third),
         (shape(1, 4, 128 * count),),
         20_000,
         scratch=(pltpu.VMEM((count + 2, 8, 128), jnp.float32),),

time: 35.9 us -> 34.6 us (0.964)
  the two profiles are of different devices: /device:TPU:68 before, /device:TPU:101 now
where the time goes in v4:
time: 34.6 us; the launch traced here: 34.5 us
  starting transfers between devices  19.7 us (57%)
  waiting for transfers between devices  9.46 us (27%)
  Pallas kernels  4.61 us (13%)
  between operations  0.69 us (2%)
    ppermute x9, starting transfers between devices, flip(): lax.ppermute(value, axis, [(i, i ^ bits) for i in range(lax.axis_size(axi...  11.6 us
    ppermute x6, starting transfers between devices, exchange(): return lax.ppermute(value, axes, route)  8.04 us
    ppermute x6, waiting for transfers between devices, exchange(): return lax.ppermute(value, axes, route)  5.57 us
    pallas_call x5, Pallas kernels, call(): pl.pallas_call(kernel, out_shape=outputs, in_specs=[pl.BlockSpec(memory_s...  4.61 us
    ppermute x9, waiting for transfers between devices, flip(): lax.ppermute(value, axis, [(i, i ^ bits) for i in range(lax.axis_size(axi...  3.88 us
  transfers between devices with their start and end apart: 15, of which 9 were waited for; matrix products, arithmetic and copies ran while one was open for 0% of the time, Pallas kernels for 4%

profile of v4, /device:TPU:101, one launch (start us, length us, event | category | flops | bytes accessed | tf_op | source)
XLA Modules:
  0.0 34.5 jit_solution(17525153820391138898)
XLA Ops:
  0.6 1.6 %face_traces.1 = (f32[4,7,7,8,128]{4,3,2,1,0:T(8,128)S(1)}, f32[49,8,128]{2,1,0:T(8,128)S(1)}, f32[49,8,128]{2,1,0:T(8,128)S(1)}, f32[14,8,128]{2,1,0:T(8,128)S(...) custom-call(f32[7,7,7,1,4,128]{5,4,3,2,1,0:T(4,128)} %rhs_hbm.1, ...), custom_call_target="tpu_custom_call" | custom-call | flops 4000000 | bytes 2951168 | tf_op jit(solution)/shard_map/face_traces/pallas_call | solution.py:493
  2.3 0.8 %collective-permute-start.4 = (f32[8,128]{1,0:T(8,128)S(1)}, f32[8,128]{1,0:T(8,128)S(1)}, u32[]{:S(2)}, u32[]{:S(2)}) collective-permute-start(f32[8,128]{1,0:T(8,128)S(1)} %get-tuple-element.25), channel_id=1, source_target_pairs={{0,1},{1,0},{2,3},{3,2},{4,5},{5,4},{6,7},{7,6},{8,9},{9,8},{10,11... | collective-permute-start | bytes 12296 | tf_op jit(solution)/shard_map/ppermute | solution.py:506
  3.0 0.9 %collective-permute-start = (f32[49,8,128]{2,1,0:T(8,128)S(1)}, f32[49,8,128]{2,1,0:T(8,128)S(1)}, u32[]{:S(2)}, u32[]{:S(2)}) collective-permute-start(f32[49,8,128]{2,1,0:T(8,128)S(1)} %get-tuple-element.21), channel_id=1, source_target_pairs={{0,64},{64,0},{128,192},{192,128},{1,65},{65,1},{129,193},{193,129... | collective-permute-start | bytes 602120 | tf_op jit(solution)/shard_map/ppermute | solution.py:506
  4.0 0.0 collective-permute-start.1
  4.0 0.0 collective-permute-start.2
  4.0 3.6 %collective-permute-start.3 = (f32[14,8,128]{2,1,0:T(8,128)S(1)}, f32[14,8,128]{2,1,0:T(8,128)S(1)}, u32[]{:S(2)}, u32[]{:S(2)}) collective-permute-start(f32[14,8,128]{2,1,0:T(8,128)S(1)} %get-tuple-element.24), channel_id=1, source_target_pairs={{0,1},{1,0},{2,3},{3,2},{4,5},{5,4},{6,7},{7,6},{8,16},{9,17},{10,... | collective-permute-start | bytes 172040 | tf_op jit(solution)/shard_map/ppermute | solution.py:516
  7.6 0.0 collective-permute-done.4.z_a
  7.6 2.1 %collective-permute-start.5 = (f32[8,128]{1,0:T(8,128)S(1)}, f32[8,128]{1,0:T(8,128)S(1)}, u32[]{:S(2)}, u32[]{:S(2)}) collective-permute-start(f32[8,128]{1,0:T(8,128)S(1)} %get-tuple-element.26), channel_id=1, source_target_pairs={{0,64},{1,2},{2,1},{3,4},{4,3},{5,6},{6,5},{7,71},{8,72},{9,10},{1... | collective-permute-start | bytes 12296 | tf_op jit(solution)/shard_map/ppermute | solution.py:516
  9.7 0.6 %own_cells.1.local = f32[4,7,7,8,128]{4,3,2,1,0:T(8,128)S(1)} custom-call(f32[4,7,7,8,128]{4,3,2,1,0:T(8,128)S(1)} %get-tuple-element.19.first), custom_call_target="tpu_custom_call" | custom-call | flops 4000000000 | bytes 1605632 | tf_op jit(solution)/shard_map/own_cells/pallas_call | solution.py:493
  10.2 0.7 %collective-permute-done.5.z_b = f32[8,128]{1,0:T(8,128)S(1)} collective-permute-done((f32[8,128]{1,0:T(8,128)S(1)}, f32[8,128]{1,0:T(8,128)S(1)}, u32[]{:S(2)}, u32[]{:S(2)}) %collective-permute-start.5) | collective-permute-done | bytes 4128 | tf_op jit(solution)/shard_map/ppermute | solution.py:516
  11.0 0.0 collective-permute-done.2.y_a
  11.0 0.0 collective-permute-done.3.y_b
  11.0 0.0 collective-permute-done.x_a
  11.0 0.0 collective-permute-done.1.x_b
  11.0 0.8 %smooth_and_restrict.1 = (f32[4,7,7,8,128]{4,3,2,1,0:T(8,128)S(1)}, f32[2,8,128]{2,1,0:T(8,128)S(1)}, f32[2,8,128]{2,1,0:T(8,128)S(1)}, f32[2,8,128]{2,1,0:T(8,128)S(1)}, f32[2,8,128]{2,1,0:T(8,128)S(1)}) custom-call(f32[4,7,7,8,128]{4,3,2,1,0:T(8,128)S(1)} %get-tuple-element.19.first, f32[4,7,7,8,128]{4,3,2,1,0:T(8,128)S(1)} %own_cells.1.local, ...), custom_call_target="tpu_custom_call" | custom-call | flops 5000000 | bytes 3885056 | tf_op jit(solution)/shard_map/smooth_and_restrict/pallas_call | solution.py:493
  11.8 0.7 %collective-permute-start.6 = (f32[2,8,128]{2,1,0:T(8,128)S(1)}, f32[2,8,128]{2,1,0:T(8,128)S(1)}, u32[]{:S(2)}, u32[]{:S(2)}) collective-permute-start(f32[2,8,128]{2,1,0:T(8,128)S(1)} %get-tuple-element.33), channel_id=1, source_target_pairs={{0,128},{64,192},{128,0},{192,64},{1,129},{65,193},{129,1},{193,65... | collective-permute-start | bytes 24584 | tf_op jit(solution)/shard_map/ppermute | solution.py:506
  12.6 2.9 %collective-permute-start.7 = (f32[2,8,128]{2,1,0:T(8,128)S(1)}, f32[2,8,128]{2,1,0:T(8,128)S(1)}, u32[]{:S(2)}, u32[]{:S(2)}) collective-permute-start(f32[2,8,128]{2,1,0:T(8,128)S(1)} %get-tuple-element.34), channel_id=1, source_target_pairs={{0,64},{64,0},{128,192},{192,128},{1,65},{65,1},{129,193},{193,129... | collective-permute-start | bytes 24584 | tf_op jit(solution)/shard_map/ppermute | solution.py:506
  15.4 0.0 collective-permute-start.8
  15.4 0.5 %collective-permute-done.6 = f32[2,8,128]{2,1,0:T(8,128)S(1)} collective-permute-done((f32[2,8,128]{2,1,0:T(8,128)S(1)}, f32[2,8,128]{2,1,0:T(8,128)S(1)}, u32[]{:S(2)}, u32[]{:S(2)}) %collective-permute-start.6) | collective-permute-done | bytes 8224 | tf_op jit(solution)/shard_map/ppermute | solution.py:506
  15.9 0.6 %collective-permute-done.7 = f32[2,8,128]{2,1,0:T(8,128)S(1)} collective-permute-done((f32[2,8,128]{2,1,0:T(8,128)S(1)}, f32[2,8,128]{2,1,0:T(8,128)S(1)}, u32[]{:S(2)}, u32[]{:S(2)}) %collective-permute-start.7) | collective-permute-done | bytes 8224 | tf_op jit(solution)/shard_map/ppermute | solution.py:506
  16.6 1.4 %collective-permute-done.8 = f32[2,8,128]{2,1,0:T(8,128)S(1)} collective-permute-done((f32[2,8,128]{2,1,0:T(8,128)S(1)}, f32[2,8,128]{2,1,0:T(8,128)S(1)}, u32[]{:S(2)}, u32[]{:S(2)}) %collective-permute-start.8) | collective-permute-done | bytes 8224 | tf_op jit(solution)/shard_map/ppermute | solution.py:516
  18.0 2.8 %collective-permute-start.9 = (f32[2,8,128]{2,1,0:T(8,128)S(1)}, f32[2,8,128]{2,1,0:T(8,128)S(1)}, u32[]{:S(2)}, u32[]{:S(2)}) collective-permute-start(f32[2,8,128]{2,1,0:T(8,128)S(1)} %multiply_add_fusion), channel_id=1, source_target_pairs={{0,1},{1,0},{2,3},{3,2},{4,5},{5,4},{6,7},{7,6},{8,9},{9,8},{10,11... | collective-permute-start | bytes 24584 | tf_op jit(solution)/shard_map/ppermute | solution.py:506
  20.8 0.8 %collective-permute-done.9 = f32[2,8,128]{2,1,0:T(8,128)S(1)} collective-permute-done((f32[2,8,128]{2,1,0:T(8,128)S(1)}, f32[2,8,128]{2,1,0:T(8,128)S(1)}, u32[]{:S(2)}, u32[]{:S(2)}) %collective-permute-start.9) | collective-permute-done | bytes 8224 | tf_op jit(solution)/shard_map/ppermute | solution.py:506
  21.6 0.0 collective-permute-start.10
  21.7 2.6 %collective-permute-done.10 = f32[2,2,8,128]{3,2,1,0:T(8,128)S(1)} collective-permute-done((f32[2,2,8,128]{3,2,1,0:T(8,128)S(1)}, f32[2,2,8,128]{3,2,1,0:T(8,128)S(1)}, u32[]{:S(2)}, u32[]{:S(2)}) %collective-permute-start.10) | collective-permute-done | bytes 16416 | tf_op jit(solution)/shard_map/ppermute | solution.py:516
  24.2 0.1 fusion.1
  24.3 2.7 %collective-permute-start.11 = (f32[2,8,128]{2,1,0:T(8,128)S(1)}, f32[2,8,128]{2,1,0:T(8,128)S(1)}, u32[]{:S(2)}, u32[]{:S(2)}) collective-permute-start(f32[2,8,128]{2,1,0:T(8,128)S(1)} %bitcast.9), channel_id=1, source_target_pairs={{0,1},{1,0},{2,3},{3,2},{4,5},{5,4},{6,7},{7,6},{8,9},{9,8},{10,11... | collective-permute-start | bytes 24584 | tf_op jit(solution)/shard_map/ppermute | solution.py:506
  27.0 0.8 %collective-permute-done.11 = f32[2,8,128]{2,1,0:T(8,128)S(1)} collective-permute-done((f32[2,8,128]{2,1,0:T(8,128)S(1)}, f32[2,8,128]{2,1,0:T(8,128)S(1)}, u32[]{:S(2)}, u32[]{:S(2)}) %collective-permute-start.11) | collective-permute-done | bytes 8224 | tf_op jit(solution)/shard_map/ppermute | solution.py:506
  27.8 2.3 %collective-permute-start.12 = (f32[2,8,128]{2,1,0:T(8,128)S(1)}, f32[2,8,128]{2,1,0:T(8,128)S(1)}, u32[]{:S(2)}, u32[]{:S(2)}) collective-permute-start(f32[2,8,128]{2,1,0:T(8,128)S(1)} %reverse_add_fusion.chip), channel_id=1, source_target_pairs={{0,2},{1,5},{2,0},{3,7},{4,6},{5,1},{6,4},{7,3},{8,10},{9,13},{10,... | collective-permute-start | bytes 24584 | tf_op jit(solution)/shard_map/ppermute | solution.py:516
  30.2 0.8 %collective-permute-start.14 = (f32[2,8,128]{2,1,0:T(8,128)S(1)}, f32[2,8,128]{2,1,0:T(8,128)S(1)}, u32[]{:S(2)}, u32[]{:S(2)}) collective-permute-start(f32[2,8,128]{2,1,0:T(8,128)S(1)} %reverse_add_fusion.chip), channel_id=1, source_target_pairs={{0,6},{1,7},{2,4},{3,5},{4,2},{5,3},{6,0},{7,1},{8,14},{9,15},{10,... | collective-permute-start | bytes 24584 | tf_op jit(solution)/shard_map/ppermute | solution.py:506
  30.9 0.9 %collective-permute-done.12.fetched = f32[2,8,128]{2,1,0:T(8,128)S(1)} collective-permute-done((f32[2,8,128]{2,1,0:T(8,128)S(1)}, f32[2,8,128]{2,1,0:T(8,128)S(1)}, u32[]{:S(2)}, u32[]{:S(2)}) %collective-permute-start.12) | collective-permute-done | bytes 8224 | tf_op jit(solution)/shard_map/ppermute | solution.py:516
  31.8 0.0 collective-permute-start.13
  31.8 0.9 %unpack_modes.1 = f32[7,7,7,1,4,128]{5,4,3,2,1,0:T(4,128)} custom-call(f32[4,7,7,8,128]{4,3,2,1,0:T(8,128)S(1)} %get-tuple-element.31.field), custom_call_target="tpu_custom_call" | custom-call | flops 200000 | bytes 1505280 | tf_op jit(solution)/shard_map/unpack_modes/pallas_call | solution.py:493
  32.8 1.1 %collective-permute-done.14.third = f32[2,8,128]{2,1,0:T(8,128)S(1)} collective-permute-done((f32[2,8,128]{2,1,0:T(8,128)S(1)}, f32[2,8,128]{2,1,0:T(8,128)S(1)}, u32[]{:S(2)}, u32[]{:S(2)}) %collective-permute-start.14) | collective-permute-done | bytes 8224 | tf_op jit(solution)/shard_map/ppermute | solution.py:506
  33.9 0.0 collective-permute-done.13.mated
  33.9 0.6 %column.1 = f32[1,4,1024]{2,1,0:T(4,128)} custom-call(f32[2,8,128]{2,1,0:T(8,128)S(1)} %reverse_add_fusion.chip, f32[2,8,128]{2,1,0:T(8,128)S(1)} %collective-permute-done.12.fetched, f32[2,8,128]{2,1,0:T(8,128)S(1)} %collective-permute-done.13.mated, f32[2,8,128]{2,1,0:T(8,128)S(1)} %collective-permute-done.14.third), custom_call_target="tpu_custom_call" | custom-call | flops 20000 | bytes 49152 | tf_op jit(solution)/shard_map/column/pallas_call | solution.py:493
  (5 shorter events, 0.0 us)
Async XLA Ops:
  2.3 5.3 %collective-permute-start.4 = (f32[8,128]{1,0:T(8,128)S(1)}, f32[8,128]{1,0:T(8,128)S(1)}, u32[]{:S(2)}, u32[]{:S(2)}) collective-permute-start(f32[8,128]{1,0:T(8,128)S(1)} %get-tuple-element.25), channel_id=1, source_target_pairs={{0,1},{1,0},{2,3},{3,2},{4,5},{5,4},{6,7},{7,6},{8,9},{9,8},{10,11... | collective-permute-start | bytes 12296 | tf_op jit(solution)/shard_map/ppermute | solution.py:506
  3.0 8.0 %collective-permute-start = (f32[49,8,128]{2,1,0:T(8,128)S(1)}, f32[49,8,128]{2,1,0:T(8,128)S(1)}, u32[]{:S(2)}, u32[]{:S(2)}) collective-permute-start(f32[49,8,128]{2,1,0:T(8,128)S(1)} %get-tuple-element.21), channel_id=1, source_target_pairs={{0,64},{64,0},{128,192},{192,128},{1,65},{65,1},{129,193},{193,129... | collective-permute-start | bytes 602120 | tf_op jit(solution)/shard_map/ppermute | solution.py:506
  4.0 7.0 %collective-permute-start.1 = (f32[49,8,128]{2,1,0:T(8,128)S(1)}, f32[49,8,128]{2,1,0:T(8,128)S(1)}, u32[]{:S(2)}, u32[]{:S(2)}) collective-permute-start(f32[49,8,128]{2,1,0:T(8,128)S(1)} %get-tuple-element.22), channel_id=1, source_target_pairs={{0,1},{1,0},{2,3},{3,2},{4,5},{5,4},{6,7},{7,6},{8,9},{9,8},{10,11... | collective-permute-start | bytes 602120 | tf_op jit(solution)/shard_map/ppermute | solution.py:516
  4.0 7.0 %collective-permute-start.2 = (f32[14,8,128]{2,1,0:T(8,128)S(1)}, f32[14,8,128]{2,1,0:T(8,128)S(1)}, u32[]{:S(2)}, u32[]{:S(2)}) collective-permute-start(f32[14,8,128]{2,1,0:T(8,128)S(1)} %get-tuple-element.23), channel_id=1, source_target_pairs={{0,8},{8,0},{16,24},{24,16},{32,40},{40,32},{48,56},{56,48},{1,9},... | collective-permute-start | bytes 172040 | tf_op jit(solution)/shard_map/ppermute | solution.py:506
  4.0 7.0 %collective-permute-start.3 = (f32[14,8,128]{2,1,0:T(8,128)S(1)}, f32[14,8,128]{2,1,0:T(8,128)S(1)}, u32[]{:S(2)}, u32[]{:S(2)}) collective-permute-start(f32[14,8,128]{2,1,0:T(8,128)S(1)} %get-tuple-element.24), channel_id=1, source_target_pairs={{0,1},{1,0},{2,3},{3,2},{4,5},{5,4},{6,7},{7,6},{8,16},{9,17},{10,... | collective-permute-start | bytes 172040 | tf_op jit(solution)/shard_map/ppermute | solution.py:516
  7.6 3.4 %collective-permute-start.5 = (f32[8,128]{1,0:T(8,128)S(1)}, f32[8,128]{1,0:T(8,128)S(1)}, u32[]{:S(2)}, u32[]{:S(2)}) collective-permute-start(f32[8,128]{1,0:T(8,128)S(1)} %get-tuple-element.26), channel_id=1, source_target_pairs={{0,64},{1,2},{2,1},{3,4},{4,3},{5,6},{6,5},{7,71},{8,72},{9,10},{1... | collective-permute-start | bytes 12296 | tf_op jit(solution)/shard_map/ppermute | solution.py:516
  11.8 4.1 %collective-permute-start.6 = (f32[2,8,128]{2,1,0:T(8,128)S(1)}, f32[2,8,128]{2,1,0:T(8,128)S(1)}, u32[]{:S(2)}, u32[]{:S(2)}) collective-permute-start(f32[2,8,128]{2,1,0:T(8,128)S(1)} %get-tuple-element.33), channel_id=1, source_target_pairs={{0,128},{64,192},{128,0},{192,64},{1,129},{65,193},{129,1},{193,65... | collective-permute-start | bytes 24584 | tf_op jit(solution)/shard_map/ppermute | solution.py:506
  12.6 4.0 %collective-permute-start.7 = (f32[2,8,128]{2,1,0:T(8,128)S(1)}, f32[2,8,128]{2,1,0:T(8,128)S(1)}, u32[]{:S(2)}, u32[]{:S(2)}) collective-permute-start(f32[2,8,128]{2,1,0:T(8,128)S(1)} %get-tuple-element.34), channel_id=1, source_target_pairs={{0,64},{64,0},{128,192},{192,128},{1,65},{65,1},{129,193},{193,129... | collective-permute-start | bytes 24584 | tf_op jit(solution)/shard_map/ppermute | solution.py:506
  15.4 2.5 %collective-permute-start.8 = (f32[2,8,128]{2,1,0:T(8,128)S(1)}, f32[2,8,128]{2,1,0:T(8,128)S(1)}, u32[]{:S(2)}, u32[]{:S(2)}) collective-permute-start(f32[2,8,128]{2,1,0:T(8,128)S(1)} %get-tuple-element.35), channel_id=1, source_target_pairs={{0,1},{1,0},{2,3},{3,2},{4,5},{5,4},{6,7},{7,6},{8,9},{9,8},{10,11... | collective-permute-start | bytes 24584 | tf_op jit(solution)/shard_map/ppermute | solution.py:516
  18.0 3.7 %collective-permute-start.9 = (f32[2,8,128]{2,1,0:T(8,128)S(1)}, f32[2,8,128]{2,1,0:T(8,128)S(1)}, u32[]{:S(2)}, u32[]{:S(2)}) collective-permute-start(f32[2,8,128]{2,1,0:T(8,128)S(1)} %multiply_add_fusion), channel_id=1, source_target_pairs={{0,1},{1,0},{2,3},{3,2},{4,5},{5,4},{6,7},{7,6},{8,9},{9,8},{10,11... | collective-permute-start | bytes 24584 | tf_op jit(solution)/shard_map/ppermute | solution.py:506
  21.6 2.6 %collective-permute-start.10 = (f32[2,2,8,128]{3,2,1,0:T(8,128)S(1)}, f32[2,2,8,128]{3,2,1,0:T(8,128)S(1)}, u32[]{:S(2)}, u32[]{:S(2)}) collective-permute-start(f32[2,2,8,128]{3,2,1,0:T(8,128)S(1)} %pad_maximum_fusion), channel_id=1, source_target_pairs={{0,64},{1,9},{2,66},{3,11},{4,68},{5,13},{6,70},{7,15},{8,16},{9,1... | collective-permute-start | bytes 49160 | tf_op jit(solution)/shard_map/ppermute | solution.py:516
  24.3 3.5 %collective-permute-start.11 = (f32[2,8,128]{2,1,0:T(8,128)S(1)}, f32[2,8,128]{2,1,0:T(8,128)S(1)}, u32[]{:S(2)}, u32[]{:S(2)}) collective-permute-start(f32[2,8,128]{2,1,0:T(8,128)S(1)} %bitcast.9), channel_id=1, source_target_pairs={{0,1},{1,0},{2,3},{3,2},{4,5},{5,4},{6,7},{7,6},{8,9},{9,8},{10,11... | collective-permute-start | bytes 24584 | tf_op jit(solution)/shard_map/ppermute | solution.py:506
  27.8 4.0 %collective-permute-start.12 = (f32[2,8,128]{2,1,0:T(8,128)S(1)}, f32[2,8,128]{2,1,0:T(8,128)S(1)}, u32[]{:S(2)}, u32[]{:S(2)}) collective-permute-start(f32[2,8,128]{2,1,0:T(8,128)S(1)} %reverse_add_fusion.chip), channel_id=1, source_target_pairs={{0,2},{1,5},{2,0},{3,7},{4,6},{5,1},{6,4},{7,3},{8,10},{9,13},{10,... | collective-permute-start | bytes 24584 | tf_op jit(solution)/shard_map/ppermute | solution.py:516
  30.2 3.7 %collective-permute-start.14 = (f32[2,8,128]{2,1,0:T(8,128)S(1)}, f32[2,8,128]{2,1,0:T(8,128)S(1)}, u32[]{:S(2)}, u32[]{:S(2)}) collective-permute-start(f32[2,8,128]{2,1,0:T(8,128)S(1)} %reverse_add_fusion.chip), channel_id=1, source_target_pairs={{0,6},{1,7},{2,4},{3,5},{4,2},{5,3},{6,0},{7,1},{8,14},{9,15},{10,... | collective-permute-start | bytes 24584 | tf_op jit(solution)/shard_map/ppermute | solution.py:506
  31.8 2.0 %collective-permute-start.13 = (f32[2,8,128]{2,1,0:T(8,128)S(1)}, f32[2,8,128]{2,1,0:T(8,128)S(1)}, u32[]{:S(2)}, u32[]{:S(2)}) collective-permute-start(f32[2,8,128]{2,1,0:T(8,128)S(1)} %collective-permute-done.12.fetched), channel_id=1, source_target_pairs={{0,1},{1,0},{2,3},{3,2},{4,5},{5,4},{6,7},{7,6},{8,9},{9,8},{10,11... | collective-permute-start | bytes 24584 | tf_op jit(solution)/shard_map/ppermute | solution.py:506

commit v5 on v4

--- a/solution.py
+++ b/solution.py
@@ -16,6 +16,9 @@
 MODES = 7
 PAIRS = 4
 FACE_ROWS = 14
+SIDE_COST = 4_000_000
+OWN_COST = 1_400_000_000
+HALO_COST = 4_000_000
 
 
 def basis_tables():
@@ -136,9 +139,21 @@
     return even + odd, even_slope + odd_slope, even - odd, odd_slope - even_slope
 
 
+def x_turn():
+    return lax.axis_index("gx") + lax.axis_index("gz")
+
+
+def goes_up(turn):
+    return jnp.full((8, 128), lax.rem(turn, 2), jnp.int32) == 0
+
+
+def has_place(axis, distance):
+    place = lax.axis_index(axis) + distance
+    return jnp.where((place >= 0) & (place < lax.axis_size(axis)), 1.0, 0.0).astype(jnp.float32)
+
+
 def trace_kernel(
-    rhs_hbm, orders_hbm, first, x_a, x_b, y_a, y_b, z_a, z_b, y_low, y_high, z_low, z_high,
-    orders, rhs, arrived,
+    rhs_hbm, orders_hbm, first, x_a, x_b, orders, rhs, arrived,
 ):
     copies = [pltpu.make_async_copy(orders_hbm, orders, arrived.at[MODES])]
     for b in range(MODES):
@@ -147,13 +162,7 @@
         copy.start()
     pairs = Pairs()
     top = pairs.top
-    row, lane = row_in_half(), lanes()
-
-    def put(ref, other_ref, index, axis, up, down):
-        even = jnp.full((8, 128), lax.rem(lax.axis_index(axis), 2), jnp.int32) == 0
-        ref[index] = jnp.where(even, up, down)
-        other_ref[index] = jnp.where(even, down, up)
-
+    upward = goes_up(x_turn())
     copies[0].wait()
     keep = keep_masks(orders[0], top)
     for b in range(MODES):
@@ -184,7 +193,13 @@
             both_slope = jnp.where(top, slope + swap(slope), slope - swap(slope))
             up = jnp.where(top, both_value, swap(both_slope))
             down = jnp.where(top, swap(both_value), both_slope)
-            put(x_a, x_b, b * MODES + e, "gx", up, down)
+            x_a[b * MODES + e] = jnp.where(upward, up, down)
+            x_b[b * MODES + e] = jnp.where(upward, down, up)
+
+
+def side_trace_kernel(first, y_a, y_b, z_a, z_b, y_low, y_high, z_low, z_high):
+    row, lane = row_in_half(), lanes()
+    y_up, z_up = goes_up(lax.axis_index("gy")), goes_up(lax.axis_index("gz"))
     packed_up = packed_down = None
     for kind in range(2):
         for i in range(PAIRS):
@@ -200,7 +215,9 @@
                 packed_up = up if q == 0 else jnp.where(row == q, up, packed_up)
                 packed_down = down if q == 0 else jnp.where(row == q, down, packed_down)
                 if q == 3:
-                    put(y_a, y_b, kind * 7 + m // 4, "gy", packed_up, packed_down)
+                    k = kind * 7 + m // 4
+                    y_a[k] = jnp.where(y_up, packed_up, packed_down)
+                    y_b[k] = jnp.where(y_up, packed_down, packed_up)
     packed_up = packed_down = jnp.zeros((8, 128), jnp.float32)
     for i in range(PAIRS):
         for b in range(MODES):
@@ -215,7 +232,8 @@
                 packed_up = jnp.where(lane == place, pltpu.roll(high, 1 + place, 1), packed_up)
                 down = pltpu.roll(low, place, 1) if place else low
                 packed_down = jnp.where(lane == place, down, packed_down)
-    put(z_a, z_b, ..., "gz", packed_up, packed_down)
+    z_a[...] = jnp.where(z_up, packed_up, packed_down)
+    z_b[...] = jnp.where(z_up, packed_down, packed_up)
 
 
 def own_kernel(first, out):
@@ -286,42 +304,13 @@
     return [[total(result[r][z]) for z in range(2)] for r in range(2)]
 
 
-def finish_kernel(
-    first, local, orders, x_a, x_b, y_a, y_b, z_a, z_b,
-    y_below, y_above, z_below, z_above, field, here, sum_a, sum_b, far,
+def side_kernel(
+    local, y_a, y_b, z_a, z_b, y_below, y_above, z_below, z_above, out
 ):
-    pairs = Pairs()
-    top = pairs.top
     row, lane = row_in_half(), lanes()
-    keep = keep_masks(orders[0], top)
-
-    def inside(axis, distance):
-        place = lax.axis_index(axis) + distance
-        return jnp.where((place >= 0) & (place < lax.axis_size(axis)), 1.0, 0.0).astype(
-            jnp.float32
-        )
-
-    def is_even(axis):
-        return jnp.full((8, 128), lax.rem(lax.axis_index(axis), 2), jnp.int32) == 0
-
-    x_has_b = inside("gx", -1) * inside("gx", 1)
-    x_even, y_even, z_even = is_even("gx"), is_even("gy"), is_even("gz")
-    x_sign = jnp.where(x_even, 1.0, -1.0)
-    y_has_low, y_has_high = inside("gy", -1), inside("gy", 1)
-    z_has_low, z_has_high = inside("gz", -1), inside("gz", 1)
-    for b in range(MODES):
-        for e in range(MODES):
-            one, two = x_a[b * MODES + e], x_has_b * x_b[b * MODES + e]
-            plus, minus = one + two, swap(x_sign * (one - two))
-            slope = 0.5 * jnp.where(top, plus, minus)
-            value = (-2.0 * PENALTY) * slope - 0.5 * jnp.where(top, minus, plus)
-            for i in range(PAIRS):
-                last = 2 * i + 1 >= MODES
-                k = odd_of(i)
-                local[i, b, e] += (
-                    pairs(NORMED[2 * i], 0.0 if last else NORMED[k]) * value
-                    + pairs(SLOPE[2 * i], 0.0 if last else SLOPE[k]) * slope
-                )
+    y_even, z_even = goes_up(lax.axis_index("gy")), goes_up(lax.axis_index("gz"))
+    y_has_low, y_has_high = has_place("gy", -1), has_place("gy", 1)
+    z_has_low, z_has_high = has_place("gz", -1), has_place("gz", 1)
     y_low, y_high = [], []
     for k in range(FACE_ROWS):
         one, two = y_a[k], y_b[k]
@@ -346,7 +335,8 @@
             for n in range(MODES):
                 value, slope = parts[n % 2]
                 add = float(NORMED[n]) * value
-                local[i, n, e] += add + float(SLOPE[n]) * slope if n else add
+                add = add + float(SLOPE[n]) * slope if n else add
+                out[i, n, e] = local[i, n, e] + add
     z_low_halo = z_has_low * jnp.where(z_even, z_b[...], z_a[...])
     z_high_halo = z_has_high * jnp.where(z_even, z_a[...], z_b[...])
     for i in range(PAIRS):
@@ -369,7 +359,33 @@
                 add = float(NORMED[e]) * value
                 if e:
                     add = add + float(SLOPE[e]) * slope
-                applied = local[i, b, e] + add
+                out[i, b, e] += add
+
+
+def finish_kernel(first, local, orders, x_a, x_b, field, here, sum_a, sum_b, far):
+    pairs = Pairs()
+    top = pairs.top
+    row, lane = row_in_half(), lanes()
+    keep = keep_masks(orders[0], top)
+    has_low, has_high = has_place("gx", -1), has_place("gx", 1)
+    upward = goes_up(x_turn())
+    one_valid = jnp.where(upward, has_high, has_low)
+    two_valid = jnp.where(upward, has_low, has_high)
+    x_sign = jnp.where(upward, 1.0, -1.0)
+    x_even = goes_up(lax.axis_index("gx"))
+    for b in range(MODES):
+        for e in range(MODES):
+            one, two = one_valid * x_a[b * MODES + e], two_valid * x_b[b * MODES + e]
+            plus, minus = one + two, swap(x_sign * (one - two))
+            slope = 0.5 * jnp.where(top, plus, minus)
+            value = (-2.0 * PENALTY) * slope - 0.5 * jnp.where(top, minus, plus)
+            for i in range(PAIRS):
+                last = 2 * i + 1 >= MODES
+                k = odd_of(i)
+                applied = local[i, b, e] + (
+                    pairs(NORMED[2 * i], 0.0 if last else NORMED[k]) * value
+                    + pairs(SLOPE[2 * i], 0.0 if last else SLOPE[k]) * slope
+                )
                 one = 2.0 * RHO_SECOND / (DELTA * PENALTY)
                 scale = pairs.once(one / diag(2 * i, b, e), one / diag(odd_of(i), b, e))
                 mask = keep(max(2 * i, b, e), max(odd_of(i), b, e))
@@ -529,6 +545,18 @@
     return exchange(value, lambda place: second_of_pair(place, k, count, 0 if k == 2 else 2, 1))
 
 
+def x_pairs(value, turn):
+    count = lax.axis_size("gx")
+
+    def partner(place):
+        if place[2] % 2 == turn:
+            place[0] ^= 1
+            return place
+        return second_of_pair(place, 0, count, 1, 1)
+
+    return exchange(value, partner)
+
+
 def both_y_sides(value):
     count = lax.axis_size("gy")
 
@@ -556,36 +584,43 @@
 
 def per_device(rhs, orders):
     cells = (PAIRS, MODES, MODES, 8, 128)
-    first, x_a, x_b, y_a, y_b, z_a, z_b, y_low, y_high, z_low, z_high, held = call(
+    sides = (shape(2, 28, 8, 128),) * 4
+    first, x_a, x_b, held = call(
         trace_kernel,
-        "face_traces",
+        "x_traces",
         tuple(pltpu.with_memory_space_constraint(v, pltpu.HBM) for v in (rhs, orders)),
         (
             shape(*cells), shape(49, 8, 128), shape(49, 8, 128),
-            shape(FACE_ROWS, 8, 128), shape(FACE_ROWS, 8, 128), shape(8, 128), shape(8, 128),
-            shape(2, 28, 8, 128), shape(2, 28, 8, 128), shape(2, 28, 8, 128), shape(2, 28, 8, 128),
             jax.ShapeDtypeStruct(orders.shape, jnp.int32),
         ),
         4_000_000,
-        scratch=(
-            pltpu.VMEM(rhs.shape, jnp.float32),
-            pltpu.SemaphoreType.DMA((MODES + 1,)),
-        ),
+        scratch=(pltpu.VMEM(rhs.shape, jnp.float32), pltpu.SemaphoreType.DMA((MODES + 1,))),
         in_hbm=True,
     )
-    x_a, x_b = flip(x_a, "gx", 1), second_pairs(x_b, "gx")
+    x_a, x_b = x_pairs(x_a, 0), x_pairs(x_b, 1)
+    y_a, y_b, z_a, z_b, y_low, y_high, z_low, z_high = call(
+        side_trace_kernel,
+        "side_traces",
+        (first,),
+        (shape(FACE_ROWS, 8, 128),) * 2 + (shape(8, 128),) * 2 + sides,
+        SIDE_COST,
+    )
     y_a, y_b = flip(y_a, "gy", 1), second_pairs(y_b, "gy")
     z_a, z_b = flip(z_a, "gz", 1), second_pairs(z_b, "gz")
-    (local,) = call(own_kernel, "own_cells", (first,), (shape(*cells),), 4_000_000_000)
+    (local,) = call(own_kernel, "own_cells", (first,), (shape(*cells),), OWN_COST)
+    (local,) = call(
+        side_kernel,
+        "side_halo",
+        (local, y_a, y_b, z_a, z_b, y_high, y_low, z_high, z_low),
+        (shape(*cells),),
+        HALO_COST,
+    )
     field, here, sum_a, sum_b, far = call(
-        finish_in_place,
+        finish_kernel,
         "smooth_and_restrict",
-        (
-            first, local, held, x_a, x_b, y_a, y_b, z_a, z_b, y_high, y_low, z_high, z_low,
-        ),
+        (first, local, held, x_a, x_b),
         (shape(*cells),) + (shape(2, 8, 128),) * 4,
         5_000_000,
-        scratch=(pltpu.VMEM(cells, jnp.float32),),
     )
     (smoothed,) = call(unpack_kernel, "unpack_modes", (field,), (shape(*rhs.shape),), 200_000)
     from_far = flip(far, "gx", 2)
@@ -621,17 +656,6 @@
     return smoothed, column
 
 
-def finish_in_place(
-    first, local, orders, x_a, x_b, y_a, y_b, z_a, z_b,
-    y_below, y_above, z_below, z_above, field, here, sum_a, sum_b, far, work,
-):
-    work[...] = local[...]
-    finish_kernel(
-        first, work, orders, x_a, x_b, y_a, y_b, z_a, z_b,
-        y_below, y_above, z_below, z_above, field, here, sum_a, sum_b, far,
-    )
-
-
 def solution(mesh):
     return jax.shard_map(
         per_device,

time: 34.6 us -> 34.7 us (level)
    ppermute x6 -> x7, starting transfers between devices: 8.04 us -> 8.45 us  [exchange(): return lax.ppermute(value, axes, route)]
    ppermute x9 -> x8, starting transfers between devices: 11.6 us -> 11.3 us  [flip(): lax.ppermute(value, axis, [(i, i ^ bits) for i in range(lax.axis_size(axi...]
    pallas_call x5 -> x7, Pallas kernels: 4.61 us -> 4.57 us  [call(): pl.pallas_call(kernel, out_shape=outputs, in_specs=[pl.BlockSpec(memory_s...]
    ppermute x6 -> x7, waiting for transfers between devices: 5.57 us -> 5.59 us  [exchange(): return lax.ppermute(value, axes, route)]
    ppermute x9 -> x8, waiting for transfers between devices: 3.88 us -> 3.88 us  [flip(): lax.ppermute(value, axis, [(i, i ^ bits) for i in range(lax.axis_size(axi...]
  transfers between devices with their start and end apart: 15 -> 15, of which waited for: 9 -> 9; matrix products, arithmetic and copies ran while one was open for 0% -> 0% of each run, Pallas kernels for 4% -> 6%
where the time goes in v5:
time: 34.7 us; the launch traced here: 34.6 us
  starting transfers between devices  19.7 us (57%)
  waiting for transfers between devices  9.47 us (27%)
  Pallas kernels  4.57 us (13%)
  between operations  0.71 us (2%)
    ppermute x8, starting transfers between devices, flip(): lax.ppermute(value, axis, [(i, i ^ bits) for i in range(lax.axis_size(axi...  11.3 us
    ppermute x7, starting transfers between devices, exchange(): return lax.ppermute(value, axes, route)  8.45 us
    ppermute x7, waiting for transfers between devices, exchange(): return lax.ppermute(value, axes, route)  5.59 us
    pallas_call x7, Pallas kernels, call(): pl.pallas_call(kernel, out_shape=outputs, in_specs=[pl.BlockSpec(memory_s...  4.57 us
    ppermute x8, waiting for transfers between devices, flip(): lax.ppermute(value, axis, [(i, i ^ bits) for i in range(lax.axis_size(axi...  3.88 us
  transfers between devices with their start and end apart: 15, of which 9 were waited for; matrix products, arithmetic and copies ran while one was open for 0% of the time, Pallas kernels for 6%

profile of v5, /device:TPU:101, one launch (start us, length us, event | category | flops | bytes accessed | tf_op | source)
XLA Modules:
  0.0 34.6 jit_solution(8349477121708064980)
XLA Ops:
  0.6 1.3 %x_traces.1 = (f32[4,7,7,8,128]{4,3,2,1,0:T(8,128)S(1)}, f32[49,8,128]{2,1,0:T(8,128)S(1)}, f32[49,8,128]{2,1,0:T(8,128)S(1)}, s32[1,4,128]{2,1,0:T(4,128)S(1)}) custom-call(f32[7,7,7,1,4,128]{5,4,3,2,1,0:T(4,128)} %rhs_hbm.1, s32[1,4,128]{2,1,0:T(4,128)} %orders_hbm.1), custom_call_target="tpu_custom_call" | custom-call | flops 4000000 | bytes 1910784 | tf_op jit(solution)/shard_map/x_traces/pallas_call | solution.py:509
  2.0 0.3 collective-permute-start.4
  2.3 0.8 %collective-permute-start.5 = (f32[49,8,128]{2,1,0:T(8,128)S(1)}, f32[49,8,128]{2,1,0:T(8,128)S(1)}, u32[]{:S(2)}, u32[]{:S(2)}) collective-permute-start(f32[49,8,128]{2,1,0:T(8,128)S(1)} %get-tuple-element.30), channel_id=1, source_target_pairs={{0,8},{1,65},{2,10},{3,67},{4,12},{5,69},{6,14},{7,71},{8,0},{9,73... | collective-permute-start | bytes 602120 | tf_op jit(solution)/shard_map/ppermute | solution.py:532
  3.1 0.3 side_traces.1
  3.3 0.9 %collective-permute-start.2 = (f32[8,128]{1,0:T(8,128)S(1)}, f32[8,128]{1,0:T(8,128)S(1)}, u32[]{:S(2)}, u32[]{:S(2)}) collective-permute-start(f32[8,128]{1,0:T(8,128)S(1)} %get-tuple-element.22), channel_id=1, source_target_pairs={{0,1},{1,0},{2,3},{3,2},{4,5},{5,4},{6,7},{7,6},{8,9},{9,8},{10,11... | collective-permute-start | bytes 12296 | tf_op jit(solution)/shard_map/ppermute | solution.py:522
  4.3 0.6 %collective-permute-start = (f32[14,8,128]{2,1,0:T(8,128)S(1)}, f32[14,8,128]{2,1,0:T(8,128)S(1)}, u32[]{:S(2)}, u32[]{:S(2)}) collective-permute-start(f32[14,8,128]{2,1,0:T(8,128)S(1)} %get-tuple-element.20), channel_id=1, source_target_pairs={{0,8},{8,0},{16,24},{24,16},{32,40},{40,32},{48,56},{56,48},{1,9},... | collective-permute-start | bytes 172040 | tf_op jit(solution)/shard_map/ppermute | solution.py:522
  4.9 3.0 %collective-permute-start.1 = (f32[14,8,128]{2,1,0:T(8,128)S(1)}, f32[14,8,128]{2,1,0:T(8,128)S(1)}, u32[]{:S(2)}, u32[]{:S(2)}) collective-permute-start(f32[14,8,128]{2,1,0:T(8,128)S(1)} %get-tuple-element.21), channel_id=1, source_target_pairs={{0,1},{1,0},{2,3},{3,2},{4,5},{5,4},{6,7},{7,6},{8,16},{9,17},{10,... | collective-permute-start | bytes 172040 | tf_op jit(solution)/shard_map/ppermute | solution.py:532
  7.9 0.0 collective-permute-done.2.z_a
  7.9 2.0 %collective-permute-start.3 = (f32[8,128]{1,0:T(8,128)S(1)}, f32[8,128]{1,0:T(8,128)S(1)}, u32[]{:S(2)}, u32[]{:S(2)}) collective-permute-start(f32[8,128]{1,0:T(8,128)S(1)} %get-tuple-element.23), channel_id=1, source_target_pairs={{0,64},{1,2},{2,1},{3,4},{4,3},{5,6},{6,5},{7,71},{8,72},{9,10},{1... | collective-permute-start | bytes 12296 | tf_op jit(solution)/shard_map/ppermute | solution.py:532
  9.9 0.6 %own_cells.1.local = f32[4,7,7,8,128]{4,3,2,1,0:T(8,128)S(1)} custom-call(f32[4,7,7,8,128]{4,3,2,1,0:T(8,128)S(1)} %get-tuple-element.19.first), custom_call_target="tpu_custom_call" | custom-call | flops 1400000000 | bytes 1605632 | tf_op jit(solution)/shard_map/own_cells/pallas_call | solution.py:509
  10.5 0.7 %collective-permute-done.3.z_b = f32[8,128]{1,0:T(8,128)S(1)} collective-permute-done((f32[8,128]{1,0:T(8,128)S(1)}, f32[8,128]{1,0:T(8,128)S(1)}, u32[]{:S(2)}, u32[]{:S(2)}) %collective-permute-start.3) | collective-permute-done | bytes 4128 | tf_op jit(solution)/shard_map/ppermute | solution.py:532
  11.2 0.0 collective-permute-done.y_a
  11.2 0.0 collective-permute-done.1.y_b
  11.2 0.4 %side_halo.1.local = f32[4,7,7,8,128]{4,3,2,1,0:T(8,128)S(1)} custom-call(f32[4,7,7,8,128]{4,3,2,1,0:T(8,128)S(1)} %own_cells.1.local, f32[14,8,128]{2,1,0:T(8,128)S(1)} %collective-permute-done.y_a, f32[14,8,128]{2,1,0:T(8,128)S(1)} %collective-permute-done.1.y_b, f32[8,128]{1,0:T(8,128)S(1)} %collective-permute-done.2.z_a, ...), custom_call_target="tpu_custom_call" | custom-call | flops 4000000 | bytes 2646016 | tf_op jit(solution)/shard_map/side_halo/pallas_call | solution.py:509
  11.6 0.0 collective-permute-done.4.x_a
  11.6 0.0 collective-permute-done.5.x_b
  11.6 0.4 %smooth_and_restrict.1 = (f32[4,7,7,8,128]{4,3,2,1,0:T(8,128)S(1)}, f32[2,8,128]{2,1,0:T(8,128)S(1)}, f32[2,8,128]{2,1,0:T(8,128)S(1)}, f32[2,8,128]{2,1,0:T(8,128)S(1)}, f32[2,8,128]{2,1,0:T(8,128)S(1)}) custom-call(f32[4,7,7,8,128]{4,3,2,1,0:T(8,128)S(1)} %get-tuple-element.19.first, f32[4,7,7,8,128]{4,3,2,1,0:T(8,128)S(1)} %side_halo.1.local, ...), custom_call_target="tpu_custom_call" | custom-call | flops 5000000 | bytes 2844672 | tf_op jit(solution)/shard_map/smooth_and_restrict/pallas_call | solution.py:509
  12.1 1.4 %collective-permute-start.6 = (f32[2,8,128]{2,1,0:T(8,128)S(1)}, f32[2,8,128]{2,1,0:T(8,128)S(1)}, u32[]{:S(2)}, u32[]{:S(2)}) collective-permute-start(f32[2,8,128]{2,1,0:T(8,128)S(1)} %get-tuple-element.33), channel_id=1, source_target_pairs={{0,128},{64,192},{128,0},{192,64},{1,129},{65,193},{129,1},{193,65... | collective-permute-start | bytes 24584 | tf_op jit(solution)/shard_map/ppermute | solution.py:522
  13.5 2.0 %collective-permute-start.7 = (f32[2,8,128]{2,1,0:T(8,128)S(1)}, f32[2,8,128]{2,1,0:T(8,128)S(1)}, u32[]{:S(2)}, u32[]{:S(2)}) collective-permute-start(f32[2,8,128]{2,1,0:T(8,128)S(1)} %get-tuple-element.34), channel_id=1, source_target_pairs={{0,64},{64,0},{128,192},{192,128},{1,65},{65,1},{129,193},{193,129... | collective-permute-start | bytes 24584 | tf_op jit(solution)/shard_map/ppermute | solution.py:522
  15.5 0.0 collective-permute-start.8
  15.5 0.7 %collective-permute-done.6 = f32[2,8,128]{2,1,0:T(8,128)S(1)} collective-permute-done((f32[2,8,128]{2,1,0:T(8,128)S(1)}, f32[2,8,128]{2,1,0:T(8,128)S(1)}, u32[]{:S(2)}, u32[]{:S(2)}) %collective-permute-start.6) | collective-permute-done | bytes 8224 | tf_op jit(solution)/shard_map/ppermute | solution.py:522
  16.2 0.5 %collective-permute-done.7 = f32[2,8,128]{2,1,0:T(8,128)S(1)} collective-permute-done((f32[2,8,128]{2,1,0:T(8,128)S(1)}, f32[2,8,128]{2,1,0:T(8,128)S(1)}, u32[]{:S(2)}, u32[]{:S(2)}) %collective-permute-start.7) | collective-permute-done | bytes 8224 | tf_op jit(solution)/shard_map/ppermute | solution.py:522
  16.6 1.4 %collective-permute-done.8 = f32[2,8,128]{2,1,0:T(8,128)S(1)} collective-permute-done((f32[2,8,128]{2,1,0:T(8,128)S(1)}, f32[2,8,128]{2,1,0:T(8,128)S(1)}, u32[]{:S(2)}, u32[]{:S(2)}) %collective-permute-start.8) | collective-permute-done | bytes 8224 | tf_op jit(solution)/shard_map/ppermute | solution.py:532
  18.1 2.8 %collective-permute-start.9 = (f32[2,8,128]{2,1,0:T(8,128)S(1)}, f32[2,8,128]{2,1,0:T(8,128)S(1)}, u32[]{:S(2)}, u32[]{:S(2)}) collective-permute-start(f32[2,8,128]{2,1,0:T(8,128)S(1)} %multiply_add_fusion), channel_id=1, source_target_pairs={{0,1},{1,0},{2,3},{3,2},{4,5},{5,4},{6,7},{7,6},{8,9},{9,8},{10,11... | collective-permute-start | bytes 24584 | tf_op jit(solution)/shard_map/ppermute | solution.py:522
  20.9 0.8 %collective-permute-done.9 = f32[2,8,128]{2,1,0:T(8,128)S(1)} collective-permute-done((f32[2,8,128]{2,1,0:T(8,128)S(1)}, f32[2,8,128]{2,1,0:T(8,128)S(1)}, u32[]{:S(2)}, u32[]{:S(2)}) %collective-permute-start.9) | collective-permute-done | bytes 8224 | tf_op jit(solution)/shard_map/ppermute | solution.py:522
  21.7 0.0 collective-permute-start.10
  21.7 2.6 %collective-permute-done.10 = f32[2,2,8,128]{3,2,1,0:T(8,128)S(1)} collective-permute-done((f32[2,2,8,128]{3,2,1,0:T(8,128)S(1)}, f32[2,2,8,128]{3,2,1,0:T(8,128)S(1)}, u32[]{:S(2)}, u32[]{:S(2)}) %collective-permute-start.10) | collective-permute-done | bytes 16416 | tf_op jit(solution)/shard_map/ppermute | solution.py:532
  24.3 0.1 fusion.1
  24.4 2.7 %collective-permute-start.11 = (f32[2,8,128]{2,1,0:T(8,128)S(1)}, f32[2,8,128]{2,1,0:T(8,128)S(1)}, u32[]{:S(2)}, u32[]{:S(2)}) collective-permute-start(f32[2,8,128]{2,1,0:T(8,128)S(1)} %bitcast.9), channel_id=1, source_target_pairs={{0,1},{1,0},{2,3},{3,2},{4,5},{5,4},{6,7},{7,6},{8,9},{9,8},{10,11... | collective-permute-start | bytes 24584 | tf_op jit(solution)/shard_map/ppermute | solution.py:522
  27.1 0.8 %collective-permute-done.11 = f32[2,8,128]{2,1,0:T(8,128)S(1)} collective-permute-done((f32[2,8,128]{2,1,0:T(8,128)S(1)}, f32[2,8,128]{2,1,0:T(8,128)S(1)}, u32[]{:S(2)}, u32[]{:S(2)}) %collective-permute-start.11) | collective-permute-done | bytes 8224 | tf_op jit(solution)/shard_map/ppermute | solution.py:522
  27.9 2.3 %collective-permute-start.12 = (f32[2,8,128]{2,1,0:T(8,128)S(1)}, f32[2,8,128]{2,1,0:T(8,128)S(1)}, u32[]{:S(2)}, u32[]{:S(2)}) collective-permute-start(f32[2,8,128]{2,1,0:T(8,128)S(1)} %reverse_add_fusion.chip), channel_id=1, source_target_pairs={{0,2},{1,5},{2,0},{3,7},{4,6},{5,1},{6,4},{7,3},{8,10},{9,13},{10,... | collective-permute-start | bytes 24584 | tf_op jit(solution)/shard_map/ppermute | solution.py:532
  30.2 0.8 %collective-permute-start.14 = (f32[2,8,128]{2,1,0:T(8,128)S(1)}, f32[2,8,128]{2,1,0:T(8,128)S(1)}, u32[]{:S(2)}, u32[]{:S(2)}) collective-permute-start(f32[2,8,128]{2,1,0:T(8,128)S(1)} %reverse_add_fusion.chip), channel_id=1, source_target_pairs={{0,6},{1,7},{2,4},{3,5},{4,2},{5,3},{6,0},{7,1},{8,14},{9,15},{10,... | collective-permute-start | bytes 24584 | tf_op jit(solution)/shard_map/ppermute | solution.py:522
  31.0 0.9 %collective-permute-done.12.fetched = f32[2,8,128]{2,1,0:T(8,128)S(1)} collective-permute-done((f32[2,8,128]{2,1,0:T(8,128)S(1)}, f32[2,8,128]{2,1,0:T(8,128)S(1)}, u32[]{:S(2)}, u32[]{:S(2)}) %collective-permute-start.12) | collective-permute-done | bytes 8224 | tf_op jit(solution)/shard_map/ppermute | solution.py:532
  31.9 0.0 collective-permute-start.13
  31.9 0.9 %unpack_modes.1 = f32[7,7,7,1,4,128]{5,4,3,2,1,0:T(4,128)} custom-call(f32[4,7,7,8,128]{4,3,2,1,0:T(8,128)S(1)} %get-tuple-element.31.field), custom_call_target="tpu_custom_call" | custom-call | flops 200000 | bytes 1505280 | tf_op jit(solution)/shard_map/unpack_modes/pallas_call | solution.py:509
  32.8 1.1 %collective-permute-done.14.third = f32[2,8,128]{2,1,0:T(8,128)S(1)} collective-permute-done((f32[2,8,128]{2,1,0:T(8,128)S(1)}, f32[2,8,128]{2,1,0:T(8,128)S(1)}, u32[]{:S(2)}, u32[]{:S(2)}) %collective-permute-start.14) | collective-permute-done | bytes 8224 | tf_op jit(solution)/shard_map/ppermute | solution.py:522
  33.9 0.0 collective-permute-done.13.mated
  33.9 0.6 %column.1 = f32[1,4,1024]{2,1,0:T(4,128)} custom-call(f32[2,8,128]{2,1,0:T(8,128)S(1)} %reverse_add_fusion.chip, f32[2,8,128]{2,1,0:T(8,128)S(1)} %collective-permute-done.12.fetched, f32[2,8,128]{2,1,0:T(8,128)S(1)} %collective-permute-done.13.mated, f32[2,8,128]{2,1,0:T(8,128)S(1)} %collective-permute-done.14.third), custom_call_target="tpu_custom_call" | custom-call | flops 20000 | bytes 49152 | tf_op jit(solution)/shard_map/column/pallas_call | solution.py:509
  (5 shorter events, 0.0 us)
Async XLA Ops:
  2.0 9.6 %collective-permute-start.4 = (f32[49,8,128]{2,1,0:T(8,128)S(1)}, f32[49,8,128]{2,1,0:T(8,128)S(1)}, u32[]{:S(2)}, u32[]{:S(2)}) collective-permute-start(f32[49,8,128]{2,1,0:T(8,128)S(1)} %get-tuple-element.29), channel_id=1, source_target_pairs={{0,64},{1,9},{2,66},{3,11},{4,68},{5,13},{6,70},{7,15},{8,72},{9,1... | collective-permute-start | bytes 602120 | tf_op jit(solution)/shard_map/ppermute | solution.py:532
  2.3 9.3 %collective-permute-start.5 = (f32[49,8,128]{2,1,0:T(8,128)S(1)}, f32[49,8,128]{2,1,0:T(8,128)S(1)}, u32[]{:S(2)}, u32[]{:S(2)}) collective-permute-start(f32[49,8,128]{2,1,0:T(8,128)S(1)} %get-tuple-element.30), channel_id=1, source_target_pairs={{0,8},{1,65},{2,10},{3,67},{4,12},{5,69},{6,14},{7,71},{8,0},{9,73... | collective-permute-start | bytes 602120 | tf_op jit(solution)/shard_map/ppermute | solution.py:532
  3.3 4.5 %collective-permute-start.2 = (f32[8,128]{1,0:T(8,128)S(1)}, f32[8,128]{1,0:T(8,128)S(1)}, u32[]{:S(2)}, u32[]{:S(2)}) collective-permute-start(f32[8,128]{1,0:T(8,128)S(1)} %get-tuple-element.22), channel_id=1, source_target_pairs={{0,1},{1,0},{2,3},{3,2},{4,5},{5,4},{6,7},{7,6},{8,9},{9,8},{10,11... | collective-permute-start | bytes 12296 | tf_op jit(solution)/shard_map/ppermute | solution.py:522
  4.3 6.9 %collective-permute-start = (f32[14,8,128]{2,1,0:T(8,128)S(1)}, f32[14,8,128]{2,1,0:T(8,128)S(1)}, u32[]{:S(2)}, u32[]{:S(2)}) collective-permute-start(f32[14,8,128]{2,1,0:T(8,128)S(1)} %get-tuple-element.20), channel_id=1, source_target_pairs={{0,8},{8,0},{16,24},{24,16},{32,40},{40,32},{48,56},{56,48},{1,9},... | collective-permute-start | bytes 172040 | tf_op jit(solution)/shard_map/ppermute | solution.py:522
  4.9 6.3 %collective-permute-start.1 = (f32[14,8,128]{2,1,0:T(8,128)S(1)}, f32[14,8,128]{2,1,0:T(8,128)S(1)}, u32[]{:S(2)}, u32[]{:S(2)}) collective-permute-start(f32[14,8,128]{2,1,0:T(8,128)S(1)} %get-tuple-element.21), channel_id=1, source_target_pairs={{0,1},{1,0},{2,3},{3,2},{4,5},{5,4},{6,7},{7,6},{8,16},{9,17},{10,... | collective-permute-start | bytes 172040 | tf_op jit(solution)/shard_map/ppermute | solution.py:532
  7.9 3.3 %collective-permute-start.3 = (f32[8,128]{1,0:T(8,128)S(1)}, f32[8,128]{1,0:T(8,128)S(1)}, u32[]{:S(2)}, u32[]{:S(2)}) collective-permute-start(f32[8,128]{1,0:T(8,128)S(1)} %get-tuple-element.23), channel_id=1, source_target_pairs={{0,64},{1,2},{2,1},{3,4},{4,3},{5,6},{6,5},{7,71},{8,72},{9,10},{1... | collective-permute-start | bytes 12296 | tf_op jit(solution)/shard_map/ppermute | solution.py:532
  12.1 4.1 %collective-permute-start.6 = (f32[2,8,128]{2,1,0:T(8,128)S(1)}, f32[2,8,128]{2,1,0:T(8,128)S(1)}, u32[]{:S(2)}, u32[]{:S(2)}) collective-permute-start(f32[2,8,128]{2,1,0:T(8,128)S(1)} %get-tuple-element.33), channel_id=1, source_target_pairs={{0,128},{64,192},{128,0},{192,64},{1,129},{65,193},{129,1},{193,65... | collective-permute-start | bytes 24584 | tf_op jit(solution)/shard_map/ppermute | solution.py:522
  13.5 3.1 %collective-permute-start.7 = (f32[2,8,128]{2,1,0:T(8,128)S(1)}, f32[2,8,128]{2,1,0:T(8,128)S(1)}, u32[]{:S(2)}, u32[]{:S(2)}) collective-permute-start(f32[2,8,128]{2,1,0:T(8,128)S(1)} %get-tuple-element.34), channel_id=1, source_target_pairs={{0,64},{64,0},{128,192},{192,128},{1,65},{65,1},{129,193},{193,129... | collective-permute-start | bytes 24584 | tf_op jit(solution)/shard_map/ppermute | solution.py:522
  15.5 2.5 %collective-permute-start.8 = (f32[2,8,128]{2,1,0:T(8,128)S(1)}, f32[2,8,128]{2,1,0:T(8,128)S(1)}, u32[]{:S(2)}, u32[]{:S(2)}) collective-permute-start(f32[2,8,128]{2,1,0:T(8,128)S(1)} %get-tuple-element.35), channel_id=1, source_target_pairs={{0,1},{1,0},{2,3},{3,2},{4,5},{5,4},{6,7},{7,6},{8,9},{9,8},{10,11... | collective-permute-start | bytes 24584 | tf_op jit(solution)/shard_map/ppermute | solution.py:532
  18.1 3.6 %collective-permute-start.9 = (f32[2,8,128]{2,1,0:T(8,128)S(1)}, f32[2,8,128]{2,1,0:T(8,128)S(1)}, u32[]{:S(2)}, u32[]{:S(2)}) collective-permute-start(f32[2,8,128]{2,1,0:T(8,128)S(1)} %multiply_add_fusion), channel_id=1, source_target_pairs={{0,1},{1,0},{2,3},{3,2},{4,5},{5,4},{6,7},{7,6},{8,9},{9,8},{10,11... | collective-permute-start | bytes 24584 | tf_op jit(solution)/shard_map/ppermute | solution.py:522
  21.7 2.6 %collective-permute-start.10 = (f32[2,2,8,128]{3,2,1,0:T(8,128)S(1)}, f32[2,2,8,128]{3,2,1,0:T(8,128)S(1)}, u32[]{:S(2)}, u32[]{:S(2)}) collective-permute-start(f32[2,2,8,128]{3,2,1,0:T(8,128)S(1)} %pad_maximum_fusion), channel_id=1, source_target_pairs={{0,64},{1,9},{2,66},{3,11},{4,68},{5,13},{6,70},{7,15},{8,16},{9,1... | collective-permute-start | bytes 49160 | tf_op jit(solution)/shard_map/ppermute | solution.py:532
  24.4 3.5 %collective-permute-start.11 = (f32[2,8,128]{2,1,0:T(8,128)S(1)}, f32[2,8,128]{2,1,0:T(8,128)S(1)}, u32[]{:S(2)}, u32[]{:S(2)}) collective-permute-start(f32[2,8,128]{2,1,0:T(8,128)S(1)} %bitcast.9), channel_id=1, source_target_pairs={{0,1},{1,0},{2,3},{3,2},{4,5},{5,4},{6,7},{7,6},{8,9},{9,8},{10,11... | collective-permute-start | bytes 24584 | tf_op jit(solution)/shard_map/ppermute | solution.py:522
  27.9 4.0 %collective-permute-start.12 = (f32[2,8,128]{2,1,0:T(8,128)S(1)}, f32[2,8,128]{2,1,0:T(8,128)S(1)}, u32[]{:S(2)}, u32[]{:S(2)}) collective-permute-start(f32[2,8,128]{2,1,0:T(8,128)S(1)} %reverse_add_fusion.chip), channel_id=1, source_target_pairs={{0,2},{1,5},{2,0},{3,7},{4,6},{5,1},{6,4},{7,3},{8,10},{9,13},{10,... | collective-permute-start | bytes 24584 | tf_op jit(solution)/shard_map/ppermute | solution.py:532
  30.2 3.7 %collective-permute-start.14 = (f32[2,8,128]{2,1,0:T(8,128)S(1)}, f32[2,8,128]{2,1,0:T(8,128)S(1)}, u32[]{:S(2)}, u32[]{:S(2)}) collective-permute-start(f32[2,8,128]{2,1,0:T(8,128)S(1)} %reverse_add_fusion.chip), channel_id=1, source_target_pairs={{0,6},{1,7},{2,4},{3,5},{4,2},{5,3},{6,0},{7,1},{8,14},{9,15},{10,... | collective-permute-start | bytes 24584 | tf_op jit(solution)/shard_map/ppermute | solution.py:522
  31.9 2.0 %collective-permute-start.13 = (f32[2,8,128]{2,1,0:T(8,128)S(1)}, f32[2,8,128]{2,1,0:T(8,128)S(1)}, u32[]{:S(2)}, u32[]{:S(2)}) collective-permute-start(f32[2,8,128]{2,1,0:T(8,128)S(1)} %collective-permute-done.12.fetched), channel_id=1, source_target_pairs={{0,1},{1,0},{2,3},{3,2},{4,5},{5,4},{6,7},{7,6},{8,9},{9,8},{10,11... | collective-permute-start | bytes 24584 | tf_op jit(solution)/shard_map/ppermute | solution.py:522

commit v6 on v5

--- a/solution.py
+++ b/solution.py
@@ -305,7 +305,7 @@
 
 
 def side_kernel(
-    local, y_a, y_b, z_a, z_b, y_below, y_above, z_below, z_above, out
+    local, z_b, y_a, y_b, z_a, y_below, y_above, z_below, z_above, out
 ):
     row, lane = row_in_half(), lanes()
     y_even, z_even = goes_up(lax.axis_index("gy")), goes_up(lax.axis_index("gz"))
@@ -605,13 +605,14 @@
         (shape(FACE_ROWS, 8, 128),) * 2 + (shape(8, 128),) * 2 + sides,
         SIDE_COST,
     )
+    z_b = second_pairs(z_b, "gz")
     y_a, y_b = flip(y_a, "gy", 1), second_pairs(y_b, "gy")
-    z_a, z_b = flip(z_a, "gz", 1), second_pairs(z_b, "gz")
+    z_a = flip(z_a, "gz", 1)
     (local,) = call(own_kernel, "own_cells", (first,), (shape(*cells),), OWN_COST)
     (local,) = call(
         side_kernel,
         "side_halo",
-        (local, y_a, y_b, z_a, z_b, y_high, y_low, z_high, z_low),
+        (local, z_b, y_a, y_b, z_a, y_high, y_low, z_high, z_low),
         (shape(*cells),),
         HALO_COST,
     )

time: 34.7 us -> 34.5 us (level)
  starting transfers between devices: 19.7 us -> 19.3 us
    ppermute x8, starting transfers between devices: 11.3 us -> 9.76 us  [flip(): lax.ppermute(value, axis, [(i, i ^ bits) for i in range(lax.axis_size(axi...]
    ppermute x7, starting transfers between devices: 8.45 us -> 9.54 us  [exchange(): return lax.ppermute(value, axes, route)]
    ppermute x8, waiting for transfers between devices: 3.88 us -> 4.5 us  [flip(): lax.ppermute(value, axis, [(i, i ^ bits) for i in range(lax.axis_size(axi...]
    ppermute x7, waiting for transfers between devices: 5.59 us -> 5.07 us  [exchange(): return lax.ppermute(value, axes, route)]
where the time goes in v6:
time: 34.5 us; the launch traced here: 34.2 us
  starting transfers between devices  19.3 us (56%)
  waiting for transfers between devices  9.57 us (28%)
  Pallas kernels  4.57 us (13%)
  between operations  0.71 us (2%)
    ppermute x8, starting transfers between devices, flip(): lax.ppermute(value, axis, [(i, i ^ bits) for i in range(lax.axis_size(axi...  9.76 us
    ppermute x7, starting transfers between devices, exchange(): return lax.ppermute(value, axes, route)  9.54 us
    ppermute x7, waiting for transfers between devices, exchange(): return lax.ppermute(value, axes, route)  5.07 us
    pallas_call x7, Pallas kernels, call(): pl.pallas_call(kernel, out_shape=outputs, in_specs=[pl.BlockSpec(memory_s...  4.57 us
    ppermute x8, waiting for transfers between devices, flip(): lax.ppermute(value, axis, [(i, i ^ bits) for i in range(lax.axis_size(axi...  4.5 us
  transfers between devices with their start and end apart: 15, of which 9 were waited for; matrix products, arithmetic and copies ran while one was open for 0% of the time, Pallas kernels for 6%

profile of v6, /device:TPU:101, one launch (start us, length us, event | category | flops | bytes accessed | tf_op | source)
XLA Modules:
  0.0 34.2 jit_solution(933539574383091069)
XLA Ops:
  0.6 1.3 %x_traces.1 = (f32[4,7,7,8,128]{4,3,2,1,0:T(8,128)S(1)}, f32[49,8,128]{2,1,0:T(8,128)S(1)}, f32[49,8,128]{2,1,0:T(8,128)S(1)}, s32[1,4,128]{2,1,0:T(4,128)S(1)}) custom-call(f32[7,7,7,1,4,128]{5,4,3,2,1,0:T(4,128)} %rhs_hbm.1, s32[1,4,128]{2,1,0:T(4,128)} %orders_hbm.1), custom_call_target="tpu_custom_call" | custom-call | flops 4000000 | bytes 1910784 | tf_op jit(solution)/shard_map/x_traces/pallas_call | solution.py:509
  2.0 0.3 collective-permute-start.4
  2.3 0.8 %collective-permute-start.5 = (f32[49,8,128]{2,1,0:T(8,128)S(1)}, f32[49,8,128]{2,1,0:T(8,128)S(1)}, u32[]{:S(2)}, u32[]{:S(2)}) collective-permute-start(f32[49,8,128]{2,1,0:T(8,128)S(1)} %get-tuple-element.30), channel_id=1, source_target_pairs={{0,8},{1,65},{2,10},{3,67},{4,12},{5,69},{6,14},{7,71},{8,0},{9,73... | collective-permute-start | bytes 602120 | tf_op jit(solution)/shard_map/ppermute | solution.py:532
  3.1 0.3 side_traces.1
  3.3 2.1 %collective-permute-start = (f32[8,128]{1,0:T(8,128)S(1)}, f32[8,128]{1,0:T(8,128)S(1)}, u32[]{:S(2)}, u32[]{:S(2)}) collective-permute-start(f32[8,128]{1,0:T(8,128)S(1)} %get-tuple-element.20), channel_id=1, source_target_pairs={{0,64},{1,2},{2,1},{3,4},{4,3},{5,6},{6,5},{7,71},{8,72},{9,10},{1... | collective-permute-start | bytes 12296 | tf_op jit(solution)/shard_map/ppermute | solution.py:532
  5.5 0.0 collective-permute-start.1
  5.5 3.6 %collective-permute-start.2 = (f32[14,8,128]{2,1,0:T(8,128)S(1)}, f32[14,8,128]{2,1,0:T(8,128)S(1)}, u32[]{:S(2)}, u32[]{:S(2)}) collective-permute-start(f32[14,8,128]{2,1,0:T(8,128)S(1)} %get-tuple-element.22), channel_id=1, source_target_pairs={{0,1},{1,0},{2,3},{3,2},{4,5},{5,4},{6,7},{7,6},{8,16},{9,17},{10,... | collective-permute-start | bytes 172040 | tf_op jit(solution)/shard_map/ppermute | solution.py:532
  9.0 0.0 collective-permute-done.z_b
  9.1 1.2 %collective-permute-start.3 = (f32[8,128]{1,0:T(8,128)S(1)}, f32[8,128]{1,0:T(8,128)S(1)}, u32[]{:S(2)}, u32[]{:S(2)}) collective-permute-start(f32[8,128]{1,0:T(8,128)S(1)} %get-tuple-element.23), channel_id=1, source_target_pairs={{0,1},{1,0},{2,3},{3,2},{4,5},{5,4},{6,7},{7,6},{8,9},{9,8},{10,11... | collective-permute-start | bytes 12296 | tf_op jit(solution)/shard_map/ppermute | solution.py:522
  10.3 0.6 %own_cells.1.local = f32[4,7,7,8,128]{4,3,2,1,0:T(8,128)S(1)} custom-call(f32[4,7,7,8,128]{4,3,2,1,0:T(8,128)S(1)} %get-tuple-element.19.first), custom_call_target="tpu_custom_call" | custom-call | flops 1400000000 | bytes 1605632 | tf_op jit(solution)/shard_map/own_cells/pallas_call | solution.py:509
  10.8 0.2 collective-permute-done.3.z_a
  11.1 0.0 collective-permute-done.1.y_a
  11.1 0.0 collective-permute-done.2.y_b
  11.1 0.4 %side_halo.1.local = f32[4,7,7,8,128]{4,3,2,1,0:T(8,128)S(1)} custom-call(f32[4,7,7,8,128]{4,3,2,1,0:T(8,128)S(1)} %own_cells.1.local, f32[8,128]{1,0:T(8,128)S(1)} %collective-permute-done.z_b, f32[14,8,128]{2,1,0:T(8,128)S(1)} %collective-permute-done.1.y_a, f32[14,8,128]{2,1,0:T(8,128)S(1)} %collective-permute-done.2.y_b, ...), custom_call_target="tpu_custom_call" | custom-call | flops 4000000 | bytes 2646016 | tf_op jit(solution)/shard_map/side_halo/pallas_call | solution.py:509
  11.5 0.0 collective-permute-done.4.x_a
  11.5 0.0 collective-permute-done.5.x_b
  11.5 0.4 %smooth_and_restrict.1 = (f32[4,7,7,8,128]{4,3,2,1,0:T(8,128)S(1)}, f32[2,8,128]{2,1,0:T(8,128)S(1)}, f32[2,8,128]{2,1,0:T(8,128)S(1)}, f32[2,8,128]{2,1,0:T(8,128)S(1)}, f32[2,8,128]{2,1,0:T(8,128)S(1)}) custom-call(f32[4,7,7,8,128]{4,3,2,1,0:T(8,128)S(1)} %get-tuple-element.19.first, f32[4,7,7,8,128]{4,3,2,1,0:T(8,128)S(1)} %side_halo.1.local, ...), custom_call_target="tpu_custom_call" | custom-call | flops 5000000 | bytes 2844672 | tf_op jit(solution)/shard_map/smooth_and_restrict/pallas_call | solution.py:509
  12.0 1.5 %collective-permute-start.6 = (f32[2,8,128]{2,1,0:T(8,128)S(1)}, f32[2,8,128]{2,1,0:T(8,128)S(1)}, u32[]{:S(2)}, u32[]{:S(2)}) collective-permute-start(f32[2,8,128]{2,1,0:T(8,128)S(1)} %get-tuple-element.33), channel_id=1, source_target_pairs={{0,128},{64,192},{128,0},{192,64},{1,129},{65,193},{129,1},{193,65... | collective-permute-start | bytes 24584 | tf_op jit(solution)/shard_map/ppermute | solution.py:522
  13.4 2.0 %collective-permute-start.7 = (f32[2,8,128]{2,1,0:T(8,128)S(1)}, f32[2,8,128]{2,1,0:T(8,128)S(1)}, u32[]{:S(2)}, u32[]{:S(2)}) collective-permute-start(f32[2,8,128]{2,1,0:T(8,128)S(1)} %get-tuple-element.34), channel_id=1, source_target_pairs={{0,64},{64,0},{128,192},{192,128},{1,65},{65,1},{129,193},{193,129... | collective-permute-start | bytes 24584 | tf_op jit(solution)/shard_map/ppermute | solution.py:522
  15.5 0.0 collective-permute-start.8
  15.5 0.6 %collective-permute-done.6 = f32[2,8,128]{2,1,0:T(8,128)S(1)} collective-permute-done((f32[2,8,128]{2,1,0:T(8,128)S(1)}, f32[2,8,128]{2,1,0:T(8,128)S(1)}, u32[]{:S(2)}, u32[]{:S(2)}) %collective-permute-start.6) | collective-permute-done | bytes 8224 | tf_op jit(solution)/shard_map/ppermute | solution.py:522
  16.1 0.5 %collective-permute-done.7 = f32[2,8,128]{2,1,0:T(8,128)S(1)} collective-permute-done((f32[2,8,128]{2,1,0:T(8,128)S(1)}, f32[2,8,128]{2,1,0:T(8,128)S(1)}, u32[]{:S(2)}, u32[]{:S(2)}) %collective-permute-start.7) | collective-permute-done | bytes 8224 | tf_op jit(solution)/shard_map/ppermute | solution.py:522
  16.6 1.7 %collective-permute-done.8 = f32[2,8,128]{2,1,0:T(8,128)S(1)} collective-permute-done((f32[2,8,128]{2,1,0:T(8,128)S(1)}, f32[2,8,128]{2,1,0:T(8,128)S(1)}, u32[]{:S(2)}, u32[]{:S(2)}) %collective-permute-start.8) | collective-permute-done | bytes 8224 | tf_op jit(solution)/shard_map/ppermute | solution.py:532
  18.3 1.8 %collective-permute-start.9 = (f32[2,8,128]{2,1,0:T(8,128)S(1)}, f32[2,8,128]{2,1,0:T(8,128)S(1)}, u32[]{:S(2)}, u32[]{:S(2)}) collective-permute-start(f32[2,8,128]{2,1,0:T(8,128)S(1)} %multiply_add_fusion), channel_id=1, source_target_pairs={{0,1},{1,0},{2,3},{3,2},{4,5},{5,4},{6,7},{7,6},{8,9},{9,8},{10,11... | collective-permute-start | bytes 24584 | tf_op jit(solution)/shard_map/ppermute | solution.py:522
  20.1 0.8 %collective-permute-done.9 = f32[2,8,128]{2,1,0:T(8,128)S(1)} collective-permute-done((f32[2,8,128]{2,1,0:T(8,128)S(1)}, f32[2,8,128]{2,1,0:T(8,128)S(1)}, u32[]{:S(2)}, u32[]{:S(2)}) %collective-permute-start.9) | collective-permute-done | bytes 8224 | tf_op jit(solution)/shard_map/ppermute | solution.py:522
  20.9 0.0 collective-permute-start.10
  20.9 2.6 %collective-permute-done.10 = f32[2,2,8,128]{3,2,1,0:T(8,128)S(1)} collective-permute-done((f32[2,2,8,128]{3,2,1,0:T(8,128)S(1)}, f32[2,2,8,128]{3,2,1,0:T(8,128)S(1)}, u32[]{:S(2)}, u32[]{:S(2)}) %collective-permute-start.10) | collective-permute-done | bytes 16416 | tf_op jit(solution)/shard_map/ppermute | solution.py:532
  23.5 0.1 fusion.1
  23.6 2.8 %collective-permute-start.11 = (f32[2,8,128]{2,1,0:T(8,128)S(1)}, f32[2,8,128]{2,1,0:T(8,128)S(1)}, u32[]{:S(2)}, u32[]{:S(2)}) collective-permute-start(f32[2,8,128]{2,1,0:T(8,128)S(1)} %bitcast.9), channel_id=1, source_target_pairs={{0,1},{1,0},{2,3},{3,2},{4,5},{5,4},{6,7},{7,6},{8,9},{9,8},{10,11... | collective-permute-start | bytes 24584 | tf_op jit(solution)/shard_map/ppermute | solution.py:522
  26.4 0.8 %collective-permute-done.11 = f32[2,8,128]{2,1,0:T(8,128)S(1)} collective-permute-done((f32[2,8,128]{2,1,0:T(8,128)S(1)}, f32[2,8,128]{2,1,0:T(8,128)S(1)}, u32[]{:S(2)}, u32[]{:S(2)}) %collective-permute-start.11) | collective-permute-done | bytes 8224 | tf_op jit(solution)/shard_map/ppermute | solution.py:522
  27.2 2.7 %collective-permute-start.12 = (f32[2,8,128]{2,1,0:T(8,128)S(1)}, f32[2,8,128]{2,1,0:T(8,128)S(1)}, u32[]{:S(2)}, u32[]{:S(2)}) collective-permute-start(f32[2,8,128]{2,1,0:T(8,128)S(1)} %reverse_add_fusion.chip), channel_id=1, source_target_pairs={{0,2},{1,5},{2,0},{3,7},{4,6},{5,1},{6,4},{7,3},{8,10},{9,13},{10,... | collective-permute-start | bytes 24584 | tf_op jit(solution)/shard_map/ppermute | solution.py:532
  29.9 0.5 %collective-permute-start.14 = (f32[2,8,128]{2,1,0:T(8,128)S(1)}, f32[2,8,128]{2,1,0:T(8,128)S(1)}, u32[]{:S(2)}, u32[]{:S(2)}) collective-permute-start(f32[2,8,128]{2,1,0:T(8,128)S(1)} %reverse_add_fusion.chip), channel_id=1, source_target_pairs={{0,6},{1,7},{2,4},{3,5},{4,2},{5,3},{6,0},{7,1},{8,14},{9,15},{10,... | collective-permute-start | bytes 24584 | tf_op jit(solution)/shard_map/ppermute | solution.py:522
  30.4 0.8 %collective-permute-done.12.fetched = f32[2,8,128]{2,1,0:T(8,128)S(1)} collective-permute-done((f32[2,8,128]{2,1,0:T(8,128)S(1)}, f32[2,8,128]{2,1,0:T(8,128)S(1)}, u32[]{:S(2)}, u32[]{:S(2)}) %collective-permute-start.12) | collective-permute-done | bytes 8224 | tf_op jit(solution)/shard_map/ppermute | solution.py:532
  31.2 0.0 collective-permute-start.13
  31.2 0.9 %unpack_modes.1 = f32[7,7,7,1,4,128]{5,4,3,2,1,0:T(4,128)} custom-call(f32[4,7,7,8,128]{4,3,2,1,0:T(8,128)S(1)} %get-tuple-element.31.field), custom_call_target="tpu_custom_call" | custom-call | flops 200000 | bytes 1505280 | tf_op jit(solution)/shard_map/unpack_modes/pallas_call | solution.py:509
  32.1 1.5 %collective-permute-done.14.third = f32[2,8,128]{2,1,0:T(8,128)S(1)} collective-permute-done((f32[2,8,128]{2,1,0:T(8,128)S(1)}, f32[2,8,128]{2,1,0:T(8,128)S(1)}, u32[]{:S(2)}, u32[]{:S(2)}) %collective-permute-start.14) | collective-permute-done | bytes 8224 | tf_op jit(solution)/shard_map/ppermute | solution.py:522
  33.6 0.0 collective-permute-done.13.mated
  33.6 0.6 %column.1 = f32[1,4,1024]{2,1,0:T(4,128)} custom-call(f32[2,8,128]{2,1,0:T(8,128)S(1)} %reverse_add_fusion.chip, f32[2,8,128]{2,1,0:T(8,128)S(1)} %collective-permute-done.12.fetched, f32[2,8,128]{2,1,0:T(8,128)S(1)} %collective-permute-done.13.mated, f32[2,8,128]{2,1,0:T(8,128)S(1)} %collective-permute-done.14.third), custom_call_target="tpu_custom_call" | custom-call | flops 20000 | bytes 49152 | tf_op jit(solution)/shard_map/column/pallas_call | solution.py:509
  (5 shorter events, 0.0 us)
Async XLA Ops:
  2.0 9.5 %collective-permute-start.4 = (f32[49,8,128]{2,1,0:T(8,128)S(1)}, f32[49,8,128]{2,1,0:T(8,128)S(1)}, u32[]{:S(2)}, u32[]{:S(2)}) collective-permute-start(f32[49,8,128]{2,1,0:T(8,128)S(1)} %get-tuple-element.29), channel_id=1, source_target_pairs={{0,64},{1,9},{2,66},{3,11},{4,68},{5,13},{6,70},{7,15},{8,72},{9,1... | collective-permute-start | bytes 602120 | tf_op jit(solution)/shard_map/ppermute | solution.py:532
  2.3 9.2 %collective-permute-start.5 = (f32[49,8,128]{2,1,0:T(8,128)S(1)}, f32[49,8,128]{2,1,0:T(8,128)S(1)}, u32[]{:S(2)}, u32[]{:S(2)}) collective-permute-start(f32[49,8,128]{2,1,0:T(8,128)S(1)} %get-tuple-element.30), channel_id=1, source_target_pairs={{0,8},{1,65},{2,10},{3,67},{4,12},{5,69},{6,14},{7,71},{8,0},{9,73... | collective-permute-start | bytes 602120 | tf_op jit(solution)/shard_map/ppermute | solution.py:532
  3.3 5.7 %collective-permute-start = (f32[8,128]{1,0:T(8,128)S(1)}, f32[8,128]{1,0:T(8,128)S(1)}, u32[]{:S(2)}, u32[]{:S(2)}) collective-permute-start(f32[8,128]{1,0:T(8,128)S(1)} %get-tuple-element.20), channel_id=1, source_target_pairs={{0,64},{1,2},{2,1},{3,4},{4,3},{5,6},{6,5},{7,71},{8,72},{9,10},{1... | collective-permute-start | bytes 12296 | tf_op jit(solution)/shard_map/ppermute | solution.py:532
  5.5 5.6 %collective-permute-start.1 = (f32[14,8,128]{2,1,0:T(8,128)S(1)}, f32[14,8,128]{2,1,0:T(8,128)S(1)}, u32[]{:S(2)}, u32[]{:S(2)}) collective-permute-start(f32[14,8,128]{2,1,0:T(8,128)S(1)} %get-tuple-element.21), channel_id=1, source_target_pairs={{0,8},{8,0},{16,24},{24,16},{32,40},{40,32},{48,56},{56,48},{1,9},... | collective-permute-start | bytes 172040 | tf_op jit(solution)/shard_map/ppermute | solution.py:522
  5.5 5.6 %collective-permute-start.2 = (f32[14,8,128]{2,1,0:T(8,128)S(1)}, f32[14,8,128]{2,1,0:T(8,128)S(1)}, u32[]{:S(2)}, u32[]{:S(2)}) collective-permute-start(f32[14,8,128]{2,1,0:T(8,128)S(1)} %get-tuple-element.22), channel_id=1, source_target_pairs={{0,1},{1,0},{2,3},{3,2},{4,5},{5,4},{6,7},{7,6},{8,16},{9,17},{10,... | collective-permute-start | bytes 172040 | tf_op jit(solution)/shard_map/ppermute | solution.py:532
  9.1 2.0 %collective-permute-start.3 = (f32[8,128]{1,0:T(8,128)S(1)}, f32[8,128]{1,0:T(8,128)S(1)}, u32[]{:S(2)}, u32[]{:S(2)}) collective-permute-start(f32[8,128]{1,0:T(8,128)S(1)} %get-tuple-element.23), channel_id=1, source_target_pairs={{0,1},{1,0},{2,3},{3,2},{4,5},{5,4},{6,7},{7,6},{8,9},{9,8},{10,11... | collective-permute-start | bytes 12296 | tf_op jit(solution)/shard_map/ppermute | solution.py:522
  12.0 4.1 %collective-permute-start.6 = (f32[2,8,128]{2,1,0:T(8,128)S(1)}, f32[2,8,128]{2,1,0:T(8,128)S(1)}, u32[]{:S(2)}, u32[]{:S(2)}) collective-permute-start(f32[2,8,128]{2,1,0:T(8,128)S(1)} %get-tuple-element.33), channel_id=1, source_target_pairs={{0,128},{64,192},{128,0},{192,64},{1,129},{65,193},{129,1},{193,65... | collective-permute-start | bytes 24584 | tf_op jit(solution)/shard_map/ppermute | solution.py:522
  13.4 3.2 %collective-permute-start.7 = (f32[2,8,128]{2,1,0:T(8,128)S(1)}, f32[2,8,128]{2,1,0:T(8,128)S(1)}, u32[]{:S(2)}, u32[]{:S(2)}) collective-permute-start(f32[2,8,128]{2,1,0:T(8,128)S(1)} %get-tuple-element.34), channel_id=1, source_target_pairs={{0,64},{64,0},{128,192},{192,128},{1,65},{65,1},{129,193},{193,129... | collective-permute-start | bytes 24584 | tf_op jit(solution)/shard_map/ppermute | solution.py:522
  15.5 2.8 %collective-permute-start.8 = (f32[2,8,128]{2,1,0:T(8,128)S(1)}, f32[2,8,128]{2,1,0:T(8,128)S(1)}, u32[]{:S(2)}, u32[]{:S(2)}) collective-permute-start(f32[2,8,128]{2,1,0:T(8,128)S(1)} %get-tuple-element.35), channel_id=1, source_target_pairs={{0,1},{1,0},{2,3},{3,2},{4,5},{5,4},{6,7},{7,6},{8,9},{9,8},{10,11... | collective-permute-start | bytes 24584 | tf_op jit(solution)/shard_map/ppermute | solution.py:532
  18.3 2.6 %collective-permute-start.9 = (f32[2,8,128]{2,1,0:T(8,128)S(1)}, f32[2,8,128]{2,1,0:T(8,128)S(1)}, u32[]{:S(2)}, u32[]{:S(2)}) collective-permute-start(f32[2,8,128]{2,1,0:T(8,128)S(1)} %multiply_add_fusion), channel_id=1, source_target_pairs={{0,1},{1,0},{2,3},{3,2},{4,5},{5,4},{6,7},{7,6},{8,9},{9,8},{10,11... | collective-permute-start | bytes 24584 | tf_op jit(solution)/shard_map/ppermute | solution.py:522
  20.9 2.6 %collective-permute-start.10 = (f32[2,2,8,128]{3,2,1,0:T(8,128)S(1)}, f32[2,2,8,128]{3,2,1,0:T(8,128)S(1)}, u32[]{:S(2)}, u32[]{:S(2)}) collective-permute-start(f32[2,2,8,128]{3,2,1,0:T(8,128)S(1)} %pad_maximum_fusion), channel_id=1, source_target_pairs={{0,64},{1,9},{2,66},{3,11},{4,68},{5,13},{6,70},{7,15},{8,16},{9,1... | collective-permute-start | bytes 49160 | tf_op jit(solution)/shard_map/ppermute | solution.py:532
  23.6 3.6 %collective-permute-start.11 = (f32[2,8,128]{2,1,0:T(8,128)S(1)}, f32[2,8,128]{2,1,0:T(8,128)S(1)}, u32[]{:S(2)}, u32[]{:S(2)}) collective-permute-start(f32[2,8,128]{2,1,0:T(8,128)S(1)} %bitcast.9), channel_id=1, source_target_pairs={{0,1},{1,0},{2,3},{3,2},{4,5},{5,4},{6,7},{7,6},{8,9},{9,8},{10,11... | collective-permute-start | bytes 24584 | tf_op jit(solution)/shard_map/ppermute | solution.py:522
  27.2 4.0 %collective-permute-start.12 = (f32[2,8,128]{2,1,0:T(8,128)S(1)}, f32[2,8,128]{2,1,0:T(8,128)S(1)}, u32[]{:S(2)}, u32[]{:S(2)}) collective-permute-start(f32[2,8,128]{2,1,0:T(8,128)S(1)} %reverse_add_fusion.chip), channel_id=1, source_target_pairs={{0,2},{1,5},{2,0},{3,7},{4,6},{5,1},{6,4},{7,3},{8,10},{9,13},{10,... | collective-permute-start | bytes 24584 | tf_op jit(solution)/shard_map/ppermute | solution.py:532
  29.9 3.7 %collective-permute-start.14 = (f32[2,8,128]{2,1,0:T(8,128)S(1)}, f32[2,8,128]{2,1,0:T(8,128)S(1)}, u32[]{:S(2)}, u32[]{:S(2)}) collective-permute-start(f32[2,8,128]{2,1,0:T(8,128)S(1)} %reverse_add_fusion.chip), channel_id=1, source_target_pairs={{0,6},{1,7},{2,4},{3,5},{4,2},{5,3},{6,0},{7,1},{8,14},{9,15},{10,... | collective-permute-start | bytes 24584 | tf_op jit(solution)/shard_map/ppermute | solution.py:522
  31.2 2.4 %collective-permute-start.13 = (f32[2,8,128]{2,1,0:T(8,128)S(1)}, f32[2,8,128]{2,1,0:T(8,128)S(1)}, u32[]{:S(2)}, u32[]{:S(2)}) collective-permute-start(f32[2,8,128]{2,1,0:T(8,128)S(1)} %collective-permute-done.12.fetched), channel_id=1, source_target_pairs={{0,1},{1,0},{2,3},{3,2},{4,5},{5,4},{6,7},{7,6},{8,9},{9,8},{10,11... | collective-permute-start | bytes 24584 | tf_op jit(solution)/shard_map/ppermute | solution.py:522

commit v7 on v5

--- a/solution.py
+++ b/solution.py
@@ -305,7 +305,7 @@
 
 
 def side_kernel(
-    local, y_a, y_b, z_a, z_b, y_below, y_above, z_below, z_above, out
+    local, y_b, y_a, z_a, z_b, y_below, y_above, z_below, z_above, out
 ):
     row, lane = row_in_half(), lanes()
     y_even, z_even = goes_up(lax.axis_index("gy")), goes_up(lax.axis_index("gz"))
@@ -562,9 +562,9 @@
 
     def partner(place):
         if place[2] % 2:
-            place[1] ^= 1
-            return place
-        return second_of_pair(place, 1, count, 0, 1)
+            return second_of_pair(place, 1, count, 0, 1)
+        place[1] ^= 1
+        return place
 
     return exchange(value, partner)
 
@@ -605,13 +605,14 @@
         (shape(FACE_ROWS, 8, 128),) * 2 + (shape(8, 128),) * 2 + sides,
         SIDE_COST,
     )
-    y_a, y_b = flip(y_a, "gy", 1), second_pairs(y_b, "gy")
+    y_b = second_pairs(y_b, "gy")
+    y_a = flip(y_a, "gy", 1)
     z_a, z_b = flip(z_a, "gz", 1), second_pairs(z_b, "gz")
     (local,) = call(own_kernel, "own_cells", (first,), (shape(*cells),), OWN_COST)
     (local,) = call(
         side_kernel,
         "side_halo",
-        (local, y_a, y_b, z_a, z_b, y_high, y_low, z_high, z_low),
+        (local, y_b, y_a, z_a, z_b, y_high, y_low, z_high, z_low),
         (shape(*cells),),
         HALO_COST,
     )
@@ -635,7 +636,7 @@
     count = lax.axis_size("gz")
     chip = jnp.stack([sums, flip(sums, "gz", 1)])
     from_beside = both_y_sides(chip)
-    from_low = (lax.axis_index("gy") + lax.axis_index("gz")) % 2 == 0
+    from_low = (lax.axis_index("gy") + lax.axis_index("gz")) % 2 == 1
     row = lax.broadcasted_iota(jnp.int32, (1, 1, 4, 1), 2)
     wanted = jnp.where(from_low, row < 2, row == 3)
     valid = jnp.where(from_low, inside("gy", -1), inside("gy", 1))

time: 34.7 us -> 34.4 us (level)
  the two profiles are of different devices: /device:TPU:101 before, /device:TPU:69 now
where the time goes in v7:
time: 34.4 us; the launch traced here: 34.3 us
  starting transfers between devices  19.4 us (56%)
  waiting for transfers between devices  9.48 us (28%)
  Pallas kernels  4.57 us (13%)
  between operations  0.72 us (2%)
    ppermute x8, starting transfers between devices, flip(): lax.ppermute(value, axis, [(i, i ^ bits) for i in range(lax.axis_size(axi...  12.3 us
    ppermute x7, starting transfers between devices, exchange(): return lax.ppermute(value, axes, route)  7.11 us
    ppermute x7, waiting for transfers between devices, exchange(): return lax.ppermute(value, axes, route)  5.6 us
    pallas_call x7, Pallas kernels, call(): pl.pallas_call(kernel, out_shape=outputs, in_specs=[pl.BlockSpec(memory_s...  4.57 us
    ppermute x8, waiting for transfers between devices, flip(): lax.ppermute(value, axis, [(i, i ^ bits) for i in range(lax.axis_size(axi...  3.88 us
  transfers between devices with their start and end apart: 15, of which 9 were waited for; matrix products, arithmetic and copies ran while one was open for 0% of the time, Pallas kernels for 6%

profile of v7, /device:TPU:69, one launch (start us, length us, event | category | flops | bytes accessed | tf_op | source)
XLA Modules:
  0.0 34.3 jit_solution(12058318308623708643)
XLA Ops:
  0.6 1.3 %x_traces.1 = (f32[4,7,7,8,128]{4,3,2,1,0:T(8,128)S(1)}, f32[49,8,128]{2,1,0:T(8,128)S(1)}, f32[49,8,128]{2,1,0:T(8,128)S(1)}, s32[1,4,128]{2,1,0:T(4,128)S(1)}) custom-call(f32[7,7,7,1,4,128]{5,4,3,2,1,0:T(4,128)} %rhs_hbm.1, s32[1,4,128]{2,1,0:T(4,128)} %orders_hbm.1), custom_call_target="tpu_custom_call" | custom-call | flops 4000000 | bytes 1910784 | tf_op jit(solution)/shard_map/x_traces/pallas_call | solution.py:509
  2.0 0.3 collective-permute-start.4
  2.3 2.3 %collective-permute-start.5 = (f32[49,8,128]{2,1,0:T(8,128)S(1)}, f32[49,8,128]{2,1,0:T(8,128)S(1)}, u32[]{:S(2)}, u32[]{:S(2)}) collective-permute-start(f32[49,8,128]{2,1,0:T(8,128)S(1)} %get-tuple-element.30), channel_id=1, source_target_pairs={{0,8},{1,65},{2,10},{3,67},{4,12},{5,69},{6,14},{7,71},{8,0},{9,73... | collective-permute-start | bytes 602120 | tf_op jit(solution)/shard_map/ppermute | solution.py:532
  4.6 0.3 side_traces.1
  4.9 0.1 collective-permute-start.2
  5.0 0.1 collective-permute-start
  5.1 3.7 %collective-permute-start.1 = (f32[14,8,128]{2,1,0:T(8,128)S(1)}, f32[14,8,128]{2,1,0:T(8,128)S(1)}, u32[]{:S(2)}, u32[]{:S(2)}) collective-permute-start(f32[14,8,128]{2,1,0:T(8,128)S(1)} %get-tuple-element.21), channel_id=1, source_target_pairs={{0,8},{8,0},{16,24},{24,16},{32,40},{40,32},{48,56},{56,48},{1,9},... | collective-permute-start | bytes 172040 | tf_op jit(solution)/shard_map/ppermute | solution.py:522
  8.8 0.0 collective-permute-done.2.z_a
  8.8 2.0 %collective-permute-start.3 = (f32[8,128]{1,0:T(8,128)S(1)}, f32[8,128]{1,0:T(8,128)S(1)}, u32[]{:S(2)}, u32[]{:S(2)}) collective-permute-start(f32[8,128]{1,0:T(8,128)S(1)} %get-tuple-element.23), channel_id=1, source_target_pairs={{0,64},{1,2},{2,1},{3,4},{4,3},{5,6},{6,5},{7,71},{8,72},{9,10},{1... | collective-permute-start | bytes 12296 | tf_op jit(solution)/shard_map/ppermute | solution.py:532
  10.8 0.6 %own_cells.1.local = f32[4,7,7,8,128]{4,3,2,1,0:T(8,128)S(1)} custom-call(f32[4,7,7,8,128]{4,3,2,1,0:T(8,128)S(1)} %get-tuple-element.19.first), custom_call_target="tpu_custom_call" | custom-call | flops 1400000000 | bytes 1605632 | tf_op jit(solution)/shard_map/own_cells/pallas_call | solution.py:509
  11.4 0.7 %collective-permute-done.3.z_b = f32[8,128]{1,0:T(8,128)S(1)} collective-permute-done((f32[8,128]{1,0:T(8,128)S(1)}, f32[8,128]{1,0:T(8,128)S(1)}, u32[]{:S(2)}, u32[]{:S(2)}) %collective-permute-start.3) | collective-permute-done | bytes 4128 | tf_op jit(solution)/shard_map/ppermute | solution.py:532
  12.1 0.0 collective-permute-done.y_b
  12.1 0.0 collective-permute-done.1.y_a
  12.1 0.4 %side_halo.1.local = f32[4,7,7,8,128]{4,3,2,1,0:T(8,128)S(1)} custom-call(f32[4,7,7,8,128]{4,3,2,1,0:T(8,128)S(1)} %own_cells.1.local, f32[14,8,128]{2,1,0:T(8,128)S(1)} %collective-permute-done.y_b, f32[14,8,128]{2,1,0:T(8,128)S(1)} %collective-permute-done.1.y_a, f32[8,128]{1,0:T(8,128)S(1)} %collective-permute-done.2.z_a, ...), custom_call_target="tpu_custom_call" | custom-call | flops 4000000 | bytes 2646016 | tf_op jit(solution)/shard_map/side_halo/pallas_call | solution.py:509
  12.5 0.0 collective-permute-done.4.x_a
  12.5 0.0 collective-permute-done.5.x_b
  12.5 0.4 %smooth_and_restrict.1 = (f32[4,7,7,8,128]{4,3,2,1,0:T(8,128)S(1)}, f32[2,8,128]{2,1,0:T(8,128)S(1)}, f32[2,8,128]{2,1,0:T(8,128)S(1)}, f32[2,8,128]{2,1,0:T(8,128)S(1)}, f32[2,8,128]{2,1,0:T(8,128)S(1)}) custom-call(f32[4,7,7,8,128]{4,3,2,1,0:T(8,128)S(1)} %get-tuple-element.19.first, f32[4,7,7,8,128]{4,3,2,1,0:T(8,128)S(1)} %side_halo.1.local, ...), custom_call_target="tpu_custom_call" | custom-call | flops 5000000 | bytes 2844672 | tf_op jit(solution)/shard_map/smooth_and_restrict/pallas_call | solution.py:509
  13.0 1.4 %collective-permute-start.6 = (f32[2,8,128]{2,1,0:T(8,128)S(1)}, f32[2,8,128]{2,1,0:T(8,128)S(1)}, u32[]{:S(2)}, u32[]{:S(2)}) collective-permute-start(f32[2,8,128]{2,1,0:T(8,128)S(1)} %get-tuple-element.33), channel_id=1, source_target_pairs={{0,128},{64,192},{128,0},{192,64},{1,129},{65,193},{129,1},{193,65... | collective-permute-start | bytes 24584 | tf_op jit(solution)/shard_map/ppermute | solution.py:522
  14.4 2.0 %collective-permute-start.7 = (f32[2,8,128]{2,1,0:T(8,128)S(1)}, f32[2,8,128]{2,1,0:T(8,128)S(1)}, u32[]{:S(2)}, u32[]{:S(2)}) collective-permute-start(f32[2,8,128]{2,1,0:T(8,128)S(1)} %get-tuple-element.34), channel_id=1, source_target_pairs={{0,64},{64,0},{128,192},{192,128},{1,65},{65,1},{129,193},{193,129... | collective-permute-start | bytes 24584 | tf_op jit(solution)/shard_map/ppermute | solution.py:522
  16.4 0.0 collective-permute-start.8
  16.4 0.7 %collective-permute-done.6 = f32[2,8,128]{2,1,0:T(8,128)S(1)} collective-permute-done((f32[2,8,128]{2,1,0:T(8,128)S(1)}, f32[2,8,128]{2,1,0:T(8,128)S(1)}, u32[]{:S(2)}, u32[]{:S(2)}) %collective-permute-start.6) | collective-permute-done | bytes 8224 | tf_op jit(solution)/shard_map/ppermute | solution.py:522
  17.1 0.5 %collective-permute-done.7 = f32[2,8,128]{2,1,0:T(8,128)S(1)} collective-permute-done((f32[2,8,128]{2,1,0:T(8,128)S(1)}, f32[2,8,128]{2,1,0:T(8,128)S(1)}, u32[]{:S(2)}, u32[]{:S(2)}) %collective-permute-start.7) | collective-permute-done | bytes 8224 | tf_op jit(solution)/shard_map/ppermute | solution.py:522
  17.5 1.4 %collective-permute-done.8 = f32[2,8,128]{2,1,0:T(8,128)S(1)} collective-permute-done((f32[2,8,128]{2,1,0:T(8,128)S(1)}, f32[2,8,128]{2,1,0:T(8,128)S(1)}, u32[]{:S(2)}, u32[]{:S(2)}) %collective-permute-start.8) | collective-permute-done | bytes 8224 | tf_op jit(solution)/shard_map/ppermute | solution.py:532
  19.0 2.8 %collective-permute-start.9 = (f32[2,8,128]{2,1,0:T(8,128)S(1)}, f32[2,8,128]{2,1,0:T(8,128)S(1)}, u32[]{:S(2)}, u32[]{:S(2)}) collective-permute-start(f32[2,8,128]{2,1,0:T(8,128)S(1)} %multiply_add_fusion), channel_id=1, source_target_pairs={{0,1},{1,0},{2,3},{3,2},{4,5},{5,4},{6,7},{7,6},{8,9},{9,8},{10,11... | collective-permute-start | bytes 24584 | tf_op jit(solution)/shard_map/ppermute | solution.py:522
  21.8 0.8 %collective-permute-done.9 = f32[2,8,128]{2,1,0:T(8,128)S(1)} collective-permute-done((f32[2,8,128]{2,1,0:T(8,128)S(1)}, f32[2,8,128]{2,1,0:T(8,128)S(1)}, u32[]{:S(2)}, u32[]{:S(2)}) %collective-permute-start.9) | collective-permute-done | bytes 8224 | tf_op jit(solution)/shard_map/ppermute | solution.py:522
  22.6 0.0 collective-permute-start.10
  22.6 2.6 %collective-permute-done.10 = f32[2,2,8,128]{3,2,1,0:T(8,128)S(1)} collective-permute-done((f32[2,2,8,128]{3,2,1,0:T(8,128)S(1)}, f32[2,2,8,128]{3,2,1,0:T(8,128)S(1)}, u32[]{:S(2)}, u32[]{:S(2)}) %collective-permute-start.10) | collective-permute-done | bytes 16416 | tf_op jit(solution)/shard_map/ppermute | solution.py:532
  25.2 0.1 fusion.1
  25.3 1.5 %collective-permute-start.11 = (f32[2,8,128]{2,1,0:T(8,128)S(1)}, f32[2,8,128]{2,1,0:T(8,128)S(1)}, u32[]{:S(2)}, u32[]{:S(2)}) collective-permute-start(f32[2,8,128]{2,1,0:T(8,128)S(1)} %bitcast.9), channel_id=1, source_target_pairs={{0,1},{1,0},{2,3},{3,2},{4,5},{5,4},{6,7},{7,6},{8,9},{9,8},{10,11... | collective-permute-start | bytes 24584 | tf_op jit(solution)/shard_map/ppermute | solution.py:522
  26.8 0.8 %collective-permute-done.11 = f32[2,8,128]{2,1,0:T(8,128)S(1)} collective-permute-done((f32[2,8,128]{2,1,0:T(8,128)S(1)}, f32[2,8,128]{2,1,0:T(8,128)S(1)}, u32[]{:S(2)}, u32[]{:S(2)}) %collective-permute-start.11) | collective-permute-done | bytes 8224 | tf_op jit(solution)/shard_map/ppermute | solution.py:522
  27.6 2.3 %collective-permute-start.12 = (f32[2,8,128]{2,1,0:T(8,128)S(1)}, f32[2,8,128]{2,1,0:T(8,128)S(1)}, u32[]{:S(2)}, u32[]{:S(2)}) collective-permute-start(f32[2,8,128]{2,1,0:T(8,128)S(1)} %reverse_add_fusion.chip), channel_id=1, source_target_pairs={{0,2},{1,5},{2,0},{3,7},{4,6},{5,1},{6,4},{7,3},{8,10},{9,13},{10,... | collective-permute-start | bytes 24584 | tf_op jit(solution)/shard_map/ppermute | solution.py:532
  29.9 0.8 %collective-permute-start.14 = (f32[2,8,128]{2,1,0:T(8,128)S(1)}, f32[2,8,128]{2,1,0:T(8,128)S(1)}, u32[]{:S(2)}, u32[]{:S(2)}) collective-permute-start(f32[2,8,128]{2,1,0:T(8,128)S(1)} %reverse_add_fusion.chip), channel_id=1, source_target_pairs={{0,6},{1,7},{2,4},{3,5},{4,2},{5,3},{6,0},{7,1},{8,14},{9,15},{10,... | collective-permute-start | bytes 24584 | tf_op jit(solution)/shard_map/ppermute | solution.py:522
  30.7 0.9 %collective-permute-done.12.fetched = f32[2,8,128]{2,1,0:T(8,128)S(1)} collective-permute-done((f32[2,8,128]{2,1,0:T(8,128)S(1)}, f32[2,8,128]{2,1,0:T(8,128)S(1)}, u32[]{:S(2)}, u32[]{:S(2)}) %collective-permute-start.12) | collective-permute-done | bytes 8224 | tf_op jit(solution)/shard_map/ppermute | solution.py:532
  31.6 0.0 collective-permute-start.13
  31.6 0.9 %unpack_modes.1 = f32[7,7,7,1,4,128]{5,4,3,2,1,0:T(4,128)} custom-call(f32[4,7,7,8,128]{4,3,2,1,0:T(8,128)S(1)} %get-tuple-element.31.field), custom_call_target="tpu_custom_call" | custom-call | flops 200000 | bytes 1505280 | tf_op jit(solution)/shard_map/unpack_modes/pallas_call | solution.py:509
  32.5 1.1 %collective-permute-done.14.third = f32[2,8,128]{2,1,0:T(8,128)S(1)} collective-permute-done((f32[2,8,128]{2,1,0:T(8,128)S(1)}, f32[2,8,128]{2,1,0:T(8,128)S(1)}, u32[]{:S(2)}, u32[]{:S(2)}) %collective-permute-start.14) | collective-permute-done | bytes 8224 | tf_op jit(solution)/shard_map/ppermute | solution.py:522
  33.6 0.0 collective-permute-done.13.mated
  33.6 0.6 %column.1 = f32[1,4,1024]{2,1,0:T(4,128)} custom-call(f32[2,8,128]{2,1,0:T(8,128)S(1)} %reverse_add_fusion.chip, f32[2,8,128]{2,1,0:T(8,128)S(1)} %collective-permute-done.12.fetched, f32[2,8,128]{2,1,0:T(8,128)S(1)} %collective-permute-done.13.mated, f32[2,8,128]{2,1,0:T(8,128)S(1)} %collective-permute-done.14.third), custom_call_target="tpu_custom_call" | custom-call | flops 20000 | bytes 49152 | tf_op jit(solution)/shard_map/column/pallas_call | solution.py:509
  (5 shorter events, 0.0 us)
Async XLA Ops:
  2.0 10.6 %collective-permute-start.4 = (f32[49,8,128]{2,1,0:T(8,128)S(1)}, f32[49,8,128]{2,1,0:T(8,128)S(1)}, u32[]{:S(2)}, u32[]{:S(2)}) collective-permute-start(f32[49,8,128]{2,1,0:T(8,128)S(1)} %get-tuple-element.29), channel_id=1, source_target_pairs={{0,64},{1,9},{2,66},{3,11},{4,68},{5,13},{6,70},{7,15},{8,72},{9,1... | collective-permute-start | bytes 602120 | tf_op jit(solution)/shard_map/ppermute | solution.py:532
  2.3 10.2 %collective-permute-start.5 = (f32[49,8,128]{2,1,0:T(8,128)S(1)}, f32[49,8,128]{2,1,0:T(8,128)S(1)}, u32[]{:S(2)}, u32[]{:S(2)}) collective-permute-start(f32[49,8,128]{2,1,0:T(8,128)S(1)} %get-tuple-element.30), channel_id=1, source_target_pairs={{0,8},{1,65},{2,10},{3,67},{4,12},{5,69},{6,14},{7,71},{8,0},{9,73... | collective-permute-start | bytes 602120 | tf_op jit(solution)/shard_map/ppermute | solution.py:532
  4.9 3.9 %collective-permute-start.2 = (f32[8,128]{1,0:T(8,128)S(1)}, f32[8,128]{1,0:T(8,128)S(1)}, u32[]{:S(2)}, u32[]{:S(2)}) collective-permute-start(f32[8,128]{1,0:T(8,128)S(1)} %get-tuple-element.22), channel_id=1, source_target_pairs={{0,1},{1,0},{2,3},{3,2},{4,5},{5,4},{6,7},{7,6},{8,9},{9,8},{10,11... | collective-permute-start | bytes 12296 | tf_op jit(solution)/shard_map/ppermute | solution.py:522
  5.0 7.1 %collective-permute-start = (f32[14,8,128]{2,1,0:T(8,128)S(1)}, f32[14,8,128]{2,1,0:T(8,128)S(1)}, u32[]{:S(2)}, u32[]{:S(2)}) collective-permute-start(f32[14,8,128]{2,1,0:T(8,128)S(1)} %get-tuple-element.20), channel_id=1, source_target_pairs={{0,1},{1,0},{2,3},{3,2},{4,5},{5,4},{6,7},{7,6},{8,16},{9,17},{10,... | collective-permute-start | bytes 172040 | tf_op jit(solution)/shard_map/ppermute | solution.py:532
  5.1 7.0 %collective-permute-start.1 = (f32[14,8,128]{2,1,0:T(8,128)S(1)}, f32[14,8,128]{2,1,0:T(8,128)S(1)}, u32[]{:S(2)}, u32[]{:S(2)}) collective-permute-start(f32[14,8,128]{2,1,0:T(8,128)S(1)} %get-tuple-element.21), channel_id=1, source_target_pairs={{0,8},{8,0},{16,24},{24,16},{32,40},{40,32},{48,56},{56,48},{1,9},... | collective-permute-start | bytes 172040 | tf_op jit(solution)/shard_map/ppermute | solution.py:522
  8.8 3.3 %collective-permute-start.3 = (f32[8,128]{1,0:T(8,128)S(1)}, f32[8,128]{1,0:T(8,128)S(1)}, u32[]{:S(2)}, u32[]{:S(2)}) collective-permute-start(f32[8,128]{1,0:T(8,128)S(1)} %get-tuple-element.23), channel_id=1, source_target_pairs={{0,64},{1,2},{2,1},{3,4},{4,3},{5,6},{6,5},{7,71},{8,72},{9,10},{1... | collective-permute-start | bytes 12296 | tf_op jit(solution)/shard_map/ppermute | solution.py:532
  13.0 4.1 %collective-permute-start.6 = (f32[2,8,128]{2,1,0:T(8,128)S(1)}, f32[2,8,128]{2,1,0:T(8,128)S(1)}, u32[]{:S(2)}, u32[]{:S(2)}) collective-permute-start(f32[2,8,128]{2,1,0:T(8,128)S(1)} %get-tuple-element.33), channel_id=1, source_target_pairs={{0,128},{64,192},{128,0},{192,64},{1,129},{65,193},{129,1},{193,65... | collective-permute-start | bytes 24584 | tf_op jit(solution)/shard_map/ppermute | solution.py:522
  14.4 3.1 %collective-permute-start.7 = (f32[2,8,128]{2,1,0:T(8,128)S(1)}, f32[2,8,128]{2,1,0:T(8,128)S(1)}, u32[]{:S(2)}, u32[]{:S(2)}) collective-permute-start(f32[2,8,128]{2,1,0:T(8,128)S(1)} %get-tuple-element.34), channel_id=1, source_target_pairs={{0,64},{64,0},{128,192},{192,128},{1,65},{65,1},{129,193},{193,129... | collective-permute-start | bytes 24584 | tf_op jit(solution)/shard_map/ppermute | solution.py:522
  16.4 2.6 %collective-permute-start.8 = (f32[2,8,128]{2,1,0:T(8,128)S(1)}, f32[2,8,128]{2,1,0:T(8,128)S(1)}, u32[]{:S(2)}, u32[]{:S(2)}) collective-permute-start(f32[2,8,128]{2,1,0:T(8,128)S(1)} %get-tuple-element.35), channel_id=1, source_target_pairs={{0,1},{1,0},{2,3},{3,2},{4,5},{5,4},{6,7},{7,6},{8,9},{9,8},{10,11... | collective-permute-start | bytes 24584 | tf_op jit(solution)/shard_map/ppermute | solution.py:532
  19.0 3.6 %collective-permute-start.9 = (f32[2,8,128]{2,1,0:T(8,128)S(1)}, f32[2,8,128]{2,1,0:T(8,128)S(1)}, u32[]{:S(2)}, u32[]{:S(2)}) collective-permute-start(f32[2,8,128]{2,1,0:T(8,128)S(1)} %multiply_add_fusion), channel_id=1, source_target_pairs={{0,1},{1,0},{2,3},{3,2},{4,5},{5,4},{6,7},{7,6},{8,9},{9,8},{10,11... | collective-permute-start | bytes 24584 | tf_op jit(solution)/shard_map/ppermute | solution.py:522
  22.6 2.6 %collective-permute-start.10 = (f32[2,2,8,128]{3,2,1,0:T(8,128)S(1)}, f32[2,2,8,128]{3,2,1,0:T(8,128)S(1)}, u32[]{:S(2)}, u32[]{:S(2)}) collective-permute-start(f32[2,2,8,128]{3,2,1,0:T(8,128)S(1)} %pad_maximum_fusion), channel_id=1, source_target_pairs={{0,8},{1,65},{2,10},{3,67},{4,12},{5,69},{6,14},{7,71},{8,0},{9,17... | collective-permute-start | bytes 49160 | tf_op jit(solution)/shard_map/ppermute | solution.py:532
  25.3 2.3 %collective-permute-start.11 = (f32[2,8,128]{2,1,0:T(8,128)S(1)}, f32[2,8,128]{2,1,0:T(8,128)S(1)}, u32[]{:S(2)}, u32[]{:S(2)}) collective-permute-start(f32[2,8,128]{2,1,0:T(8,128)S(1)} %bitcast.9), channel_id=1, source_target_pairs={{0,1},{1,0},{2,3},{3,2},{4,5},{5,4},{6,7},{7,6},{8,9},{9,8},{10,11... | collective-permute-start | bytes 24584 | tf_op jit(solution)/shard_map/ppermute | solution.py:522
  27.6 4.0 %collective-permute-start.12 = (f32[2,8,128]{2,1,0:T(8,128)S(1)}, f32[2,8,128]{2,1,0:T(8,128)S(1)}, u32[]{:S(2)}, u32[]{:S(2)}) collective-permute-start(f32[2,8,128]{2,1,0:T(8,128)S(1)} %reverse_add_fusion.chip), channel_id=1, source_target_pairs={{0,2},{1,5},{2,0},{3,7},{4,6},{5,1},{6,4},{7,3},{8,10},{9,13},{10,... | collective-permute-start | bytes 24584 | tf_op jit(solution)/shard_map/ppermute | solution.py:532
  29.9 3.7 %collective-permute-start.14 = (f32[2,8,128]{2,1,0:T(8,128)S(1)}, f32[2,8,128]{2,1,0:T(8,128)S(1)}, u32[]{:S(2)}, u32[]{:S(2)}) collective-permute-start(f32[2,8,128]{2,1,0:T(8,128)S(1)} %reverse_add_fusion.chip), channel_id=1, source_target_pairs={{0,6},{1,7},{2,4},{3,5},{4,2},{5,3},{6,0},{7,1},{8,14},{9,15},{10,... | collective-permute-start | bytes 24584 | tf_op jit(solution)/shard_map/ppermute | solution.py:522
  31.6 2.0 %collective-permute-start.13 = (f32[2,8,128]{2,1,0:T(8,128)S(1)}, f32[2,8,128]{2,1,0:T(8,128)S(1)}, u32[]{:S(2)}, u32[]{:S(2)}) collective-permute-start(f32[2,8,128]{2,1,0:T(8,128)S(1)} %collective-permute-done.12.fetched), channel_id=1, source_target_pairs={{0,1},{1,0},{2,3},{3,2},{4,5},{5,4},{6,7},{7,6},{8,9},{9,8},{10,11... | collective-permute-start | bytes 24584 | tf_op jit(solution)/shard_map/ppermute | solution.py:522

commit v8 on v7

--- a/solution.py
+++ b/solution.py
@@ -305,7 +305,7 @@
 
 
 def side_kernel(
-    local, y_b, y_a, z_a, z_b, y_below, y_above, z_below, z_above, out
+    local, y_a, y_b, z_a, z_b, y_below, y_above, z_below, z_above, out
 ):
     row, lane = row_in_half(), lanes()
     y_even, z_even = goes_up(lax.axis_index("gy")), goes_up(lax.axis_index("gz"))
@@ -454,7 +454,8 @@
         far[z] = jnp.where(top, swap(outer[0][z]), outer[1][z])
 
 
-def unpack_kernel(field, smoothed):
+def unpack_kernel(field, here, smoothed, here_again):
+    here_again[...] = here[...]
     for b in range(MODES):
         for e in range(MODES):
             for i in range(PAIRS):
@@ -605,14 +606,13 @@
         (shape(FACE_ROWS, 8, 128),) * 2 + (shape(8, 128),) * 2 + sides,
         SIDE_COST,
     )
-    y_b = second_pairs(y_b, "gy")
-    y_a = flip(y_a, "gy", 1)
+    y_a, y_b = flip(y_a, "gy", 1), second_pairs(y_b, "gy")
     z_a, z_b = flip(z_a, "gz", 1), second_pairs(z_b, "gz")
     (local,) = call(own_kernel, "own_cells", (first,), (shape(*cells),), OWN_COST)
     (local,) = call(
         side_kernel,
         "side_halo",
-        (local, y_b, y_a, z_a, z_b, y_high, y_low, z_high, z_low),
+        (local, y_a, y_b, z_a, z_b, y_high, y_low, z_high, z_low),
         (shape(*cells),),
         HALO_COST,
     )
@@ -623,7 +623,13 @@
         (shape(*cells),) + (shape(2, 8, 128),) * 4,
         5_000_000,
     )
-    (smoothed,) = call(unpack_kernel, "unpack_modes", (field,), (shape(*rhs.shape),), 200_000)
+    smoothed, here = call(
+        unpack_kernel,
+        "unpack_modes",
+        (field, here),
+        (shape(*rhs.shape), shape(2, 8, 128)),
+        200_000,
+    )
     from_far = flip(far, "gx", 2)
     from_a = flip(sum_a, "gx", 1)
     from_b = second_pairs(sum_b, "gx")

time: 34.4 us -> 33.5 us (0.974)
  the two profiles are of different devices: /device:TPU:69 before, /device:TPU:101 now
where the time goes in v8:
time: 33.5 us; the launch traced here: 33.4 us
  starting transfers between devices  18.8 us (56%)
  waiting for transfers between devices  9.28 us (28%)
  Pallas kernels  4.57 us (14%)
  between operations  0.69 us (2%)
    ppermute x7, starting transfers between devices, exchange(): return lax.ppermute(value, axes, route)  9.94 us
    ppermute x8, starting transfers between devices, flip(): lax.ppermute(value, axis, [(i, i ^ bits) for i in range(lax.axis_size(axi...  8.85 us
    ppermute x7, waiting for transfers between devices, exchange(): return lax.ppermute(value, axes, route)  5.34 us
    pallas_call x7, Pallas kernels, call(): pl.pallas_call(kernel, out_shape=outputs, in_specs=[pl.BlockSpec(memory_s...  4.57 us
    ppermute x8, waiting for transfers between devices, flip(): lax.ppermute(value, axis, [(i, i ^ bits) for i in range(lax.axis_size(axi...  3.94 us
  transfers between devices with their start and end apart: 15, of which 8 were waited for; matrix products, arithmetic and copies ran while one was open for 0% of the time, Pallas kernels for 7%

profile of v8, /device:TPU:101, one launch (start us, length us, event | category | flops | bytes accessed | tf_op | source)
XLA Modules:
  0.0 33.4 jit_solution(1007027107958939451)
XLA Ops:
  0.6 1.3 %x_traces.1 = (f32[4,7,7,8,128]{4,3,2,1,0:T(8,128)S(1)}, f32[49,8,128]{2,1,0:T(8,128)S(1)}, f32[49,8,128]{2,1,0:T(8,128)S(1)}, s32[1,4,128]{2,1,0:T(4,128)S(1)}) custom-call(f32[7,7,7,1,4,128]{5,4,3,2,1,0:T(4,128)} %rhs_hbm.1, s32[1,4,128]{2,1,0:T(4,128)} %orders_hbm.1), custom_call_target="tpu_custom_call" | custom-call | flops 4000000 | bytes 1910784 | tf_op jit(solution)/shard_map/x_traces/pallas_call | solution.py:510
  2.0 0.3 %collective-permute-start.4 = (f32[49,8,128]{2,1,0:T(8,128)S(1)}, f32[49,8,128]{2,1,0:T(8,128)S(1)}, u32[]{:S(2)}, u32[]{:S(2)}) collective-permute-start(f32[49,8,128]{2,1,0:T(8,128)S(1)} %get-tuple-element.31), channel_id=1, source_target_pairs={{0,64},{1,9},{2,66},{3,11},{4,68},{5,13},{6,70},{7,15},{8,72},{9,1... | collective-permute-start | bytes 602120 | tf_op jit(solution)/shard_map/ppermute | solution.py:533
  2.3 0.8 %collective-permute-start.5 = (f32[49,8,128]{2,1,0:T(8,128)S(1)}, f32[49,8,128]{2,1,0:T(8,128)S(1)}, u32[]{:S(2)}, u32[]{:S(2)}) collective-permute-start(f32[49,8,128]{2,1,0:T(8,128)S(1)} %get-tuple-element.32), channel_id=1, source_target_pairs={{0,8},{1,65},{2,10},{3,67},{4,12},{5,69},{6,14},{7,71},{8,0},{9,73... | collective-permute-start | bytes 602120 | tf_op jit(solution)/shard_map/ppermute | solution.py:533
  3.1 0.3 side_traces.1
  3.3 0.9 %collective-permute-start.2 = (f32[8,128]{1,0:T(8,128)S(1)}, f32[8,128]{1,0:T(8,128)S(1)}, u32[]{:S(2)}, u32[]{:S(2)}) collective-permute-start(f32[8,128]{1,0:T(8,128)S(1)} %get-tuple-element.24), channel_id=1, source_target_pairs={{0,1},{1,0},{2,3},{3,2},{4,5},{5,4},{6,7},{7,6},{8,9},{9,8},{10,11... | collective-permute-start | bytes 12296 | tf_op jit(solution)/shard_map/ppermute | solution.py:523
  4.3 0.6 %collective-permute-start = (f32[14,8,128]{2,1,0:T(8,128)S(1)}, f32[14,8,128]{2,1,0:T(8,128)S(1)}, u32[]{:S(2)}, u32[]{:S(2)}) collective-permute-start(f32[14,8,128]{2,1,0:T(8,128)S(1)} %get-tuple-element.22), channel_id=1, source_target_pairs={{0,8},{8,0},{16,24},{24,16},{32,40},{40,32},{48,56},{56,48},{1,9},... | collective-permute-start | bytes 172040 | tf_op jit(solution)/shard_map/ppermute | solution.py:523
  4.9 3.0 %collective-permute-start.1 = (f32[14,8,128]{2,1,0:T(8,128)S(1)}, f32[14,8,128]{2,1,0:T(8,128)S(1)}, u32[]{:S(2)}, u32[]{:S(2)}) collective-permute-start(f32[14,8,128]{2,1,0:T(8,128)S(1)} %get-tuple-element.23), channel_id=1, source_target_pairs={{0,1},{1,0},{2,3},{3,2},{4,5},{5,4},{6,7},{7,6},{8,16},{9,17},{10,... | collective-permute-start | bytes 172040 | tf_op jit(solution)/shard_map/ppermute | solution.py:533
  7.9 0.0 collective-permute-done.2.z_a
  7.9 2.0 %collective-permute-start.3 = (f32[8,128]{1,0:T(8,128)S(1)}, f32[8,128]{1,0:T(8,128)S(1)}, u32[]{:S(2)}, u32[]{:S(2)}) collective-permute-start(f32[8,128]{1,0:T(8,128)S(1)} %get-tuple-element.25), channel_id=1, source_target_pairs={{0,64},{1,2},{2,1},{3,4},{4,3},{5,6},{6,5},{7,71},{8,72},{9,10},{1... | collective-permute-start | bytes 12296 | tf_op jit(solution)/shard_map/ppermute | solution.py:533
  9.9 0.6 %own_cells.1.local = f32[4,7,7,8,128]{4,3,2,1,0:T(8,128)S(1)} custom-call(f32[4,7,7,8,128]{4,3,2,1,0:T(8,128)S(1)} %get-tuple-element.21.first), custom_call_target="tpu_custom_call" | custom-call | flops 1400000000 | bytes 1605632 | tf_op jit(solution)/shard_map/own_cells/pallas_call | solution.py:510
  10.5 0.7 %collective-permute-done.3.z_b = f32[8,128]{1,0:T(8,128)S(1)} collective-permute-done((f32[8,128]{1,0:T(8,128)S(1)}, f32[8,128]{1,0:T(8,128)S(1)}, u32[]{:S(2)}, u32[]{:S(2)}) %collective-permute-start.3) | collective-permute-done | bytes 4128 | tf_op jit(solution)/shard_map/ppermute | solution.py:533
  11.2 0.0 collective-permute-done.y_a
  11.2 0.0 collective-permute-done.1.y_b
  11.2 0.4 %side_halo.1.local = f32[4,7,7,8,128]{4,3,2,1,0:T(8,128)S(1)} custom-call(f32[4,7,7,8,128]{4,3,2,1,0:T(8,128)S(1)} %own_cells.1.local, f32[14,8,128]{2,1,0:T(8,128)S(1)} %collective-permute-done.y_a, f32[14,8,128]{2,1,0:T(8,128)S(1)} %collective-permute-done.1.y_b, f32[8,128]{1,0:T(8,128)S(1)} %collective-permute-done.2.z_a, ...), custom_call_target="tpu_custom_call" | custom-call | flops 4000000 | bytes 2646016 | tf_op jit(solution)/shard_map/side_halo/pallas_call | solution.py:510
  11.6 0.0 collective-permute-done.4.x_a
  11.6 0.0 collective-permute-done.5.x_b
  11.6 0.4 %smooth_and_restrict.1 = (f32[4,7,7,8,128]{4,3,2,1,0:T(8,128)S(1)}, f32[2,8,128]{2,1,0:T(8,128)S(1)}, f32[2,8,128]{2,1,0:T(8,128)S(1)}, f32[2,8,128]{2,1,0:T(8,128)S(1)}, f32[2,8,128]{2,1,0:T(8,128)S(1)}) custom-call(f32[4,7,7,8,128]{4,3,2,1,0:T(8,128)S(1)} %get-tuple-element.21.first, f32[4,7,7,8,128]{4,3,2,1,0:T(8,128)S(1)} %side_halo.1.local, ...), custom_call_target="tpu_custom_call" | custom-call | flops 5000000 | bytes 2844672 | tf_op jit(solution)/shard_map/smooth_and_restrict/pallas_call | solution.py:510
  12.1 1.4 %collective-permute-start.6 = (f32[2,8,128]{2,1,0:T(8,128)S(1)}, f32[2,8,128]{2,1,0:T(8,128)S(1)}, u32[]{:S(2)}, u32[]{:S(2)}) collective-permute-start(f32[2,8,128]{2,1,0:T(8,128)S(1)} %get-tuple-element.37), channel_id=1, source_target_pairs={{0,128},{64,192},{128,0},{192,64},{1,129},{65,193},{129,1},{193,65... | collective-permute-start | bytes 24584 | tf_op jit(solution)/shard_map/ppermute | solution.py:523
  13.5 2.0 %collective-permute-start.7 = (f32[2,8,128]{2,1,0:T(8,128)S(1)}, f32[2,8,128]{2,1,0:T(8,128)S(1)}, u32[]{:S(2)}, u32[]{:S(2)}) collective-permute-start(f32[2,8,128]{2,1,0:T(8,128)S(1)} %get-tuple-element.38), channel_id=1, source_target_pairs={{0,64},{64,0},{128,192},{192,128},{1,65},{65,1},{129,193},{193,129... | collective-permute-start | bytes 24584 | tf_op jit(solution)/shard_map/ppermute | solution.py:523
  15.5 0.0 collective-permute-start.8
  15.5 0.9 %unpack_modes.1 = (f32[7,7,7,1,4,128]{5,4,3,2,1,0:T(4,128)}, f32[2,8,128]{2,1,0:T(8,128)S(1)}) custom-call(f32[4,7,7,8,128]{4,3,2,1,0:T(8,128)S(1)} %get-tuple-element.33.field, f32[2,8,128]{2,1,0:T(8,128)S(1)} %get-tuple-element.34.here), custom_call_target="tpu_custom_call" | custom-call | flops 200000 | bytes 1521664 | tf_op jit(solution)/shard_map/unpack_modes/pallas_call | solution.py:510
  16.5 0.0 collective-permute-done.6
  16.5 0.2 collective-permute-done.7
  16.6 1.4 %collective-permute-done.8 = f32[2,8,128]{2,1,0:T(8,128)S(1)} collective-permute-done((f32[2,8,128]{2,1,0:T(8,128)S(1)}, f32[2,8,128]{2,1,0:T(8,128)S(1)}, u32[]{:S(2)}, u32[]{:S(2)}) %collective-permute-start.8) | collective-permute-done | bytes 8224 | tf_op jit(solution)/shard_map/ppermute | solution.py:533
  18.1 2.8 %collective-permute-start.9 = (f32[2,8,128]{2,1,0:T(8,128)S(1)}, f32[2,8,128]{2,1,0:T(8,128)S(1)}, u32[]{:S(2)}, u32[]{:S(2)}) collective-permute-start(f32[2,8,128]{2,1,0:T(8,128)S(1)} %multiply_add_fusion), channel_id=1, source_target_pairs={{0,1},{1,0},{2,3},{3,2},{4,5},{5,4},{6,7},{7,6},{8,9},{9,8},{10,11... | collective-permute-start | bytes 24584 | tf_op jit(solution)/shard_map/ppermute | solution.py:523
  20.9 0.8 %collective-permute-done.9 = f32[2,8,128]{2,1,0:T(8,128)S(1)} collective-permute-done((f32[2,8,128]{2,1,0:T(8,128)S(1)}, f32[2,8,128]{2,1,0:T(8,128)S(1)}, u32[]{:S(2)}, u32[]{:S(2)}) %collective-permute-start.9) | collective-permute-done | bytes 8224 | tf_op jit(solution)/shard_map/ppermute | solution.py:523
  21.7 1.5 %collective-permute-start.10 = (f32[2,2,8,128]{3,2,1,0:T(8,128)S(1)}, f32[2,2,8,128]{3,2,1,0:T(8,128)S(1)}, u32[]{:S(2)}, u32[]{:S(2)}) collective-permute-start(f32[2,2,8,128]{3,2,1,0:T(8,128)S(1)} %pad_maximum_fusion), channel_id=1, source_target_pairs={{0,8},{1,65},{2,10},{3,67},{4,12},{5,69},{6,14},{7,71},{8,0},{9,17... | collective-permute-start | bytes 49160 | tf_op jit(solution)/shard_map/ppermute | solution.py:533
  23.2 2.3 %collective-permute-done.10 = f32[2,2,8,128]{3,2,1,0:T(8,128)S(1)} collective-permute-done((f32[2,2,8,128]{3,2,1,0:T(8,128)S(1)}, f32[2,2,8,128]{3,2,1,0:T(8,128)S(1)}, u32[]{:S(2)}, u32[]{:S(2)}) %collective-permute-start.10) | collective-permute-done | bytes 16416 | tf_op jit(solution)/shard_map/ppermute | solution.py:533
  25.5 0.1 fusion.1
  25.6 0.3 collective-permute-start.11
  25.9 0.9 %collective-permute-done.11 = f32[2,8,128]{2,1,0:T(8,128)S(1)} collective-permute-done((f32[2,8,128]{2,1,0:T(8,128)S(1)}, f32[2,8,128]{2,1,0:T(8,128)S(1)}, u32[]{:S(2)}, u32[]{:S(2)}) %collective-permute-start.11) | collective-permute-done | bytes 8224 | tf_op jit(solution)/shard_map/ppermute | solution.py:523
  26.7 2.3 %collective-permute-start.12 = (f32[2,8,128]{2,1,0:T(8,128)S(1)}, f32[2,8,128]{2,1,0:T(8,128)S(1)}, u32[]{:S(2)}, u32[]{:S(2)}) collective-permute-start(f32[2,8,128]{2,1,0:T(8,128)S(1)} %reverse_add_fusion.chip), channel_id=1, source_target_pairs={{0,2},{1,5},{2,0},{3,7},{4,6},{5,1},{6,4},{7,3},{8,10},{9,13},{10,... | collective-permute-start | bytes 24584 | tf_op jit(solution)/shard_map/ppermute | solution.py:533
  29.1 0.8 %collective-permute-start.14 = (f32[2,8,128]{2,1,0:T(8,128)S(1)}, f32[2,8,128]{2,1,0:T(8,128)S(1)}, u32[]{:S(2)}, u32[]{:S(2)}) collective-permute-start(f32[2,8,128]{2,1,0:T(8,128)S(1)} %reverse_add_fusion.chip), channel_id=1, source_target_pairs={{0,6},{1,7},{2,4},{3,5},{4,2},{5,3},{6,0},{7,1},{8,14},{9,15},{10,... | collective-permute-start | bytes 24584 | tf_op jit(solution)/shard_map/ppermute | solution.py:523
  29.9 0.9 %collective-permute-done.12.fetched = f32[2,8,128]{2,1,0:T(8,128)S(1)} collective-permute-done((f32[2,8,128]{2,1,0:T(8,128)S(1)}, f32[2,8,128]{2,1,0:T(8,128)S(1)}, u32[]{:S(2)}, u32[]{:S(2)}) %collective-permute-start.12) | collective-permute-done | bytes 8224 | tf_op jit(solution)/shard_map/ppermute | solution.py:533
  30.7 0.0 collective-permute-start.13
  30.8 2.0 %collective-permute-done.14.third = f32[2,8,128]{2,1,0:T(8,128)S(1)} collective-permute-done((f32[2,8,128]{2,1,0:T(8,128)S(1)}, f32[2,8,128]{2,1,0:T(8,128)S(1)}, u32[]{:S(2)}, u32[]{:S(2)}) %collective-permute-start.14) | collective-permute-done | bytes 8224 | tf_op jit(solution)/shard_map/ppermute | solution.py:523
  32.8 0.0 collective-permute-done.13.mated
  32.8 0.6 %column.1 = f32[1,4,1024]{2,1,0:T(4,128)} custom-call(f32[2,8,128]{2,1,0:T(8,128)S(1)} %reverse_add_fusion.chip, f32[2,8,128]{2,1,0:T(8,128)S(1)} %collective-permute-done.12.fetched, f32[2,8,128]{2,1,0:T(8,128)S(1)} %collective-permute-done.13.mated, f32[2,8,128]{2,1,0:T(8,128)S(1)} %collective-permute-done.14.third), custom_call_target="tpu_custom_call" | custom-call | flops 20000 | bytes 49152 | tf_op jit(solution)/shard_map/column/pallas_call | solution.py:510
  (5 shorter events, 0.0 us)
Async XLA Ops:
  2.0 9.6 %collective-permute-start.4 = (f32[49,8,128]{2,1,0:T(8,128)S(1)}, f32[49,8,128]{2,1,0:T(8,128)S(1)}, u32[]{:S(2)}, u32[]{:S(2)}) collective-permute-start(f32[49,8,128]{2,1,0:T(8,128)S(1)} %get-tuple-element.31), channel_id=1, source_target_pairs={{0,64},{1,9},{2,66},{3,11},{4,68},{5,13},{6,70},{7,15},{8,72},{9,1... | collective-permute-start | bytes 602120 | tf_op jit(solution)/shard_map/ppermute | solution.py:533
  2.3 9.3 %collective-permute-start.5 = (f32[49,8,128]{2,1,0:T(8,128)S(1)}, f32[49,8,128]{2,1,0:T(8,128)S(1)}, u32[]{:S(2)}, u32[]{:S(2)}) collective-permute-start(f32[49,8,128]{2,1,0:T(8,128)S(1)} %get-tuple-element.32), channel_id=1, source_target_pairs={{0,8},{1,65},{2,10},{3,67},{4,12},{5,69},{6,14},{7,71},{8,0},{9,73... | collective-permute-start | bytes 602120 | tf_op jit(solution)/shard_map/ppermute | solution.py:533
  3.3 4.5 %collective-permute-start.2 = (f32[8,128]{1,0:T(8,128)S(1)}, f32[8,128]{1,0:T(8,128)S(1)}, u32[]{:S(2)}, u32[]{:S(2)}) collective-permute-start(f32[8,128]{1,0:T(8,128)S(1)} %get-tuple-element.24), channel_id=1, source_target_pairs={{0,1},{1,0},{2,3},{3,2},{4,5},{5,4},{6,7},{7,6},{8,9},{9,8},{10,11... | collective-permute-start | bytes 12296 | tf_op jit(solution)/shard_map/ppermute | solution.py:523
  4.3 6.9 %collective-permute-start = (f32[14,8,128]{2,1,0:T(8,128)S(1)}, f32[14,8,128]{2,1,0:T(8,128)S(1)}, u32[]{:S(2)}, u32[]{:S(2)}) collective-permute-start(f32[14,8,128]{2,1,0:T(8,128)S(1)} %get-tuple-element.22), channel_id=1, source_target_pairs={{0,8},{8,0},{16,24},{24,16},{32,40},{40,32},{48,56},{56,48},{1,9},... | collective-permute-start | bytes 172040 | tf_op jit(solution)/shard_map/ppermute | solution.py:523
  4.9 6.3 %collective-permute-start.1 = (f32[14,8,128]{2,1,0:T(8,128)S(1)}, f32[14,8,128]{2,1,0:T(8,128)S(1)}, u32[]{:S(2)}, u32[]{:S(2)}) collective-permute-start(f32[14,8,128]{2,1,0:T(8,128)S(1)} %get-tuple-element.23), channel_id=1, source_target_pairs={{0,1},{1,0},{2,3},{3,2},{4,5},{5,4},{6,7},{7,6},{8,16},{9,17},{10,... | collective-permute-start | bytes 172040 | tf_op jit(solution)/shard_map/ppermute | solution.py:533
  7.9 3.3 %collective-permute-start.3 = (f32[8,128]{1,0:T(8,128)S(1)}, f32[8,128]{1,0:T(8,128)S(1)}, u32[]{:S(2)}, u32[]{:S(2)}) collective-permute-start(f32[8,128]{1,0:T(8,128)S(1)} %get-tuple-element.25), channel_id=1, source_target_pairs={{0,64},{1,2},{2,1},{3,4},{4,3},{5,6},{6,5},{7,71},{8,72},{9,10},{1... | collective-permute-start | bytes 12296 | tf_op jit(solution)/shard_map/ppermute | solution.py:533
  12.1 4.4 %collective-permute-start.6 = (f32[2,8,128]{2,1,0:T(8,128)S(1)}, f32[2,8,128]{2,1,0:T(8,128)S(1)}, u32[]{:S(2)}, u32[]{:S(2)}) collective-permute-start(f32[2,8,128]{2,1,0:T(8,128)S(1)} %get-tuple-element.37), channel_id=1, source_target_pairs={{0,128},{64,192},{128,0},{192,64},{1,129},{65,193},{129,1},{193,65... | collective-permute-start | bytes 24584 | tf_op jit(solution)/shard_map/ppermute | solution.py:523
  13.5 3.1 %collective-permute-start.7 = (f32[2,8,128]{2,1,0:T(8,128)S(1)}, f32[2,8,128]{2,1,0:T(8,128)S(1)}, u32[]{:S(2)}, u32[]{:S(2)}) collective-permute-start(f32[2,8,128]{2,1,0:T(8,128)S(1)} %get-tuple-element.38), channel_id=1, source_target_pairs={{0,64},{64,0},{128,192},{192,128},{1,65},{65,1},{129,193},{193,129... | collective-permute-start | bytes 24584 | tf_op jit(solution)/shard_map/ppermute | solution.py:523
  15.5 2.5 %collective-permute-start.8 = (f32[2,8,128]{2,1,0:T(8,128)S(1)}, f32[2,8,128]{2,1,0:T(8,128)S(1)}, u32[]{:S(2)}, u32[]{:S(2)}) collective-permute-start(f32[2,8,128]{2,1,0:T(8,128)S(1)} %get-tuple-element.39), channel_id=1, source_target_pairs={{0,1},{1,0},{2,3},{3,2},{4,5},{5,4},{6,7},{7,6},{8,9},{9,8},{10,11... | collective-permute-start | bytes 24584 | tf_op jit(solution)/shard_map/ppermute | solution.py:533
  18.1 3.6 %collective-permute-start.9 = (f32[2,8,128]{2,1,0:T(8,128)S(1)}, f32[2,8,128]{2,1,0:T(8,128)S(1)}, u32[]{:S(2)}, u32[]{:S(2)}) collective-permute-start(f32[2,8,128]{2,1,0:T(8,128)S(1)} %multiply_add_fusion), channel_id=1, source_target_pairs={{0,1},{1,0},{2,3},{3,2},{4,5},{5,4},{6,7},{7,6},{8,9},{9,8},{10,11... | collective-permute-start | bytes 24584 | tf_op jit(solution)/shard_map/ppermute | solution.py:523
  21.7 3.8 %collective-permute-start.10 = (f32[2,2,8,128]{3,2,1,0:T(8,128)S(1)}, f32[2,2,8,128]{3,2,1,0:T(8,128)S(1)}, u32[]{:S(2)}, u32[]{:S(2)}) collective-permute-start(f32[2,2,8,128]{3,2,1,0:T(8,128)S(1)} %pad_maximum_fusion), channel_id=1, source_target_pairs={{0,8},{1,65},{2,10},{3,67},{4,12},{5,69},{6,14},{7,71},{8,0},{9,17... | collective-permute-start | bytes 49160 | tf_op jit(solution)/shard_map/ppermute | solution.py:533
  25.6 1.2 %collective-permute-start.11 = (f32[2,8,128]{2,1,0:T(8,128)S(1)}, f32[2,8,128]{2,1,0:T(8,128)S(1)}, u32[]{:S(2)}, u32[]{:S(2)}) collective-permute-start(f32[2,8,128]{2,1,0:T(8,128)S(1)} %bitcast.9), channel_id=1, source_target_pairs={{0,1},{1,0},{2,3},{3,2},{4,5},{5,4},{6,7},{7,6},{8,9},{9,8},{10,11... | collective-permute-start | bytes 24584 | tf_op jit(solution)/shard_map/ppermute | solution.py:523
  26.7 4.0 %collective-permute-start.12 = (f32[2,8,128]{2,1,0:T(8,128)S(1)}, f32[2,8,128]{2,1,0:T(8,128)S(1)}, u32[]{:S(2)}, u32[]{:S(2)}) collective-permute-start(f32[2,8,128]{2,1,0:T(8,128)S(1)} %reverse_add_fusion.chip), channel_id=1, source_target_pairs={{0,2},{1,5},{2,0},{3,7},{4,6},{5,1},{6,4},{7,3},{8,10},{9,13},{10,... | collective-permute-start | bytes 24584 | tf_op jit(solution)/shard_map/ppermute | solution.py:533
  29.1 3.7 %collective-permute-start.14 = (f32[2,8,128]{2,1,0:T(8,128)S(1)}, f32[2,8,128]{2,1,0:T(8,128)S(1)}, u32[]{:S(2)}, u32[]{:S(2)}) collective-permute-start(f32[2,8,128]{2,1,0:T(8,128)S(1)} %reverse_add_fusion.chip), channel_id=1, source_target_pairs={{0,6},{1,7},{2,4},{3,5},{4,2},{5,3},{6,0},{7,1},{8,14},{9,15},{10,... | collective-permute-start | bytes 24584 | tf_op jit(solution)/shard_map/ppermute | solution.py:523
  30.7 2.0 %collective-permute-start.13 = (f32[2,8,128]{2,1,0:T(8,128)S(1)}, f32[2,8,128]{2,1,0:T(8,128)S(1)}, u32[]{:S(2)}, u32[]{:S(2)}) collective-permute-start(f32[2,8,128]{2,1,0:T(8,128)S(1)} %collective-permute-done.12.fetched), channel_id=1, source_target_pairs={{0,1},{1,0},{2,3},{3,2},{4,5},{5,4},{6,7},{7,6},{8,9},{9,8},{10,11... | collective-permute-start | bytes 24584 | tf_op jit(solution)/shard_map/ppermute | solution.py:523

commit v9 on v8

--- a/solution.py
+++ b/solution.py
@@ -236,7 +236,8 @@
     z_b[...] = jnp.where(z_up, packed_down, packed_up)
 
 
-def own_kernel(first, out):
+def own_kernel(first, early, out, early_again):
+    early_again[...] = early[...]
     pairs = Pairs()
     for b in range(MODES):
         for e in range(MODES):
@@ -305,7 +306,7 @@
 
 
 def side_kernel(
-    local, y_a, y_b, z_a, z_b, y_below, y_above, z_below, z_above, out
+    local, y_a, y_b, z_b, z_a, y_below, y_above, z_below, z_above, out
 ):
     row, lane = row_in_half(), lanes()
     y_even, z_even = goes_up(lax.axis_index("gy")), goes_up(lax.axis_index("gz"))
@@ -607,12 +608,15 @@
         SIDE_COST,
     )
     y_a, y_b = flip(y_a, "gy", 1), second_pairs(y_b, "gy")
-    z_a, z_b = flip(z_a, "gz", 1), second_pairs(z_b, "gz")
-    (local,) = call(own_kernel, "own_cells", (first,), (shape(*cells),), OWN_COST)
+    z_b = second_pairs(z_b, "gz")
+    z_a = flip(z_a, "gz", 1)
+    local, y_a = call(
+        own_kernel, "own_cells", (first, y_a), (shape(*cells), shape(FACE_ROWS, 8, 128)), OWN_COST
+    )
     (local,) = call(
         side_kernel,
         "side_halo",
-        (local, y_a, y_b, z_a, z_b, y_high, y_low, z_high, z_low),
+        (local, y_a, y_b, z_b, z_a, y_high, y_low, z_high, z_low),
         (shape(*cells),),
         HALO_COST,
     )

time: 33.5 us -> 33.4 us (level)
  waiting for transfers between devices: 9.28 us -> 8.76 us
  starting transfers between devices: 18.8 us -> 19.2 us
    ppermute x7, waiting for transfers between devices: 5.34 us -> 4.64 us  [exchange(): return lax.ppermute(value, axes, route)]
    ppermute x8, starting transfers between devices: 8.85 us -> 9.44 us  [flip(): lax.ppermute(value, axis, [(i, i ^ bits) for i in range(lax.axis_size(axi...]
  transfers between devices with their start and end apart: 15 -> 15, of which waited for: 8 -> 9; matrix products, arithmetic and copies ran while one was open for 0% -> 0% of each run, Pallas kernels for 7% -> 7%
where the time goes in v9:
time: 33.4 us; the launch traced here: 33.3 us
  starting transfers between devices  19.2 us (57%)
  waiting for transfers between devices  8.76 us (26%)
  Pallas kernels  4.57 us (14%)
  between operations  0.69 us (2%)
    ppermute x7, starting transfers between devices, exchange(): return lax.ppermute(value, axes, route)  9.76 us
    ppermute x8, starting transfers between devices, flip(): lax.ppermute(value, axis, [(i, i ^ bits) for i in range(lax.axis_size(axi...  9.44 us
    ppermute x7, waiting for transfers between devices, exchange(): return lax.ppermute(value, axes, route)  4.64 us
    pallas_call x7, Pallas kernels, call(): pl.pallas_call(kernel, out_shape=outputs, in_specs=[pl.BlockSpec(memory_s...  4.57 us
    ppermute x8, waiting for transfers between devices, flip(): lax.ppermute(value, axis, [(i, i ^ bits) for i in range(lax.axis_size(axi...  4.13 us
  transfers between devices with their start and end apart: 15, of which 9 were waited for; matrix products, arithmetic and copies ran while one was open for 0% of the time, Pallas kernels for 7%

profile of v9, /device:TPU:101, one launch (start us, length us, event | category | flops | bytes accessed | tf_op | source)
XLA Modules:
  0.0 33.3 jit_solution(16452628553329526558)
XLA Ops:
  0.6 1.3 %x_traces.1 = (f32[4,7,7,8,128]{4,3,2,1,0:T(8,128)S(1)}, f32[49,8,128]{2,1,0:T(8,128)S(1)}, f32[49,8,128]{2,1,0:T(8,128)S(1)}, s32[1,4,128]{2,1,0:T(4,128)S(1)}) custom-call(f32[7,7,7,1,4,128]{5,4,3,2,1,0:T(4,128)} %rhs_hbm.1, s32[1,4,128]{2,1,0:T(4,128)} %orders_hbm.1), custom_call_target="tpu_custom_call" | custom-call | flops 4000000 | bytes 1910784 | tf_op jit(solution)/shard_map/x_traces/pallas_call | solution.py:511
  2.0 0.3 %collective-permute-start.4 = (f32[49,8,128]{2,1,0:T(8,128)S(1)}, f32[49,8,128]{2,1,0:T(8,128)S(1)}, u32[]{:S(2)}, u32[]{:S(2)}) collective-permute-start(f32[49,8,128]{2,1,0:T(8,128)S(1)} %get-tuple-element.35), channel_id=1, source_target_pairs={{0,64},{1,9},{2,66},{3,11},{4,68},{5,13},{6,70},{7,15},{8,72},{9,1... | collective-permute-start | bytes 602120 | tf_op jit(solution)/shard_map/ppermute | solution.py:534
  2.3 0.8 %collective-permute-start.5 = (f32[49,8,128]{2,1,0:T(8,128)S(1)}, f32[49,8,128]{2,1,0:T(8,128)S(1)}, u32[]{:S(2)}, u32[]{:S(2)}) collective-permute-start(f32[49,8,128]{2,1,0:T(8,128)S(1)} %get-tuple-element.36), channel_id=1, source_target_pairs={{0,8},{1,65},{2,10},{3,67},{4,12},{5,69},{6,14},{7,71},{8,0},{9,73... | collective-permute-start | bytes 602120 | tf_op jit(solution)/shard_map/ppermute | solution.py:534
  3.1 0.3 side_traces.1
  3.3 1.5 %collective-permute-start = (f32[14,8,128]{2,1,0:T(8,128)S(1)}, f32[14,8,128]{2,1,0:T(8,128)S(1)}, u32[]{:S(2)}, u32[]{:S(2)}) collective-permute-start(f32[14,8,128]{2,1,0:T(8,128)S(1)} %get-tuple-element.24), channel_id=1, source_target_pairs={{0,8},{8,0},{16,24},{24,16},{32,40},{40,32},{48,56},{56,48},{1,9},... | collective-permute-start | bytes 172040 | tf_op jit(solution)/shard_map/ppermute | solution.py:524
  4.8 2.8 %collective-permute-start.1 = (f32[14,8,128]{2,1,0:T(8,128)S(1)}, f32[14,8,128]{2,1,0:T(8,128)S(1)}, u32[]{:S(2)}, u32[]{:S(2)}) collective-permute-start(f32[14,8,128]{2,1,0:T(8,128)S(1)} %get-tuple-element.27), channel_id=1, source_target_pairs={{0,1},{1,0},{2,3},{3,2},{4,5},{5,4},{6,7},{7,6},{8,16},{9,17},{10,... | collective-permute-start | bytes 172040 | tf_op jit(solution)/shard_map/ppermute | solution.py:534
  7.6 2.0 %collective-permute-start.2 = (f32[8,128]{1,0:T(8,128)S(1)}, f32[8,128]{1,0:T(8,128)S(1)}, u32[]{:S(2)}, u32[]{:S(2)}) collective-permute-start(f32[8,128]{1,0:T(8,128)S(1)} %get-tuple-element.28), channel_id=1, source_target_pairs={{0,64},{1,2},{2,1},{3,4},{4,3},{5,6},{6,5},{7,71},{8,72},{9,10},{1... | collective-permute-start | bytes 12296 | tf_op jit(solution)/shard_map/ppermute | solution.py:534
  9.6 0.0 collective-permute-done.early
  9.6 0.7 %collective-permute-start.3 = (f32[8,128]{1,0:T(8,128)S(1)}, f32[8,128]{1,0:T(8,128)S(1)}, u32[]{:S(2)}, u32[]{:S(2)}) collective-permute-start(f32[8,128]{1,0:T(8,128)S(1)} %get-tuple-element.29), channel_id=1, source_target_pairs={{0,1},{1,0},{2,3},{3,2},{4,5},{5,4},{6,7},{7,6},{8,9},{9,8},{10,11... | collective-permute-start | bytes 12296 | tf_op jit(solution)/shard_map/ppermute | solution.py:524
  10.3 0.6 %own_cells.1 = (f32[4,7,7,8,128]{4,3,2,1,0:T(8,128)S(1)}, f32[14,8,128]{2,1,0:T(8,128)S(1)}) custom-call(f32[4,7,7,8,128]{4,3,2,1,0:T(8,128)S(1)} %get-tuple-element.23.first, f32[14,8,128]{2,1,0:T(8,128)S(1)} %collective-permute-done.early), custom_call_target="tpu_custom_call" | custom-call | flops 1400000000 | bytes 1720320 | tf_op jit(solution)/shard_map/own_cells/pallas_call | solution.py:511
  10.8 0.1 collective-permute-done.2.z_b
  10.9 0.2 collective-permute-done.3.z_a
  11.1 0.0 collective-permute-done.1.y_b
  11.1 0.4 %side_halo.1.local = f32[4,7,7,8,128]{4,3,2,1,0:T(8,128)S(1)} custom-call(f32[4,7,7,8,128]{4,3,2,1,0:T(8,128)S(1)} %get-tuple-element.25.local, f32[14,8,128]{2,1,0:T(8,128)S(1)} %get-tuple-element.26.y_a, f32[14,8,128]{2,1,0:T(8,128)S(1)} %collective-permute-done.1.y_b, f32[8,128]{1,0:T(8,128)S(1)} %collective-permute-done.2.z_b, ...), custom_call_target="tpu_custom_call" | custom-call | flops 4000000 | bytes 2646016 | tf_op jit(solution)/shard_map/side_halo/pallas_call | solution.py:511
  11.5 0.0 collective-permute-done.4.x_a
  11.5 0.0 collective-permute-done.5.x_b
  11.5 0.4 %smooth_and_restrict.1 = (f32[4,7,7,8,128]{4,3,2,1,0:T(8,128)S(1)}, f32[2,8,128]{2,1,0:T(8,128)S(1)}, f32[2,8,128]{2,1,0:T(8,128)S(1)}, f32[2,8,128]{2,1,0:T(8,128)S(1)}, f32[2,8,128]{2,1,0:T(8,128)S(1)}) custom-call(f32[4,7,7,8,128]{4,3,2,1,0:T(8,128)S(1)} %get-tuple-element.23.first, f32[4,7,7,8,128]{4,3,2,1,0:T(8,128)S(1)} %side_halo.1.local, ...), custom_call_target="tpu_custom_call" | custom-call | flops 5000000 | bytes 2844672 | tf_op jit(solution)/shard_map/smooth_and_restrict/pallas_call | solution.py:511
  12.0 1.5 %collective-permute-start.6 = (f32[2,8,128]{2,1,0:T(8,128)S(1)}, f32[2,8,128]{2,1,0:T(8,128)S(1)}, u32[]{:S(2)}, u32[]{:S(2)}) collective-permute-start(f32[2,8,128]{2,1,0:T(8,128)S(1)} %get-tuple-element.41), channel_id=1, source_target_pairs={{0,128},{64,192},{128,0},{192,64},{1,129},{65,193},{129,1},{193,65... | collective-permute-start | bytes 24584 | tf_op jit(solution)/shard_map/ppermute | solution.py:524
  13.4 2.0 %collective-permute-start.7 = (f32[2,8,128]{2,1,0:T(8,128)S(1)}, f32[2,8,128]{2,1,0:T(8,128)S(1)}, u32[]{:S(2)}, u32[]{:S(2)}) collective-permute-start(f32[2,8,128]{2,1,0:T(8,128)S(1)} %get-tuple-element.42), channel_id=1, source_target_pairs={{0,64},{64,0},{128,192},{192,128},{1,65},{65,1},{129,193},{193,129... | collective-permute-start | bytes 24584 | tf_op jit(solution)/shard_map/ppermute | solution.py:524
  15.4 0.0 collective-permute-start.8
  15.4 0.9 %unpack_modes.1 = (f32[7,7,7,1,4,128]{5,4,3,2,1,0:T(4,128)}, f32[2,8,128]{2,1,0:T(8,128)S(1)}) custom-call(f32[4,7,7,8,128]{4,3,2,1,0:T(8,128)S(1)} %get-tuple-element.37.field, f32[2,8,128]{2,1,0:T(8,128)S(1)} %get-tuple-element.38.here), custom_call_target="tpu_custom_call" | custom-call | flops 200000 | bytes 1521664 | tf_op jit(solution)/shard_map/unpack_modes/pallas_call | solution.py:511
  16.4 0.0 collective-permute-done.6
  16.4 0.2 collective-permute-done.7
  16.5 1.4 %collective-permute-done.8 = f32[2,8,128]{2,1,0:T(8,128)S(1)} collective-permute-done((f32[2,8,128]{2,1,0:T(8,128)S(1)}, f32[2,8,128]{2,1,0:T(8,128)S(1)}, u32[]{:S(2)}, u32[]{:S(2)}) %collective-permute-start.8) | collective-permute-done | bytes 8224 | tf_op jit(solution)/shard_map/ppermute | solution.py:534
  17.9 2.8 %collective-permute-start.9 = (f32[2,8,128]{2,1,0:T(8,128)S(1)}, f32[2,8,128]{2,1,0:T(8,128)S(1)}, u32[]{:S(2)}, u32[]{:S(2)}) collective-permute-start(f32[2,8,128]{2,1,0:T(8,128)S(1)} %multiply_add_fusion), channel_id=1, source_target_pairs={{0,1},{1,0},{2,3},{3,2},{4,5},{5,4},{6,7},{7,6},{8,9},{9,8},{10,11... | collective-permute-start | bytes 24584 | tf_op jit(solution)/shard_map/ppermute | solution.py:524
  20.8 0.8 %collective-permute-done.9 = f32[2,8,128]{2,1,0:T(8,128)S(1)} collective-permute-done((f32[2,8,128]{2,1,0:T(8,128)S(1)}, f32[2,8,128]{2,1,0:T(8,128)S(1)}, u32[]{:S(2)}, u32[]{:S(2)}) %collective-permute-start.9) | collective-permute-done | bytes 8224 | tf_op jit(solution)/shard_map/ppermute | solution.py:524
  21.6 1.5 %collective-permute-start.10 = (f32[2,2,8,128]{3,2,1,0:T(8,128)S(1)}, f32[2,2,8,128]{3,2,1,0:T(8,128)S(1)}, u32[]{:S(2)}, u32[]{:S(2)}) collective-permute-start(f32[2,2,8,128]{3,2,1,0:T(8,128)S(1)} %pad_maximum_fusion), channel_id=1, source_target_pairs={{0,8},{1,65},{2,10},{3,67},{4,12},{5,69},{6,14},{7,71},{8,0},{9,17... | collective-permute-start | bytes 49160 | tf_op jit(solution)/shard_map/ppermute | solution.py:534
  23.1 2.3 %collective-permute-done.10 = f32[2,2,8,128]{3,2,1,0:T(8,128)S(1)} collective-permute-done((f32[2,2,8,128]{3,2,1,0:T(8,128)S(1)}, f32[2,2,8,128]{3,2,1,0:T(8,128)S(1)}, u32[]{:S(2)}, u32[]{:S(2)}) %collective-permute-start.10) | collective-permute-done | bytes 16416 | tf_op jit(solution)/shard_map/ppermute | solution.py:534
  25.4 0.1 fusion.1
  25.5 0.3 collective-permute-start.11
  25.7 0.9 %collective-permute-done.11 = f32[2,8,128]{2,1,0:T(8,128)S(1)} collective-permute-done((f32[2,8,128]{2,1,0:T(8,128)S(1)}, f32[2,8,128]{2,1,0:T(8,128)S(1)}, u32[]{:S(2)}, u32[]{:S(2)}) %collective-permute-start.11) | collective-permute-done | bytes 8224 | tf_op jit(solution)/shard_map/ppermute | solution.py:524
  26.6 2.3 %collective-permute-start.12 = (f32[2,8,128]{2,1,0:T(8,128)S(1)}, f32[2,8,128]{2,1,0:T(8,128)S(1)}, u32[]{:S(2)}, u32[]{:S(2)}) collective-permute-start(f32[2,8,128]{2,1,0:T(8,128)S(1)} %reverse_add_fusion.chip), channel_id=1, source_target_pairs={{0,2},{1,5},{2,0},{3,7},{4,6},{5,1},{6,4},{7,3},{8,10},{9,13},{10,... | collective-permute-start | bytes 24584 | tf_op jit(solution)/shard_map/ppermute | solution.py:534
  29.0 0.8 %collective-permute-start.14 = (f32[2,8,128]{2,1,0:T(8,128)S(1)}, f32[2,8,128]{2,1,0:T(8,128)S(1)}, u32[]{:S(2)}, u32[]{:S(2)}) collective-permute-start(f32[2,8,128]{2,1,0:T(8,128)S(1)} %reverse_add_fusion.chip), channel_id=1, source_target_pairs={{0,6},{1,7},{2,4},{3,5},{4,2},{5,3},{6,0},{7,1},{8,14},{9,15},{10,... | collective-permute-start | bytes 24584 | tf_op jit(solution)/shard_map/ppermute | solution.py:524
  29.8 0.9 %collective-permute-done.12.fetched = f32[2,8,128]{2,1,0:T(8,128)S(1)} collective-permute-done((f32[2,8,128]{2,1,0:T(8,128)S(1)}, f32[2,8,128]{2,1,0:T(8,128)S(1)}, u32[]{:S(2)}, u32[]{:S(2)}) %collective-permute-start.12) | collective-permute-done | bytes 8224 | tf_op jit(solution)/shard_map/ppermute | solution.py:534
  30.6 0.0 collective-permute-start.13
  30.7 2.0 %collective-permute-done.14.third = f32[2,8,128]{2,1,0:T(8,128)S(1)} collective-permute-done((f32[2,8,128]{2,1,0:T(8,128)S(1)}, f32[2,8,128]{2,1,0:T(8,128)S(1)}, u32[]{:S(2)}, u32[]{:S(2)}) %collective-permute-start.14) | collective-permute-done | bytes 8224 | tf_op jit(solution)/shard_map/ppermute | solution.py:524
  32.7 0.0 collective-permute-done.13.mated
  32.7 0.6 %column.1 = f32[1,4,1024]{2,1,0:T(4,128)} custom-call(f32[2,8,128]{2,1,0:T(8,128)S(1)} %reverse_add_fusion.chip, f32[2,8,128]{2,1,0:T(8,128)S(1)} %collective-permute-done.12.fetched, f32[2,8,128]{2,1,0:T(8,128)S(1)} %collective-permute-done.13.mated, f32[2,8,128]{2,1,0:T(8,128)S(1)} %collective-permute-done.14.third), custom_call_target="tpu_custom_call" | custom-call | flops 20000 | bytes 49152 | tf_op jit(solution)/shard_map/column/pallas_call | solution.py:511
  (5 shorter events, 0.0 us)
Async XLA Ops:
  2.0 9.6 %collective-permute-start.4 = (f32[49,8,128]{2,1,0:T(8,128)S(1)}, f32[49,8,128]{2,1,0:T(8,128)S(1)}, u32[]{:S(2)}, u32[]{:S(2)}) collective-permute-start(f32[49,8,128]{2,1,0:T(8,128)S(1)} %get-tuple-element.35), channel_id=1, source_target_pairs={{0,64},{1,9},{2,66},{3,11},{4,68},{5,13},{6,70},{7,15},{8,72},{9,1... | collective-permute-start | bytes 602120 | tf_op jit(solution)/shard_map/ppermute | solution.py:534
  2.3 9.2 %collective-permute-start.5 = (f32[49,8,128]{2,1,0:T(8,128)S(1)}, f32[49,8,128]{2,1,0:T(8,128)S(1)}, u32[]{:S(2)}, u32[]{:S(2)}) collective-permute-start(f32[49,8,128]{2,1,0:T(8,128)S(1)} %get-tuple-element.36), channel_id=1, source_target_pairs={{0,8},{1,65},{2,10},{3,67},{4,12},{5,69},{6,14},{7,71},{8,0},{9,73... | collective-permute-start | bytes 602120 | tf_op jit(solution)/shard_map/ppermute | solution.py:534
  3.3 6.3 %collective-permute-start = (f32[14,8,128]{2,1,0:T(8,128)S(1)}, f32[14,8,128]{2,1,0:T(8,128)S(1)}, u32[]{:S(2)}, u32[]{:S(2)}) collective-permute-start(f32[14,8,128]{2,1,0:T(8,128)S(1)} %get-tuple-element.24), channel_id=1, source_target_pairs={{0,8},{8,0},{16,24},{24,16},{32,40},{40,32},{48,56},{56,48},{1,9},... | collective-permute-start | bytes 172040 | tf_op jit(solution)/shard_map/ppermute | solution.py:524
  4.8 6.3 %collective-permute-start.1 = (f32[14,8,128]{2,1,0:T(8,128)S(1)}, f32[14,8,128]{2,1,0:T(8,128)S(1)}, u32[]{:S(2)}, u32[]{:S(2)}) collective-permute-start(f32[14,8,128]{2,1,0:T(8,128)S(1)} %get-tuple-element.27), channel_id=1, source_target_pairs={{0,1},{1,0},{2,3},{3,2},{4,5},{5,4},{6,7},{7,6},{8,16},{9,17},{10,... | collective-permute-start | bytes 172040 | tf_op jit(solution)/shard_map/ppermute | solution.py:534
  7.6 3.3 %collective-permute-start.2 = (f32[8,128]{1,0:T(8,128)S(1)}, f32[8,128]{1,0:T(8,128)S(1)}, u32[]{:S(2)}, u32[]{:S(2)}) collective-permute-start(f32[8,128]{1,0:T(8,128)S(1)} %get-tuple-element.28), channel_id=1, source_target_pairs={{0,64},{1,2},{2,1},{3,4},{4,3},{5,6},{6,5},{7,71},{8,72},{9,10},{1... | collective-permute-start | bytes 12296 | tf_op jit(solution)/shard_map/ppermute | solution.py:534
  9.6 1.5 %collective-permute-start.3 = (f32[8,128]{1,0:T(8,128)S(1)}, f32[8,128]{1,0:T(8,128)S(1)}, u32[]{:S(2)}, u32[]{:S(2)}) collective-permute-start(f32[8,128]{1,0:T(8,128)S(1)} %get-tuple-element.29), channel_id=1, source_target_pairs={{0,1},{1,0},{2,3},{3,2},{4,5},{5,4},{6,7},{7,6},{8,9},{9,8},{10,11... | collective-permute-start | bytes 12296 | tf_op jit(solution)/shard_map/ppermute | solution.py:524
  12.0 4.4 %collective-permute-start.6 = (f32[2,8,128]{2,1,0:T(8,128)S(1)}, f32[2,8,128]{2,1,0:T(8,128)S(1)}, u32[]{:S(2)}, u32[]{:S(2)}) collective-permute-start(f32[2,8,128]{2,1,0:T(8,128)S(1)} %get-tuple-element.41), channel_id=1, source_target_pairs={{0,128},{64,192},{128,0},{192,64},{1,129},{65,193},{129,1},{193,65... | collective-permute-start | bytes 24584 | tf_op jit(solution)/shard_map/ppermute | solution.py:524
  13.4 3.1 %collective-permute-start.7 = (f32[2,8,128]{2,1,0:T(8,128)S(1)}, f32[2,8,128]{2,1,0:T(8,128)S(1)}, u32[]{:S(2)}, u32[]{:S(2)}) collective-permute-start(f32[2,8,128]{2,1,0:T(8,128)S(1)} %get-tuple-element.42), channel_id=1, source_target_pairs={{0,64},{64,0},{128,192},{192,128},{1,65},{65,1},{129,193},{193,129... | collective-permute-start | bytes 24584 | tf_op jit(solution)/shard_map/ppermute | solution.py:524
  15.4 2.5 %collective-permute-start.8 = (f32[2,8,128]{2,1,0:T(8,128)S(1)}, f32[2,8,128]{2,1,0:T(8,128)S(1)}, u32[]{:S(2)}, u32[]{:S(2)}) collective-permute-start(f32[2,8,128]{2,1,0:T(8,128)S(1)} %get-tuple-element.43), channel_id=1, source_target_pairs={{0,1},{1,0},{2,3},{3,2},{4,5},{5,4},{6,7},{7,6},{8,9},{9,8},{10,11... | collective-permute-start | bytes 24584 | tf_op jit(solution)/shard_map/ppermute | solution.py:534
  17.9 3.7 %collective-permute-start.9 = (f32[2,8,128]{2,1,0:T(8,128)S(1)}, f32[2,8,128]{2,1,0:T(8,128)S(1)}, u32[]{:S(2)}, u32[]{:S(2)}) collective-permute-start(f32[2,8,128]{2,1,0:T(8,128)S(1)} %multiply_add_fusion), channel_id=1, source_target_pairs={{0,1},{1,0},{2,3},{3,2},{4,5},{5,4},{6,7},{7,6},{8,9},{9,8},{10,11... | collective-permute-start | bytes 24584 | tf_op jit(solution)/shard_map/ppermute | solution.py:524
  21.6 3.8 %collective-permute-start.10 = (f32[2,2,8,128]{3,2,1,0:T(8,128)S(1)}, f32[2,2,8,128]{3,2,1,0:T(8,128)S(1)}, u32[]{:S(2)}, u32[]{:S(2)}) collective-permute-start(f32[2,2,8,128]{3,2,1,0:T(8,128)S(1)} %pad_maximum_fusion), channel_id=1, source_target_pairs={{0,8},{1,65},{2,10},{3,67},{4,12},{5,69},{6,14},{7,71},{8,0},{9,17... | collective-permute-start | bytes 49160 | tf_op jit(solution)/shard_map/ppermute | solution.py:534
  25.5 1.2 %collective-permute-start.11 = (f32[2,8,128]{2,1,0:T(8,128)S(1)}, f32[2,8,128]{2,1,0:T(8,128)S(1)}, u32[]{:S(2)}, u32[]{:S(2)}) collective-permute-start(f32[2,8,128]{2,1,0:T(8,128)S(1)} %bitcast.9), channel_id=1, source_target_pairs={{0,1},{1,0},{2,3},{3,2},{4,5},{5,4},{6,7},{7,6},{8,9},{9,8},{10,11... | collective-permute-start | bytes 24584 | tf_op jit(solution)/shard_map/ppermute | solution.py:524
  26.6 4.0 %collective-permute-start.12 = (f32[2,8,128]{2,1,0:T(8,128)S(1)}, f32[2,8,128]{2,1,0:T(8,128)S(1)}, u32[]{:S(2)}, u32[]{:S(2)}) collective-permute-start(f32[2,8,128]{2,1,0:T(8,128)S(1)} %reverse_add_fusion.chip), channel_id=1, source_target_pairs={{0,2},{1,5},{2,0},{3,7},{4,6},{5,1},{6,4},{7,3},{8,10},{9,13},{10,... | collective-permute-start | bytes 24584 | tf_op jit(solution)/shard_map/ppermute | solution.py:534
  29.0 3.7 %collective-permute-start.14 = (f32[2,8,128]{2,1,0:T(8,128)S(1)}, f32[2,8,128]{2,1,0:T(8,128)S(1)}, u32[]{:S(2)}, u32[]{:S(2)}) collective-permute-start(f32[2,8,128]{2,1,0:T(8,128)S(1)} %reverse_add_fusion.chip), channel_id=1, source_target_pairs={{0,6},{1,7},{2,4},{3,5},{4,2},{5,3},{6,0},{7,1},{8,14},{9,15},{10,... | collective-permute-start | bytes 24584 | tf_op jit(solution)/shard_map/ppermute | solution.py:524
  30.6 2.0 %collective-permute-start.13 = (f32[2,8,128]{2,1,0:T(8,128)S(1)}, f32[2,8,128]{2,1,0:T(8,128)S(1)}, u32[]{:S(2)}, u32[]{:S(2)}) collective-permute-start(f32[2,8,128]{2,1,0:T(8,128)S(1)} %collective-permute-done.12.fetched), channel_id=1, source_target_pairs={{0,1},{1,0},{2,3},{3,2},{4,5},{5,4},{6,7},{7,6},{8,9},{9,8},{10,11... | collective-permute-start | bytes 24584 | tf_op jit(solution)/shard_map/ppermute | solution.py:524

commit v10 on v9

--- a/solution.py
+++ b/solution.py
@@ -363,7 +363,7 @@
                 out[i, b, e] += add
 
 
-def finish_kernel(first, local, orders, x_a, x_b, field, here, sum_a, sum_b, far):
+def finish_kernel(first, local, orders, x_a, x_b, field, parts):
     pairs = Pairs()
     top = pairs.top
     row, lane = row_in_half(), lanes()
@@ -447,12 +447,12 @@
     near = sum_to_vertices(near, pairs, row, lane)
     outer = sum_to_vertices(outer, pairs, row, lane)
     for z in range(2):
-        here[z] = jnp.where(top, near[0][z], swap(near[1][z]))
+        parts[0, z] = jnp.where(top, near[0][z], swap(near[1][z]))
         ahead = jnp.where(top, swap(near[0][z]), near[1][z])
         behind = jnp.where(top, outer[0][z], swap(outer[1][z]))
-        sum_a[z] = jnp.where(x_even, ahead, behind)
-        sum_b[z] = jnp.where(x_even, behind, ahead)
-        far[z] = jnp.where(top, swap(outer[0][z]), outer[1][z])
+        parts[1, z] = jnp.where(x_even, ahead, behind)
+        parts[2, z] = jnp.where(x_even, behind, ahead)
+        parts[3, z] = jnp.where(top, swap(outer[0][z]), outer[1][z])
 
 
 def unpack_kernel(field, here, smoothed, here_again):
@@ -466,7 +466,7 @@
                     smoothed[2 * i + 1, b, e, 0] = value[4:]
 
 
-def column_kernel(chip, fetched, mated, third, column, blocks):
+def column_kernel(chip, third, fetched, mated, column, blocks):
     count = lax.axis_size("gz")
     me = lax.axis_index("gz")
     core, place = lax.rem(me, 2), lax.div(me, 2)
@@ -559,6 +559,14 @@
     return exchange(value, partner)
 
 
+def far_or_beside(value):
+    def partner(place):
+        place[0] ^= 2 if place[2] % 2 else 1
+        return place
+
+    return exchange(value, partner)
+
+
 def both_y_sides(value):
     count = lax.axis_size("gy")
 
@@ -620,46 +628,46 @@
         (shape(*cells),),
         HALO_COST,
     )
-    field, here, sum_a, sum_b, far = call(
+    field, parts = call(
         finish_kernel,
         "smooth_and_restrict",
         (first, local, held, x_a, x_b),
-        (shape(*cells),) + (shape(2, 8, 128),) * 4,
+        (shape(*cells), shape(4, 2, 8, 128)),
         5_000_000,
     )
+    count = lax.axis_size("gz")
+    both = jnp.stack([parts, flip(parts, "gz", 1)])
+    first_core = lax.axis_index("gz") % 2 == 0
+    from_one = far_or_beside(jnp.where(first_core, both[:, 1], both[:, 3]))
+    from_two = second_pairs(both[:, 2], "gx")
     smoothed, here = call(
         unpack_kernel,
         "unpack_modes",
-        (field, here),
-        (shape(*rhs.shape), shape(2, 8, 128)),
+        (field, both[:, 0]),
+        (shape(*rhs.shape), shape(2, 2, 8, 128)),
         200_000,
     )
-    from_far = flip(far, "gx", 2)
-    from_a = flip(sum_a, "gx", 1)
-    from_b = second_pairs(sum_b, "gx")
     sums = (
-        here
-        + inside("gx", -2) * from_far
-        + from_a
-        + inside("gx", -1) * inside("gx", 1) * from_b
-    )
-    count = lax.axis_size("gz")
-    chip = jnp.stack([sums, flip(sums, "gz", 1)])
-    from_beside = both_y_sides(chip)
+        jnp.where(first_core, 1.0, inside("gx", -2)) * from_one
+        + jnp.where(first_core, 0.0, inside("gx", -1) * inside("gx", 1)) * from_two
+        + jnp.where(first_core, 0.0, here)
+    )
+    chip = sums + flip(sums, "gz", 1)[::-1]
+    from_beside = both_y_sides(chip[:, :, 4:].reshape(2, 8, 128)).reshape(2, 2, 4, 128)
     from_low = (lax.axis_index("gy") + lax.axis_index("gz")) % 2 == 1
     row = lax.broadcasted_iota(jnp.int32, (1, 1, 4, 1), 2)
     wanted = jnp.where(from_low, row < 2, row == 3)
     valid = jnp.where(from_low, inside("gy", -1), inside("gy", 1))
-    edges = jnp.where(wanted, from_beside[:, :, 4:], 0.0) * valid
+    edges = jnp.where(wanted, from_beside, 0.0) * valid
     edges = edges.reshape(2, 8, 128)
     mated = flip(edges, "gz", 1)
     owned = chip[:, :, :4].reshape(2, 8, 128) + edges + mated[::-1]
+    third = flip(owned, "gz", 6)
     fetched = two_chips(owned)
-    third = flip(owned, "gz", 6)
     (column,) = call(
         column_kernel,
         "column",
-        (owned, fetched, flip(fetched, "gz", 1), third),
+        (owned, third, fetched, flip(fetched, "gz", 1)),
         (shape(1, 4, 128 * count),),
         20_000,
         scratch=(pltpu.VMEM((count + 2, 8, 128), jnp.float32),),

time: 33.4 us -> 32.9 us (0.985)
  starting transfers between devices: 19.2 us -> 16.1 us
  waiting for transfers between devices: 8.76 us -> 11.1 us
    ppermute x8 -> x7, starting transfers between devices: 9.44 us -> 4.4 us  [flip(): lax.ppermute(value, axis, [(i, i ^ bits) for i in range(lax.axis_size(axi...]
    ppermute x7 -> x8, starting transfers between devices: 9.76 us -> 11.7 us  [exchange(): return lax.ppermute(value, axes, route)]
    ppermute x7 -> x8, waiting for transfers between devices: 4.64 us -> 6.09 us  [exchange(): return lax.ppermute(value, axes, route)]
    ppermute x8 -> x7, waiting for transfers between devices: 4.13 us -> 4.97 us  [flip(): lax.ppermute(value, axis, [(i, i ^ bits) for i in range(lax.axis_size(axi...]
  transfers between devices with their start and end apart: 15 -> 15, of which waited for: 9 -> 10; matrix products, arithmetic and copies ran while one was open for 0% -> 0% of each run, Pallas kernels for 7% -> 7%
where the time goes in v10:
time: 32.9 us; the launch traced here: 32.7 us
  starting transfers between devices  16.1 us (49%)
  waiting for transfers between devices  11.1 us (34%)
  Pallas kernels  4.57 us (14%)
  between operations  0.69 us (2%)
    ppermute x8, starting transfers between devices, exchange(): return lax.ppermute(value, axes, route)  11.7 us
    ppermute x8, waiting for transfers between devices, exchange(): return lax.ppermute(value, axes, route)  6.09 us
    ppermute x7, waiting for transfers between devices, flip(): lax.ppermute(value, axis, [(i, i ^ bits) for i in range(lax.axis_size(axi...  4.97 us
    pallas_call x7, Pallas kernels, call(): pl.pallas_call(kernel, out_shape=outputs, in_specs=[pl.BlockSpec(memory_s...  4.57 us
    ppermute x7, starting transfers between devices, flip(): lax.ppermute(value, axis, [(i, i ^ bits) for i in range(lax.axis_size(axi...  4.4 us
  transfers between devices with their start and end apart: 15, of which 10 were waited for; matrix products, arithmetic and copies ran while one was open for 0% of the time, Pallas kernels for 7%

profile of v10, /device:TPU:101, one launch (start us, length us, event | category | flops | bytes accessed | tf_op | source)
XLA Modules:
  0.0 32.7 jit_solution(1486370387311517164)
XLA Ops:
  0.6 1.3 %x_traces.1 = (f32[4,7,7,8,128]{4,3,2,1,0:T(8,128)S(1)}, f32[49,8,128]{2,1,0:T(8,128)S(1)}, f32[49,8,128]{2,1,0:T(8,128)S(1)}, s32[1,4,128]{2,1,0:T(4,128)S(1)}) custom-call(f32[7,7,7,1,4,128]{5,4,3,2,1,0:T(4,128)} %rhs_hbm.1, s32[1,4,128]{2,1,0:T(4,128)} %orders_hbm.1), custom_call_target="tpu_custom_call" | custom-call | flops 4000000 | bytes 1910784 | tf_op jit(solution)/shard_map/x_traces/pallas_call | solution.py:511
  2.0 0.3 %collective-permute-start.4 = (f32[49,8,128]{2,1,0:T(8,128)S(1)}, f32[49,8,128]{2,1,0:T(8,128)S(1)}, u32[]{:S(2)}, u32[]{:S(2)}) collective-permute-start(f32[49,8,128]{2,1,0:T(8,128)S(1)} %get-tuple-element.32), channel_id=1, source_target_pairs={{0,64},{1,9},{2,66},{3,11},{4,68},{5,13},{6,70},{7,15},{8,72},{9,1... | collective-permute-start | bytes 602120 | tf_op jit(solution)/shard_map/ppermute | solution.py:534
  2.3 0.8 %collective-permute-start.5 = (f32[49,8,128]{2,1,0:T(8,128)S(1)}, f32[49,8,128]{2,1,0:T(8,128)S(1)}, u32[]{:S(2)}, u32[]{:S(2)}) collective-permute-start(f32[49,8,128]{2,1,0:T(8,128)S(1)} %get-tuple-element.33), channel_id=1, source_target_pairs={{0,8},{1,65},{2,10},{3,67},{4,12},{5,69},{6,14},{7,71},{8,0},{9,73... | collective-permute-start | bytes 602120 | tf_op jit(solution)/shard_map/ppermute | solution.py:534
  3.1 0.3 side_traces.1
  3.3 1.5 %collective-permute-start = (f32[14,8,128]{2,1,0:T(8,128)S(1)}, f32[14,8,128]{2,1,0:T(8,128)S(1)}, u32[]{:S(2)}, u32[]{:S(2)}) collective-permute-start(f32[14,8,128]{2,1,0:T(8,128)S(1)} %get-tuple-element.21), channel_id=1, source_target_pairs={{0,8},{8,0},{16,24},{24,16},{32,40},{40,32},{48,56},{56,48},{1,9},... | collective-permute-start | bytes 172040 | tf_op jit(solution)/shard_map/ppermute | solution.py:524
  4.8 2.8 %collective-permute-start.1 = (f32[14,8,128]{2,1,0:T(8,128)S(1)}, f32[14,8,128]{2,1,0:T(8,128)S(1)}, u32[]{:S(2)}, u32[]{:S(2)}) collective-permute-start(f32[14,8,128]{2,1,0:T(8,128)S(1)} %get-tuple-element.24), channel_id=1, source_target_pairs={{0,1},{1,0},{2,3},{3,2},{4,5},{5,4},{6,7},{7,6},{8,16},{9,17},{10,... | collective-permute-start | bytes 172040 | tf_op jit(solution)/shard_map/ppermute | solution.py:534
  7.6 2.0 %collective-permute-start.2 = (f32[8,128]{1,0:T(8,128)S(1)}, f32[8,128]{1,0:T(8,128)S(1)}, u32[]{:S(2)}, u32[]{:S(2)}) collective-permute-start(f32[8,128]{1,0:T(8,128)S(1)} %get-tuple-element.25), channel_id=1, source_target_pairs={{0,64},{1,2},{2,1},{3,4},{4,3},{5,6},{6,5},{7,71},{8,72},{9,10},{1... | collective-permute-start | bytes 12296 | tf_op jit(solution)/shard_map/ppermute | solution.py:534
  9.6 0.0 collective-permute-done.early
  9.6 0.7 %collective-permute-start.3 = (f32[8,128]{1,0:T(8,128)S(1)}, f32[8,128]{1,0:T(8,128)S(1)}, u32[]{:S(2)}, u32[]{:S(2)}) collective-permute-start(f32[8,128]{1,0:T(8,128)S(1)} %get-tuple-element.26), channel_id=1, source_target_pairs={{0,1},{1,0},{2,3},{3,2},{4,5},{5,4},{6,7},{7,6},{8,9},{9,8},{10,11... | collective-permute-start | bytes 12296 | tf_op jit(solution)/shard_map/ppermute | solution.py:524
  10.3 0.6 %own_cells.1 = (f32[4,7,7,8,128]{4,3,2,1,0:T(8,128)S(1)}, f32[14,8,128]{2,1,0:T(8,128)S(1)}) custom-call(f32[4,7,7,8,128]{4,3,2,1,0:T(8,128)S(1)} %get-tuple-element.20.first, f32[14,8,128]{2,1,0:T(8,128)S(1)} %collective-permute-done.early), custom_call_target="tpu_custom_call" | custom-call | flops 1400000000 | bytes 1720320 | tf_op jit(solution)/shard_map/own_cells/pallas_call | solution.py:511
  10.8 0.1 collective-permute-done.2.z_b
  10.9 0.2 collective-permute-done.3.z_a
  11.1 0.0 collective-permute-done.1.y_b
  11.1 0.4 %side_halo.1.local = f32[4,7,7,8,128]{4,3,2,1,0:T(8,128)S(1)} custom-call(f32[4,7,7,8,128]{4,3,2,1,0:T(8,128)S(1)} %get-tuple-element.22.local, f32[14,8,128]{2,1,0:T(8,128)S(1)} %get-tuple-element.23.y_a, f32[14,8,128]{2,1,0:T(8,128)S(1)} %collective-permute-done.1.y_b, f32[8,128]{1,0:T(8,128)S(1)} %collective-permute-done.2.z_b, ...), custom_call_target="tpu_custom_call" | custom-call | flops 4000000 | bytes 2646016 | tf_op jit(solution)/shard_map/side_halo/pallas_call | solution.py:511
  11.5 0.0 collective-permute-done.4.x_a
  11.5 0.0 collective-permute-done.5.x_b
  11.5 0.4 %smooth_and_restrict.1 = (f32[4,7,7,8,128]{4,3,2,1,0:T(8,128)S(1)}, f32[4,2,8,128]{3,2,1,0:T(8,128)S(1)}) custom-call(f32[4,7,7,8,128]{4,3,2,1,0:T(8,128)S(1)} %get-tuple-element.20.first, f32[4,7,7,8,128]{4,3,2,1,0:T(8,128)S(1)} %side_halo.1.local, s32[1,4,128]{2,1,0:T(4,128)S(1)} %get-tuple-element.31.orders, ...), custom_call_target="tpu_custom_call" | custom-call | flops 5000000 | bytes 2844672 | tf_op jit(solution)/shard_map/smooth_and_restrict/pallas_call | solution.py:511
  12.0 1.0 %collective-permute-start.6 = (f32[4,2,8,128]{3,2,1,0:T(8,128)S(1)}, f32[4,2,8,128]{3,2,1,0:T(8,128)S(1)}, u32[]{:S(2)}, u32[]{:S(2)}) collective-permute-start(f32[4,2,8,128]{3,2,1,0:T(8,128)S(1)} %get-tuple-element.35), channel_id=1, source_target_pairs={{0,1},{1,0},{2,3},{3,2},{4,5},{5,4},{6,7},{7,6},{8,9},{9,8},{10,11... | collective-permute-start | bytes 98312 | tf_op jit(solution)/shard_map/ppermute | solution.py:524
  13.0 0.9 %collective-permute-done.6 = f32[4,2,8,128]{3,2,1,0:T(8,128)S(1)} collective-permute-done((f32[4,2,8,128]{3,2,1,0:T(8,128)S(1)}, f32[4,2,8,128]{3,2,1,0:T(8,128)S(1)}, u32[]{:S(2)}, u32[]{:S(2)}) %collective-permute-start.6) | collective-permute-done | bytes 32800 | tf_op jit(solution)/shard_map/ppermute | solution.py:524
  13.9 1.7 %collective-permute-start.8 = (f32[2,2,8,128]{3,2,1,0:T(8,128)S(1)}, f32[2,2,8,128]{3,2,1,0:T(8,128)S(1)}, u32[]{:S(2)}, u32[]{:S(2)}) collective-permute-start(f32[2,2,8,128]{3,2,1,0:T(8,128)S(1)} %get-tuple-element.40), channel_id=1, source_target_pairs={{0,1},{1,0},{2,3},{3,2},{4,5},{5,4},{6,7},{7,6},{8,9},{9,8},{10,11... | collective-permute-start | bytes 49160 | tf_op jit(solution)/shard_map/ppermute | solution.py:534
  15.6 0.1 collective-permute-start.7
  15.7 0.9 %unpack_modes.1 = (f32[7,7,7,1,4,128]{5,4,3,2,1,0:T(4,128)}, f32[2,2,8,128]{3,2,1,0:T(8,128)S(1)}) custom-call(f32[4,7,7,8,128]{4,3,2,1,0:T(8,128)S(1)} %get-tuple-element.34.field, f32[2,2,8,128]{3,2,1,0:T(8,128)S(1)} %get-tuple-element.39.here), custom_call_target="tpu_custom_call" | custom-call | flops 200000 | bytes 1538048 | tf_op jit(solution)/shard_map/unpack_modes/pallas_call | solution.py:511
  16.7 0.1 collective-permute-done.8
  16.7 3.0 %collective-permute-done.7 = f32[2,2,8,128]{3,2,1,0:T(8,128)S(1)} collective-permute-done((f32[2,2,8,128]{3,2,1,0:T(8,128)S(1)}, f32[2,2,8,128]{3,2,1,0:T(8,128)S(1)}, u32[]{:S(2)}, u32[]{:S(2)}) %collective-permute-start.7) | collective-permute-done | bytes 16416 | tf_op jit(solution)/shard_map/ppermute | solution.py:534
  19.7 0.3 collective-permute-start.9
  20.0 0.9 %collective-permute-done.9 = f32[2,2,8,128]{3,2,1,0:T(8,128)S(1)} collective-permute-done((f32[2,2,8,128]{3,2,1,0:T(8,128)S(1)}, f32[2,2,8,128]{3,2,1,0:T(8,128)S(1)}, u32[]{:S(2)}, u32[]{:S(2)}) %collective-permute-start.9) | collective-permute-done | bytes 16416 | tf_op jit(solution)/shard_map/ppermute | solution.py:524
  20.9 1.6 %collective-permute-start.10 = (f32[2,8,128]{2,1,0:T(8,128)S(1)}, f32[2,8,128]{2,1,0:T(8,128)S(1)}, u32[]{:S(2)}, u32[]{:S(2)}) collective-permute-start(f32[2,8,128]{2,1,0:T(8,128)S(1)} %bitcast.13), channel_id=1, source_target_pairs={{0,8},{1,65},{2,10},{3,67},{4,12},{5,69},{6,14},{7,71},{8,0},{9,17... | collective-permute-start | bytes 24584 | tf_op jit(solution)/shard_map/ppermute | solution.py:534
  22.5 0.1 broadcast_in_dim.22
  22.6 2.1 %collective-permute-done.10 = f32[2,8,128]{2,1,0:T(8,128)S(1)} collective-permute-done((f32[2,8,128]{2,1,0:T(8,128)S(1)}, f32[2,8,128]{2,1,0:T(8,128)S(1)}, u32[]{:S(2)}, u32[]{:S(2)}) %collective-permute-start.10) | collective-permute-done | bytes 8224 | tf_op jit(solution)/shard_map/ppermute | solution.py:534
  24.7 0.1 select_multiply_fusion
  24.8 0.2 collective-permute-start.11
  25.0 1.0 %collective-permute-done.11 = f32[2,8,128]{2,1,0:T(8,128)S(1)} collective-permute-done((f32[2,8,128]{2,1,0:T(8,128)S(1)}, f32[2,8,128]{2,1,0:T(8,128)S(1)}, u32[]{:S(2)}, u32[]{:S(2)}) %collective-permute-start.11) | collective-permute-done | bytes 8224 | tf_op jit(solution)/shard_map/ppermute | solution.py:524
  26.0 0.1 reverse_add_fusion.1.chip
  26.0 2.3 %collective-permute-start.13 = (f32[2,8,128]{2,1,0:T(8,128)S(1)}, f32[2,8,128]{2,1,0:T(8,128)S(1)}, u32[]{:S(2)}, u32[]{:S(2)}) collective-permute-start(f32[2,8,128]{2,1,0:T(8,128)S(1)} %reverse_add_fusion.1.chip), channel_id=1, source_target_pairs={{0,2},{1,5},{2,0},{3,7},{4,6},{5,1},{6,4},{7,3},{8,10},{9,13},{10,... | collective-permute-start | bytes 24584 | tf_op jit(solution)/shard_map/ppermute | solution.py:534
  28.4 0.8 %collective-permute-start.12 = (f32[2,8,128]{2,1,0:T(8,128)S(1)}, f32[2,8,128]{2,1,0:T(8,128)S(1)}, u32[]{:S(2)}, u32[]{:S(2)}) collective-permute-start(f32[2,8,128]{2,1,0:T(8,128)S(1)} %reverse_add_fusion.1.chip), channel_id=1, source_target_pairs={{0,6},{1,7},{2,4},{3,5},{4,2},{5,3},{6,0},{7,1},{8,14},{9,15},{10,... | collective-permute-start | bytes 24584 | tf_op jit(solution)/shard_map/ppermute | solution.py:524
  29.2 0.9 %collective-permute-done.13.fetched = f32[2,8,128]{2,1,0:T(8,128)S(1)} collective-permute-done((f32[2,8,128]{2,1,0:T(8,128)S(1)}, f32[2,8,128]{2,1,0:T(8,128)S(1)}, u32[]{:S(2)}, u32[]{:S(2)}) %collective-permute-start.13) | collective-permute-done | bytes 8224 | tf_op jit(solution)/shard_map/ppermute | solution.py:534
  30.0 0.0 collective-permute-start.14
  30.0 2.0 %collective-permute-done.12.third = f32[2,8,128]{2,1,0:T(8,128)S(1)} collective-permute-done((f32[2,8,128]{2,1,0:T(8,128)S(1)}, f32[2,8,128]{2,1,0:T(8,128)S(1)}, u32[]{:S(2)}, u32[]{:S(2)}) %collective-permute-start.12) | collective-permute-done | bytes 8224 | tf_op jit(solution)/shard_map/ppermute | solution.py:524
  32.1 0.0 collective-permute-done.14.mated
  32.1 0.6 %column.1 = f32[1,4,1024]{2,1,0:T(4,128)} custom-call(f32[2,8,128]{2,1,0:T(8,128)S(1)} %reverse_add_fusion.1.chip, f32[2,8,128]{2,1,0:T(8,128)S(1)} %collective-permute-done.12.third, f32[2,8,128]{2,1,0:T(8,128)S(1)} %collective-permute-done.13.fetched, f32[2,8,128]{2,1,0:T(8,128)S(1)} %collective-permute-done.14.mated), custom_call_target="tpu_custom_call" | custom-call | flops 20000 | bytes 49152 | tf_op jit(solution)/shard_map/column/pallas_call | solution.py:511
  (6 shorter events, 0.0 us)
Async XLA Ops:
  2.0 9.6 %collective-permute-start.4 = (f32[49,8,128]{2,1,0:T(8,128)S(1)}, f32[49,8,128]{2,1,0:T(8,128)S(1)}, u32[]{:S(2)}, u32[]{:S(2)}) collective-permute-start(f32[49,8,128]{2,1,0:T(8,128)S(1)} %get-tuple-element.32), channel_id=1, source_target_pairs={{0,64},{1,9},{2,66},{3,11},{4,68},{5,13},{6,70},{7,15},{8,72},{9,1... | collective-permute-start | bytes 602120 | tf_op jit(solution)/shard_map/ppermute | solution.py:534
  2.3 9.2 %collective-permute-start.5 = (f32[49,8,128]{2,1,0:T(8,128)S(1)}, f32[49,8,128]{2,1,0:T(8,128)S(1)}, u32[]{:S(2)}, u32[]{:S(2)}) collective-permute-start(f32[49,8,128]{2,1,0:T(8,128)S(1)} %get-tuple-element.33), channel_id=1, source_target_pairs={{0,8},{1,65},{2,10},{3,67},{4,12},{5,69},{6,14},{7,71},{8,0},{9,73... | collective-permute-start | bytes 602120 | tf_op jit(solution)/shard_map/ppermute | solution.py:534
  3.3 6.3 %collective-permute-start = (f32[14,8,128]{2,1,0:T(8,128)S(1)}, f32[14,8,128]{2,1,0:T(8,128)S(1)}, u32[]{:S(2)}, u32[]{:S(2)}) collective-permute-start(f32[14,8,128]{2,1,0:T(8,128)S(1)} %get-tuple-element.21), channel_id=1, source_target_pairs={{0,8},{8,0},{16,24},{24,16},{32,40},{40,32},{48,56},{56,48},{1,9},... | collective-permute-start | bytes 172040 | tf_op jit(solution)/shard_map/ppermute | solution.py:524
  4.8 6.3 %collective-permute-start.1 = (f32[14,8,128]{2,1,0:T(8,128)S(1)}, f32[14,8,128]{2,1,0:T(8,128)S(1)}, u32[]{:S(2)}, u32[]{:S(2)}) collective-permute-start(f32[14,8,128]{2,1,0:T(8,128)S(1)} %get-tuple-element.24), channel_id=1, source_target_pairs={{0,1},{1,0},{2,3},{3,2},{4,5},{5,4},{6,7},{7,6},{8,16},{9,17},{10,... | collective-permute-start | bytes 172040 | tf_op jit(solution)/shard_map/ppermute | solution.py:534
  7.6 3.3 %collective-permute-start.2 = (f32[8,128]{1,0:T(8,128)S(1)}, f32[8,128]{1,0:T(8,128)S(1)}, u32[]{:S(2)}, u32[]{:S(2)}) collective-permute-start(f32[8,128]{1,0:T(8,128)S(1)} %get-tuple-element.25), channel_id=1, source_target_pairs={{0,64},{1,2},{2,1},{3,4},{4,3},{5,6},{6,5},{7,71},{8,72},{9,10},{1... | collective-permute-start | bytes 12296 | tf_op jit(solution)/shard_map/ppermute | solution.py:534
  9.6 1.5 %collective-permute-start.3 = (f32[8,128]{1,0:T(8,128)S(1)}, f32[8,128]{1,0:T(8,128)S(1)}, u32[]{:S(2)}, u32[]{:S(2)}) collective-permute-start(f32[8,128]{1,0:T(8,128)S(1)} %get-tuple-element.26), channel_id=1, source_target_pairs={{0,1},{1,0},{2,3},{3,2},{4,5},{5,4},{6,7},{7,6},{8,9},{9,8},{10,11... | collective-permute-start | bytes 12296 | tf_op jit(solution)/shard_map/ppermute | solution.py:524
  12.0 1.9 %collective-permute-start.6 = (f32[4,2,8,128]{3,2,1,0:T(8,128)S(1)}, f32[4,2,8,128]{3,2,1,0:T(8,128)S(1)}, u32[]{:S(2)}, u32[]{:S(2)}) collective-permute-start(f32[4,2,8,128]{3,2,1,0:T(8,128)S(1)} %get-tuple-element.35), channel_id=1, source_target_pairs={{0,1},{1,0},{2,3},{3,2},{4,5},{5,4},{6,7},{7,6},{8,9},{9,8},{10,11... | collective-permute-start | bytes 98312 | tf_op jit(solution)/shard_map/ppermute | solution.py:524
  13.9 2.9 %collective-permute-start.8 = (f32[2,2,8,128]{3,2,1,0:T(8,128)S(1)}, f32[2,2,8,128]{3,2,1,0:T(8,128)S(1)}, u32[]{:S(2)}, u32[]{:S(2)}) collective-permute-start(f32[2,2,8,128]{3,2,1,0:T(8,128)S(1)} %get-tuple-element.40), channel_id=1, source_target_pairs={{0,1},{1,0},{2,3},{3,2},{4,5},{5,4},{6,7},{7,6},{8,9},{9,8},{10,11... | collective-permute-start | bytes 49160 | tf_op jit(solution)/shard_map/ppermute | solution.py:534
  15.6 4.1 %collective-permute-start.7 = (f32[2,2,8,128]{3,2,1,0:T(8,128)S(1)}, f32[2,2,8,128]{3,2,1,0:T(8,128)S(1)}, u32[]{:S(2)}, u32[]{:S(2)}) collective-permute-start(f32[2,2,8,128]{3,2,1,0:T(8,128)S(1)} %get-tuple-element.38), channel_id=1, source_target_pairs={{0,64},{1,129},{2,66},{3,131},{4,68},{5,133},{6,70},{7,135},{8,72}... | collective-permute-start | bytes 49160 | tf_op jit(solution)/shard_map/ppermute | solution.py:534
  19.7 1.2 %collective-permute-start.9 = (f32[2,2,8,128]{3,2,1,0:T(8,128)S(1)}, f32[2,2,8,128]{3,2,1,0:T(8,128)S(1)}, u32[]{:S(2)}, u32[]{:S(2)}) collective-permute-start(f32[2,2,8,128]{3,2,1,0:T(8,128)S(1)} %select_add_fusion), channel_id=1, source_target_pairs={{0,1},{1,0},{2,3},{3,2},{4,5},{5,4},{6,7},{7,6},{8,9},{9,8},{10,11... | collective-permute-start | bytes 49160 | tf_op jit(solution)/shard_map/ppermute | solution.py:524
  20.9 3.8 %collective-permute-start.10 = (f32[2,8,128]{2,1,0:T(8,128)S(1)}, f32[2,8,128]{2,1,0:T(8,128)S(1)}, u32[]{:S(2)}, u32[]{:S(2)}) collective-permute-start(f32[2,8,128]{2,1,0:T(8,128)S(1)} %bitcast.13), channel_id=1, source_target_pairs={{0,8},{1,65},{2,10},{3,67},{4,12},{5,69},{6,14},{7,71},{8,0},{9,17... | collective-permute-start | bytes 24584 | tf_op jit(solution)/shard_map/ppermute | solution.py:534
  24.8 1.2 %collective-permute-start.11 = (f32[2,8,128]{2,1,0:T(8,128)S(1)}, f32[2,8,128]{2,1,0:T(8,128)S(1)}, u32[]{:S(2)}, u32[]{:S(2)}) collective-permute-start(f32[2,8,128]{2,1,0:T(8,128)S(1)} %select_multiply_fusion), channel_id=1, source_target_pairs={{0,1},{1,0},{2,3},{3,2},{4,5},{5,4},{6,7},{7,6},{8,9},{9,8},{10,11... | collective-permute-start | bytes 24584 | tf_op jit(solution)/shard_map/ppermute | solution.py:524
  26.0 4.0 %collective-permute-start.13 = (f32[2,8,128]{2,1,0:T(8,128)S(1)}, f32[2,8,128]{2,1,0:T(8,128)S(1)}, u32[]{:S(2)}, u32[]{:S(2)}) collective-permute-start(f32[2,8,128]{2,1,0:T(8,128)S(1)} %reverse_add_fusion.1.chip), channel_id=1, source_target_pairs={{0,2},{1,5},{2,0},{3,7},{4,6},{5,1},{6,4},{7,3},{8,10},{9,13},{10,... | collective-permute-start | bytes 24584 | tf_op jit(solution)/shard_map/ppermute | solution.py:534
  28.4 3.7 %collective-permute-start.12 = (f32[2,8,128]{2,1,0:T(8,128)S(1)}, f32[2,8,128]{2,1,0:T(8,128)S(1)}, u32[]{:S(2)}, u32[]{:S(2)}) collective-permute-start(f32[2,8,128]{2,1,0:T(8,128)S(1)} %reverse_add_fusion.1.chip), channel_id=1, source_target_pairs={{0,6},{1,7},{2,4},{3,5},{4,2},{5,3},{6,0},{7,1},{8,14},{9,15},{10,... | collective-permute-start | bytes 24584 | tf_op jit(solution)/shard_map/ppermute | solution.py:524
  30.0 2.0 %collective-permute-start.14 = (f32[2,8,128]{2,1,0:T(8,128)S(1)}, f32[2,8,128]{2,1,0:T(8,128)S(1)}, u32[]{:S(2)}, u32[]{:S(2)}) collective-permute-start(f32[2,8,128]{2,1,0:T(8,128)S(1)} %collective-permute-done.13.fetched), channel_id=1, source_target_pairs={{0,1},{1,0},{2,3},{3,2},{4,5},{5,4},{6,7},{7,6},{8,9},{9,8},{10,11... | collective-permute-start | bytes 24584 | tf_op jit(solution)/shard_map/ppermute | solution.py:524

commit v11 on v10

--- a/solution.py
+++ b/solution.py
@@ -638,8 +638,8 @@
     count = lax.axis_size("gz")
     both = jnp.stack([parts, flip(parts, "gz", 1)])
     first_core = lax.axis_index("gz") % 2 == 0
+    from_two = second_pairs(both[:, 2], "gx")
     from_one = far_or_beside(jnp.where(first_core, both[:, 1], both[:, 3]))
-    from_two = second_pairs(both[:, 2], "gx")
     smoothed, here = call(
         unpack_kernel,
         "unpack_modes",
@@ -648,8 +648,8 @@
         200_000,
     )
     sums = (
-        jnp.where(first_core, 1.0, inside("gx", -2)) * from_one
-        + jnp.where(first_core, 0.0, inside("gx", -1) * inside("gx", 1)) * from_two
+        jnp.where(first_core, 0.0, inside("gx", -1) * inside("gx", 1)) * from_two
+        + jnp.where(first_core, 1.0, inside("gx", -2)) * from_one
         + jnp.where(first_core, 0.0, here)
     )
     chip = sums + flip(sums, "gz", 1)[::-1]

time: 32.9 us -> 32.7 us (level)
  waiting for transfers between devices: 11.1 us -> 7.95 us
  starting transfers between devices: 16.1 us -> 19 us
    ppermute x8, waiting for transfers between devices: 6.09 us -> 3.12 us  [exchange(): return lax.ppermute(value, axes, route)]
    ppermute x7, starting transfers between devices: 4.4 us -> 5.85 us  [flip(): lax.ppermute(value, axis, [(i, i ^ bits) for i in range(lax.axis_size(axi...]
    ppermute x8, starting transfers between devices: 11.7 us -> 13.1 us  [exchange(): return lax.ppermute(value, axes, route)]
where the time goes in v11:
time: 32.7 us; the launch traced here: 32.5 us
  starting transfers between devices  19 us (58%)
  waiting for transfers between devices  7.95 us (24%)
  Pallas kernels  4.57 us (14%)
  between operations  0.69 us (2%)
    ppermute x8, starting transfers between devices, exchange(): return lax.ppermute(value, axes, route)  13.1 us
    ppermute x7, starting transfers between devices, flip(): lax.ppermute(value, axis, [(i, i ^ bits) for i in range(lax.axis_size(axi...  5.85 us
    ppermute x7, waiting for transfers between devices, flip(): lax.ppermute(value, axis, [(i, i ^ bits) for i in range(lax.axis_size(axi...  4.82 us
    pallas_call x7, Pallas kernels, call(): pl.pallas_call(kernel, out_shape=outputs, in_specs=[pl.BlockSpec(memory_s...  4.57 us
    ppermute x8, waiting for transfers between devices, exchange(): return lax.ppermute(value, axes, route)  3.12 us
  transfers between devices with their start and end apart: 15, of which 10 were waited for; matrix products, arithmetic and copies ran while one was open for 0% of the time, Pallas kernels for 7%

profile of v11, /device:TPU:101, one launch (start us, length us, event | category | flops | bytes accessed | tf_op | source)
XLA Modules:
  0.0 32.5 jit_solution(7194350111464910244)
XLA Ops:
  0.6 1.3 %x_traces.1 = (f32[4,7,7,8,128]{4,3,2,1,0:T(8,128)S(1)}, f32[49,8,128]{2,1,0:T(8,128)S(1)}, f32[49,8,128]{2,1,0:T(8,128)S(1)}, s32[1,4,128]{2,1,0:T(4,128)S(1)}) custom-call(f32[7,7,7,1,4,128]{5,4,3,2,1,0:T(4,128)} %rhs_hbm.1, s32[1,4,128]{2,1,0:T(4,128)} %orders_hbm.1), custom_call_target="tpu_custom_call" | custom-call | flops 4000000 | bytes 1910784 | tf_op jit(solution)/shard_map/x_traces/pallas_call | solution.py:511
  2.0 0.3 %collective-permute-start.4 = (f32[49,8,128]{2,1,0:T(8,128)S(1)}, f32[49,8,128]{2,1,0:T(8,128)S(1)}, u32[]{:S(2)}, u32[]{:S(2)}) collective-permute-start(f32[49,8,128]{2,1,0:T(8,128)S(1)} %get-tuple-element.32), channel_id=1, source_target_pairs={{0,64},{1,9},{2,66},{3,11},{4,68},{5,13},{6,70},{7,15},{8,72},{9,1... | collective-permute-start | bytes 602120 | tf_op jit(solution)/shard_map/ppermute | solution.py:534
  2.3 0.8 %collective-permute-start.5 = (f32[49,8,128]{2,1,0:T(8,128)S(1)}, f32[49,8,128]{2,1,0:T(8,128)S(1)}, u32[]{:S(2)}, u32[]{:S(2)}) collective-permute-start(f32[49,8,128]{2,1,0:T(8,128)S(1)} %get-tuple-element.33), channel_id=1, source_target_pairs={{0,8},{1,65},{2,10},{3,67},{4,12},{5,69},{6,14},{7,71},{8,0},{9,73... | collective-permute-start | bytes 602120 | tf_op jit(solution)/shard_map/ppermute | solution.py:534
  3.1 0.3 side_traces.1
  3.3 1.5 %collective-permute-start = (f32[14,8,128]{2,1,0:T(8,128)S(1)}, f32[14,8,128]{2,1,0:T(8,128)S(1)}, u32[]{:S(2)}, u32[]{:S(2)}) collective-permute-start(f32[14,8,128]{2,1,0:T(8,128)S(1)} %get-tuple-element.21), channel_id=1, source_target_pairs={{0,8},{8,0},{16,24},{24,16},{32,40},{40,32},{48,56},{56,48},{1,9},... | collective-permute-start | bytes 172040 | tf_op jit(solution)/shard_map/ppermute | solution.py:524
  4.8 2.8 %collective-permute-start.1 = (f32[14,8,128]{2,1,0:T(8,128)S(1)}, f32[14,8,128]{2,1,0:T(8,128)S(1)}, u32[]{:S(2)}, u32[]{:S(2)}) collective-permute-start(f32[14,8,128]{2,1,0:T(8,128)S(1)} %get-tuple-element.24), channel_id=1, source_target_pairs={{0,1},{1,0},{2,3},{3,2},{4,5},{5,4},{6,7},{7,6},{8,16},{9,17},{10,... | collective-permute-start | bytes 172040 | tf_op jit(solution)/shard_map/ppermute | solution.py:534
  7.6 2.0 %collective-permute-start.2 = (f32[8,128]{1,0:T(8,128)S(1)}, f32[8,128]{1,0:T(8,128)S(1)}, u32[]{:S(2)}, u32[]{:S(2)}) collective-permute-start(f32[8,128]{1,0:T(8,128)S(1)} %get-tuple-element.25), channel_id=1, source_target_pairs={{0,64},{1,2},{2,1},{3,4},{4,3},{5,6},{6,5},{7,71},{8,72},{9,10},{1... | collective-permute-start | bytes 12296 | tf_op jit(solution)/shard_map/ppermute | solution.py:534
  9.6 0.0 collective-permute-done.early
  9.6 0.7 %collective-permute-start.3 = (f32[8,128]{1,0:T(8,128)S(1)}, f32[8,128]{1,0:T(8,128)S(1)}, u32[]{:S(2)}, u32[]{:S(2)}) collective-permute-start(f32[8,128]{1,0:T(8,128)S(1)} %get-tuple-element.26), channel_id=1, source_target_pairs={{0,1},{1,0},{2,3},{3,2},{4,5},{5,4},{6,7},{7,6},{8,9},{9,8},{10,11... | collective-permute-start | bytes 12296 | tf_op jit(solution)/shard_map/ppermute | solution.py:524
  10.3 0.6 %own_cells.1 = (f32[4,7,7,8,128]{4,3,2,1,0:T(8,128)S(1)}, f32[14,8,128]{2,1,0:T(8,128)S(1)}) custom-call(f32[4,7,7,8,128]{4,3,2,1,0:T(8,128)S(1)} %get-tuple-element.20.first, f32[14,8,128]{2,1,0:T(8,128)S(1)} %collective-permute-done.early), custom_call_target="tpu_custom_call" | custom-call | flops 1400000000 | bytes 1720320 | tf_op jit(solution)/shard_map/own_cells/pallas_call | solution.py:511
  10.8 0.1 collective-permute-done.2.z_b
  10.9 0.2 collective-permute-done.3.z_a
  11.1 0.0 collective-permute-done.1.y_b
  11.1 0.4 %side_halo.1.local = f32[4,7,7,8,128]{4,3,2,1,0:T(8,128)S(1)} custom-call(f32[4,7,7,8,128]{4,3,2,1,0:T(8,128)S(1)} %get-tuple-element.22.local, f32[14,8,128]{2,1,0:T(8,128)S(1)} %get-tuple-element.23.y_a, f32[14,8,128]{2,1,0:T(8,128)S(1)} %collective-permute-done.1.y_b, f32[8,128]{1,0:T(8,128)S(1)} %collective-permute-done.2.z_b, ...), custom_call_target="tpu_custom_call" | custom-call | flops 4000000 | bytes 2646016 | tf_op jit(solution)/shard_map/side_halo/pallas_call | solution.py:511
  11.5 0.0 collective-permute-done.4.x_a
  11.5 0.0 collective-permute-done.5.x_b
  11.5 0.4 %smooth_and_restrict.1 = (f32[4,7,7,8,128]{4,3,2,1,0:T(8,128)S(1)}, f32[4,2,8,128]{3,2,1,0:T(8,128)S(1)}) custom-call(f32[4,7,7,8,128]{4,3,2,1,0:T(8,128)S(1)} %get-tuple-element.20.first, f32[4,7,7,8,128]{4,3,2,1,0:T(8,128)S(1)} %side_halo.1.local, s32[1,4,128]{2,1,0:T(4,128)S(1)} %get-tuple-element.31.orders, ...), custom_call_target="tpu_custom_call" | custom-call | flops 5000000 | bytes 2844672 | tf_op jit(solution)/shard_map/smooth_and_restrict/pallas_call | solution.py:511
  12.0 1.0 %collective-permute-start.6 = (f32[4,2,8,128]{3,2,1,0:T(8,128)S(1)}, f32[4,2,8,128]{3,2,1,0:T(8,128)S(1)}, u32[]{:S(2)}, u32[]{:S(2)}) collective-permute-start(f32[4,2,8,128]{3,2,1,0:T(8,128)S(1)} %get-tuple-element.35), channel_id=1, source_target_pairs={{0,1},{1,0},{2,3},{3,2},{4,5},{5,4},{6,7},{7,6},{8,9},{9,8},{10,11... | collective-permute-start | bytes 98312 | tf_op jit(solution)/shard_map/ppermute | solution.py:524
  13.0 0.9 %collective-permute-done.6 = f32[4,2,8,128]{3,2,1,0:T(8,128)S(1)} collective-permute-done((f32[4,2,8,128]{3,2,1,0:T(8,128)S(1)}, f32[4,2,8,128]{3,2,1,0:T(8,128)S(1)}, u32[]{:S(2)}, u32[]{:S(2)}) %collective-permute-start.6) | collective-permute-done | bytes 32800 | tf_op jit(solution)/shard_map/ppermute | solution.py:524
  13.9 1.5 %collective-permute-start.8 = (f32[2,2,8,128]{3,2,1,0:T(8,128)S(1)}, f32[2,2,8,128]{3,2,1,0:T(8,128)S(1)}, u32[]{:S(2)}, u32[]{:S(2)}) collective-permute-start(f32[2,2,8,128]{3,2,1,0:T(8,128)S(1)} %get-tuple-element.40), channel_id=1, source_target_pairs={{0,64},{1,129},{2,66},{3,131},{4,68},{5,133},{6,70},{7,135},{8,72}... | collective-permute-start | bytes 49160 | tf_op jit(solution)/shard_map/ppermute | solution.py:534
  15.4 1.2 %collective-permute-start.7 = (f32[2,2,8,128]{3,2,1,0:T(8,128)S(1)}, f32[2,2,8,128]{3,2,1,0:T(8,128)S(1)}, u32[]{:S(2)}, u32[]{:S(2)}) collective-permute-start(f32[2,2,8,128]{3,2,1,0:T(8,128)S(1)} %get-tuple-element.38), channel_id=1, source_target_pairs={{0,1},{1,0},{2,3},{3,2},{4,5},{5,4},{6,7},{7,6},{8,9},{9,8},{10,11... | collective-permute-start | bytes 49160 | tf_op jit(solution)/shard_map/ppermute | solution.py:534
  16.6 0.9 %unpack_modes.1 = (f32[7,7,7,1,4,128]{5,4,3,2,1,0:T(4,128)}, f32[2,2,8,128]{3,2,1,0:T(8,128)S(1)}) custom-call(f32[4,7,7,8,128]{4,3,2,1,0:T(8,128)S(1)} %get-tuple-element.34.field, f32[2,2,8,128]{3,2,1,0:T(8,128)S(1)} %get-tuple-element.39.here), custom_call_target="tpu_custom_call" | custom-call | flops 200000 | bytes 1538048 | tf_op jit(solution)/shard_map/unpack_modes/pallas_call | solution.py:511
  17.6 0.4 %collective-permute-done.8 = f32[2,2,8,128]{3,2,1,0:T(8,128)S(1)} collective-permute-done((f32[2,2,8,128]{3,2,1,0:T(8,128)S(1)}, f32[2,2,8,128]{3,2,1,0:T(8,128)S(1)}, u32[]{:S(2)}, u32[]{:S(2)}) %collective-permute-start.8) | collective-permute-done | bytes 16416 | tf_op jit(solution)/shard_map/ppermute | solution.py:534
  18.0 0.2 collective-permute-done.7
  18.2 1.7 %collective-permute-start.9 = (f32[2,2,8,128]{3,2,1,0:T(8,128)S(1)}, f32[2,2,8,128]{3,2,1,0:T(8,128)S(1)}, u32[]{:S(2)}, u32[]{:S(2)}) collective-permute-start(f32[2,2,8,128]{3,2,1,0:T(8,128)S(1)} %select_add_fusion), channel_id=1, source_target_pairs={{0,1},{1,0},{2,3},{3,2},{4,5},{5,4},{6,7},{7,6},{8,9},{9,8},{10,11... | collective-permute-start | bytes 49160 | tf_op jit(solution)/shard_map/ppermute | solution.py:524
  19.8 0.8 %collective-permute-done.9 = f32[2,2,8,128]{3,2,1,0:T(8,128)S(1)} collective-permute-done((f32[2,2,8,128]{3,2,1,0:T(8,128)S(1)}, f32[2,2,8,128]{3,2,1,0:T(8,128)S(1)}, u32[]{:S(2)}, u32[]{:S(2)}) %collective-permute-start.9) | collective-permute-done | bytes 16416 | tf_op jit(solution)/shard_map/ppermute | solution.py:524
  20.7 2.1 %collective-permute-start.10 = (f32[2,8,128]{2,1,0:T(8,128)S(1)}, f32[2,8,128]{2,1,0:T(8,128)S(1)}, u32[]{:S(2)}, u32[]{:S(2)}) collective-permute-start(f32[2,8,128]{2,1,0:T(8,128)S(1)} %bitcast.13), channel_id=1, source_target_pairs={{0,8},{1,65},{2,10},{3,67},{4,12},{5,69},{6,14},{7,71},{8,0},{9,17... | collective-permute-start | bytes 24584 | tf_op jit(solution)/shard_map/ppermute | solution.py:534
  22.8 0.1 broadcast_in_dim.22
  22.9 1.6 %collective-permute-done.10 = f32[2,8,128]{2,1,0:T(8,128)S(1)} collective-permute-done((f32[2,8,128]{2,1,0:T(8,128)S(1)}, f32[2,8,128]{2,1,0:T(8,128)S(1)}, u32[]{:S(2)}, u32[]{:S(2)}) %collective-permute-start.10) | collective-permute-done | bytes 8224 | tf_op jit(solution)/shard_map/ppermute | solution.py:534
  24.5 0.1 select_multiply_fusion
  24.5 0.3 collective-permute-start.11
  24.8 0.9 %collective-permute-done.11 = f32[2,8,128]{2,1,0:T(8,128)S(1)} collective-permute-done((f32[2,8,128]{2,1,0:T(8,128)S(1)}, f32[2,8,128]{2,1,0:T(8,128)S(1)}, u32[]{:S(2)}, u32[]{:S(2)}) %collective-permute-start.11) | collective-permute-done | bytes 8224 | tf_op jit(solution)/shard_map/ppermute | solution.py:524
  25.7 0.1 reverse_add_fusion.1.chip
  25.8 2.3 %collective-permute-start.13 = (f32[2,8,128]{2,1,0:T(8,128)S(1)}, f32[2,8,128]{2,1,0:T(8,128)S(1)}, u32[]{:S(2)}, u32[]{:S(2)}) collective-permute-start(f32[2,8,128]{2,1,0:T(8,128)S(1)} %reverse_add_fusion.1.chip), channel_id=1, source_target_pairs={{0,2},{1,5},{2,0},{3,7},{4,6},{5,1},{6,4},{7,3},{8,10},{9,13},{10,... | collective-permute-start | bytes 24584 | tf_op jit(solution)/shard_map/ppermute | solution.py:534
  28.1 0.8 %collective-permute-start.12 = (f32[2,8,128]{2,1,0:T(8,128)S(1)}, f32[2,8,128]{2,1,0:T(8,128)S(1)}, u32[]{:S(2)}, u32[]{:S(2)}) collective-permute-start(f32[2,8,128]{2,1,0:T(8,128)S(1)} %reverse_add_fusion.1.chip), channel_id=1, source_target_pairs={{0,6},{1,7},{2,4},{3,5},{4,2},{5,3},{6,0},{7,1},{8,14},{9,15},{10,... | collective-permute-start | bytes 24584 | tf_op jit(solution)/shard_map/ppermute | solution.py:524
  28.9 0.9 %collective-permute-done.13.fetched = f32[2,8,128]{2,1,0:T(8,128)S(1)} collective-permute-done((f32[2,8,128]{2,1,0:T(8,128)S(1)}, f32[2,8,128]{2,1,0:T(8,128)S(1)}, u32[]{:S(2)}, u32[]{:S(2)}) %collective-permute-start.13) | collective-permute-done | bytes 8224 | tf_op jit(solution)/shard_map/ppermute | solution.py:534
  29.8 0.0 collective-permute-start.14
  29.8 2.0 %collective-permute-done.12.third = f32[2,8,128]{2,1,0:T(8,128)S(1)} collective-permute-done((f32[2,8,128]{2,1,0:T(8,128)S(1)}, f32[2,8,128]{2,1,0:T(8,128)S(1)}, u32[]{:S(2)}, u32[]{:S(2)}) %collective-permute-start.12) | collective-permute-done | bytes 8224 | tf_op jit(solution)/shard_map/ppermute | solution.py:524
  31.8 0.0 collective-permute-done.14.mated
  31.8 0.6 %column.1 = f32[1,4,1024]{2,1,0:T(4,128)} custom-call(f32[2,8,128]{2,1,0:T(8,128)S(1)} %reverse_add_fusion.1.chip, f32[2,8,128]{2,1,0:T(8,128)S(1)} %collective-permute-done.12.third, f32[2,8,128]{2,1,0:T(8,128)S(1)} %collective-permute-done.13.fetched, f32[2,8,128]{2,1,0:T(8,128)S(1)} %collective-permute-done.14.mated), custom_call_target="tpu_custom_call" | custom-call | flops 20000 | bytes 49152 | tf_op jit(solution)/shard_map/column/pallas_call | solution.py:511
  (6 shorter events, 0.0 us)
Async XLA Ops:
  2.0 9.6 %collective-permute-start.4 = (f32[49,8,128]{2,1,0:T(8,128)S(1)}, f32[49,8,128]{2,1,0:T(8,128)S(1)}, u32[]{:S(2)}, u32[]{:S(2)}) collective-permute-start(f32[49,8,128]{2,1,0:T(8,128)S(1)} %get-tuple-element.32), channel_id=1, source_target_pairs={{0,64},{1,9},{2,66},{3,11},{4,68},{5,13},{6,70},{7,15},{8,72},{9,1... | collective-permute-start | bytes 602120 | tf_op jit(solution)/shard_map/ppermute | solution.py:534
  2.3 9.2 %collective-permute-start.5 = (f32[49,8,128]{2,1,0:T(8,128)S(1)}, f32[49,8,128]{2,1,0:T(8,128)S(1)}, u32[]{:S(2)}, u32[]{:S(2)}) collective-permute-start(f32[49,8,128]{2,1,0:T(8,128)S(1)} %get-tuple-element.33), channel_id=1, source_target_pairs={{0,8},{1,65},{2,10},{3,67},{4,12},{5,69},{6,14},{7,71},{8,0},{9,73... | collective-permute-start | bytes 602120 | tf_op jit(solution)/shard_map/ppermute | solution.py:534
  3.3 6.3 %collective-permute-start = (f32[14,8,128]{2,1,0:T(8,128)S(1)}, f32[14,8,128]{2,1,0:T(8,128)S(1)}, u32[]{:S(2)}, u32[]{:S(2)}) collective-permute-start(f32[14,8,128]{2,1,0:T(8,128)S(1)} %get-tuple-element.21), channel_id=1, source_target_pairs={{0,8},{8,0},{16,24},{24,16},{32,40},{40,32},{48,56},{56,48},{1,9},... | collective-permute-start | bytes 172040 | tf_op jit(solution)/shard_map/ppermute | solution.py:524
  4.8 6.3 %collective-permute-start.1 = (f32[14,8,128]{2,1,0:T(8,128)S(1)}, f32[14,8,128]{2,1,0:T(8,128)S(1)}, u32[]{:S(2)}, u32[]{:S(2)}) collective-permute-start(f32[14,8,128]{2,1,0:T(8,128)S(1)} %get-tuple-element.24), channel_id=1, source_target_pairs={{0,1},{1,0},{2,3},{3,2},{4,5},{5,4},{6,7},{7,6},{8,16},{9,17},{10,... | collective-permute-start | bytes 172040 | tf_op jit(solution)/shard_map/ppermute | solution.py:534
  7.6 3.3 %collective-permute-start.2 = (f32[8,128]{1,0:T(8,128)S(1)}, f32[8,128]{1,0:T(8,128)S(1)}, u32[]{:S(2)}, u32[]{:S(2)}) collective-permute-start(f32[8,128]{1,0:T(8,128)S(1)} %get-tuple-element.25), channel_id=1, source_target_pairs={{0,64},{1,2},{2,1},{3,4},{4,3},{5,6},{6,5},{7,71},{8,72},{9,10},{1... | collective-permute-start | bytes 12296 | tf_op jit(solution)/shard_map/ppermute | solution.py:534
  9.6 1.5 %collective-permute-start.3 = (f32[8,128]{1,0:T(8,128)S(1)}, f32[8,128]{1,0:T(8,128)S(1)}, u32[]{:S(2)}, u32[]{:S(2)}) collective-permute-start(f32[8,128]{1,0:T(8,128)S(1)} %get-tuple-element.26), channel_id=1, source_target_pairs={{0,1},{1,0},{2,3},{3,2},{4,5},{5,4},{6,7},{7,6},{8,9},{9,8},{10,11... | collective-permute-start | bytes 12296 | tf_op jit(solution)/shard_map/ppermute | solution.py:524
  12.0 1.9 %collective-permute-start.6 = (f32[4,2,8,128]{3,2,1,0:T(8,128)S(1)}, f32[4,2,8,128]{3,2,1,0:T(8,128)S(1)}, u32[]{:S(2)}, u32[]{:S(2)}) collective-permute-start(f32[4,2,8,128]{3,2,1,0:T(8,128)S(1)} %get-tuple-element.35), channel_id=1, source_target_pairs={{0,1},{1,0},{2,3},{3,2},{4,5},{5,4},{6,7},{7,6},{8,9},{9,8},{10,11... | collective-permute-start | bytes 98312 | tf_op jit(solution)/shard_map/ppermute | solution.py:524
  13.9 4.1 %collective-permute-start.8 = (f32[2,2,8,128]{3,2,1,0:T(8,128)S(1)}, f32[2,2,8,128]{3,2,1,0:T(8,128)S(1)}, u32[]{:S(2)}, u32[]{:S(2)}) collective-permute-start(f32[2,2,8,128]{3,2,1,0:T(8,128)S(1)} %get-tuple-element.40), channel_id=1, source_target_pairs={{0,64},{1,129},{2,66},{3,131},{4,68},{5,133},{6,70},{7,135},{8,72}... | collective-permute-start | bytes 49160 | tf_op jit(solution)/shard_map/ppermute | solution.py:534
  15.4 2.7 %collective-permute-start.7 = (f32[2,2,8,128]{3,2,1,0:T(8,128)S(1)}, f32[2,2,8,128]{3,2,1,0:T(8,128)S(1)}, u32[]{:S(2)}, u32[]{:S(2)}) collective-permute-start(f32[2,2,8,128]{3,2,1,0:T(8,128)S(1)} %get-tuple-element.38), channel_id=1, source_target_pairs={{0,1},{1,0},{2,3},{3,2},{4,5},{5,4},{6,7},{7,6},{8,9},{9,8},{10,11... | collective-permute-start | bytes 49160 | tf_op jit(solution)/shard_map/ppermute | solution.py:534
  18.2 2.5 %collective-permute-start.9 = (f32[2,2,8,128]{3,2,1,0:T(8,128)S(1)}, f32[2,2,8,128]{3,2,1,0:T(8,128)S(1)}, u32[]{:S(2)}, u32[]{:S(2)}) collective-permute-start(f32[2,2,8,128]{3,2,1,0:T(8,128)S(1)} %select_add_fusion), channel_id=1, source_target_pairs={{0,1},{1,0},{2,3},{3,2},{4,5},{5,4},{6,7},{7,6},{8,9},{9,8},{10,11... | collective-permute-start | bytes 49160 | tf_op jit(solution)/shard_map/ppermute | solution.py:524
  20.7 3.8 %collective-permute-start.10 = (f32[2,8,128]{2,1,0:T(8,128)S(1)}, f32[2,8,128]{2,1,0:T(8,128)S(1)}, u32[]{:S(2)}, u32[]{:S(2)}) collective-permute-start(f32[2,8,128]{2,1,0:T(8,128)S(1)} %bitcast.13), channel_id=1, source_target_pairs={{0,8},{1,65},{2,10},{3,67},{4,12},{5,69},{6,14},{7,71},{8,0},{9,17... | collective-permute-start | bytes 24584 | tf_op jit(solution)/shard_map/ppermute | solution.py:534
  24.5 1.2 %collective-permute-start.11 = (f32[2,8,128]{2,1,0:T(8,128)S(1)}, f32[2,8,128]{2,1,0:T(8,128)S(1)}, u32[]{:S(2)}, u32[]{:S(2)}) collective-permute-start(f32[2,8,128]{2,1,0:T(8,128)S(1)} %select_multiply_fusion), channel_id=1, source_target_pairs={{0,1},{1,0},{2,3},{3,2},{4,5},{5,4},{6,7},{7,6},{8,9},{9,8},{10,11... | collective-permute-start | bytes 24584 | tf_op jit(solution)/shard_map/ppermute | solution.py:524
  25.8 4.0 %collective-permute-start.13 = (f32[2,8,128]{2,1,0:T(8,128)S(1)}, f32[2,8,128]{2,1,0:T(8,128)S(1)}, u32[]{:S(2)}, u32[]{:S(2)}) collective-permute-start(f32[2,8,128]{2,1,0:T(8,128)S(1)} %reverse_add_fusion.1.chip), channel_id=1, source_target_pairs={{0,2},{1,5},{2,0},{3,7},{4,6},{5,1},{6,4},{7,3},{8,10},{9,13},{10,... | collective-permute-start | bytes 24584 | tf_op jit(solution)/shard_map/ppermute | solution.py:534
  28.1 3.7 %collective-permute-start.12 = (f32[2,8,128]{2,1,0:T(8,128)S(1)}, f32[2,8,128]{2,1,0:T(8,128)S(1)}, u32[]{:S(2)}, u32[]{:S(2)}) collective-permute-start(f32[2,8,128]{2,1,0:T(8,128)S(1)} %reverse_add_fusion.1.chip), channel_id=1, source_target_pairs={{0,6},{1,7},{2,4},{3,5},{4,2},{5,3},{6,0},{7,1},{8,14},{9,15},{10,... | collective-permute-start | bytes 24584 | tf_op jit(solution)/shard_map/ppermute | solution.py:524
  29.8 2.0 %collective-permute-start.14 = (f32[2,8,128]{2,1,0:T(8,128)S(1)}, f32[2,8,128]{2,1,0:T(8,128)S(1)}, u32[]{:S(2)}, u32[]{:S(2)}) collective-permute-start(f32[2,8,128]{2,1,0:T(8,128)S(1)} %collective-permute-done.13.fetched), channel_id=1, source_target_pairs={{0,1},{1,0},{2,3},{3,2},{4,5},{5,4},{6,7},{7,6},{8,9},{9,8},{10,11... | collective-permute-start | bytes 24584 | tf_op jit(solution)/shard_map/ppermute | solution.py:524

commit v12 on v11

--- a/solution.py
+++ b/solution.py
@@ -472,15 +472,16 @@
     core, place = lax.rem(me, 2), lax.div(me, 2)
     beside = place + 1 - 2 * lax.rem(place, 2)
     across = lax.rem(place + 2, 4)
-    asked = beside + core * (across - beside)
+    mirrored = 3 - place
+    asked = mirrored + core * (across - mirrored)
     zero = jnp.zeros((8, 128), jnp.float32)
     blocks[0] = zero
     blocks[count + 1] = zero
     for source, sender, pair in (
         (place, core, chip),
         (asked, core, fetched),
-        (beside + across - asked, 1 - core, mated),
-        (3 - place, core, third),
+        (mirrored + across - asked, 1 - core, mated),
+        (beside, core, third),
     ):
         blocks[2 * source + sender + 1] = pair[0]
         blocks[2 * source + 2 - sender] = pair[1]
@@ -581,7 +582,7 @@
 
 def two_chips(value):
     def partner(place):
-        place[2] ^= 4 if place[2] % 2 else 2
+        place[2] ^= 4 if place[2] % 2 else 6
         return place
 
     return exchange(value, partner)
@@ -662,7 +663,7 @@
     edges = edges.reshape(2, 8, 128)
     mated = flip(edges, "gz", 1)
     owned = chip[:, :, :4].reshape(2, 8, 128) + edges + mated[::-1]
-    third = flip(owned, "gz", 6)
+    third = flip(owned, "gz", 2)
     fetched = two_chips(owned)
     (column,) = call(
         column_kernel,

time: 32.7 us -> 32.5 us (level)
  waiting for transfers between devices: 7.95 us -> 7.11 us
  starting transfers between devices: 19 us -> 19.7 us
    ppermute x7, waiting for transfers between devices: 4.82 us -> 3.61 us  [flip(): lax.ppermute(value, axis, [(i, i ^ bits) for i in range(lax.axis_size(axi...]
    ppermute x7, starting transfers between devices: 5.85 us -> 6.61 us  [flip(): lax.ppermute(value, axis, [(i, i ^ bits) for i in range(lax.axis_size(axi...]
    ppermute x8, waiting for transfers between devices: 3.12 us -> 3.5 us  [exchange(): return lax.ppermute(value, axes, route)]
where the time goes in v12:
time: 32.5 us; the launch traced here: 32.4 us
  starting transfers between devices  19.7 us (61%)
  waiting for transfers between devices  7.11 us (22%)
  Pallas kernels  4.57 us (14%)
  between operations  0.69 us (2%)
    ppermute x8, starting transfers between devices, exchange(): return lax.ppermute(value, axes, route)  13.1 us
    ppermute x7, starting transfers between devices, flip(): lax.ppermute(value, axis, [(i, i ^ bits) for i in range(lax.axis_size(axi...  6.61 us
    pallas_call x7, Pallas kernels, call(): pl.pallas_call(kernel, out_shape=outputs, in_specs=[pl.BlockSpec(memory_s...  4.57 us
    ppermute x7, waiting for transfers between devices, flip(): lax.ppermute(value, axis, [(i, i ^ bits) for i in range(lax.axis_size(axi...  3.61 us
    ppermute x8, waiting for transfers between devices, exchange(): return lax.ppermute(value, axes, route)  3.5 us
  transfers between devices with their start and end apart: 15, of which 10 were waited for; matrix products, arithmetic and copies ran while one was open for 0% of the time, Pallas kernels for 7%

profile of v12, /device:TPU:101, one launch (start us, length us, event | category | flops | bytes accessed | tf_op | source)
XLA Modules:
  0.0 32.4 jit_solution(11379880328610907087)
XLA Ops:
  0.6 1.3 %x_traces.1 = (f32[4,7,7,8,128]{4,3,2,1,0:T(8,128)S(1)}, f32[49,8,128]{2,1,0:T(8,128)S(1)}, f32[49,8,128]{2,1,0:T(8,128)S(1)}, s32[1,4,128]{2,1,0:T(4,128)S(1)}) custom-call(f32[7,7,7,1,4,128]{5,4,3,2,1,0:T(4,128)} %rhs_hbm.1, s32[1,4,128]{2,1,0:T(4,128)} %orders_hbm.1), custom_call_target="tpu_custom_call" | custom-call | flops 4000000 | bytes 1910784 | tf_op jit(solution)/shard_map/x_traces/pallas_call | solution.py:512
  2.0 0.3 %collective-permute-start.4 = (f32[49,8,128]{2,1,0:T(8,128)S(1)}, f32[49,8,128]{2,1,0:T(8,128)S(1)}, u32[]{:S(2)}, u32[]{:S(2)}) collective-permute-start(f32[49,8,128]{2,1,0:T(8,128)S(1)} %get-tuple-element.32), channel_id=1, source_target_pairs={{0,64},{1,9},{2,66},{3,11},{4,68},{5,13},{6,70},{7,15},{8,72},{9,1... | collective-permute-start | bytes 602120 | tf_op jit(solution)/shard_map/ppermute | solution.py:535
  2.3 0.8 %collective-permute-start.5 = (f32[49,8,128]{2,1,0:T(8,128)S(1)}, f32[49,8,128]{2,1,0:T(8,128)S(1)}, u32[]{:S(2)}, u32[]{:S(2)}) collective-permute-start(f32[49,8,128]{2,1,0:T(8,128)S(1)} %get-tuple-element.33), channel_id=1, source_target_pairs={{0,8},{1,65},{2,10},{3,67},{4,12},{5,69},{6,14},{7,71},{8,0},{9,73... | collective-permute-start | bytes 602120 | tf_op jit(solution)/shard_map/ppermute | solution.py:535
  3.1 0.3 side_traces.1
  3.3 1.5 %collective-permute-start = (f32[14,8,128]{2,1,0:T(8,128)S(1)}, f32[14,8,128]{2,1,0:T(8,128)S(1)}, u32[]{:S(2)}, u32[]{:S(2)}) collective-permute-start(f32[14,8,128]{2,1,0:T(8,128)S(1)} %get-tuple-element.21), channel_id=1, source_target_pairs={{0,8},{8,0},{16,24},{24,16},{32,40},{40,32},{48,56},{56,48},{1,9},... | collective-permute-start | bytes 172040 | tf_op jit(solution)/shard_map/ppermute | solution.py:525
  4.8 2.8 %collective-permute-start.1 = (f32[14,8,128]{2,1,0:T(8,128)S(1)}, f32[14,8,128]{2,1,0:T(8,128)S(1)}, u32[]{:S(2)}, u32[]{:S(2)}) collective-permute-start(f32[14,8,128]{2,1,0:T(8,128)S(1)} %get-tuple-element.24), channel_id=1, source_target_pairs={{0,1},{1,0},{2,3},{3,2},{4,5},{5,4},{6,7},{7,6},{8,16},{9,17},{10,... | collective-permute-start | bytes 172040 | tf_op jit(solution)/shard_map/ppermute | solution.py:535
  7.6 2.0 %collective-permute-start.2 = (f32[8,128]{1,0:T(8,128)S(1)}, f32[8,128]{1,0:T(8,128)S(1)}, u32[]{:S(2)}, u32[]{:S(2)}) collective-permute-start(f32[8,128]{1,0:T(8,128)S(1)} %get-tuple-element.25), channel_id=1, source_target_pairs={{0,64},{1,2},{2,1},{3,4},{4,3},{5,6},{6,5},{7,71},{8,72},{9,10},{1... | collective-permute-start | bytes 12296 | tf_op jit(solution)/shard_map/ppermute | solution.py:535
  9.6 0.0 collective-permute-done.early
  9.6 0.7 %collective-permute-start.3 = (f32[8,128]{1,0:T(8,128)S(1)}, f32[8,128]{1,0:T(8,128)S(1)}, u32[]{:S(2)}, u32[]{:S(2)}) collective-permute-start(f32[8,128]{1,0:T(8,128)S(1)} %get-tuple-element.26), channel_id=1, source_target_pairs={{0,1},{1,0},{2,3},{3,2},{4,5},{5,4},{6,7},{7,6},{8,9},{9,8},{10,11... | collective-permute-start | bytes 12296 | tf_op jit(solution)/shard_map/ppermute | solution.py:525
  10.3 0.6 %own_cells.1 = (f32[4,7,7,8,128]{4,3,2,1,0:T(8,128)S(1)}, f32[14,8,128]{2,1,0:T(8,128)S(1)}) custom-call(f32[4,7,7,8,128]{4,3,2,1,0:T(8,128)S(1)} %get-tuple-element.20.first, f32[14,8,128]{2,1,0:T(8,128)S(1)} %collective-permute-done.early), custom_call_target="tpu_custom_call" | custom-call | flops 1400000000 | bytes 1720320 | tf_op jit(solution)/shard_map/own_cells/pallas_call | solution.py:512
  10.8 0.1 collective-permute-done.2.z_b
  10.9 0.2 collective-permute-done.3.z_a
  11.1 0.0 collective-permute-done.1.y_b
  11.1 0.4 %side_halo.1.local = f32[4,7,7,8,128]{4,3,2,1,0:T(8,128)S(1)} custom-call(f32[4,7,7,8,128]{4,3,2,1,0:T(8,128)S(1)} %get-tuple-element.22.local, f32[14,8,128]{2,1,0:T(8,128)S(1)} %get-tuple-element.23.y_a, f32[14,8,128]{2,1,0:T(8,128)S(1)} %collective-permute-done.1.y_b, f32[8,128]{1,0:T(8,128)S(1)} %collective-permute-done.2.z_b, ...), custom_call_target="tpu_custom_call" | custom-call | flops 4000000 | bytes 2646016 | tf_op jit(solution)/shard_map/side_halo/pallas_call | solution.py:512
  11.5 0.0 collective-permute-done.4.x_a
  11.5 0.0 collective-permute-done.5.x_b
  11.5 0.4 %smooth_and_restrict.1 = (f32[4,7,7,8,128]{4,3,2,1,0:T(8,128)S(1)}, f32[4,2,8,128]{3,2,1,0:T(8,128)S(1)}) custom-call(f32[4,7,7,8,128]{4,3,2,1,0:T(8,128)S(1)} %get-tuple-element.20.first, f32[4,7,7,8,128]{4,3,2,1,0:T(8,128)S(1)} %side_halo.1.local, s32[1,4,128]{2,1,0:T(4,128)S(1)} %get-tuple-element.31.orders, ...), custom_call_target="tpu_custom_call" | custom-call | flops 5000000 | bytes 2844672 | tf_op jit(solution)/shard_map/smooth_and_restrict/pallas_call | solution.py:512
  12.0 1.0 %collective-permute-start.6 = (f32[4,2,8,128]{3,2,1,0:T(8,128)S(1)}, f32[4,2,8,128]{3,2,1,0:T(8,128)S(1)}, u32[]{:S(2)}, u32[]{:S(2)}) collective-permute-start(f32[4,2,8,128]{3,2,1,0:T(8,128)S(1)} %get-tuple-element.35), channel_id=1, source_target_pairs={{0,1},{1,0},{2,3},{3,2},{4,5},{5,4},{6,7},{7,6},{8,9},{9,8},{10,11... | collective-permute-start | bytes 98312 | tf_op jit(solution)/shard_map/ppermute | solution.py:525
  13.0 0.9 %collective-permute-done.6 = f32[4,2,8,128]{3,2,1,0:T(8,128)S(1)} collective-permute-done((f32[4,2,8,128]{3,2,1,0:T(8,128)S(1)}, f32[4,2,8,128]{3,2,1,0:T(8,128)S(1)}, u32[]{:S(2)}, u32[]{:S(2)}) %collective-permute-start.6) | collective-permute-done | bytes 32800 | tf_op jit(solution)/shard_map/ppermute | solution.py:525
  13.9 1.5 %collective-permute-start.8 = (f32[2,2,8,128]{3,2,1,0:T(8,128)S(1)}, f32[2,2,8,128]{3,2,1,0:T(8,128)S(1)}, u32[]{:S(2)}, u32[]{:S(2)}) collective-permute-start(f32[2,2,8,128]{3,2,1,0:T(8,128)S(1)} %get-tuple-element.40), channel_id=1, source_target_pairs={{0,64},{1,129},{2,66},{3,131},{4,68},{5,133},{6,70},{7,135},{8,72}... | collective-permute-start | bytes 49160 | tf_op jit(solution)/shard_map/ppermute | solution.py:535
  15.4 1.2 %collective-permute-start.7 = (f32[2,2,8,128]{3,2,1,0:T(8,128)S(1)}, f32[2,2,8,128]{3,2,1,0:T(8,128)S(1)}, u32[]{:S(2)}, u32[]{:S(2)}) collective-permute-start(f32[2,2,8,128]{3,2,1,0:T(8,128)S(1)} %get-tuple-element.38), channel_id=1, source_target_pairs={{0,1},{1,0},{2,3},{3,2},{4,5},{5,4},{6,7},{7,6},{8,9},{9,8},{10,11... | collective-permute-start | bytes 49160 | tf_op jit(solution)/shard_map/ppermute | solution.py:535
  16.6 0.9 %unpack_modes.1 = (f32[7,7,7,1,4,128]{5,4,3,2,1,0:T(4,128)}, f32[2,2,8,128]{3,2,1,0:T(8,128)S(1)}) custom-call(f32[4,7,7,8,128]{4,3,2,1,0:T(8,128)S(1)} %get-tuple-element.34.field, f32[2,2,8,128]{3,2,1,0:T(8,128)S(1)} %get-tuple-element.39.here), custom_call_target="tpu_custom_call" | custom-call | flops 200000 | bytes 1538048 | tf_op jit(solution)/shard_map/unpack_modes/pallas_call | solution.py:512
  17.6 0.4 %collective-permute-done.8 = f32[2,2,8,128]{3,2,1,0:T(8,128)S(1)} collective-permute-done((f32[2,2,8,128]{3,2,1,0:T(8,128)S(1)}, f32[2,2,8,128]{3,2,1,0:T(8,128)S(1)}, u32[]{:S(2)}, u32[]{:S(2)}) %collective-permute-start.8) | collective-permute-done | bytes 16416 | tf_op jit(solution)/shard_map/ppermute | solution.py:535
  18.0 0.2 collective-permute-done.7
  18.2 1.7 %collective-permute-start.9 = (f32[2,2,8,128]{3,2,1,0:T(8,128)S(1)}, f32[2,2,8,128]{3,2,1,0:T(8,128)S(1)}, u32[]{:S(2)}, u32[]{:S(2)}) collective-permute-start(f32[2,2,8,128]{3,2,1,0:T(8,128)S(1)} %select_add_fusion), channel_id=1, source_target_pairs={{0,1},{1,0},{2,3},{3,2},{4,5},{5,4},{6,7},{7,6},{8,9},{9,8},{10,11... | collective-permute-start | bytes 49160 | tf_op jit(solution)/shard_map/ppermute | solution.py:525
  19.8 0.8 %collective-permute-done.9 = f32[2,2,8,128]{3,2,1,0:T(8,128)S(1)} collective-permute-done((f32[2,2,8,128]{3,2,1,0:T(8,128)S(1)}, f32[2,2,8,128]{3,2,1,0:T(8,128)S(1)}, u32[]{:S(2)}, u32[]{:S(2)}) %collective-permute-start.9) | collective-permute-done | bytes 16416 | tf_op jit(solution)/shard_map/ppermute | solution.py:525
  20.7 2.1 %collective-permute-start.10 = (f32[2,8,128]{2,1,0:T(8,128)S(1)}, f32[2,8,128]{2,1,0:T(8,128)S(1)}, u32[]{:S(2)}, u32[]{:S(2)}) collective-permute-start(f32[2,8,128]{2,1,0:T(8,128)S(1)} %bitcast.13), channel_id=1, source_target_pairs={{0,8},{1,65},{2,10},{3,67},{4,12},{5,69},{6,14},{7,71},{8,0},{9,17... | collective-permute-start | bytes 24584 | tf_op jit(solution)/shard_map/ppermute | solution.py:535
  22.8 0.1 broadcast_in_dim.22
  22.9 1.6 %collective-permute-done.10 = f32[2,8,128]{2,1,0:T(8,128)S(1)} collective-permute-done((f32[2,8,128]{2,1,0:T(8,128)S(1)}, f32[2,8,128]{2,1,0:T(8,128)S(1)}, u32[]{:S(2)}, u32[]{:S(2)}) %collective-permute-start.10) | collective-permute-done | bytes 8224 | tf_op jit(solution)/shard_map/ppermute | solution.py:535
  24.5 0.1 select_multiply_fusion
  24.5 0.3 collective-permute-start.11
  24.8 0.9 %collective-permute-done.11 = f32[2,8,128]{2,1,0:T(8,128)S(1)} collective-permute-done((f32[2,8,128]{2,1,0:T(8,128)S(1)}, f32[2,8,128]{2,1,0:T(8,128)S(1)}, u32[]{:S(2)}, u32[]{:S(2)}) %collective-permute-start.11) | collective-permute-done | bytes 8224 | tf_op jit(solution)/shard_map/ppermute | solution.py:525
  25.7 0.1 reverse_add_fusion.1.chip
  25.8 2.3 %collective-permute-start.13 = (f32[2,8,128]{2,1,0:T(8,128)S(1)}, f32[2,8,128]{2,1,0:T(8,128)S(1)}, u32[]{:S(2)}, u32[]{:S(2)}) collective-permute-start(f32[2,8,128]{2,1,0:T(8,128)S(1)} %reverse_add_fusion.1.chip), channel_id=1, source_target_pairs={{0,6},{1,5},{2,4},{3,7},{4,2},{5,1},{6,0},{7,3},{8,14},{9,13},{10,... | collective-permute-start | bytes 24584 | tf_op jit(solution)/shard_map/ppermute | solution.py:535
  28.1 0.4 %collective-permute-start.12 = (f32[2,8,128]{2,1,0:T(8,128)S(1)}, f32[2,8,128]{2,1,0:T(8,128)S(1)}, u32[]{:S(2)}, u32[]{:S(2)}) collective-permute-start(f32[2,8,128]{2,1,0:T(8,128)S(1)} %reverse_add_fusion.1.chip), channel_id=1, source_target_pairs={{0,2},{1,3},{2,0},{3,1},{4,6},{5,7},{6,4},{7,5},{8,10},{9,11},{10,... | collective-permute-start | bytes 24584 | tf_op jit(solution)/shard_map/ppermute | solution.py:525
  28.5 1.3 %collective-permute-done.13.fetched = f32[2,8,128]{2,1,0:T(8,128)S(1)} collective-permute-done((f32[2,8,128]{2,1,0:T(8,128)S(1)}, f32[2,8,128]{2,1,0:T(8,128)S(1)}, u32[]{:S(2)}, u32[]{:S(2)}) %collective-permute-start.13) | collective-permute-done | bytes 8224 | tf_op jit(solution)/shard_map/ppermute | solution.py:535
  29.8 1.1 %collective-permute-start.14 = (f32[2,8,128]{2,1,0:T(8,128)S(1)}, f32[2,8,128]{2,1,0:T(8,128)S(1)}, u32[]{:S(2)}, u32[]{:S(2)}) collective-permute-start(f32[2,8,128]{2,1,0:T(8,128)S(1)} %collective-permute-done.13.fetched), channel_id=1, source_target_pairs={{0,1},{1,0},{2,3},{3,2},{4,5},{5,4},{6,7},{7,6},{8,9},{9,8},{10,11... | collective-permute-start | bytes 24584 | tf_op jit(solution)/shard_map/ppermute | solution.py:525
  30.9 0.0 collective-permute-done.12.third
  30.9 0.8 %collective-permute-done.14.mated = f32[2,8,128]{2,1,0:T(8,128)S(1)} collective-permute-done((f32[2,8,128]{2,1,0:T(8,128)S(1)}, f32[2,8,128]{2,1,0:T(8,128)S(1)}, u32[]{:S(2)}, u32[]{:S(2)}) %collective-permute-start.14) | collective-permute-done | bytes 8224 | tf_op jit(solution)/shard_map/ppermute | solution.py:525
  31.8 0.6 %column.1 = f32[1,4,1024]{2,1,0:T(4,128)} custom-call(f32[2,8,128]{2,1,0:T(8,128)S(1)} %reverse_add_fusion.1.chip, f32[2,8,128]{2,1,0:T(8,128)S(1)} %collective-permute-done.12.third, f32[2,8,128]{2,1,0:T(8,128)S(1)} %collective-permute-done.13.fetched, f32[2,8,128]{2,1,0:T(8,128)S(1)} %collective-permute-done.14.mated), custom_call_target="tpu_custom_call" | custom-call | flops 20000 | bytes 49152 | tf_op jit(solution)/shard_map/column/pallas_call | solution.py:512
  (6 shorter events, 0.0 us)
Async XLA Ops:
  2.0 9.6 %collective-permute-start.4 = (f32[49,8,128]{2,1,0:T(8,128)S(1)}, f32[49,8,128]{2,1,0:T(8,128)S(1)}, u32[]{:S(2)}, u32[]{:S(2)}) collective-permute-start(f32[49,8,128]{2,1,0:T(8,128)S(1)} %get-tuple-element.32), channel_id=1, source_target_pairs={{0,64},{1,9},{2,66},{3,11},{4,68},{5,13},{6,70},{7,15},{8,72},{9,1... | collective-permute-start | bytes 602120 | tf_op jit(solution)/shard_map/ppermute | solution.py:535
  2.3 9.2 %collective-permute-start.5 = (f32[49,8,128]{2,1,0:T(8,128)S(1)}, f32[49,8,128]{2,1,0:T(8,128)S(1)}, u32[]{:S(2)}, u32[]{:S(2)}) collective-permute-start(f32[49,8,128]{2,1,0:T(8,128)S(1)} %get-tuple-element.33), channel_id=1, source_target_pairs={{0,8},{1,65},{2,10},{3,67},{4,12},{5,69},{6,14},{7,71},{8,0},{9,73... | collective-permute-start | bytes 602120 | tf_op jit(solution)/shard_map/ppermute | solution.py:535
  3.3 6.3 %collective-permute-start = (f32[14,8,128]{2,1,0:T(8,128)S(1)}, f32[14,8,128]{2,1,0:T(8,128)S(1)}, u32[]{:S(2)}, u32[]{:S(2)}) collective-permute-start(f32[14,8,128]{2,1,0:T(8,128)S(1)} %get-tuple-element.21), channel_id=1, source_target_pairs={{0,8},{8,0},{16,24},{24,16},{32,40},{40,32},{48,56},{56,48},{1,9},... | collective-permute-start | bytes 172040 | tf_op jit(solution)/shard_map/ppermute | solution.py:525
  4.8 6.3 %collective-permute-start.1 = (f32[14,8,128]{2,1,0:T(8,128)S(1)}, f32[14,8,128]{2,1,0:T(8,128)S(1)}, u32[]{:S(2)}, u32[]{:S(2)}) collective-permute-start(f32[14,8,128]{2,1,0:T(8,128)S(1)} %get-tuple-element.24), channel_id=1, source_target_pairs={{0,1},{1,0},{2,3},{3,2},{4,5},{5,4},{6,7},{7,6},{8,16},{9,17},{10,... | collective-permute-start | bytes 172040 | tf_op jit(solution)/shard_map/ppermute | solution.py:535
  7.6 3.3 %collective-permute-start.2 = (f32[8,128]{1,0:T(8,128)S(1)}, f32[8,128]{1,0:T(8,128)S(1)}, u32[]{:S(2)}, u32[]{:S(2)}) collective-permute-start(f32[8,128]{1,0:T(8,128)S(1)} %get-tuple-element.25), channel_id=1, source_target_pairs={{0,64},{1,2},{2,1},{3,4},{4,3},{5,6},{6,5},{7,71},{8,72},{9,10},{1... | collective-permute-start | bytes 12296 | tf_op jit(solution)/shard_map/ppermute | solution.py:535
  9.6 1.5 %collective-permute-start.3 = (f32[8,128]{1,0:T(8,128)S(1)}, f32[8,128]{1,0:T(8,128)S(1)}, u32[]{:S(2)}, u32[]{:S(2)}) collective-permute-start(f32[8,128]{1,0:T(8,128)S(1)} %get-tuple-element.26), channel_id=1, source_target_pairs={{0,1},{1,0},{2,3},{3,2},{4,5},{5,4},{6,7},{7,6},{8,9},{9,8},{10,11... | collective-permute-start | bytes 12296 | tf_op jit(solution)/shard_map/ppermute | solution.py:525
  12.0 1.9 %collective-permute-start.6 = (f32[4,2,8,128]{3,2,1,0:T(8,128)S(1)}, f32[4,2,8,128]{3,2,1,0:T(8,128)S(1)}, u32[]{:S(2)}, u32[]{:S(2)}) collective-permute-start(f32[4,2,8,128]{3,2,1,0:T(8,128)S(1)} %get-tuple-element.35), channel_id=1, source_target_pairs={{0,1},{1,0},{2,3},{3,2},{4,5},{5,4},{6,7},{7,6},{8,9},{9,8},{10,11... | collective-permute-start | bytes 98312 | tf_op jit(solution)/shard_map/ppermute | solution.py:525
  13.9 4.1 %collective-permute-start.8 = (f32[2,2,8,128]{3,2,1,0:T(8,128)S(1)}, f32[2,2,8,128]{3,2,1,0:T(8,128)S(1)}, u32[]{:S(2)}, u32[]{:S(2)}) collective-permute-start(f32[2,2,8,128]{3,2,1,0:T(8,128)S(1)} %get-tuple-element.40), channel_id=1, source_target_pairs={{0,64},{1,129},{2,66},{3,131},{4,68},{5,133},{6,70},{7,135},{8,72}... | collective-permute-start | bytes 49160 | tf_op jit(solution)/shard_map/ppermute | solution.py:535
  15.4 2.7 %collective-permute-start.7 = (f32[2,2,8,128]{3,2,1,0:T(8,128)S(1)}, f32[2,2,8,128]{3,2,1,0:T(8,128)S(1)}, u32[]{:S(2)}, u32[]{:S(2)}) collective-permute-start(f32[2,2,8,128]{3,2,1,0:T(8,128)S(1)} %get-tuple-element.38), channel_id=1, source_target_pairs={{0,1},{1,0},{2,3},{3,2},{4,5},{5,4},{6,7},{7,6},{8,9},{9,8},{10,11... | collective-permute-start | bytes 49160 | tf_op jit(solution)/shard_map/ppermute | solution.py:535
  18.2 2.5 %collective-permute-start.9 = (f32[2,2,8,128]{3,2,1,0:T(8,128)S(1)}, f32[2,2,8,128]{3,2,1,0:T(8,128)S(1)}, u32[]{:S(2)}, u32[]{:S(2)}) collective-permute-start(f32[2,2,8,128]{3,2,1,0:T(8,128)S(1)} %select_add_fusion), channel_id=1, source_target_pairs={{0,1},{1,0},{2,3},{3,2},{4,5},{5,4},{6,7},{7,6},{8,9},{9,8},{10,11... | collective-permute-start | bytes 49160 | tf_op jit(solution)/shard_map/ppermute | solution.py:525
  20.7 3.8 %collective-permute-start.10 = (f32[2,8,128]{2,1,0:T(8,128)S(1)}, f32[2,8,128]{2,1,0:T(8,128)S(1)}, u32[]{:S(2)}, u32[]{:S(2)}) collective-permute-start(f32[2,8,128]{2,1,0:T(8,128)S(1)} %bitcast.13), channel_id=1, source_target_pairs={{0,8},{1,65},{2,10},{3,67},{4,12},{5,69},{6,14},{7,71},{8,0},{9,17... | collective-permute-start | bytes 24584 | tf_op jit(solution)/shard_map/ppermute | solution.py:535
  24.5 1.2 %collective-permute-start.11 = (f32[2,8,128]{2,1,0:T(8,128)S(1)}, f32[2,8,128]{2,1,0:T(8,128)S(1)}, u32[]{:S(2)}, u32[]{:S(2)}) collective-permute-start(f32[2,8,128]{2,1,0:T(8,128)S(1)} %select_multiply_fusion), channel_id=1, source_target_pairs={{0,1},{1,0},{2,3},{3,2},{4,5},{5,4},{6,7},{7,6},{8,9},{9,8},{10,11... | collective-permute-start | bytes 24584 | tf_op jit(solution)/shard_map/ppermute | solution.py:525
  25.8 4.0 %collective-permute-start.13 = (f32[2,8,128]{2,1,0:T(8,128)S(1)}, f32[2,8,128]{2,1,0:T(8,128)S(1)}, u32[]{:S(2)}, u32[]{:S(2)}) collective-permute-start(f32[2,8,128]{2,1,0:T(8,128)S(1)} %reverse_add_fusion.1.chip), channel_id=1, source_target_pairs={{0,6},{1,5},{2,4},{3,7},{4,2},{5,1},{6,0},{7,3},{8,14},{9,13},{10,... | collective-permute-start | bytes 24584 | tf_op jit(solution)/shard_map/ppermute | solution.py:535
  28.1 2.8 %collective-permute-start.12 = (f32[2,8,128]{2,1,0:T(8,128)S(1)}, f32[2,8,128]{2,1,0:T(8,128)S(1)}, u32[]{:S(2)}, u32[]{:S(2)}) collective-permute-start(f32[2,8,128]{2,1,0:T(8,128)S(1)} %reverse_add_fusion.1.chip), channel_id=1, source_target_pairs={{0,2},{1,3},{2,0},{3,1},{4,6},{5,7},{6,4},{7,5},{8,10},{9,11},{10,... | collective-permute-start | bytes 24584 | tf_op jit(solution)/shard_map/ppermute | solution.py:525
  29.8 2.0 %collective-permute-start.14 = (f32[2,8,128]{2,1,0:T(8,128)S(1)}, f32[2,8,128]{2,1,0:T(8,128)S(1)}, u32[]{:S(2)}, u32[]{:S(2)}) collective-permute-start(f32[2,8,128]{2,1,0:T(8,128)S(1)} %collective-permute-done.13.fetched), channel_id=1, source_target_pairs={{0,1},{1,0},{2,3},{3,2},{4,5},{5,4},{6,7},{7,6},{8,9},{9,8},{10,11... | collective-permute-start | bytes 24584 | tf_op jit(solution)/shard_map/ppermute | solution.py:525

commit v13 on v11

--- a/solution.py
+++ b/solution.py
@@ -363,7 +363,7 @@
                 out[i, b, e] += add
 
 
-def finish_kernel(first, local, orders, x_a, x_b, field, parts):
+def finish_kernel(first, local, orders, x_a, x_b, field, here, parts):
     pairs = Pairs()
     top = pairs.top
     row, lane = row_in_half(), lanes()
@@ -447,12 +447,12 @@
     near = sum_to_vertices(near, pairs, row, lane)
     outer = sum_to_vertices(outer, pairs, row, lane)
     for z in range(2):
-        parts[0, z] = jnp.where(top, near[0][z], swap(near[1][z]))
+        here[z] = jnp.where(top, near[0][z], swap(near[1][z]))
         ahead = jnp.where(top, swap(near[0][z]), near[1][z])
         behind = jnp.where(top, outer[0][z], swap(outer[1][z]))
-        parts[1, z] = jnp.where(x_even, ahead, behind)
-        parts[2, z] = jnp.where(x_even, behind, ahead)
-        parts[3, z] = jnp.where(top, swap(outer[0][z]), outer[1][z])
+        parts[0, z] = jnp.where(x_even, ahead, behind)
+        parts[1, z] = jnp.where(x_even, behind, ahead)
+        parts[2, z] = jnp.where(top, swap(outer[0][z]), outer[1][z])
 
 
 def unpack_kernel(field, here, smoothed, here_again):
@@ -628,29 +628,29 @@
         (shape(*cells),),
         HALO_COST,
     )
-    field, parts = call(
+    field, here, parts = call(
         finish_kernel,
         "smooth_and_restrict",
         (first, local, held, x_a, x_b),
-        (shape(*cells), shape(4, 2, 8, 128)),
+        (shape(*cells), shape(2, 8, 128), shape(3, 2, 8, 128)),
         5_000_000,
     )
     count = lax.axis_size("gz")
     both = jnp.stack([parts, flip(parts, "gz", 1)])
     first_core = lax.axis_index("gz") % 2 == 0
-    from_two = second_pairs(both[:, 2], "gx")
-    from_one = far_or_beside(jnp.where(first_core, both[:, 1], both[:, 3]))
+    from_two = second_pairs(both[:, 1], "gx")
+    from_one = far_or_beside(jnp.where(first_core, both[:, 0], both[:, 2]))
     smoothed, here = call(
         unpack_kernel,
         "unpack_modes",
-        (field, both[:, 0]),
-        (shape(*rhs.shape), shape(2, 2, 8, 128)),
+        (field, here),
+        (shape(*rhs.shape), shape(2, 8, 128)),
         200_000,
     )
     sums = (
         jnp.where(first_core, 0.0, inside("gx", -1) * inside("gx", 1)) * from_two
         + jnp.where(first_core, 1.0, inside("gx", -2)) * from_one
-        + jnp.where(first_core, 0.0, here)
+        + jnp.stack([here, jnp.zeros_like(here)])
     )
     chip = sums + flip(sums, "gz", 1)[::-1]
     from_beside = both_y_sides(chip[:, :, 4:].reshape(2, 8, 128)).reshape(2, 2, 4, 128)

time: 32.7 us -> 32.7 us (level)
  no operation moved by 1% of the time
where the time goes in v13:
time: 32.7 us; the launch traced here: 32.4 us
  starting transfers between devices  19 us (58%)
  waiting for transfers between devices  7.94 us (24%)
  Pallas kernels  4.57 us (14%)
  between operations  0.69 us (2%)
    ppermute x8, starting transfers between devices, exchange(): return lax.ppermute(value, axes, route)  13.1 us
    ppermute x7, starting transfers between devices, flip(): lax.ppermute(value, axis, [(i, i ^ bits) for i in range(lax.axis_size(axi...  5.85 us
    ppermute x7, waiting for transfers between devices, flip(): lax.ppermute(value, axis, [(i, i ^ bits) for i in range(lax.axis_size(axi...  4.81 us
    pallas_call x7, Pallas kernels, call(): pl.pallas_call(kernel, out_shape=outputs, in_specs=[pl.BlockSpec(memory_s...  4.57 us
    ppermute x8, waiting for transfers between devices, exchange(): return lax.ppermute(value, axes, route)  3.12 us
  transfers between devices with their start and end apart: 15, of which 10 were waited for; matrix products, arithmetic and copies ran while one was open for 0% of the time, Pallas kernels for 7%

profile of v13, /device:TPU:101, one launch (start us, length us, event | category | flops | bytes accessed | tf_op | source)
XLA Modules:
  0.0 32.4 jit_solution(11607240683770910135)
XLA Ops:
  0.6 1.3 %x_traces.1 = (f32[4,7,7,8,128]{4,3,2,1,0:T(8,128)S(1)}, f32[49,8,128]{2,1,0:T(8,128)S(1)}, f32[49,8,128]{2,1,0:T(8,128)S(1)}, s32[1,4,128]{2,1,0:T(4,128)S(1)}) custom-call(f32[7,7,7,1,4,128]{5,4,3,2,1,0:T(4,128)} %rhs_hbm.1, s32[1,4,128]{2,1,0:T(4,128)} %orders_hbm.1), custom_call_target="tpu_custom_call" | custom-call | flops 4000000 | bytes 1910784 | tf_op jit(solution)/shard_map/x_traces/pallas_call | solution.py:511
  2.0 0.3 %collective-permute-start.4 = (f32[49,8,128]{2,1,0:T(8,128)S(1)}, f32[49,8,128]{2,1,0:T(8,128)S(1)}, u32[]{:S(2)}, u32[]{:S(2)}) collective-permute-start(f32[49,8,128]{2,1,0:T(8,128)S(1)} %get-tuple-element.33), channel_id=1, source_target_pairs={{0,64},{1,9},{2,66},{3,11},{4,68},{5,13},{6,70},{7,15},{8,72},{9,1... | collective-permute-start | bytes 602120 | tf_op jit(solution)/shard_map/ppermute | solution.py:534
  2.3 0.8 %collective-permute-start.5 = (f32[49,8,128]{2,1,0:T(8,128)S(1)}, f32[49,8,128]{2,1,0:T(8,128)S(1)}, u32[]{:S(2)}, u32[]{:S(2)}) collective-permute-start(f32[49,8,128]{2,1,0:T(8,128)S(1)} %get-tuple-element.34), channel_id=1, source_target_pairs={{0,8},{1,65},{2,10},{3,67},{4,12},{5,69},{6,14},{7,71},{8,0},{9,73... | collective-permute-start | bytes 602120 | tf_op jit(solution)/shard_map/ppermute | solution.py:534
  3.1 0.3 side_traces.1
  3.3 1.5 %collective-permute-start = (f32[14,8,128]{2,1,0:T(8,128)S(1)}, f32[14,8,128]{2,1,0:T(8,128)S(1)}, u32[]{:S(2)}, u32[]{:S(2)}) collective-permute-start(f32[14,8,128]{2,1,0:T(8,128)S(1)} %get-tuple-element.22), channel_id=1, source_target_pairs={{0,8},{8,0},{16,24},{24,16},{32,40},{40,32},{48,56},{56,48},{1,9},... | collective-permute-start | bytes 172040 | tf_op jit(solution)/shard_map/ppermute | solution.py:524
  4.8 2.8 %collective-permute-start.1 = (f32[14,8,128]{2,1,0:T(8,128)S(1)}, f32[14,8,128]{2,1,0:T(8,128)S(1)}, u32[]{:S(2)}, u32[]{:S(2)}) collective-permute-start(f32[14,8,128]{2,1,0:T(8,128)S(1)} %get-tuple-element.25), channel_id=1, source_target_pairs={{0,1},{1,0},{2,3},{3,2},{4,5},{5,4},{6,7},{7,6},{8,16},{9,17},{10,... | collective-permute-start | bytes 172040 | tf_op jit(solution)/shard_map/ppermute | solution.py:534
  7.6 2.0 %collective-permute-start.2 = (f32[8,128]{1,0:T(8,128)S(1)}, f32[8,128]{1,0:T(8,128)S(1)}, u32[]{:S(2)}, u32[]{:S(2)}) collective-permute-start(f32[8,128]{1,0:T(8,128)S(1)} %get-tuple-element.26), channel_id=1, source_target_pairs={{0,64},{1,2},{2,1},{3,4},{4,3},{5,6},{6,5},{7,71},{8,72},{9,10},{1... | collective-permute-start | bytes 12296 | tf_op jit(solution)/shard_map/ppermute | solution.py:534
  9.6 0.0 collective-permute-done.early
  9.6 0.7 %collective-permute-start.3 = (f32[8,128]{1,0:T(8,128)S(1)}, f32[8,128]{1,0:T(8,128)S(1)}, u32[]{:S(2)}, u32[]{:S(2)}) collective-permute-start(f32[8,128]{1,0:T(8,128)S(1)} %get-tuple-element.27), channel_id=1, source_target_pairs={{0,1},{1,0},{2,3},{3,2},{4,5},{5,4},{6,7},{7,6},{8,9},{9,8},{10,11... | collective-permute-start | bytes 12296 | tf_op jit(solution)/shard_map/ppermute | solution.py:524
  10.3 0.6 %own_cells.1 = (f32[4,7,7,8,128]{4,3,2,1,0:T(8,128)S(1)}, f32[14,8,128]{2,1,0:T(8,128)S(1)}) custom-call(f32[4,7,7,8,128]{4,3,2,1,0:T(8,128)S(1)} %get-tuple-element.21.first, f32[14,8,128]{2,1,0:T(8,128)S(1)} %collective-permute-done.early), custom_call_target="tpu_custom_call" | custom-call | flops 1400000000 | bytes 1720320 | tf_op jit(solution)/shard_map/own_cells/pallas_call | solution.py:511
  10.8 0.1 collective-permute-done.2.z_b
  10.9 0.2 collective-permute-done.3.z_a
  11.1 0.0 collective-permute-done.1.y_b
  11.1 0.4 %side_halo.1.local = f32[4,7,7,8,128]{4,3,2,1,0:T(8,128)S(1)} custom-call(f32[4,7,7,8,128]{4,3,2,1,0:T(8,128)S(1)} %get-tuple-element.23.local, f32[14,8,128]{2,1,0:T(8,128)S(1)} %get-tuple-element.24.y_a, f32[14,8,128]{2,1,0:T(8,128)S(1)} %collective-permute-done.1.y_b, f32[8,128]{1,0:T(8,128)S(1)} %collective-permute-done.2.z_b, ...), custom_call_target="tpu_custom_call" | custom-call | flops 4000000 | bytes 2646016 | tf_op jit(solution)/shard_map/side_halo/pallas_call | solution.py:511
  11.5 0.0 collective-permute-done.4.x_a
  11.5 0.0 collective-permute-done.5.x_b
  11.5 0.4 %smooth_and_restrict.1 = (f32[4,7,7,8,128]{4,3,2,1,0:T(8,128)S(1)}, f32[2,8,128]{2,1,0:T(8,128)S(1)}, f32[3,2,8,128]{3,2,1,0:T(8,128)S(1)}) custom-call(f32[4,7,7,8,128]{4,3,2,1,0:T(8,128)S(1)} %get-tuple-element.21.first, f32[4,7,7,8,128]{4,3,2,1,0:T(8,128)S(1)} %side_halo.1.local, s32[1,4,128]{2,1,0:T(4,128)S(1)} %get-tuple-element.32.orders, ...), custom_call_target="tpu_custom_call" | custom-call | flops 5000000 | bytes 2844672 | tf_op jit(solution)/shard_map/smooth_and_restrict/pallas_call | solution.py:511
  12.0 1.0 %collective-permute-start.6 = (f32[3,2,8,128]{3,2,1,0:T(8,128)S(1)}, f32[3,2,8,128]{3,2,1,0:T(8,128)S(1)}, u32[]{:S(2)}, u32[]{:S(2)}) collective-permute-start(f32[3,2,8,128]{3,2,1,0:T(8,128)S(1)} %get-tuple-element.38), channel_id=1, source_target_pairs={{0,1},{1,0},{2,3},{3,2},{4,5},{5,4},{6,7},{7,6},{8,9},{9,8},{10,11... | collective-permute-start | bytes 73736 | tf_op jit(solution)/shard_map/ppermute | solution.py:524
  13.0 0.8 %collective-permute-done.6 = f32[3,2,8,128]{3,2,1,0:T(8,128)S(1)} collective-permute-done((f32[3,2,8,128]{3,2,1,0:T(8,128)S(1)}, f32[3,2,8,128]{3,2,1,0:T(8,128)S(1)}, u32[]{:S(2)}, u32[]{:S(2)}) %collective-permute-start.6) | collective-permute-done | bytes 24608 | tf_op jit(solution)/shard_map/ppermute | solution.py:524
  13.9 1.5 %collective-permute-start.8 = (f32[2,2,8,128]{3,2,1,0:T(8,128)S(1)}, f32[2,2,8,128]{3,2,1,0:T(8,128)S(1)}, u32[]{:S(2)}, u32[]{:S(2)}) collective-permute-start(f32[2,2,8,128]{3,2,1,0:T(8,128)S(1)} %get-tuple-element.41), channel_id=1, source_target_pairs={{0,64},{1,129},{2,66},{3,131},{4,68},{5,133},{6,70},{7,135},{8,72}... | collective-permute-start | bytes 49160 | tf_op jit(solution)/shard_map/ppermute | solution.py:534
  15.4 1.2 %collective-permute-start.7 = (f32[2,2,8,128]{3,2,1,0:T(8,128)S(1)}, f32[2,2,8,128]{3,2,1,0:T(8,128)S(1)}, u32[]{:S(2)}, u32[]{:S(2)}) collective-permute-start(f32[2,2,8,128]{3,2,1,0:T(8,128)S(1)} %get-tuple-element.40), channel_id=1, source_target_pairs={{0,1},{1,0},{2,3},{3,2},{4,5},{5,4},{6,7},{7,6},{8,9},{9,8},{10,11... | collective-permute-start | bytes 49160 | tf_op jit(solution)/shard_map/ppermute | solution.py:534
  16.6 0.9 %unpack_modes.1 = (f32[7,7,7,1,4,128]{5,4,3,2,1,0:T(4,128)}, f32[2,8,128]{2,1,0:T(8,128)S(1)}) custom-call(f32[4,7,7,8,128]{4,3,2,1,0:T(8,128)S(1)} %get-tuple-element.35.field, f32[2,8,128]{2,1,0:T(8,128)S(1)} %get-tuple-element.36.here), custom_call_target="tpu_custom_call" | custom-call | flops 200000 | bytes 1521664 | tf_op jit(solution)/shard_map/unpack_modes/pallas_call | solution.py:511
  17.5 0.4 %collective-permute-done.8 = f32[2,2,8,128]{3,2,1,0:T(8,128)S(1)} collective-permute-done((f32[2,2,8,128]{3,2,1,0:T(8,128)S(1)}, f32[2,2,8,128]{3,2,1,0:T(8,128)S(1)}, u32[]{:S(2)}, u32[]{:S(2)}) %collective-permute-start.8) | collective-permute-done | bytes 16416 | tf_op jit(solution)/shard_map/ppermute | solution.py:534
  18.0 0.2 collective-permute-done.7
  18.1 1.6 %collective-permute-start.9 = (f32[2,2,8,128]{3,2,1,0:T(8,128)S(1)}, f32[2,2,8,128]{3,2,1,0:T(8,128)S(1)}, u32[]{:S(2)}, u32[]{:S(2)}) collective-permute-start(f32[2,2,8,128]{3,2,1,0:T(8,128)S(1)} %pad_add_fusion), channel_id=1, source_target_pairs={{0,1},{1,0},{2,3},{3,2},{4,5},{5,4},{6,7},{7,6},{8,9},{9,8},{10,11... | collective-permute-start | bytes 49160 | tf_op jit(solution)/shard_map/ppermute | solution.py:524
  19.8 0.8 %collective-permute-done.9 = f32[2,2,8,128]{3,2,1,0:T(8,128)S(1)} collective-permute-done((f32[2,2,8,128]{3,2,1,0:T(8,128)S(1)}, f32[2,2,8,128]{3,2,1,0:T(8,128)S(1)}, u32[]{:S(2)}, u32[]{:S(2)}) %collective-permute-start.9) | collective-permute-done | bytes 16416 | tf_op jit(solution)/shard_map/ppermute | solution.py:524
  20.6 2.1 %collective-permute-start.10 = (f32[2,8,128]{2,1,0:T(8,128)S(1)}, f32[2,8,128]{2,1,0:T(8,128)S(1)}, u32[]{:S(2)}, u32[]{:S(2)}) collective-permute-start(f32[2,8,128]{2,1,0:T(8,128)S(1)} %bitcast.13), channel_id=1, source_target_pairs={{0,8},{1,65},{2,10},{3,67},{4,12},{5,69},{6,14},{7,71},{8,0},{9,17... | collective-permute-start | bytes 24584 | tf_op jit(solution)/shard_map/ppermute | solution.py:534
  22.8 0.1 broadcast_in_dim.17
  22.9 1.6 %collective-permute-done.10 = f32[2,8,128]{2,1,0:T(8,128)S(1)} collective-permute-done((f32[2,8,128]{2,1,0:T(8,128)S(1)}, f32[2,8,128]{2,1,0:T(8,128)S(1)}, u32[]{:S(2)}, u32[]{:S(2)}) %collective-permute-start.10) | collective-permute-done | bytes 8224 | tf_op jit(solution)/shard_map/ppermute | solution.py:534
  24.4 0.1 select_multiply_fusion
  24.5 0.3 collective-permute-start.11
  24.8 0.9 %collective-permute-done.11 = f32[2,8,128]{2,1,0:T(8,128)S(1)} collective-permute-done((f32[2,8,128]{2,1,0:T(8,128)S(1)}, f32[2,8,128]{2,1,0:T(8,128)S(1)}, u32[]{:S(2)}, u32[]{:S(2)}) %collective-permute-start.11) | collective-permute-done | bytes 8224 | tf_op jit(solution)/shard_map/ppermute | solution.py:524
  25.7 0.1 reverse_add_fusion.1.chip
  25.8 2.3 %collective-permute-start.13 = (f32[2,8,128]{2,1,0:T(8,128)S(1)}, f32[2,8,128]{2,1,0:T(8,128)S(1)}, u32[]{:S(2)}, u32[]{:S(2)}) collective-permute-start(f32[2,8,128]{2,1,0:T(8,128)S(1)} %reverse_add_fusion.1.chip), channel_id=1, source_target_pairs={{0,2},{1,5},{2,0},{3,7},{4,6},{5,1},{6,4},{7,3},{8,10},{9,13},{10,... | collective-permute-start | bytes 24584 | tf_op jit(solution)/shard_map/ppermute | solution.py:534
  28.1 0.8 %collective-permute-start.12 = (f32[2,8,128]{2,1,0:T(8,128)S(1)}, f32[2,8,128]{2,1,0:T(8,128)S(1)}, u32[]{:S(2)}, u32[]{:S(2)}) collective-permute-start(f32[2,8,128]{2,1,0:T(8,128)S(1)} %reverse_add_fusion.1.chip), channel_id=1, source_target_pairs={{0,6},{1,7},{2,4},{3,5},{4,2},{5,3},{6,0},{7,1},{8,14},{9,15},{10,... | collective-permute-start | bytes 24584 | tf_op jit(solution)/shard_map/ppermute | solution.py:524
  28.9 0.9 %collective-permute-done.13.fetched = f32[2,8,128]{2,1,0:T(8,128)S(1)} collective-permute-done((f32[2,8,128]{2,1,0:T(8,128)S(1)}, f32[2,8,128]{2,1,0:T(8,128)S(1)}, u32[]{:S(2)}, u32[]{:S(2)}) %collective-permute-start.13) | collective-permute-done | bytes 8224 | tf_op jit(solution)/shard_map/ppermute | solution.py:534
  29.8 0.0 collective-permute-start.14
  29.8 2.0 %collective-permute-done.12.third = f32[2,8,128]{2,1,0:T(8,128)S(1)} collective-permute-done((f32[2,8,128]{2,1,0:T(8,128)S(1)}, f32[2,8,128]{2,1,0:T(8,128)S(1)}, u32[]{:S(2)}, u32[]{:S(2)}) %collective-permute-start.12) | collective-permute-done | bytes 8224 | tf_op jit(solution)/shard_map/ppermute | solution.py:524
  31.8 0.0 collective-permute-done.14.mated
  31.8 0.6 %column.1 = f32[1,4,1024]{2,1,0:T(4,128)} custom-call(f32[2,8,128]{2,1,0:T(8,128)S(1)} %reverse_add_fusion.1.chip, f32[2,8,128]{2,1,0:T(8,128)S(1)} %collective-permute-done.12.third, f32[2,8,128]{2,1,0:T(8,128)S(1)} %collective-permute-done.13.fetched, f32[2,8,128]{2,1,0:T(8,128)S(1)} %collective-permute-done.14.mated), custom_call_target="tpu_custom_call" | custom-call | flops 20000 | bytes 49152 | tf_op jit(solution)/shard_map/column/pallas_call | solution.py:511
  (6 shorter events, 0.0 us)
Async XLA Ops:
  2.0 9.6 %collective-permute-start.4 = (f32[49,8,128]{2,1,0:T(8,128)S(1)}, f32[49,8,128]{2,1,0:T(8,128)S(1)}, u32[]{:S(2)}, u32[]{:S(2)}) collective-permute-start(f32[49,8,128]{2,1,0:T(8,128)S(1)} %get-tuple-element.33), channel_id=1, source_target_pairs={{0,64},{1,9},{2,66},{3,11},{4,68},{5,13},{6,70},{7,15},{8,72},{9,1... | collective-permute-start | bytes 602120 | tf_op jit(solution)/shard_map/ppermute | solution.py:534
  2.3 9.2 %collective-permute-start.5 = (f32[49,8,128]{2,1,0:T(8,128)S(1)}, f32[49,8,128]{2,1,0:T(8,128)S(1)}, u32[]{:S(2)}, u32[]{:S(2)}) collective-permute-start(f32[49,8,128]{2,1,0:T(8,128)S(1)} %get-tuple-element.34), channel_id=1, source_target_pairs={{0,8},{1,65},{2,10},{3,67},{4,12},{5,69},{6,14},{7,71},{8,0},{9,73... | collective-permute-start | bytes 602120 | tf_op jit(solution)/shard_map/ppermute | solution.py:534
  3.3 6.3 %collective-permute-start = (f32[14,8,128]{2,1,0:T(8,128)S(1)}, f32[14,8,128]{2,1,0:T(8,128)S(1)}, u32[]{:S(2)}, u32[]{:S(2)}) collective-permute-start(f32[14,8,128]{2,1,0:T(8,128)S(1)} %get-tuple-element.22), channel_id=1, source_target_pairs={{0,8},{8,0},{16,24},{24,16},{32,40},{40,32},{48,56},{56,48},{1,9},... | collective-permute-start | bytes 172040 | tf_op jit(solution)/shard_map/ppermute | solution.py:524
  4.8 6.3 %collective-permute-start.1 = (f32[14,8,128]{2,1,0:T(8,128)S(1)}, f32[14,8,128]{2,1,0:T(8,128)S(1)}, u32[]{:S(2)}, u32[]{:S(2)}) collective-permute-start(f32[14,8,128]{2,1,0:T(8,128)S(1)} %get-tuple-element.25), channel_id=1, source_target_pairs={{0,1},{1,0},{2,3},{3,2},{4,5},{5,4},{6,7},{7,6},{8,16},{9,17},{10,... | collective-permute-start | bytes 172040 | tf_op jit(solution)/shard_map/ppermute | solution.py:534
  7.6 3.3 %collective-permute-start.2 = (f32[8,128]{1,0:T(8,128)S(1)}, f32[8,128]{1,0:T(8,128)S(1)}, u32[]{:S(2)}, u32[]{:S(2)}) collective-permute-start(f32[8,128]{1,0:T(8,128)S(1)} %get-tuple-element.26), channel_id=1, source_target_pairs={{0,64},{1,2},{2,1},{3,4},{4,3},{5,6},{6,5},{7,71},{8,72},{9,10},{1... | collective-permute-start | bytes 12296 | tf_op jit(solution)/shard_map/ppermute | solution.py:534
  9.6 1.5 %collective-permute-start.3 = (f32[8,128]{1,0:T(8,128)S(1)}, f32[8,128]{1,0:T(8,128)S(1)}, u32[]{:S(2)}, u32[]{:S(2)}) collective-permute-start(f32[8,128]{1,0:T(8,128)S(1)} %get-tuple-element.27), channel_id=1, source_target_pairs={{0,1},{1,0},{2,3},{3,2},{4,5},{5,4},{6,7},{7,6},{8,9},{9,8},{10,11... | collective-permute-start | bytes 12296 | tf_op jit(solution)/shard_map/ppermute | solution.py:524
  12.0 1.9 %collective-permute-start.6 = (f32[3,2,8,128]{3,2,1,0:T(8,128)S(1)}, f32[3,2,8,128]{3,2,1,0:T(8,128)S(1)}, u32[]{:S(2)}, u32[]{:S(2)}) collective-permute-start(f32[3,2,8,128]{3,2,1,0:T(8,128)S(1)} %get-tuple-element.38), channel_id=1, source_target_pairs={{0,1},{1,0},{2,3},{3,2},{4,5},{5,4},{6,7},{7,6},{8,9},{9,8},{10,11... | collective-permute-start | bytes 73736 | tf_op jit(solution)/shard_map/ppermute | solution.py:524
  13.9 4.1 %collective-permute-start.8 = (f32[2,2,8,128]{3,2,1,0:T(8,128)S(1)}, f32[2,2,8,128]{3,2,1,0:T(8,128)S(1)}, u32[]{:S(2)}, u32[]{:S(2)}) collective-permute-start(f32[2,2,8,128]{3,2,1,0:T(8,128)S(1)} %get-tuple-element.41), channel_id=1, source_target_pairs={{0,64},{1,129},{2,66},{3,131},{4,68},{5,133},{6,70},{7,135},{8,72}... | collective-permute-start | bytes 49160 | tf_op jit(solution)/shard_map/ppermute | solution.py:534
  15.4 2.7 %collective-permute-start.7 = (f32[2,2,8,128]{3,2,1,0:T(8,128)S(1)}, f32[2,2,8,128]{3,2,1,0:T(8,128)S(1)}, u32[]{:S(2)}, u32[]{:S(2)}) collective-permute-start(f32[2,2,8,128]{3,2,1,0:T(8,128)S(1)} %get-tuple-element.40), channel_id=1, source_target_pairs={{0,1},{1,0},{2,3},{3,2},{4,5},{5,4},{6,7},{7,6},{8,9},{9,8},{10,11... | collective-permute-start | bytes 49160 | tf_op jit(solution)/shard_map/ppermute | solution.py:534
  18.1 2.5 %collective-permute-start.9 = (f32[2,2,8,128]{3,2,1,0:T(8,128)S(1)}, f32[2,2,8,128]{3,2,1,0:T(8,128)S(1)}, u32[]{:S(2)}, u32[]{:S(2)}) collective-permute-start(f32[2,2,8,128]{3,2,1,0:T(8,128)S(1)} %pad_add_fusion), channel_id=1, source_target_pairs={{0,1},{1,0},{2,3},{3,2},{4,5},{5,4},{6,7},{7,6},{8,9},{9,8},{10,11... | collective-permute-start | bytes 49160 | tf_op jit(solution)/shard_map/ppermute | solution.py:524
  20.6 3.8 %collective-permute-start.10 = (f32[2,8,128]{2,1,0:T(8,128)S(1)}, f32[2,8,128]{2,1,0:T(8,128)S(1)}, u32[]{:S(2)}, u32[]{:S(2)}) collective-permute-start(f32[2,8,128]{2,1,0:T(8,128)S(1)} %bitcast.13), channel_id=1, source_target_pairs={{0,8},{1,65},{2,10},{3,67},{4,12},{5,69},{6,14},{7,71},{8,0},{9,17... | collective-permute-start | bytes 24584 | tf_op jit(solution)/shard_map/ppermute | solution.py:534
  24.5 1.2 %collective-permute-start.11 = (f32[2,8,128]{2,1,0:T(8,128)S(1)}, f32[2,8,128]{2,1,0:T(8,128)S(1)}, u32[]{:S(2)}, u32[]{:S(2)}) collective-permute-start(f32[2,8,128]{2,1,0:T(8,128)S(1)} %select_multiply_fusion), channel_id=1, source_target_pairs={{0,1},{1,0},{2,3},{3,2},{4,5},{5,4},{6,7},{7,6},{8,9},{9,8},{10,11... | collective-permute-start | bytes 24584 | tf_op jit(solution)/shard_map/ppermute | solution.py:524
  25.8 4.0 %collective-permute-start.13 = (f32[2,8,128]{2,1,0:T(8,128)S(1)}, f32[2,8,128]{2,1,0:T(8,128)S(1)}, u32[]{:S(2)}, u32[]{:S(2)}) collective-permute-start(f32[2,8,128]{2,1,0:T(8,128)S(1)} %reverse_add_fusion.1.chip), channel_id=1, source_target_pairs={{0,2},{1,5},{2,0},{3,7},{4,6},{5,1},{6,4},{7,3},{8,10},{9,13},{10,... | collective-permute-start | bytes 24584 | tf_op jit(solution)/shard_map/ppermute | solution.py:534
  28.1 3.7 %collective-permute-start.12 = (f32[2,8,128]{2,1,0:T(8,128)S(1)}, f32[2,8,128]{2,1,0:T(8,128)S(1)}, u32[]{:S(2)}, u32[]{:S(2)}) collective-permute-start(f32[2,8,128]{2,1,0:T(8,128)S(1)} %reverse_add_fusion.1.chip), channel_id=1, source_target_pairs={{0,6},{1,7},{2,4},{3,5},{4,2},{5,3},{6,0},{7,1},{8,14},{9,15},{10,... | collective-permute-start | bytes 24584 | tf_op jit(solution)/shard_map/ppermute | solution.py:524
  29.8 2.0 %collective-permute-start.14 = (f32[2,8,128]{2,1,0:T(8,128)S(1)}, f32[2,8,128]{2,1,0:T(8,128)S(1)}, u32[]{:S(2)}, u32[]{:S(2)}) collective-permute-start(f32[2,8,128]{2,1,0:T(8,128)S(1)} %collective-permute-done.13.fetched), channel_id=1, source_target_pairs={{0,1},{1,0},{2,3},{3,2},{4,5},{5,4},{6,7},{7,6},{8,9},{9,8},{10,11... | collective-permute-start | bytes 24584 | tf_op jit(solution)/shard_map/ppermute | solution.py:524
